TPU v7x, 32 devices: a whole 2x2x4 slice. The times are simulated.
32 devices in a mesh: row: 4 (over z), col: 8 (over y, x, core).
Axes of the slice: x: 2, y: 2, z: 4, core: 2. Of those that a mesh axis runs over, the one named last changes fastest.
Arguments:
- density: float32 [8192, 8192], P('row', 'col'), may hold values from -0.01171875 to 0.01171875
- h_core: float32 [8192, 8192], P('row', 'col'), may hold values from -6 to 6
- phi: float32 [64, 1024, 512], P(('row', 'col')), may hold values from -6 to 6
- v_ext: float32 [64, 1024], P(('row', 'col')), may hold values from -6 to 6
- tile_blocks: int32 [64, 4], replicated, may hold values from 0 to 63, as said below
- tile_count: int32 [64], replicated, may hold values from 3 to 4
Outputs:
- hamiltonian: float32 [8192, 8192], P('row', 'col')
- dm_ham: float32 [8192, 8192], P('row', 'col')
Inputs may be any that keep to these rules, and one draw needn't show every extreme that they name: Tile t belongs to device t // 2, devices counted as row index * col size + col index. Over all slots of one device's 2 tiles, the numbers tile_blocks // 8 are all different; within one tile the numbers tile_blocks // 16 are all different. So every device gets at most one live block pair of its tiles from any one device, and on some draws a device pair does exchange exactly one such pair.
All inputs are finite; a program needn't handle non-finite values.
Results may differ from a plain program's by a relative error of at most 0.004.
Values may be sent and summed in bfloat16 or wider, within the bound.
No kernel may reach another device: no remote copies, remote signals or barrier semaphores. Data moves between devices by JAX's collectives and lax.ppermute only.
A program may use at most 192 MiB of HBM per device.

v0:
```python
import jax
import jax.numpy as jnp
from jax import lax
from jax.sharding import PartitionSpec as P

BLK = 128


cube_coef = 0.5
cell_volume = 0.03125


def body(density, h_core, phi, v_ext, tile_blocks, tile_count):
    nrow = lax.axis_size("row")
    ncol = lax.axis_size("col")
    ndev = nrow * ncol
    row_idx = lax.axis_index("row")
    col_idx = lax.axis_index("col")
    myself = row_idx * ncol + col_idx
    rows_loc, cols_loc = density.shape
    width = BLK
    rowb = rows_loc // width
    colb = cols_loc // width
    tdev, npts, local = phi.shape
    maxb = tile_blocks.shape[1]
    blocks = tile_blocks.reshape(ndev, tdev, maxb)
    counts = tile_count.reshape(ndev, tdev)
    slot_live = jnp.arange(maxb, dtype=jnp.int32)[None, None, :] < counts[:, :, None]
    holder = (blocks // rowb)[:, :, :, None] * ncol + (blocks // colb)[:, :, None, :]
    pair_live = slot_live[:, :, :, None] & slot_live[:, :, None, :]
    row_block = jnp.broadcast_to(blocks[:, :, :, None], holder.shape).reshape(ndev, -1)
    col_block = jnp.broadcast_to(blocks[:, :, None, :], holder.shape).reshape(ndev, -1)
    match = (pair_live & (holder == myself)).reshape(ndev, -1)
    present = jnp.any(match, axis=1)
    match_int = match.astype(jnp.int32)
    row_pick = jnp.sum(match_int * row_block, axis=1) - row_idx * rowb
    col_pick = jnp.sum(match_int * col_block, axis=1) - col_idx * colb
    row_pick = jnp.where(present, row_pick, 0)
    col_pick = jnp.where(present, col_pick, 0)
    dm_tiles = density.reshape(rowb, width, colb, width)
    outgoing = dm_tiles[row_pick, :, col_pick, :] * present[:, None, None].astype(jnp.float32)
    incoming = lax.all_to_all(outgoing, ("row", "col"), split_axis=0, concat_axis=0, tiled=True)
    own_holder = lax.dynamic_index_in_dim(holder, myself, 0, keepdims=False)
    own_live = lax.dynamic_index_in_dim(pair_live, myself, 0, keepdims=False)
    own_slots = lax.dynamic_index_in_dim(slot_live, myself, 0, keepdims=False)
    local_dm = incoming[own_holder] * own_live[:, :, :, None, None].astype(jnp.float32)
    local_dm = local_dm.transpose(0, 1, 3, 2, 4).reshape(tdev, local, local)
    column_live = jnp.repeat(own_slots, width, axis=1).astype(jnp.float32)
    masked = phi * column_live[:, None, :]
    spread = jnp.einsum(
        "tgk,tkl->tgl",
        masked,
        local_dm,
        precision=lax.Precision.HIGHEST,
        preferred_element_type=jnp.float32,
    )
    rho = jnp.sum(spread * masked, axis=2)
    potential = v_ext + rho + cube_coef * rho * rho * rho
    weighted = masked * potential[:, :, None]
    local_ham = cell_volume * jnp.einsum(
        "tgk,tgl->tkl",
        weighted,
        masked,
        precision=lax.Precision.HIGHEST,
        preferred_element_type=jnp.float32,
    )
    ham_pieces = (
        local_ham.reshape(tdev, maxb, width, maxb, width)
        .transpose(0, 1, 3, 2, 4)
        .reshape(-1, width, width)
    )
    npairs = ham_pieces.shape[0]
    chosen = (
        own_holder.reshape(-1)[None, :] == jnp.arange(ndev, dtype=jnp.int32)[:, None]
    ) & own_live.reshape(-1)[None, :]
    found = jnp.any(chosen, axis=1)
    pick = jnp.sum(chosen.astype(jnp.int32) * jnp.arange(npairs, dtype=jnp.int32)[None, :], axis=1)
    returning = ham_pieces[pick] * found[:, None, None].astype(jnp.float32)
    arriving = lax.all_to_all(returning, ("row", "col"), split_axis=0, concat_axis=0, tiled=True)
    target = row_pick * colb + col_pick
    weights = (
        (jnp.arange(rowb * colb, dtype=jnp.int32)[:, None] == target[None, :]) & present[None, :]
    ).astype(jnp.float32)
    summed = jnp.einsum(
        "qs,sxy->qxy",
        weights,
        arriving,
        precision=lax.Precision.HIGHEST,
        preferred_element_type=jnp.float32,
    )
    hamiltonian = h_core + summed.reshape(rowb, colb, width, width).transpose(0, 2, 1, 3).reshape(
        rows_loc, cols_loc
    )
    ham_low = hamiltonian.astype(jnp.bfloat16)
    dm_low = density.astype(jnp.bfloat16)
    ham_cols = lax.all_gather(ham_low, "row", axis=0, tiled=True)
    dm_ham = jnp.dot(
        lax.all_gather(dm_low, "col", axis=1, tiled=True),
        ham_cols,
        preferred_element_type=jnp.float32,
    )
    return (hamiltonian, dm_ham)


def solution(mesh):
    placed = (
        P("row", "col"),
        P("row", "col"),
        P(("row", "col"), None, None),
        P(("row", "col"), None),
        P(),
        P(),
    )
    return jax.shard_map(
        body,
        mesh=mesh,
        in_specs=placed,
        out_specs=(P("row", "col"), P("row", "col")),
        check_vma=False,
    )
```

profile of v0, /device:TPU:0, one launch (start us, length us, event | category | flops | bytes accessed | tf_op | source)
XLA Modules:
  0.0 702.0 jit_solution(13120362545342289840)
XLA Ops:
  7.2 0.7 lt.75
  8.3 0.8 copy.48
  9.1 0.1 fusion.16
  9.2 1.4 select_reduce_fusion
  10.7 0.7 reduce_or.18
  11.4 5.5 copy.61
  16.9 4.9 copy.50
  21.9 4.1 gather_fusion
  26.0 1.5 broadcast_multiply_fusion.1
  27.5 7.6 %all-to-all-start = ((f32[32,128,128]{2,1,0:T(8,128)}), f32[32,128,128]{2,1,0:T(8,128)}, u32[]{:S(2)}, u32[]{:S(2)}) async-start(f32[32,128,128]{2,1,0:T(8,128)} %broadcast_multiply_fusion.1), calls=%async_computation | async-start | bytes 4194304 | tf_op jit(solution)/shard_map/all_to_all | solution.py:42
  35.4 5.4 copy.49
  40.8 43.2 %all-to-all-done = f32[32,128,128]{2,1,0:T(8,128)} async-done(((f32[32,128,128]{2,1,0:T(8,128)}), f32[32,128,128]{2,1,0:T(8,128)}, u32[]{:S(2)}, u32[]{:S(2)}) %all-to-all-start) | async-done | bytes 2097184 | tf_op jit(solution)/shard_map/all_to_all | solution.py:42
  84.0 2.3 gather_fusion.1
  86.3 1.5 multiply_bitcast_fusion
  87.8 2.0 copy.51
  89.8 1.8 reshape.241
  91.7 10.5 %multiply_reduce_fusion = f32[2,1024]{1,0:T(2,128)S(1)} fusion(f32[2,1024,512]{1,2,0:T(8,128)} %copy.49, f32[2,512,512]{1,2,0:T(8,128)} %reshape.241, f32[2,512]{1,0:T(2,128)S(1)} %bitcast.63), kind=kOutput, calls=%fused_computation.7 | convolution fusion | flops 6446643200 | bytes 6303744 | tf_op jit(solution)/shard_map/tgk,tkl->tgl/dot_general | solution.py:50
  102.3 7.3 %fusion.11 = f32[2,512,512]{2,1,0:T(8,128)S(1)} fusion(f32[2,1024,512]{1,2,0:T(8,128)S(1)} %copy-done, f32[2,512]{1,0:T(2,128)S(1)} %bitcast.64, f32[2,1024]{1,0:T(2,128)S(1)} %fusion.22), kind=kOutput, calls=%fused_computation.17 | convolution fusion | flops 6446120960 | bytes 6303744 | tf_op jit(solution)/shard_map/tgk,tgl->tkl/dot_general | solution.py:60
  109.5 1.9 reshape.242
  111.5 3.2 copy.54
  114.7 2.3 gather_fusion.2
  117.0 1.5 broadcast_multiply_fusion
  118.5 4.0 all-to-all-start.1
  122.6 48.8 %all-to-all-done.1 = f32[32,128,128]{2,1,0:T(8,128)S(1)} async-done(((f32[32,128,128]{2,1,0:T(8,128)}), f32[32,128,128]{2,1,0:T(8,128)S(1)}, u32[]{:S(2)}, u32[]{:S(2)}) %all-to-all-start.1) | async-done | bytes 2097184 | tf_op jit(solution)/shard_map/all_to_all | solution.py:79
  171.4 4.4 convolution_bitcast_fusion.1
  175.8 4.2 copy.56
  180.1 13.8 %fusion.33 = (bf16[2048,1024]{1,0:T(8,128)(2,1)}, f32[2048,1024]{1,0:T(8,128)}) fusion(f32[2048,1024]{1,0:T(8,128)} %param.7, f32[256,8,8,128]{3,2,1,0:T(8,128)} %bitcast.56), kind=kLoop, calls=%fused_computation.69 | loop fusion | flops 4194304 | bytes 29360128 | tf_op jit(solution)/shard_map/convert_element_type | solution.py:94
  193.9 6.1 convert_element_type.58
  200.0 280.2 %all-gather.3.cloned.1.call-done = bf16[8192,1024]{1,0:T(8,128)(2,1)} async-done(((bf16[2048,1024]{1,0:T(8,128)(2,1)}), bf16[8192,1024]{1,0:T(8,128)(2,1)}) %all-gather.3.cloned.1.call-update) | async-done | bytes 16777232 | tf_op jit(solution)/shard_map/all_gather | solution.py:96
  480.2 161.5 %all-gather.5.cloned.1.call-done = bf16[2048,8192]{1,0:T(8,128)(2,1)} async-done(((bf16[2048,1024]{1,0:T(8,128)(2,1)}), bf16[2048,8192]{1,0:T(8,128)(2,1)}) %all-gather.5.cloned.1.call-update) | async-done | bytes 33554448 | tf_op jit(solution)/shard_map/all_gather | solution.py:98
  641.7 43.7 %convolution_bitcast_fusion = f32[2048,1024]{0,1:T(8,128)} fusion(bf16[8192,1024]{1,0:T(8,128)(2,1)} %all-gather.3.cloned.1.call-done, bf16[2048,8192]{1,0:T(8,128)(2,1)} %all-gather.5.cloned.1.call-done), kind=kOutput, calls=%fused_computation.6 | convolution fusion | flops 34359738368 | bytes 58720256 | tf_op jit(solution)/shard_map/dot_general | solution.py:97
  685.5 9.2 %copy.57 = f32[2048,1024]{1,0:T(8,128)} copy(f32[2048,1024]{0,1:T(8,128)} %convolution_bitcast_fusion) | data formatting | bytes 16777216
  (27 shorter events, 1.0 us)
Async XLA Ops:
  27.5 56.5 %all-to-all-start = ((f32[32,128,128]{2,1,0:T(8,128)}), f32[32,128,128]{2,1,0:T(8,128)}, u32[]{:S(2)}, u32[]{:S(2)}) async-start(f32[32,128,128]{2,1,0:T(8,128)} %broadcast_multiply_fusion.1), calls=%async_computation | async-start | bytes 4194304 | tf_op jit(solution)/shard_map/all_to_all | solution.py:42
  91.7 10.6 %copy-start.1 = (f32[2,1024]{1,0:T(2,128)S(1)}, f32[2,1024]{1,0:T(2,128)}, u32[]{:S(2)}) copy-start(f32[2,1024]{1,0:T(2,128)} %param.9) | copy-start | bytes 24580
  91.7 10.6 %copy-start = (f32[2,1024,512]{1,2,0:T(8,128)S(1)}, f32[2,1024,512]{1,2,0:T(8,128)}, u32[]{:S(2)}) copy-start(f32[2,1024,512]{1,2,0:T(8,128)} %copy.49) | copy-start | bytes 12582916
  118.5 52.9 %all-to-all-start.1 = ((f32[32,128,128]{2,1,0:T(8,128)}), f32[32,128,128]{2,1,0:T(8,128)S(1)}, u32[]{:S(2)}, u32[]{:S(2)}) async-start(f32[32,128,128]{2,1,0:T(8,128)} %broadcast_multiply_fusion), calls=%async_computation.1 | async-start | bytes 4194304 | tf_op jit(solution)/shard_map/all_to_all | solution.py:79
  122.5 357.7 %all-gather.3.cloned.1.call-start = ((), (), s32[]{:S(2)}) async-start(), calls=%async_computation.2 | async-start | bytes 20971520 | tf_op jit(solution)/shard_map/all_gather | solution.py:96
  193.9 447.8 %all-gather.5.cloned.1.call-start = ((), (), s32[]{:S(2)}) async-start(), calls=%async_computation.3 | async-start | bytes 37748736 | tf_op jit(solution)/shard_map/all_gather | solution.py:98
Sparse Core Ops, SparseCore 0:
  194.0 286.1 all-gather.2
  482.7 158.9 all-gather.4
where the time goes:
time: 708 us; the launch traced here: 702 us
  waiting for transfers between devices  534 us (75%)
  matrix products  66 us (9%)
  local copies, waits for them, and re-layouts  48.6 us (7%)
  other arithmetic  27.3 us (4%)
  between operations  14.7 us (2%)
  starting transfers between devices  11.7 us (2%)
    all_gather x1, waiting for transfers between devices, body(): ham_cols = lax.all_gather(ham_low, 'row', axis=0, tiled=True)  280 us
    all_gather x1, waiting for transfers between devices, body(): lax.all_gather(dm_low, 'col', axis=1, tiled=True)  161 us
    all_to_all x1, waiting for transfers between devices, body(): lax.all_to_all(returning, ('row', 'col'), split_axis=0, concat_axis=0, ti...  48.8 us
    dot_general x1, matrix products, body(): jnp.dot(lax.all_gather(dm_low, 'col', axis=1, tiled=True), ham_cols, pref...  43.7 us
    all_to_all x1, waiting for transfers between devices, body(): lax.all_to_all(outgoing, ('row', 'col'), split_axis=0, concat_axis=0, til...  43.2 us
    unnamed x10, local copies, waits for them, and re-layouts  20.9 us
  transfers between devices with their start and end apart: 4, of which 4 were waited for; matrix products, arithmetic and copies ran while one was open for 2% of the time, Pallas kernels for 0%

commit v1 on v0

v1 whole, which is shorter than its diff:
```python
import jax
import jax.numpy as jnp
from jax import lax
from jax.experimental import pallas as pl
from jax.experimental.pallas import tpu as pltpu
from jax.sharding import PartitionSpec as P

BLK = 128

cube_coef = 0.5
cell_volume = 0.03125
DM_SCALE = float(2**20)

F32 = jnp.float32
BF16 = jnp.bfloat16
MIB = 1 << 20


def gather_kernel(row_ref, col_ref, dens_ref, out_ref, sems):
    n = out_ref.shape[0]

    def copy(s):
        r = pl.multiple_of(row_ref[s] * BLK, BLK)
        c = pl.multiple_of(col_ref[s] * BLK, BLK)
        return pltpu.make_async_copy(
            dens_ref.at[pl.ds(r, BLK), pl.ds(c, BLK)], out_ref.at[s], sems.at[s]
        )

    def start(s, carry):
        copy(s).start()
        return carry

    def wait(s, carry):
        copy(s).wait()
        return carry

    lax.fori_loop(0, n, start, 0)
    lax.fori_loop(0, n, wait, 0)


def gather_blocks(density, row_pick, col_pick):
    n = row_pick.shape[0]
    return pl.pallas_call(
        gather_kernel,
        grid_spec=pltpu.PrefetchScalarGridSpec(
            num_scalar_prefetch=2,
            grid=(1,),
            in_specs=[pl.BlockSpec(memory_space=pl.ANY)],
            out_specs=pl.BlockSpec((n, BLK, BLK), lambda i, *_: (0, 0, 0)),
            scratch_shapes=[pltpu.SemaphoreType.DMA((n,))],
        ),
        out_shape=jax.ShapeDtypeStruct((n, BLK, BLK), F32),
        compiler_params=pltpu.CompilerParams(vmem_limit_bytes=24 * MIB),
        cost_estimate=pl.CostEstimate(
            flops=0, bytes_accessed=2 * n * BLK * BLK * 4, transcendentals=0
        ),
        name="gather_blocks",
    )(row_pick, col_pick, density)


def split(x):
    hi = x.astype(BF16)
    return hi, (x - hi.astype(F32)).astype(BF16)


def dot3(a, b, dims):
    (ah, al), (bh, bl) = a, b

    def one(x, y):
        return lax.dot_general(x, y, (dims, ((), ())), preferred_element_type=F32)

    return one(ah, bh) + (one(al, bh) + one(ah, bl))


def tile_kernel(hold_ref, count_ref, in_ref, phi_ref, v_ref, out_ref, dh_ref, dl_ref):
    t = pl.program_id(0)
    maxb = phi_ref.shape[2] // BLK
    for i in range(maxb):
        for j in range(maxb):
            blk = in_ref[hold_ref[t, i * maxb + j]] * (1.0 / DM_SCALE)
            hi, lo = split(blk)
            dh_ref[i * BLK : (i + 1) * BLK, j * BLK : (j + 1) * BLK] = hi
            dl_ref[i * BLK : (i + 1) * BLK, j * BLK : (j + 1) * BLK] = lo
    basis = phi_ref[0]
    column = lax.broadcasted_iota(jnp.int32, basis.shape, 1)
    count = count_ref[t]
    masked = jnp.where(column < count * BLK, basis, 0.0)
    ms = split(masked)
    spread = dot3(ms, (dh_ref[...], dl_ref[...]), ((1,), (0,)))
    rho = jnp.sum(spread * masked, axis=1, keepdims=True)
    potential = v_ref[0] + rho + cube_coef * rho * rho * rho
    ws = split(masked * (potential * cell_volume))
    ham = dot3(ws, ms, ((0,), (0,))).astype(BF16)
    for i in range(maxb):
        for j in range(maxb):

            @pl.when((i < count) & (j < count))
            def _():
                out_ref[hold_ref[t, i * maxb + j]] = ham[
                    i * BLK : (i + 1) * BLK, j * BLK : (j + 1) * BLK
                ]


def tile_ham(incoming, phi, v_ext, hold, counts):
    n = incoming.shape[0]
    tdev, npts, local = phi.shape
    flops = tdev * 3 * 2 * 2 * npts * local * local
    return pl.pallas_call(
        tile_kernel,
        grid_spec=pltpu.PrefetchScalarGridSpec(
            num_scalar_prefetch=2,
            grid=(tdev,),
            in_specs=[
                pl.BlockSpec((n, BLK, BLK), lambda t, *_: (0, 0, 0)),
                pl.BlockSpec((1, npts, local), lambda t, *_: (t, 0, 0)),
                pl.BlockSpec((1, npts, 1), lambda t, *_: (t, 0, 0)),
            ],
            out_specs=pl.BlockSpec((n, BLK, BLK), lambda t, *_: (0, 0, 0)),
            scratch_shapes=[
                pltpu.VMEM((local, local), BF16),
                pltpu.VMEM((local, local), BF16),
            ],
        ),
        out_shape=jax.ShapeDtypeStruct((n, BLK, BLK), BF16),
        compiler_params=pltpu.CompilerParams(vmem_limit_bytes=56 * MIB),
        cost_estimate=pl.CostEstimate(
            flops=flops, bytes_accessed=tdev * npts * local * 4, transcendentals=0
        ),
        name="tile_ham",
    )(hold, counts, incoming, phi, v_ext[:, :, None])


def assemble_kernel(row_ref, col_ref, present_ref, in_ref, h_ref, out_ref, low_ref):
    step = pl.program_id(0)
    n = in_ref.shape[0]
    per = h_ref.shape[0] // BLK
    out_ref[...] = h_ref[...]

    def add(s, carry):
        r = row_ref[s]

        @pl.when((present_ref[s] > 0) & (r // per == step))
        def _():
            rows = pl.ds(pl.multiple_of((r - step * per) * BLK, BLK), BLK)
            cols = pl.ds(pl.multiple_of(col_ref[s] * BLK, BLK), BLK)
            out_ref[rows, cols] = out_ref[rows, cols] + in_ref[s].astype(F32)

        return carry

    lax.fori_loop(0, n, add, 0)
    low_ref[...] = out_ref[...].astype(BF16)


def assemble(h_core, arriving, row_pick, col_pick, present):
    rows, cols = h_core.shape
    n = arriving.shape[0]
    bm = 2 * BLK
    return pl.pallas_call(
        assemble_kernel,
        grid_spec=pltpu.PrefetchScalarGridSpec(
            num_scalar_prefetch=3,
            grid=(rows // bm,),
            in_specs=[
                pl.BlockSpec((n, BLK, BLK), lambda i, *_: (0, 0, 0)),
                pl.BlockSpec((bm, cols), lambda i, *_: (i, 0)),
            ],
            out_specs=[
                pl.BlockSpec((bm, cols), lambda i, *_: (i, 0)),
                pl.BlockSpec((bm, cols), lambda i, *_: (i, 0)),
            ],
        ),
        out_shape=[
            jax.ShapeDtypeStruct((rows, cols), F32),
            jax.ShapeDtypeStruct((rows, cols), BF16),
        ],
        compiler_params=pltpu.CompilerParams(vmem_limit_bytes=32 * MIB),
        cost_estimate=pl.CostEstimate(
            flops=rows * cols, bytes_accessed=rows * cols * 10, transcendentals=0
        ),
        name="assemble",
    )(row_pick, col_pick, present, arriving, h_core)


def product(total, dm_panel, pieces):
    ncol, rows, width = dm_panel.shape
    depth, cols = pieces[0][0][0].shape
    per = depth // width
    bm = min(512, rows)
    counts = [len(c) for c, _, _ in pieces]
    npiece = len(pieces)
    nh = sum(counts)
    scalars = jnp.stack(
        [jnp.asarray(s, jnp.int32) for _, _, s in pieces]
        + [jnp.asarray(w, jnp.int32) for _, w, _ in pieces]
    )

    def kernel(sc_ref, *refs):
        h_refs = refs[:nh]
        d_refs = refs[nh : nh + npiece]
        rest = refs[nh + npiece :]
        if total is not None:
            c_ref, rest = rest[0], rest[1:]
        out_ref = rest[0]
        held = rest[1 : 1 + npiece]
        sems = rest[1 + npiece]

        @pl.when(pl.program_id(0) == 0)
        def _():
            at = 0
            for p in range(npiece):
                for q in range(counts[p]):

                    @pl.when(sc_ref[npiece + p] == q)
                    def _(p=p, at=at):
                        pltpu.make_async_copy(h_refs[at], held[p], sems.at[p]).start()

                    at += 1
            first = 0
            for p in range(npiece):
                pltpu.make_async_copy(h_refs[first], held[p], sems.at[p]).wait()
                first += counts[p]

        acc = None
        for p in range(npiece):
            for q in range(per):
                part = jnp.dot(
                    d_refs[p][q],
                    held[p][q * width : (q + 1) * width, :],
                    preferred_element_type=F32,
                )
                acc = part if acc is None else acc + part
        if total is not None:
            acc = acc + c_ref[...]
        out_ref[...] = acc

    def d_map(p):
        return lambda i, sc: (sc[p], i, 0)

    c_spec = pl.BlockSpec((bm, cols), lambda i, sc: (i, 0))
    args = [h for c, _, _ in pieces for h in c] + [dm_panel] * npiece
    in_specs = [pl.BlockSpec(memory_space=pl.ANY)] * nh + [
        pl.BlockSpec((per, bm, width), d_map(p)) for p in range(npiece)
    ]
    aliases = {}
    if total is not None:
        aliases = {1 + len(args): 0}
        args.append(total)
        in_specs.append(c_spec)
    return pl.pallas_call(
        kernel,
        grid_spec=pltpu.PrefetchScalarGridSpec(
            num_scalar_prefetch=1,
            grid=(rows // bm,),
            in_specs=in_specs,
            out_specs=c_spec,
            scratch_shapes=[pltpu.VMEM((depth, cols), BF16)] * npiece
            + [pltpu.SemaphoreType.DMA((npiece,))],
        ),
        out_shape=jax.ShapeDtypeStruct((rows, cols), F32),
        input_output_aliases=aliases,
        compiler_params=pltpu.CompilerParams(vmem_limit_bytes=56 * MIB),
        cost_estimate=pl.CostEstimate(
            flops=2 * npiece * rows * depth * cols,
            bytes_accessed=npiece * (rows + cols) * depth * 2 + rows * cols * 8,
            transcendentals=0,
        ),
        name="product",
    )(scalars, *args)


def body(density, h_core, phi, v_ext, tile_blocks, tile_count):
    nrow = lax.axis_size("row")
    ncol = lax.axis_size("col")
    ndev = nrow * ncol
    row_idx = lax.axis_index("row")
    col_idx = lax.axis_index("col")
    myself = row_idx * ncol + col_idx
    rows_loc, cols_loc = density.shape
    rowb = rows_loc // BLK
    colb = cols_loc // BLK
    tdev, npts, local = phi.shape
    maxb = tile_blocks.shape[1]

    dm_low = density.astype(BF16)
    dm_panel = lax.all_gather(dm_low, "col", axis=0, tiled=False)

    blocks = tile_blocks.reshape(ndev, tdev, maxb)
    counts = tile_count.reshape(ndev, tdev)
    live = jnp.arange(maxb, dtype=jnp.int32)[None, None, :] < counts[:, :, None]
    row_hit = live & (blocks // rowb == row_idx)
    col_hit = live & (blocks // colb == col_idx)
    both = jnp.any(row_hit, axis=2) & jnp.any(col_hit, axis=2)
    row_in = jnp.sum(jnp.where(row_hit, blocks - row_idx * rowb, 0), axis=2)
    col_in = jnp.sum(jnp.where(col_hit, blocks - col_idx * colb, 0), axis=2)
    row_pick = jnp.sum(jnp.where(both, row_in, 0), axis=1)
    col_pick = jnp.sum(jnp.where(both, col_in, 0), axis=1)
    present = jnp.any(both, axis=1).astype(jnp.int32)
    mine = lax.dynamic_index_in_dim(blocks, myself, 0, keepdims=False)
    my_counts = lax.dynamic_index_in_dim(counts, myself, 0, keepdims=False)
    hold = ((mine // rowb)[:, :, None] * ncol + (mine // colb)[:, None, :]).reshape(tdev, -1)

    outgoing = (gather_blocks(density, row_pick, col_pick) * DM_SCALE).astype(jnp.float16)
    incoming = lax.all_to_all(outgoing, ("row", "col"), split_axis=0, concat_axis=0, tiled=True)
    returning = tile_ham(incoming.astype(F32), phi, v_ext, hold, my_counts)
    arriving = lax.all_to_all(returning, ("row", "col"), split_axis=0, concat_axis=0, tiled=True)
    hamiltonian, ham_low = assemble(h_core, arriving, row_pick, col_pick, present)

    if nrow == 4:
        swap = [(0, 1), (1, 0), (2, 3), (3, 2)]
        cross = [(1, 2), (2, 1)]
        outward = [(1, 0), (2, 3)]
        partner = lax.ppermute(ham_low, "row", swap)
        near_mid = lax.ppermute(ham_low, "row", cross)
        far_mid = lax.ppermute(partner, "row", cross)
        near_end = lax.ppermute(near_mid, "row", outward)
        far_end = lax.ppermute(far_mid, "row", outward)
        low = row_idx < 2
        is_end = ((row_idx == 0) | (row_idx == 3)).astype(jnp.int32)
        pair_idx = row_idx + 1 - 2 * (row_idx % 2)
        near_idx = jnp.where(low, 2, 1)
        far_idx = jnp.where(low, 3, 0)
        total = product(None, dm_panel, [((ham_low,), 0, row_idx), ((partner,), 0, pair_idx)])
        total = product(total, dm_panel, [((near_mid, near_end), is_end, near_idx)])
        total = product(total, dm_panel, [((far_mid, far_end), is_end, far_idx)])
    else:
        ham_panel = lax.all_gather(ham_low, "row", axis=0, tiled=False)
        total = None
        for k in range(nrow):
            total = product(total, dm_panel, [((ham_panel[k],), 0, k)])
    return hamiltonian, total


def solution(mesh):
    placed = (
        P("row", "col"),
        P("row", "col"),
        P(("row", "col"), None, None),
        P(("row", "col"), None),
        P(),
        P(),
    )
    return jax.shard_map(
        body,
        mesh=mesh,
        in_specs=placed,
        out_specs=(P("row", "col"), P("row", "col")),
        check_vma=False,
    )
```

time: 708 us -> 416 us (0.59)
  waiting for transfers between devices: 534 us -> 273 us
  Pallas kernels: 0 us -> 84.8 us
  matrix products: 66 us -> 0 us
  local copies, waits for them, and re-layouts: 48.6 us -> 11.9 us
  other arithmetic: 27.3 us -> 11.2 us
  starting transfers between devices: 11.7 us -> 20.2 us
    all_gather x2 -> x1, waiting for transfers between devices: 442 us -> 0.01 us  [body(): dm_panel = lax.all_gather(dm_low, 'col', axis=0, tiled=False)]
    ppermute x0 -> x5, waiting for transfers between devices: none -> 223 us  [the longest x1 87.3 us: body(): partner = lax.ppermute(ham_low, 'row', swap)]
    pallas_call x0 -> x6, Pallas kernels: none -> 84.8 us  [the longest x3 60.3 us: product(): pl.pallas_call(kernel, grid_spec=pltpu.PrefetchScalarGridSpec(num_scalar_...]
    dot_general x4 -> x0, matrix products: 66 us -> none  [the longest x1 43.7 us: body(): jnp.dot(lax.all_gather(dm_low, 'col', axis=1, tiled=True), ham_cols, pref...]
    all_to_all x1, waiting for transfers between devices: 48.8 us -> 26.1 us  [body(): lax.all_to_all(returning, ('row', 'col'), split_axis=0, concat_axis=0, ti...]
    all_to_all x1, waiting for transfers between devices: 43.2 us -> 23.4 us  [body(): lax.all_to_all(outgoing, ('row', 'col'), split_axis=0, concat_axis=0, til...]
    unnamed x10 -> x15, local copies, waits for them, and re-layouts: 20.9 us -> 8.9 us
    reshape x4 -> x1, local copies, waits for them, and re-layouts: 11.8 us -> 0.09 us  [body(): counts = tile_count.reshape(ndev, tdev)]
  transfers between devices with their start and end apart: 4 -> 8, of which waited for: 4 -> 5; matrix products, arithmetic and copies ran while one was open for 2% -> 2% of each run, Pallas kernels for 0% -> 16%
where the time goes in v1:
time: 416 us; the launch traced here: 415 us
  waiting for transfers between devices  273 us (66%)
  Pallas kernels  84.8 us (20%)
  starting transfers between devices  20.2 us (5%)
  between operations  14.2 us (3%)
  local copies, waits for them, and re-layouts  11.9 us (3%)
  other arithmetic  11.2 us (3%)
    ppermute x1, waiting for transfers between devices, body(): partner = lax.ppermute(ham_low, 'row', swap)  87.3 us
    ppermute x1, waiting for transfers between devices, body(): far_end = lax.ppermute(far_mid, 'row', outward)  72.1 us
    ppermute x1, waiting for transfers between devices, body(): near_end = lax.ppermute(near_mid, 'row', outward)  63.9 us
    pallas_call x3, Pallas kernels, product(): pl.pallas_call(kernel, grid_spec=pltpu.PrefetchScalarGridSpec(num_scalar_...  60.3 us
    all_to_all x1, waiting for transfers between devices, body(): lax.all_to_all(returning, ('row', 'col'), split_axis=0, concat_axis=0, ti...  26.1 us
    all_to_all x1, waiting for transfers between devices, body(): lax.all_to_all(outgoing, ('row', 'col'), split_axis=0, concat_axis=0, til...  23.4 us
    pallas_call x1, Pallas kernels, tile_ham(): pl.pallas_call(tile_kernel, grid_spec=pltpu.PrefetchScalarGridSpec(num_sc...  14.3 us
    unnamed x15, local copies, waits for them, and re-layouts  8.9 us
  transfers between devices with their start and end apart: 8, of which 5 were waited for; matrix products, arithmetic and copies ran while one was open for 2% of the time, Pallas kernels for 16%

profile of v1, /device:TPU:0, one launch (start us, length us, event | category | flops | bytes accessed | tf_op | source)
XLA Modules:
  0.0 415.0 jit_solution(2995259808032795458)
XLA Ops:
  7.2 6.1 %convert_element_type.16 = bf16[2048,1024]{1,0:T(8,128)(2,1)} convert(f32[2048,1024]{1,0:T(8,128)} %dens_ref.1) | non-fusion elementwise | flops 2097152 | bytes 12582912 | tf_op jit(solution)/shard_map/convert_element_type | solution.py:284
  13.3 0.6 copy-done.5
  14.5 3.4 copy-done
  17.9 1.7 gather_blocks.1
  19.6 1.3 multiply_convert_fusion
  20.9 7.3 %all-to-all-start = ((f16[32,128,128]{2,1,0:T(8,128)(2,1)}), f16[32,128,128]{2,1,0:T(8,128)(2,1)S(1)}, u32[]{:S(2)}, u32[]{:S(2)}) async-start(f16[32,128,128]{2,1,0:T(8,128)(2,1)} %multiply_convert_fusion), calls=%async_computation | async-start | bytes 2097152 | tf_op jit(solution)/shard_map/all_to_all | solution.py:303
  28.5 0.6 add.54.hold_ref
  29.1 1.4 copy.12.v_ref
  30.5 0.6 dynamic-slice_bitcast_fusion.count_ref
  31.1 23.4 %all-to-all-done = f16[32,128,128]{2,1,0:T(8,128)(2,1)S(1)} async-done(((f16[32,128,128]{2,1,0:T(8,128)(2,1)}), f16[32,128,128]{2,1,0:T(8,128)(2,1)S(1)}, u32[]{:S(2)}, u32[]{:S(2)}) %all-to-all-start) | async-done | bytes 1048608 | tf_op jit(solution)/shard_map/all_to_all | solution.py:303
  54.5 1.5 convert_element_type.15.in_ref
  55.9 14.3 %tile_ham.1 = bf16[32,128,128]{2,1,0:T(8,128)(2,1)} custom-call(s32[2,16]{1,0:T(2,128)} %add.54.hold_ref, s32[2]{0:T(128)} %dynamic-slice_bitcast_fusion.count_ref, f32[32,128,128]{2,1,0:T(8,128)} %convert_element_type.15.in_ref, f32[2,1024,512]{2,1,0:T(8,128)} %phi_ref.1, f32[2,1024,1]{2,1,0:T(8,128)} %copy.12.v_ref), custom_call_target="tpu_custom_call" | custom-call | flops 6442450944 | bytes 4194304 | tf_op jit(solution)/shard_map/tile_ham/pallas_call | solution.py:108
  70.2 3.7 all-to-all-start.1
  73.9 0.1 reduce_or.29
  74.0 26.1 %all-to-all-done.1.in_ref = bf16[32,128,128]{2,1,0:T(8,128)(2,1)S(1)} async-done(((bf16[32,128,128]{2,1,0:T(8,128)(2,1)}), bf16[32,128,128]{2,1,0:T(8,128)(2,1)S(1)}, u32[]{:S(2)}, u32[]{:S(2)}) %all-to-all-start.1) | async-done | bytes 1048608 | tf_op jit(solution)/shard_map/all_to_all | solution.py:305
  100.1 3.4 copy-done.1
  103.5 8.5 %assemble.1 = (f32[2048,1024]{1,0:T(8,128)}, bf16[2048,1024]{1,0:T(8,128)(2,1)S(1)}) custom-call(s32[32]{0:T(128)S(1)} %get-tuple-element.7.row_ref, s32[32]{0:T(128)S(1)} %get-tuple-element.6.col_ref, s32[32]{0:T(128)S(1)} %convert_element_type.13.present_ref, bf16[32,128,128]{2,1,0:T(8,128)(2,1)S(1)} %all-to-all-done.1.in_ref, f32[2048,1024]{1,0:T(8,128)S(1)} %copy-done.1), custom_call_target="tpu_custom_call" | custom-call | flops 2097152 | bytes 20971520 | tf_op jit(solution)/shard_map/assemble/pallas_call | solution.py:158
  112.0 0.8 collective-permute-start
  112.8 1.3 copy-done.2
  114.0 2.6 collective-permute-start.3
  116.6 87.3 %collective-permute-done.refs_1_ = bf16[2048,1024]{1,0:T(8,128)(2,1)S(1)} collective-permute-done((bf16[2048,1024]{1,0:T(8,128)(2,1)S(1)}, bf16[2048,1024]{1,0:T(8,128)(2,1)S(1)}, u32[]{:S(2)}, u32[]{:S(2)}) %collective-permute-start) | collective-permute-done | bytes 4194336 | tf_op jit(solution)/shard_map/ppermute | solution.py:312
  203.9 3.1 collective-permute-start.1
  207.1 1.3 collective-permute-start.4
  208.4 1.5 collective-permute-start.2
  209.9 0.6 pad_add_fusion.1.sc_ref
  210.5 0.7 pad_add_fusion.sc_ref
  211.2 0.6 pad_add_fusion.2.sc_ref
  211.8 26.2 %product.3.refs_3_ = f32[2048,1024]{1,0:T(8,128)} custom-call(s32[4]{0:T(128)} %pad_add_fusion.2.sc_ref, bf16[2048,1024]{1,0:T(8,128)(2,1)} %copy-done.2, bf16[2048,1024]{1,0:T(8,128)(2,1)} %copy-done.3, bf16[8,2048,1024]{2,1,0:T(8,128)(2,1)} %bitcast.28, bf16[8,2048,1024]{2,1,0:T(8,128)(2,1)} %bitcast.29), custom_call_target="tpu_custom_call" | custom-call | flops 17179869184 | bytes 41943040 | tf_op jit(solution)/shard_map/product/pallas_call | solution.py:249
  238.0 63.9 %collective-permute-done.4.refs_1_ = bf16[2048,1024]{1,0:T(8,128)(2,1)} collective-permute-done((bf16[2048,1024]{1,0:T(8,128)(2,1)}, bf16[2048,1024]{1,0:T(8,128)(2,1)}, u32[]{:S(2)}, u32[]{:S(2)}) %collective-permute-start.4) | collective-permute-done | bytes 4194336 | tf_op jit(solution)/shard_map/ppermute | solution.py:315
  301.9 17.1 %product.4.refs_3_ = f32[2048,1024]{1,0:T(8,128)} custom-call(s32[2]{0:T(128)} %pad_add_fusion.1.sc_ref, bf16[2048,1024]{1,0:T(8,128)(2,1)} %collective-permute-done.3.refs_0_, bf16[2048,1024]{1,0:T(8,128)(2,1)} %collective-permute-done.4.refs_1_, bf16[8,2048,1024]{2,1,0:T(8,128)(2,1)} %bitcast.30, ...), custom_call_target="tpu_custom_call", output_to_operand_aliasing={{}: (4, {})} | custom-call | flops 8589934592 | bytes 29360128 | tf_op jit(solution)/shard_map/product/pallas_call | solution.py:249
  319.0 72.1 %collective-permute-done.2.refs_1_ = bf16[2048,1024]{1,0:T(8,128)(2,1)} collective-permute-done((bf16[2048,1024]{1,0:T(8,128)(2,1)}, bf16[2048,1024]{1,0:T(8,128)(2,1)}, u32[]{:S(2)}, u32[]{:S(2)}) %collective-permute-start.2) | collective-permute-done | bytes 4194336 | tf_op jit(solution)/shard_map/ppermute | solution.py:316
  391.1 17.1 %product.5 = f32[2048,1024]{1,0:T(8,128)} custom-call(s32[2]{0:T(128)} %pad_add_fusion.sc_ref, bf16[2048,1024]{1,0:T(8,128)(2,1)} %collective-permute-done.1.refs_0_, bf16[2048,1024]{1,0:T(8,128)(2,1)} %collective-permute-done.2.refs_1_, bf16[8,2048,1024]{2,1,0:T(8,128)(2,1)} %bitcast.31, f32[2048,1024]{1,0:T(8,128)} %product.4.refs_3_), custom_call_target="tpu_custom_call", output_to_operand_aliasing={{}: (4, {})} | custom-call | flops 8589934592 | bytes 29360128 | tf_op jit(solution)/shard_map/product/pallas_call | solution.py:249
  (29 shorter events, 1.0 us)
Async XLA Ops:
  7.2 204.6 %all-gather.3.cloned.1.call-start = ((), (), s32[]{:S(2)}) async-start(), calls=%async_computation.2 | async-start | bytes 37748736 | tf_op jit(solution)/shard_map/all_gather | solution.py:285
  13.3 0.7 copy-start.5
  13.3 0.7 copy-start.6
  14.5 3.4 copy-start
  19.6 9.5 %copy-start.4 = (f32[2,1024]{1,0:T(2,128)S(1)}, f32[2,1024]{1,0:T(2,128)}, u32[]{:S(2)}) copy-start(f32[2,1024]{1,0:T(2,128)} %param.9) | copy-start | bytes 24580
  20.9 33.5 %all-to-all-start = ((f16[32,128,128]{2,1,0:T(8,128)(2,1)}), f16[32,128,128]{2,1,0:T(8,128)(2,1)S(1)}, u32[]{:S(2)}, u32[]{:S(2)}) async-start(f16[32,128,128]{2,1,0:T(8,128)(2,1)} %multiply_convert_fusion), calls=%async_computation | async-start | bytes 2097152 | tf_op jit(solution)/shard_map/all_to_all | solution.py:303
  70.2 29.9 %all-to-all-start.1 = ((bf16[32,128,128]{2,1,0:T(8,128)(2,1)}), bf16[32,128,128]{2,1,0:T(8,128)(2,1)S(1)}, u32[]{:S(2)}, u32[]{:S(2)}) async-start(bf16[32,128,128]{2,1,0:T(8,128)(2,1)} %tile_ham.1), calls=%async_computation.1 | async-start | bytes 2097152 | tf_op jit(solution)/shard_map/all_to_all | solution.py:305
  100.1 3.4 copy-start.1
  112.0 2.0 copy-start.2
  112.0 91.9 %collective-permute-start = (bf16[2048,1024]{1,0:T(8,128)(2,1)S(1)}, bf16[2048,1024]{1,0:T(8,128)(2,1)S(1)}, u32[]{:S(2)}, u32[]{:S(2)}) collective-permute-start(bf16[2048,1024]{1,0:T(8,128)(2,1)S(1)} %get-tuple-element.5.refs_0_), channel_id=1, source_target_pairs={{0,8},{8,0},{16,24},{24,16},{1,9},{9,1},{17,25},{25,17},{2,10},{10... | collective-permute-start | bytes 12582920 | tf_op jit(solution)/shard_map/ppermute | solution.py:312
  114.0 92.9 %collective-permute-start.3 = (bf16[2048,1024]{1,0:T(8,128)(2,1)S(1)}, bf16[2048,1024]{1,0:T(8,128)(2,1)}, u32[]{:S(2)}, u32[]{:S(2)}) collective-permute-start(bf16[2048,1024]{1,0:T(8,128)(2,1)S(1)} %get-tuple-element.5.refs_0_), channel_id=1, source_target_pairs={{8,16},{16,8},{9,17},{17,9},{10,18},{18,10},{11,19},{19,11},{12,20... | collective-permute-start | bytes 12582920 | tf_op jit(solution)/shard_map/ppermute | solution.py:313
  203.9 3.2 copy-start.3
  203.9 4.5 %collective-permute-start.1 = (bf16[2048,1024]{1,0:T(8,128)(2,1)S(1)}, bf16[2048,1024]{1,0:T(8,128)(2,1)}, u32[]{:S(2)}, u32[]{:S(2)}) collective-permute-start(bf16[2048,1024]{1,0:T(8,128)(2,1)S(1)} %collective-permute-done.refs_1_), channel_id=1, source_target_pairs={{8,16},{16,8},{9,17},{17,9},{10,18},{18,10},{11,19},{19,11},{12,20... | collective-permute-start | bytes 12582920 | tf_op jit(solution)/shard_map/ppermute | solution.py:314
  207.1 94.8 %collective-permute-start.4 = (bf16[2048,1024]{1,0:T(8,128)(2,1)}, bf16[2048,1024]{1,0:T(8,128)(2,1)}, u32[]{:S(2)}, u32[]{:S(2)}) collective-permute-start(bf16[2048,1024]{1,0:T(8,128)(2,1)} %collective-permute-done.3.refs_0_), channel_id=1, source_target_pairs={{8,0},{16,24},{9,1},{17,25},{10,2},{18,26},{11,3},{19,27},{12,4},{... | collective-permute-start | bytes 12582920 | tf_op jit(solution)/shard_map/ppermute | solution.py:315
  208.4 182.7 %collective-permute-start.2 = (bf16[2048,1024]{1,0:T(8,128)(2,1)}, bf16[2048,1024]{1,0:T(8,128)(2,1)}, u32[]{:S(2)}, u32[]{:S(2)}) collective-permute-start(bf16[2048,1024]{1,0:T(8,128)(2,1)} %collective-permute-done.1.refs_0_), channel_id=1, source_target_pairs={{8,0},{16,24},{9,1},{17,25},{10,2},{18,26},{11,3},{19,27},{12,4},{... | collective-permute-start | bytes 12582920 | tf_op jit(solution)/shard_map/ppermute | solution.py:316
Sparse Core Ops, SparseCore 0:
  13.4 185.9 all-gather.2

commit v2 on v1

v2 whole, which is shorter than its diff:
```python
import jax
import jax.numpy as jnp
from jax import lax
from jax.experimental import pallas as pl
from jax.experimental.pallas import tpu as pltpu
from jax.sharding import PartitionSpec as P

BLK = 128

cube_coef = 0.5
cell_volume = 0.03125
DM_SCALE = float(2**20)

F32 = jnp.float32
BF16 = jnp.bfloat16
MIB = 1 << 20


def gather_kernel(row_ref, col_ref, dens_ref, out_ref, sems):
    n = out_ref.shape[0]

    def copy(s):
        r = pl.multiple_of(row_ref[s] * BLK, BLK)
        c = pl.multiple_of(col_ref[s] * BLK, BLK)
        return pltpu.make_async_copy(
            dens_ref.at[pl.ds(r, BLK), pl.ds(c, BLK)], out_ref.at[s], sems.at[s]
        )

    def start(s, carry):
        copy(s).start()
        return carry

    def wait(s, carry):
        copy(s).wait()
        return carry

    lax.fori_loop(0, n, start, 0)
    lax.fori_loop(0, n, wait, 0)


def gather_blocks(density, row_pick, col_pick):
    n = row_pick.shape[0]
    return pl.pallas_call(
        gather_kernel,
        grid_spec=pltpu.PrefetchScalarGridSpec(
            num_scalar_prefetch=2,
            grid=(1,),
            in_specs=[pl.BlockSpec(memory_space=pl.ANY)],
            out_specs=pl.BlockSpec((n, BLK, BLK), lambda i, *_: (0, 0, 0)),
            scratch_shapes=[pltpu.SemaphoreType.DMA((n,))],
        ),
        out_shape=jax.ShapeDtypeStruct((n, BLK, BLK), F32),
        compiler_params=pltpu.CompilerParams(vmem_limit_bytes=56 * MIB),
        cost_estimate=pl.CostEstimate(
            flops=0, bytes_accessed=2 * n * BLK * BLK * 4, transcendentals=0
        ),
        name="gather_blocks",
    )(row_pick, col_pick, density)


def split(x):
    hi = x.astype(BF16)
    return hi, (x - hi.astype(F32)).astype(BF16)


def basis_kernel(count_ref, phi_ref, hi_ref, lo_ref, hit_ref, lot_ref):
    basis = phi_ref[0]
    column = lax.broadcasted_iota(jnp.int32, basis.shape, 1)
    masked = jnp.where(column < count_ref[pl.program_id(0)] * BLK, basis, 0.0)
    hi, lo = split(masked)
    hi_ref[0] = hi
    lo_ref[0] = lo
    hit_ref[0] = hi.T
    lot_ref[0] = lo.T


def split_basis(phi, counts):
    tdev, npts, local = phi.shape
    spec = pl.BlockSpec((1, npts, local), lambda t, *_: (t, 0, 0))
    spec_t = pl.BlockSpec((1, local, npts), lambda t, *_: (t, 0, 0))
    return pl.pallas_call(
        basis_kernel,
        grid_spec=pltpu.PrefetchScalarGridSpec(
            num_scalar_prefetch=1,
            grid=(tdev,),
            in_specs=[spec],
            out_specs=[spec, spec, spec_t, spec_t],
        ),
        out_shape=[jax.ShapeDtypeStruct((tdev, npts, local), BF16)] * 2
        + [jax.ShapeDtypeStruct((tdev, local, npts), BF16)] * 2,
        compiler_params=pltpu.CompilerParams(vmem_limit_bytes=40 * MIB),
        cost_estimate=pl.CostEstimate(
            flops=4 * phi.size, bytes_accessed=12 * phi.size, transcendentals=0
        ),
        name="split_basis",
    )(counts, phi)


def mm(x, y):
    return jnp.dot(x, y, preferred_element_type=F32)


def tile_kernel(
    hold_ref, count_ref, in_ref, hi_ref, lo_ref, hit_ref, lot_ref, v_ref, out_ref, dh_ref, dl_ref
):
    t = pl.program_id(0)
    maxb = hi_ref.shape[2] // BLK
    for i in range(maxb):
        for j in range(maxb):
            blk = in_ref[hold_ref[t, i * maxb + j]].astype(F32) * (1.0 / DM_SCALE)
            hi, lo = split(blk)
            dh_ref[i * BLK : (i + 1) * BLK, j * BLK : (j + 1) * BLK] = hi
            dl_ref[i * BLK : (i + 1) * BLK, j * BLK : (j + 1) * BLK] = lo
    count = count_ref[t]
    mh, ml = hi_ref[0], lo_ref[0]
    dh, dl = dh_ref[...], dl_ref[...]
    spread = mm(mh, dh) + (mm(ml, dh) + mm(mh, dl))
    masked = mh.astype(F32) + ml.astype(F32)
    rho = jnp.sum(spread * masked, axis=1, keepdims=True)
    potential = v_ref[0] + rho + cube_coef * rho * rho * rho
    wh, wl = split(masked * (potential * cell_volume))
    mht, mlt = hit_ref[0], lot_ref[0]
    ham = (mm(mht, wh) + (mm(mlt, wh) + mm(mht, wl))).astype(BF16)
    for i in range(maxb):
        for j in range(maxb):

            @pl.when((i < count) & (j < count))
            def _():
                out_ref[hold_ref[t, i * maxb + j]] = ham[
                    i * BLK : (i + 1) * BLK, j * BLK : (j + 1) * BLK
                ]


def tile_ham(incoming, basis, v_ext, hold, counts):
    n = incoming.shape[0]
    tdev, npts, local = basis[0].shape
    flops = tdev * 3 * 2 * 2 * npts * local * local
    spec = pl.BlockSpec((1, npts, local), lambda t, *_: (t, 0, 0))
    spec_t = pl.BlockSpec((1, local, npts), lambda t, *_: (t, 0, 0))
    return pl.pallas_call(
        tile_kernel,
        grid_spec=pltpu.PrefetchScalarGridSpec(
            num_scalar_prefetch=2,
            grid=(tdev,),
            in_specs=[
                pl.BlockSpec((n, BLK, BLK), lambda t, *_: (0, 0, 0)),
                spec,
                spec,
                spec_t,
                spec_t,
                pl.BlockSpec((1, npts, 1), lambda t, *_: (t, 0, 0)),
            ],
            out_specs=pl.BlockSpec((n, BLK, BLK), lambda t, *_: (0, 0, 0)),
            scratch_shapes=[
                pltpu.VMEM((local, local), BF16),
                pltpu.VMEM((local, local), BF16),
            ],
        ),
        out_shape=jax.ShapeDtypeStruct((n, BLK, BLK), BF16),
        compiler_params=pltpu.CompilerParams(vmem_limit_bytes=44 * MIB),
        cost_estimate=pl.CostEstimate(
            flops=flops, bytes_accessed=tdev * npts * local * 8, transcendentals=0
        ),
        name="tile_ham",
    )(hold, counts, incoming, *basis, v_ext[:, :, None])


def assemble(h_core, arriving, row_pick, col_pick, present, dtype, parts):
    rows, cols = h_core.shape
    n = arriving.shape[0]
    per = 2
    bm = per * BLK
    steps = rows // bm
    wide = cols // parts

    def kernel(row_ref, col_ref, present_ref, in_ref, h_ref, *rest):
        outs, (work_ref, num_ref, list_ref) = rest[:parts], rest[parts:]
        step = pl.program_id(0)

        @pl.when(step == 0)
        def _():
            def clear(g, carry):
                num_ref[g] = 0
                return carry

            def note(s, carry):
                @pl.when(present_ref[s] > 0)
                def _():
                    g = row_ref[s] // per
                    k = num_ref[g]
                    list_ref[g * n + k] = s
                    num_ref[g] = k + 1

                return carry

            lax.fori_loop(0, steps, clear, 0)
            lax.fori_loop(0, n, note, 0)

        work_ref[...] = h_ref[...]

        def add(k, carry):
            s = list_ref[step * n + k]
            top = pl.ds(pl.multiple_of((row_ref[s] - step * per) * BLK, BLK), BLK)
            left = pl.ds(pl.multiple_of(col_ref[s] * BLK, BLK), BLK)
            work_ref[top, left] = work_ref[top, left] + in_ref[s].astype(F32)
            return carry

        lax.fori_loop(0, num_ref[step], add, 0)
        for p in range(parts):
            outs[p][...] = work_ref[:, p * wide : (p + 1) * wide].astype(dtype)

    return pl.pallas_call(
        kernel,
        grid_spec=pltpu.PrefetchScalarGridSpec(
            num_scalar_prefetch=3,
            grid=(steps,),
            in_specs=[
                pl.BlockSpec((n, BLK, BLK), lambda i, *_: (0, 0, 0)),
                pl.BlockSpec((bm, cols), lambda i, *_: (i, 0)),
            ],
            out_specs=[pl.BlockSpec((bm, wide), lambda i, *_: (i, 0))] * parts,
            scratch_shapes=[
                pltpu.VMEM((bm, cols), F32),
                pltpu.SMEM((steps,), jnp.int32),
                pltpu.SMEM((steps * n,), jnp.int32),
            ],
        ),
        out_shape=[jax.ShapeDtypeStruct((rows, wide), dtype)] * parts,
        compiler_params=pltpu.CompilerParams(vmem_limit_bytes=56 * MIB),
        cost_estimate=pl.CostEstimate(
            flops=rows * cols, bytes_accessed=rows * cols * 6, transcendentals=0
        ),
        name="assemble",
    )(row_pick, col_pick, present, arriving, h_core)


def product(total, part, cols, dm_panel, pieces, fresh):
    ncol, rows, width = dm_panel.shape
    depth, wide = pieces[0][0][0].shape
    per = depth // width
    bm = min(512, rows)
    counts = [len(c) for c, _, _ in pieces]
    npiece = len(pieces)
    nh = sum(counts)
    scalars = jnp.stack(
        [jnp.asarray(s, jnp.int32) for _, _, s in pieces]
        + [jnp.asarray(w, jnp.int32) for _, w, _ in pieces]
    )

    def kernel(sc_ref, *refs):
        h_refs = refs[:nh]
        d_refs = refs[nh : nh + npiece]
        rest = refs[nh + npiece :]
        if total is not None:
            c_ref, rest = rest[0], rest[1:]
        out_ref = rest[0]
        held = rest[1 : 1 + npiece]
        sems = rest[1 + npiece]

        @pl.when(pl.program_id(0) == 0)
        def _():
            at = 0
            for p in range(npiece):
                for q in range(counts[p]):

                    @pl.when(sc_ref[npiece + p] == q)
                    def _(p=p, at=at):
                        pltpu.make_async_copy(h_refs[at], held[p], sems.at[p]).start()

                    at += 1
            first = 0
            for p in range(npiece):
                pltpu.make_async_copy(h_refs[first], held[p], sems.at[p]).wait()
                first += counts[p]

        acc = None
        for p in range(npiece):
            left = jnp.concatenate([d_refs[p][q] for q in range(per)], axis=1)
            term = mm(left, held[p][...])
            acc = term if acc is None else acc + term
        if not fresh:
            acc = acc + c_ref[...]
        out_ref[...] = acc

    def d_map(p):
        return lambda i, sc: (sc[p], i, 0)

    c_spec = pl.BlockSpec((bm, wide), lambda i, sc: (i, part))
    args = [h for c, _, _ in pieces for h in c] + [dm_panel] * npiece
    in_specs = [pl.BlockSpec(memory_space=pl.ANY)] * nh + [
        pl.BlockSpec((per, bm, width), d_map(p)) for p in range(npiece)
    ]
    aliases = {}
    if total is not None:
        aliases = {1 + len(args): 0}
        args.append(total)
        in_specs.append(pl.BlockSpec(memory_space=pl.ANY) if fresh else c_spec)
    return pl.pallas_call(
        kernel,
        grid_spec=pltpu.PrefetchScalarGridSpec(
            num_scalar_prefetch=1,
            grid=(rows // bm,),
            in_specs=in_specs,
            out_specs=c_spec,
            scratch_shapes=[pltpu.VMEM((depth, wide), BF16)] * npiece
            + [pltpu.SemaphoreType.DMA((npiece,))],
        ),
        out_shape=jax.ShapeDtypeStruct((rows, cols), F32),
        input_output_aliases=aliases,
        compiler_params=pltpu.CompilerParams(vmem_limit_bytes=56 * MIB),
        cost_estimate=pl.CostEstimate(
            flops=2 * npiece * rows * depth * wide,
            bytes_accessed=npiece * (rows + wide) * depth * 2 + rows * wide * 8,
            transcendentals=0,
        ),
        name="product",
    )(scalars, *args)


def body(density, h_core, phi, v_ext, tile_blocks, tile_count):
    nrow = lax.axis_size("row")
    ncol = lax.axis_size("col")
    ndev = nrow * ncol
    row_idx = lax.axis_index("row")
    col_idx = lax.axis_index("col")
    myself = row_idx * ncol + col_idx
    rows_loc, cols_loc = density.shape
    rowb = rows_loc // BLK
    colb = cols_loc // BLK
    tdev, npts, local = phi.shape
    maxb = tile_blocks.shape[1]

    blocks = tile_blocks.reshape(ndev, tdev, maxb)
    counts = tile_count.reshape(ndev, tdev)
    live = jnp.arange(maxb, dtype=jnp.int32)[None, None, :] < counts[:, :, None]
    row_hit = live & (blocks // rowb == row_idx)
    col_hit = live & (blocks // colb == col_idx)
    both = jnp.any(row_hit, axis=2) & jnp.any(col_hit, axis=2)
    row_in = jnp.sum(jnp.where(row_hit, blocks - row_idx * rowb, 0), axis=2)
    col_in = jnp.sum(jnp.where(col_hit, blocks - col_idx * colb, 0), axis=2)
    row_pick = jnp.sum(jnp.where(both, row_in, 0), axis=1)
    col_pick = jnp.sum(jnp.where(both, col_in, 0), axis=1)
    present = jnp.any(both, axis=1).astype(jnp.int32)
    mine = lax.dynamic_index_in_dim(blocks, myself, 0, keepdims=False)
    my_counts = lax.dynamic_index_in_dim(counts, myself, 0, keepdims=False)
    hold = ((mine // rowb)[:, :, None] * ncol + (mine // colb)[:, None, :]).reshape(tdev, -1)

    outgoing = (gather_blocks(density, row_pick, col_pick) * DM_SCALE).astype(jnp.float16)
    incoming = lax.all_to_all(outgoing, ("row", "col"), split_axis=0, concat_axis=0, tiled=True)

    later, _ = lax.optimization_barrier((density, outgoing))
    dm_panel = lax.all_gather(later.astype(BF16), "col", axis=0, tiled=False)

    basis = split_basis(phi, my_counts)
    returning = tile_ham(incoming.astype(F32), basis, v_ext, hold, my_counts)
    arriving = lax.all_to_all(returning, ("row", "col"), split_axis=0, concat_axis=0, tiled=True)
    where = (row_pick, col_pick, present)
    parts = 2 if nrow == 4 else 1
    low = assemble(h_core, arriving, *where, BF16, parts)
    (hamiltonian,) = assemble(h_core, arriving, *where, F32, 1)

    total = None
    if nrow == 4:
        swap = [(0, 1), (1, 0), (2, 3), (3, 2)]
        cross = [(1, 2), (2, 1)]
        outward = [(1, 0), (2, 3)]
        partner = [lax.ppermute(x, "row", swap) for x in low]
        near_mid = [lax.ppermute(x, "row", cross) for x in low]
        far_mid = [lax.ppermute(x, "row", cross) for x in partner]
        near_end = [lax.ppermute(x, "row", outward) for x in near_mid]
        far_end = [lax.ppermute(x, "row", outward) for x in far_mid]
        is_low = row_idx < 2
        is_end = ((row_idx == 0) | (row_idx == 3)).astype(jnp.int32)
        pair_idx = row_idx + 1 - 2 * (row_idx % 2)
        near_idx = jnp.where(is_low, 2, 1)
        far_idx = jnp.where(is_low, 3, 0)
        for p in range(parts):
            pieces = [((low[p],), 0, row_idx), ((partner[p],), 0, pair_idx)]
            total = product(total, p, cols_loc, dm_panel, pieces, True)
        for p in range(parts):
            pieces = [((near_mid[p], near_end[p]), is_end, near_idx)]
            total = product(total, p, cols_loc, dm_panel, pieces, False)
        for p in range(parts):
            pieces = [((far_mid[p], far_end[p]), is_end, far_idx)]
            total = product(total, p, cols_loc, dm_panel, pieces, False)
    else:
        ham_panel = lax.all_gather(low[0], "row", axis=0, tiled=False)
        for k in range(nrow):
            total = product(total, 0, cols_loc, dm_panel, [((ham_panel[k],), 0, k)], k == 0)
    return hamiltonian, total


def solution(mesh):
    placed = (
        P("row", "col"),
        P("row", "col"),
        P(("row", "col"), None, None),
        P(("row", "col"), None),
        P(),
        P(),
    )
    return jax.shard_map(
        body,
        mesh=mesh,
        in_specs=placed,
        out_specs=(P("row", "col"), P("row", "col")),
        check_vma=False,
    )
```

time: 416 us -> 408 us (0.981)
  waiting for transfers between devices: 273 us -> 226 us
  Pallas kernels: 84.8 us -> 117 us
  starting transfers between devices: 20.2 us -> 25.3 us
    ppermute x5 -> x10, waiting for transfers between devices: 223 us -> 185 us  [the longest x2 84.4 us: body(): partner = [lax.ppermute(x, 'row', swap) for x in low]]
    pallas_call x3 -> x6, Pallas kernels: 60.3 us -> 79 us  [product(): pl.pallas_call(kernel, grid_spec=pltpu.PrefetchScalarGridSpec(num_scalar_...]
    pallas_call x1 -> x3, Pallas kernels: 8.53 us -> 21.9 us  [the longest x2 19.7 us: assemble(): pl.pallas_call(kernel, grid_spec=pltpu.PrefetchScalarGridSpec(num_scalar_...]
    all_to_all x1, waiting for transfers between devices: 23.4 us -> 16 us  [body(): lax.all_to_all(outgoing, ('row', 'col'), split_axis=0, concat_axis=0, til...]
    ppermute x5 -> x10, starting transfers between devices: 9.17 us -> 14.1 us  [the longest x2 4.01 us: body(): near_mid = [lax.ppermute(x, 'row', cross) for x in low]]
    unnamed x15 -> x21, local copies, waits for them, and re-layouts: 8.9 us -> 8.68 us
  transfers between devices with their start and end apart: 8 -> 13, of which waited for: 5 -> 8; matrix products, arithmetic and copies ran while one was open for 2% -> 1% of each run, Pallas kernels for 16% -> 25%
where the time goes in v2:
time: 408 us; the launch traced here: 406 us
  waiting for transfers between devices  226 us (55%)
  Pallas kernels  117 us (29%)
  starting transfers between devices  25.3 us (6%)
  other arithmetic  14.6 us (4%)
  between operations  14.3 us (4%)
  local copies, waits for them, and re-layouts  9.57 us (2%)
    ppermute x2, waiting for transfers between devices, body(): partner = [lax.ppermute(x, 'row', swap) for x in low]  84.4 us
    pallas_call x6, Pallas kernels, product(): pl.pallas_call(kernel, grid_spec=pltpu.PrefetchScalarGridSpec(num_scalar_...  79 us
    ppermute x2, waiting for transfers between devices, body(): far_end = [lax.ppermute(x, 'row', outward) for x in far_mid]  66.1 us
    ppermute x2, waiting for transfers between devices, body(): near_end = [lax.ppermute(x, 'row', outward) for x in near_mid]  34 us
    all_to_all x1, waiting for transfers between devices, body(): lax.all_to_all(returning, ('row', 'col'), split_axis=0, concat_axis=0, ti...  25.6 us
    pallas_call x2, Pallas kernels, assemble(): pl.pallas_call(kernel, grid_spec=pltpu.PrefetchScalarGridSpec(num_scalar_...  19.7 us
    all_to_all x1, waiting for transfers between devices, body(): lax.all_to_all(outgoing, ('row', 'col'), split_axis=0, concat_axis=0, til...  16 us
    pallas_call x1, Pallas kernels, tile_ham(): pl.pallas_call(tile_kernel, grid_spec=pltpu.PrefetchScalarGridSpec(num_sc...  11.3 us
  transfers between devices with their start and end apart: 13, of which 8 were waited for; matrix products, arithmetic and copies ran while one was open for 1% of the time, Pallas kernels for 25%

profile of v2, /device:TPU:0, one launch (start us, length us, event | category | flops | bytes accessed | tf_op | source)
XLA Modules:
  0.0 406.5 jit_solution(6185129991360712702)
XLA Ops:
  9.0 4.4 %gather_blocks.1 = f32[32,128,128]{2,1,0:T(8,128)} custom-call(s32[32]{0:T(128)} %get-tuple-element.17.row_ref, s32[32]{0:T(128)} %get-tuple-element.16.col_ref, f32[2048,1024]{1,0:T(8,128)} %dens_ref.1), custom_call_target="tpu_custom_call" | custom-call | bytes 4194304 | tf_op jit(solution)/shard_map/gather_blocks/pallas_call | solution.py:43
  13.3 2.9 multiply_convert_fusion
  16.2 6.1 %convert_element_type.16 = bf16[2048,1024]{1,0:T(8,128)(2,1)} convert(f32[2048,1024]{1,0:T(8,128)} %dens_ref.1) | non-fusion elementwise | flops 2097152 | bytes 12582912 | tf_op jit(solution)/shard_map/convert_element_type | solution.py:352
  22.3 7.5 %all-to-all-start = ((f16[32,128,128]{2,1,0:T(8,128)(2,1)}), f16[32,128,128]{2,1,0:T(8,128)(2,1)}, u32[]{:S(2)}, u32[]{:S(2)}) async-start(f16[32,128,128]{2,1,0:T(8,128)(2,1)} %multiply_convert_fusion), calls=%async_computation | async-start | bytes 2097152 | tf_op jit(solution)/shard_map/all_to_all | solution.py:349
  30.6 3.2 copy-done
  33.8 2.2 split_basis.1
  36.0 1.3 copy-done.1
  37.3 1.3 copy-done.3
  38.6 1.4 copy-done.4
  40.0 16.0 %all-to-all-done = f16[32,128,128]{2,1,0:T(8,128)(2,1)} async-done(((f16[32,128,128]{2,1,0:T(8,128)(2,1)}), f16[32,128,128]{2,1,0:T(8,128)(2,1)}, u32[]{:S(2)}, u32[]{:S(2)}) %all-to-all-start) | async-done | bytes 1048608 | tf_op jit(solution)/shard_map/all_to_all | solution.py:349
  56.0 1.5 convert_element_type.15.in_ref
  57.9 11.3 %tile_ham.1 = bf16[32,128,128]{2,1,0:T(8,128)(2,1)} custom-call(s32[2,16]{1,0:T(2,128)S(1)} %add.54.hold_ref, s32[2]{0:T(128)S(1)} %dynamic-slice_bitcast_fusion.count_ref, f32[32,128,128]{2,1,0:T(8,128)S(1)} %convert_element_type.15.in_ref, bf16[2,1024,512]{2,1,0:T(8,128)(2,1)S(1)} %get-tuple-element.9.hi_ref, bf16[2,1024,512]{2,1,0:T(8,128)(2,1)S(1)} %copy-done.2, ...), custom_call_target="tpu_custom_call" | custom-call | flops 6442450944 | bytes 8388608 | tf_op jit(solution)/shard_map/tile_ham/pallas_call | solution.py:140
  69.2 3.6 all-to-all-start.1
  73.5 25.6 %all-to-all-done.1.in_ref = bf16[32,128,128]{2,1,0:T(8,128)(2,1)S(1)} async-done(((bf16[32,128,128]{2,1,0:T(8,128)(2,1)}), bf16[32,128,128]{2,1,0:T(8,128)(2,1)S(1)}, u32[]{:S(2)}, u32[]{:S(2)}) %all-to-all-start.1) | async-done | bytes 1048608 | tf_op jit(solution)/shard_map/all_to_all | solution.py:356
  100.1 9.3 %assemble.3 = (bf16[2048,512]{1,0:T(8,128)(2,1)}, bf16[2048,512]{1,0:T(8,128)(2,1)}) custom-call(s32[32]{0:T(128)} %get-tuple-element.17.row_ref, s32[32]{0:T(128)} %get-tuple-element.16.col_ref, s32[32]{0:T(128)} %convert_element_type.13.present_ref, bf16[32,128,128]{2,1,0:T(8,128)(2,1)} %copy-done.5, f32[2048,1024]{1,0:T(8,128)} %h_ref.3), custom_call_target="tpu_custom_call" | custom-call | flops 2097152 | bytes 12582912 | tf_op jit(solution)/shard_map/assemble/pallas_call | solution.py:212
  111.4 2.0 collective-permute-start.8
  113.4 2.0 collective-permute-start.6
  115.4 42.8 %collective-permute-done.3.refs_1_ = bf16[2048,512]{1,0:T(8,128)(2,1)} collective-permute-done((bf16[2048,512]{1,0:T(8,128)(2,1)}, bf16[2048,512]{1,0:T(8,128)(2,1)}, u32[]{:S(2)}, u32[]{:S(2)}) %collective-permute-start.3) | collective-permute-done | bytes 2097184 | tf_op jit(solution)/shard_map/ppermute | solution.py:367
  158.2 2.0 collective-permute-start.4
  160.2 41.6 %collective-permute-done.refs_1_ = bf16[2048,512]{1,0:T(8,128)(2,1)} collective-permute-done((bf16[2048,512]{1,0:T(8,128)(2,1)}, bf16[2048,512]{1,0:T(8,128)(2,1)}, u32[]{:S(2)}, u32[]{:S(2)}) %collective-permute-start) | collective-permute-done | bytes 2097184 | tf_op jit(solution)/shard_map/ppermute | solution.py:367
  202.6 1.3 collective-permute-start.9
  207.2 10.4 %assemble.2 = f32[2048,1024]{1,0:T(8,128)} custom-call(s32[32]{0:T(128)} %get-tuple-element.17.row_ref, s32[32]{0:T(128)} %get-tuple-element.16.col_ref, s32[32]{0:T(128)} %convert_element_type.13.present_ref, bf16[32,128,128]{2,1,0:T(8,128)(2,1)} %copy-done.5, f32[2048,1024]{1,0:T(8,128)} %h_ref.3), custom_call_target="tpu_custom_call" | custom-call | flops 2097152 | bytes 12582912 | tf_op jit(solution)/shard_map/assemble/pallas_call | solution.py:212
  218.9 1.5 collective-permute-start.2
  220.4 16.3 %product.6.refs_4_ = f32[2048,1024]{1,0:T(8,128)} custom-call(s32[4]{0:T(128)} %pad_add_fusion.2.sc_ref, bf16[2048,512]{1,0:T(8,128)(2,1)} %get-tuple-element.15.refs_0_, bf16[2048,512]{1,0:T(8,128)(2,1)} %collective-permute-done.3.refs_1_, bf16[8,2048,1024]{2,1,0:T(8,128)(2,1)} %bitcast.28, bf16[8,2048,1024]{2,1,0:T(8,128)(2,1)} %bitcast.29), custom_call_target="tpu_custom_call" | custom-call | flops 8589934592 | bytes 29360128 | tf_op jit(solution)/shard_map/product/pallas_call | solution.py:298
  236.7 16.3 %product.7.refs_3_ = f32[2048,1024]{1,0:T(8,128)} custom-call(s32[4]{0:T(128)} %pad_add_fusion.2.sc_ref, bf16[2048,512]{1,0:T(8,128)(2,1)} %get-tuple-element.13.refs_0_, bf16[2048,512]{1,0:T(8,128)(2,1)} %collective-permute-done.refs_1_, bf16[8,2048,1024]{2,1,0:T(8,128)(2,1)} %bitcast.30, ...), custom_call_target="tpu_custom_call", output_to_operand_aliasing={{}: (5, {})} | custom-call | flops 8589934592 | bytes 29360128 | tf_op jit(solution)/shard_map/product/pallas_call | solution.py:298
  253.6 11.6 %product.8.refs_3_ = f32[2048,1024]{1,0:T(8,128)} custom-call(s32[2]{0:T(128)} %pad_add_fusion.1.sc_ref, bf16[2048,512]{1,0:T(8,128)(2,1)} %collective-permute-done.8.refs_0_, bf16[2048,512]{1,0:T(8,128)(2,1)} %collective-permute-done.9.refs_1_, bf16[8,2048,1024]{2,1,0:T(8,128)(2,1)} %bitcast.32, ...), custom_call_target="tpu_custom_call", output_to_operand_aliasing={{}: (4, {})} | custom-call | flops 4294967296 | bytes 18874368 | tf_op jit(solution)/shard_map/product/pallas_call | solution.py:298
  265.3 33.3 %collective-permute-done.7.refs_1_ = bf16[2048,512]{1,0:T(8,128)(2,1)} collective-permute-done((bf16[2048,512]{1,0:T(8,128)(2,1)}, bf16[2048,512]{1,0:T(8,128)(2,1)}, u32[]{:S(2)}, u32[]{:S(2)}) %collective-permute-start.7) | collective-permute-done | bytes 2097184 | tf_op jit(solution)/shard_map/ppermute | solution.py:370
  298.6 11.6 %product.9.refs_3_ = f32[2048,1024]{1,0:T(8,128)} custom-call(s32[2]{0:T(128)} %pad_add_fusion.1.sc_ref, bf16[2048,512]{1,0:T(8,128)(2,1)} %collective-permute-done.6.refs_0_, bf16[2048,512]{1,0:T(8,128)(2,1)} %collective-permute-done.7.refs_1_, bf16[8,2048,1024]{2,1,0:T(8,128)(2,1)} %bitcast.33, ...), custom_call_target="tpu_custom_call", output_to_operand_aliasing={{}: (4, {})} | custom-call | flops 4294967296 | bytes 18874368 | tf_op jit(solution)/shard_map/product/pallas_call | solution.py:298
  310.2 33.3 %collective-permute-done.5.refs_1_ = bf16[2048,512]{1,0:T(8,128)(2,1)} collective-permute-done((bf16[2048,512]{1,0:T(8,128)(2,1)}, bf16[2048,512]{1,0:T(8,128)(2,1)}, u32[]{:S(2)}, u32[]{:S(2)}) %collective-permute-start.5) | collective-permute-done | bytes 2097184 | tf_op jit(solution)/shard_map/ppermute | solution.py:371
  343.5 11.6 %product.10.refs_3_ = f32[2048,1024]{1,0:T(8,128)} custom-call(s32[2]{0:T(128)} %pad_add_fusion.sc_ref, bf16[2048,512]{1,0:T(8,128)(2,1)} %collective-permute-done.4.refs_0_, bf16[2048,512]{1,0:T(8,128)(2,1)} %collective-permute-done.5.refs_1_, bf16[8,2048,1024]{2,1,0:T(8,128)(2,1)} %bitcast.34, ...), custom_call_target="tpu_custom_call", output_to_operand_aliasing={{}: (4, {})} | custom-call | flops 4294967296 | bytes 18874368 | tf_op jit(solution)/shard_map/product/pallas_call | solution.py:298
  355.2 32.8 %collective-permute-done.2.refs_1_ = bf16[2048,512]{1,0:T(8,128)(2,1)} collective-permute-done((bf16[2048,512]{1,0:T(8,128)(2,1)S(1)}, bf16[2048,512]{1,0:T(8,128)(2,1)}, u32[]{:S(2)}, u32[]{:S(2)}) %collective-permute-start.2) | collective-permute-done | bytes 2097184 | tf_op jit(solution)/shard_map/ppermute | solution.py:371
  388.0 11.6 %product.11 = f32[2048,1024]{1,0:T(8,128)} custom-call(s32[2]{0:T(128)} %pad_add_fusion.sc_ref, bf16[2048,512]{1,0:T(8,128)(2,1)} %copy-done.6, bf16[2048,512]{1,0:T(8,128)(2,1)} %collective-permute-done.2.refs_1_, bf16[8,2048,1024]{2,1,0:T(8,128)(2,1)} %bitcast.35, f32[2048,1024]{1,0:T(8,128)} %product.10.refs_3_), custom_call_target="tpu_custom_call", output_to_operand_aliasing={{}: (4, {})} | custom-call | flops 4294967296 | bytes 18874368 | tf_op jit(solution)/shard_map/product/pallas_call | solution.py:298
  (50 shorter events, 12.6 us)
Async XLA Ops:
  7.2 213.3 %all-gather.3.cloned.1.call-start = ((), (), s32[]{:S(2)}) async-start(), calls=%async_computation.2 | async-start | bytes 37748736 | tf_op jit(solution)/shard_map/all_gather | solution.py:352
  22.3 7.5 %copy-start.8 = (s32[64,4]{0,1:T(4,128)S(1)}, s32[64,4]{0,1:T(4,128)}, u32[]{:S(2)}) copy-start(s32[64,4]{0,1:T(4,128)} %param.10) | copy-start | bytes 3076
  22.3 7.6 %copy-start.9 = (s32[64]{0:T(128)S(1)}, s32[64]{0:T(128)}, u32[]{:S(2)}) copy-start(s32[64]{0:T(128)} %param.11) | copy-start | bytes 772
  22.3 7.9 %copy-start.7 = (f32[2,1024]{1,0:T(2,128)S(1)}, f32[2,1024]{1,0:T(2,128)}, u32[]{:S(2)}) copy-start(f32[2,1024]{1,0:T(2,128)} %param.9) | copy-start | bytes 24580
  22.3 33.7 %all-to-all-start = ((f16[32,128,128]{2,1,0:T(8,128)(2,1)}), f16[32,128,128]{2,1,0:T(8,128)(2,1)}, u32[]{:S(2)}, u32[]{:S(2)}) async-start(f16[32,128,128]{2,1,0:T(8,128)(2,1)} %multiply_convert_fusion), calls=%async_computation | async-start | bytes 2097152 | tf_op jit(solution)/shard_map/all_to_all | solution.py:349
  30.6 3.2 copy-start
  36.0 1.3 copy-start.1
  37.3 1.3 copy-start.3
  38.6 1.4 copy-start.4
  56.0 1.9 copy-start.2
  69.2 29.9 %all-to-all-start.1 = ((bf16[32,128,128]{2,1,0:T(8,128)(2,1)}), bf16[32,128,128]{2,1,0:T(8,128)(2,1)S(1)}, u32[]{:S(2)}, u32[]{:S(2)}) async-start(bf16[32,128,128]{2,1,0:T(8,128)(2,1)} %tile_ham.1), calls=%async_computation.1 | async-start | bytes 2097152 | tf_op jit(solution)/shard_map/all_to_all | solution.py:356
  99.1 1.0 copy-start.5
  109.4 48.9 %collective-permute-start.3 = (bf16[2048,512]{1,0:T(8,128)(2,1)}, bf16[2048,512]{1,0:T(8,128)(2,1)}, u32[]{:S(2)}, u32[]{:S(2)}) collective-permute-start(bf16[2048,512]{1,0:T(8,128)(2,1)} %get-tuple-element.15.refs_0_), channel_id=1, source_target_pairs={{0,8},{8,0},{16,24},{24,16},{1,9},{9,1},{17,25},{25,17},{2,10},{10... | collective-permute-start | bytes 6291464 | tf_op jit(solution)/shard_map/ppermute | solution.py:367
  110.2 91.6 %collective-permute-start = (bf16[2048,512]{1,0:T(8,128)(2,1)}, bf16[2048,512]{1,0:T(8,128)(2,1)}, u32[]{:S(2)}, u32[]{:S(2)}) collective-permute-start(bf16[2048,512]{1,0:T(8,128)(2,1)} %get-tuple-element.13.refs_0_), channel_id=1, source_target_pairs={{0,8},{8,0},{16,24},{24,16},{1,9},{9,1},{17,25},{25,17},{2,10},{10... | collective-permute-start | bytes 6291464 | tf_op jit(solution)/shard_map/ppermute | solution.py:367
  111.4 91.2 %collective-permute-start.8 = (bf16[2048,512]{1,0:T(8,128)(2,1)}, bf16[2048,512]{1,0:T(8,128)(2,1)}, u32[]{:S(2)}, u32[]{:S(2)}) collective-permute-start(bf16[2048,512]{1,0:T(8,128)(2,1)} %get-tuple-element.15.refs_0_), channel_id=1, source_target_pairs={{8,16},{16,8},{9,17},{17,9},{10,18},{18,10},{11,19},{19,11},{12,20... | collective-permute-start | bytes 6291464 | tf_op jit(solution)/shard_map/ppermute | solution.py:368
  113.4 91.9 %collective-permute-start.6 = (bf16[2048,512]{1,0:T(8,128)(2,1)}, bf16[2048,512]{1,0:T(8,128)(2,1)}, u32[]{:S(2)}, u32[]{:S(2)}) collective-permute-start(bf16[2048,512]{1,0:T(8,128)(2,1)} %get-tuple-element.13.refs_0_), channel_id=1, source_target_pairs={{8,16},{16,8},{9,17},{17,9},{10,18},{18,10},{11,19},{19,11},{12,20... | collective-permute-start | bytes 6291464 | tf_op jit(solution)/shard_map/ppermute | solution.py:368
  158.2 59.4 %collective-permute-start.4 = (bf16[2048,512]{1,0:T(8,128)(2,1)}, bf16[2048,512]{1,0:T(8,128)(2,1)}, u32[]{:S(2)}, u32[]{:S(2)}) collective-permute-start(bf16[2048,512]{1,0:T(8,128)(2,1)} %collective-permute-done.3.refs_1_), channel_id=1, source_target_pairs={{8,16},{16,8},{9,17},{17,9},{10,18},{18,10},{11,19},{19,11},{12,20... | collective-permute-start | bytes 6291464 | tf_op jit(solution)/shard_map/ppermute | solution.py:369
  201.8 17.1 %collective-permute-start.1 = (bf16[2048,512]{1,0:T(8,128)(2,1)}, bf16[2048,512]{1,0:T(8,128)(2,1)S(1)}, u32[]{:S(2)}, u32[]{:S(2)}) collective-permute-start(bf16[2048,512]{1,0:T(8,128)(2,1)} %collective-permute-done.refs_1_), channel_id=1, source_target_pairs={{8,16},{16,8},{9,17},{17,9},{10,18},{18,10},{11,19},{19,11},{12,20... | collective-permute-start | bytes 6291464 | tf_op jit(solution)/shard_map/ppermute | solution.py:369
  202.6 51.0 %collective-permute-start.9 = (bf16[2048,512]{1,0:T(8,128)(2,1)}, bf16[2048,512]{1,0:T(8,128)(2,1)}, u32[]{:S(2)}, u32[]{:S(2)}) collective-permute-start(bf16[2048,512]{1,0:T(8,128)(2,1)} %collective-permute-done.8.refs_0_), channel_id=1, source_target_pairs={{8,0},{16,24},{9,1},{17,25},{10,2},{18,26},{11,3},{19,27},{12,4},{... | collective-permute-start | bytes 6291464 | tf_op jit(solution)/shard_map/ppermute | solution.py:370
  205.3 93.3 %collective-permute-start.7 = (bf16[2048,512]{1,0:T(8,128)(2,1)}, bf16[2048,512]{1,0:T(8,128)(2,1)}, u32[]{:S(2)}, u32[]{:S(2)}) collective-permute-start(bf16[2048,512]{1,0:T(8,128)(2,1)} %collective-permute-done.6.refs_0_), channel_id=1, source_target_pairs={{8,0},{16,24},{9,1},{17,25},{10,2},{18,26},{11,3},{19,27},{12,4},{... | collective-permute-start | bytes 6291464 | tf_op jit(solution)/shard_map/ppermute | solution.py:370
  217.6 125.9 %collective-permute-start.5 = (bf16[2048,512]{1,0:T(8,128)(2,1)}, bf16[2048,512]{1,0:T(8,128)(2,1)}, u32[]{:S(2)}, u32[]{:S(2)}) collective-permute-start(bf16[2048,512]{1,0:T(8,128)(2,1)} %collective-permute-done.4.refs_0_), channel_id=1, source_target_pairs={{8,0},{16,24},{9,1},{17,25},{10,2},{18,26},{11,3},{19,27},{12,4},{... | collective-permute-start | bytes 6291464 | tf_op jit(solution)/shard_map/ppermute | solution.py:371
  218.9 17.8 %copy-start.6 = (bf16[2048,512]{1,0:T(8,128)(2,1)}, bf16[2048,512]{1,0:T(8,128)(2,1)S(1)}, u32[]{:S(2)}) copy-start(bf16[2048,512]{1,0:T(8,128)(2,1)S(1)} %collective-permute-done.1.refs_0_) | copy-start | bytes 6291460
  218.9 169.1 %collective-permute-start.2 = (bf16[2048,512]{1,0:T(8,128)(2,1)S(1)}, bf16[2048,512]{1,0:T(8,128)(2,1)}, u32[]{:S(2)}, u32[]{:S(2)}) collective-permute-start(bf16[2048,512]{1,0:T(8,128)(2,1)S(1)} %collective-permute-done.1.refs_0_), channel_id=1, source_target_pairs={{8,0},{16,24},{9,1},{17,25},{10,2},{18,26},{11,3},{19,27},{12,4},{... | collective-permute-start | bytes 6291464 | tf_op jit(solution)/shard_map/ppermute | solution.py:371
Sparse Core Ops, SparseCore 0:
  22.4 179.4 all-gather.2

commit v3 on v2

--- a/solution.py
+++ b/solution.py
@@ -165,65 +165,102 @@
     )(hold, counts, incoming, *basis, v_ext[:, :, None])
 
 
-def assemble(h_core, arriving, row_pick, col_pick, present, dtype, parts):
-    rows, cols = h_core.shape
+def assemble(h_core, arriving, picks, dtype, parts):
+    nband = len(h_core)
+    rows, cols = sum(x.shape[0] for x in h_core), h_core[0].shape[1]
     n = arriving.shape[0]
     per = 2
     bm = per * BLK
     steps = rows // bm
     wide = cols // parts
-
-    def kernel(row_ref, col_ref, present_ref, in_ref, h_ref, *rest):
-        outs, (work_ref, num_ref, list_ref) = rest[:parts], rest[parts:]
-        step = pl.program_id(0)
-
-        @pl.when(step == 0)
-        def _():
-            def clear(g, carry):
-                num_ref[g] = 0
+    widen = h_core[0].dtype != F32
+    narrow = dtype != F32
+    source = [(k, g) for k, x in enumerate(h_core) for g in range(x.shape[0] // bm)]
+
+    def kernel(row_ref, col_ref, present_ref, in_ref, *rest):
+        h_refs, outs, rest = rest[:nband], rest[nband : nband + parts], rest[nband + parts :]
+        work_ref, in_sems, out_sems, num_ref, list_ref = rest[:5]
+        rest = rest[5:]
+        raw_ref = work_ref
+        if widen:
+            raw_ref, rest = rest[0], rest[1:]
+        low_refs = rest if narrow else (work_ref,)
+
+        def band(g):
+            return pl.ds(g * bm, bm)
+
+        def read(g):
+            k, at = source[g]
+            return pltpu.make_async_copy(
+                h_refs[k].at[band(at)], raw_ref.at[band(g)], in_sems.at[g]
+            )
+
+        def write(g, p):
+            return pltpu.make_async_copy(
+                low_refs[p].at[band(g)], outs[p].at[band(g)], out_sems.at[g, p]
+            )
+
+        for g in range(steps):
+            read(g).start()
+            num_ref[g] = 0
+
+        def note(s, carry):
+            @pl.when(present_ref[s] > 0)
+            def _():
+                g = row_ref[s] // per
+                k = num_ref[g]
+                list_ref[g * n + k] = s
+                num_ref[g] = k + 1
+
+            return carry
+
+        lax.fori_loop(0, n, note, 0)
+
+        for g in range(steps):
+            read(g).wait()
+            if widen:
+                work_ref[band(g), :] = raw_ref[band(g), :].astype(F32)
+
+            def add(k, carry, g=g):
+                s = list_ref[g * n + k]
+                top = pl.ds(pl.multiple_of(row_ref[s] * BLK, BLK), BLK)
+                left = pl.ds(pl.multiple_of(col_ref[s] * BLK, BLK), BLK)
+                work_ref[top, left] = work_ref[top, left] + in_ref[s].astype(F32)
                 return carry
 
-            def note(s, carry):
-                @pl.when(present_ref[s] > 0)
-                def _():
-                    g = row_ref[s] // per
-                    k = num_ref[g]
-                    list_ref[g * n + k] = s
-                    num_ref[g] = k + 1
-
-                return carry
-
-            lax.fori_loop(0, steps, clear, 0)
-            lax.fori_loop(0, n, note, 0)
-
-        work_ref[...] = h_ref[...]
-
-        def add(k, carry):
-            s = list_ref[step * n + k]
-            top = pl.ds(pl.multiple_of((row_ref[s] - step * per) * BLK, BLK), BLK)
-            left = pl.ds(pl.multiple_of(col_ref[s] * BLK, BLK), BLK)
-            work_ref[top, left] = work_ref[top, left] + in_ref[s].astype(F32)
-            return carry
-
-        lax.fori_loop(0, num_ref[step], add, 0)
-        for p in range(parts):
-            outs[p][...] = work_ref[:, p * wide : (p + 1) * wide].astype(dtype)
-
+            lax.fori_loop(0, num_ref[g], add, 0)
+            for p in range(parts):
+                if narrow:
+                    low_refs[p][band(g), :] = work_ref[band(g), p * wide : (p + 1) * wide].astype(
+                        dtype
+                    )
+                write(g, p).start()
+        for g in range(steps):
+            for p in range(parts):
+                write(g, p).wait()
+
+    scratch = [
+        pltpu.VMEM((rows, cols), F32),
+        pltpu.SemaphoreType.DMA((steps,)),
+        pltpu.SemaphoreType.DMA((steps, parts)),
+        pltpu.SMEM((steps,), jnp.int32),
+        pltpu.SMEM((steps * n,), jnp.int32),
+    ]
+    if widen:
+        scratch.append(pltpu.VMEM((rows, cols), h_core[0].dtype))
+    if narrow:
+        scratch.extend([pltpu.VMEM((rows, wide), dtype)] * parts)
     return pl.pallas_call(
         kernel,
         grid_spec=pltpu.PrefetchScalarGridSpec(
             num_scalar_prefetch=3,
-            grid=(steps,),
+            grid=(1,),
             in_specs=[
                 pl.BlockSpec((n, BLK, BLK), lambda i, *_: (0, 0, 0)),
-                pl.BlockSpec((bm, cols), lambda i, *_: (i, 0)),
-            ],
-            out_specs=[pl.BlockSpec((bm, wide), lambda i, *_: (i, 0))] * parts,
-            scratch_shapes=[
-                pltpu.VMEM((bm, cols), F32),
-                pltpu.SMEM((steps,), jnp.int32),
-                pltpu.SMEM((steps * n,), jnp.int32),
-            ],
+            ]
+            + [pl.BlockSpec(memory_space=pl.ANY)] * nband,
+            out_specs=[pl.BlockSpec(memory_space=pl.ANY)] * parts,
+            scratch_shapes=scratch,
         ),
         out_shape=[jax.ShapeDtypeStruct((rows, wide), dtype)] * parts,
         compiler_params=pltpu.CompilerParams(vmem_limit_bytes=56 * MIB),
@@ -231,17 +268,16 @@
             flops=rows * cols, bytes_accessed=rows * cols * 6, transcendentals=0
         ),
         name="assemble",
-    )(row_pick, col_pick, present, arriving, h_core)
-
-
-def product(total, part, cols, dm_panel, pieces, fresh):
+    )(*picks, arriving, *h_core)
+
+
+def product(cols, dm_panel, pieces):
     ncol, rows, width = dm_panel.shape
-    depth, wide = pieces[0][0][0].shape
+    depth = pieces[0][0][0][0].shape[0]
     per = depth // width
     bm = min(512, rows)
-    counts = [len(c) for c, _, _ in pieces]
     npiece = len(pieces)
-    nh = sum(counts)
+    nh = sum(len(arrays) for c, _, _ in pieces for arrays in c)
     scalars = jnp.stack(
         [jnp.asarray(s, jnp.int32) for _, _, s in pieces]
         + [jnp.asarray(w, jnp.int32) for _, w, _ in pieces]
@@ -250,71 +286,149 @@
     def kernel(sc_ref, *refs):
         h_refs = refs[:nh]
         d_refs = refs[nh : nh + npiece]
-        rest = refs[nh + npiece :]
-        if total is not None:
-            c_ref, rest = rest[0], rest[1:]
-        out_ref = rest[0]
-        held = rest[1 : 1 + npiece]
-        sems = rest[1 + npiece]
+        out_ref = refs[nh + npiece]
+        held = refs[nh + npiece + 1 : -1]
+        sems = refs[-1]
 
         @pl.when(pl.program_id(0) == 0)
         def _():
             at = 0
+            for p, (candidates, _, _) in enumerate(pieces):
+                for q, arrays in enumerate(candidates):
+                    mine = h_refs[at : at + len(arrays)]
+                    at += len(arrays)
+
+                    @pl.when(sc_ref[npiece + p] == q)
+                    def _(p=p, mine=mine):
+                        left = 0
+                        for ref in mine:
+                            right = left + ref.shape[1]
+                            pltpu.make_async_copy(
+                                ref, held[p].at[:, left:right], sems.at[p]
+                            ).start()
+                            left = right
+
             for p in range(npiece):
-                for q in range(counts[p]):
-
-                    @pl.when(sc_ref[npiece + p] == q)
-                    def _(p=p, at=at):
-                        pltpu.make_async_copy(h_refs[at], held[p], sems.at[p]).start()
-
-                    at += 1
-            first = 0
-            for p in range(npiece):
-                pltpu.make_async_copy(h_refs[first], held[p], sems.at[p]).wait()
-                first += counts[p]
+                pltpu.make_async_copy(held[p], held[p], sems.at[p]).wait()
 
         acc = None
         for p in range(npiece):
-            left = jnp.concatenate([d_refs[p][q] for q in range(per)], axis=1)
-            term = mm(left, held[p][...])
-            acc = term if acc is None else acc + term
-        if not fresh:
-            acc = acc + c_ref[...]
+            for q in range(per):
+                term = mm(d_refs[p][q], held[p][q * width : (q + 1) * width, :])
+                acc = term if acc is None else acc + term
         out_ref[...] = acc
 
     def d_map(p):
         return lambda i, sc: (sc[p], i, 0)
 
-    c_spec = pl.BlockSpec((bm, wide), lambda i, sc: (i, part))
-    args = [h for c, _, _ in pieces for h in c] + [dm_panel] * npiece
-    in_specs = [pl.BlockSpec(memory_space=pl.ANY)] * nh + [
-        pl.BlockSpec((per, bm, width), d_map(p)) for p in range(npiece)
-    ]
-    aliases = {}
-    if total is not None:
-        aliases = {1 + len(args): 0}
-        args.append(total)
-        in_specs.append(pl.BlockSpec(memory_space=pl.ANY) if fresh else c_spec)
     return pl.pallas_call(
         kernel,
         grid_spec=pltpu.PrefetchScalarGridSpec(
             num_scalar_prefetch=1,
             grid=(rows // bm,),
-            in_specs=in_specs,
-            out_specs=c_spec,
-            scratch_shapes=[pltpu.VMEM((depth, wide), BF16)] * npiece
+            in_specs=[pl.BlockSpec(memory_space=pl.ANY)] * nh
+            + [pl.BlockSpec((per, bm, width), d_map(p)) for p in range(npiece)],
+            out_specs=pl.BlockSpec((bm, cols), lambda i, sc: (i, 0)),
+            scratch_shapes=[pltpu.VMEM((depth, cols), BF16)] * npiece
             + [pltpu.SemaphoreType.DMA((npiece,))],
         ),
         out_shape=jax.ShapeDtypeStruct((rows, cols), F32),
-        input_output_aliases=aliases,
         compiler_params=pltpu.CompilerParams(vmem_limit_bytes=56 * MIB),
         cost_estimate=pl.CostEstimate(
-            flops=2 * npiece * rows * depth * wide,
-            bytes_accessed=npiece * (rows + wide) * depth * 2 + rows * wide * 8,
+            flops=2 * npiece * rows * depth * cols,
+            bytes_accessed=npiece * (rows + cols) * depth * 2 + rows * cols * 4,
             transcendentals=0,
         ),
         name="product",
-    )(scalars, *args)
+    )(scalars, *[x for c, _, _ in pieces for arrays in c for x in arrays], *[dm_panel] * npiece)
+
+
+def product_add(total, part, dm_panel, candidates, which, shard):
+    ncol, rows, width = dm_panel.shape
+    depth, wide = candidates[0].shape
+    per = depth // width
+    bm = min(512, rows)
+    steps = rows // bm
+    nh = len(candidates)
+    scalars = jnp.stack([jnp.asarray(which, jnp.int32), jnp.asarray(shard, jnp.int32)])
+
+    def kernel(sc_ref, *refs):
+        h_refs = refs[:nh]
+        dm_ref, total_ref, out_ref, held, d_ref, c_ref, h_sem, d_sems, c_sems, o_sems = refs[nh:]
+        columns = pl.ds(part * wide, wide)
+
+        def read_d(i, q):
+            return pltpu.make_async_copy(
+                dm_ref.at[sc_ref[1] * per + q, pl.ds(i * bm, bm)],
+                d_ref.at[i, :, pl.ds(q * width, width)],
+                d_sems.at[i, q],
+            )
+
+        def read_c(i):
+            return pltpu.make_async_copy(
+                total_ref.at[pl.ds(i * bm, bm), columns], c_ref.at[i], c_sems.at[i]
+            )
+
+        def write(i):
+            return pltpu.make_async_copy(
+                c_ref.at[i], out_ref.at[pl.ds(i * bm, bm), columns], o_sems.at[i]
+            )
+
+        for k in range(nh):
+
+            @pl.when(sc_ref[0] == k)
+            def _(k=k):
+                pltpu.make_async_copy(h_refs[k], held, h_sem.at[0]).start()
+
+        for i in range(steps):
+            for q in range(per):
+                read_d(i, q).start()
+            read_c(i).start()
+        pltpu.make_async_copy(h_refs[0], held, h_sem.at[0]).wait()
+        for i in range(steps):
+            for q in range(per):
+                read_d(i, q).wait()
+            read_c(i).wait()
+            c_ref[i] = c_ref[i] + mm(d_ref[i], held[...])
+            write(i).start()
+        for i in range(steps):
+            write(i).wait()
+
+    return pl.pallas_call(
+        kernel,
+        grid_spec=pltpu.PrefetchScalarGridSpec(
+            num_scalar_prefetch=1,
+            grid=(1,),
+            in_specs=[pl.BlockSpec(memory_space=pl.ANY)] * (nh + 2),
+            out_specs=pl.BlockSpec(memory_space=pl.ANY),
+            scratch_shapes=[
+                pltpu.VMEM((depth, wide), BF16),
+                pltpu.VMEM((steps, bm, depth), BF16),
+                pltpu.VMEM((steps, bm, wide), F32),
+                pltpu.SemaphoreType.DMA((1,)),
+                pltpu.SemaphoreType.DMA((steps, per)),
+                pltpu.SemaphoreType.DMA((steps,)),
+                pltpu.SemaphoreType.DMA((steps,)),
+            ],
+        ),
+        out_shape=jax.ShapeDtypeStruct(total.shape, F32),
+        input_output_aliases={2 + nh: 0},
+        compiler_params=pltpu.CompilerParams(vmem_limit_bytes=56 * MIB),
+        cost_estimate=pl.CostEstimate(
+            flops=2 * rows * depth * wide,
+            bytes_accessed=(rows + wide) * depth * 2 + rows * wide * 8,
+            transcendentals=0,
+        ),
+        name="product_add",
+    )(scalars, *candidates, dm_panel, total)
+
+
+PARTS = 2
+EARLY = (2, 1, 1, 1, 3)
+
+
+def tie(x, y):
+    return lax.optimization_barrier((x, y))
 
 
 def body(density, h_core, phi, v_ext, tile_blocks, tile_count):
@@ -329,64 +443,96 @@
     colb = cols_loc // BLK
     tdev, npts, local = phi.shape
     maxb = tile_blocks.shape[1]
+    line = nrow == 4
+
+    inward = [(0, 1), (3, 2)]
+    cross = [(1, 2), (2, 1)]
+    outward = [(1, 0), (2, 3)]
 
     blocks = tile_blocks.reshape(ndev, tdev, maxb)
     counts = tile_count.reshape(ndev, tdev)
     live = jnp.arange(maxb, dtype=jnp.int32)[None, None, :] < counts[:, :, None]
-    row_hit = live & (blocks // rowb == row_idx)
     col_hit = live & (blocks // colb == col_idx)
-    both = jnp.any(row_hit, axis=2) & jnp.any(col_hit, axis=2)
-    row_in = jnp.sum(jnp.where(row_hit, blocks - row_idx * rowb, 0), axis=2)
     col_in = jnp.sum(jnp.where(col_hit, blocks - col_idx * colb, 0), axis=2)
-    row_pick = jnp.sum(jnp.where(both, row_in, 0), axis=1)
-    col_pick = jnp.sum(jnp.where(both, col_in, 0), axis=1)
-    present = jnp.any(both, axis=1).astype(jnp.int32)
+
+    def picks_of(row):
+        row_hit = live & (blocks // rowb == row)
+        both = jnp.any(row_hit, axis=2) & jnp.any(col_hit, axis=2)
+        row_in = jnp.sum(jnp.where(row_hit, blocks - row * rowb, 0), axis=2)
+        row_pick = jnp.sum(jnp.where(both, row_in, 0), axis=1)
+        col_pick = jnp.sum(jnp.where(both, col_in, 0), axis=1)
+        return row_pick, col_pick, jnp.any(both, axis=1).astype(jnp.int32)
+
+    picks = picks_of(row_idx)
     mine = lax.dynamic_index_in_dim(blocks, myself, 0, keepdims=False)
     my_counts = lax.dynamic_index_in_dim(counts, myself, 0, keepdims=False)
     hold = ((mine // rowb)[:, :, None] * ncol + (mine // colb)[:, None, :]).reshape(tdev, -1)
 
-    outgoing = (gather_blocks(density, row_pick, col_pick) * DM_SCALE).astype(jnp.float16)
+    if line:
+        unit = rows_loc // sum(EARLY)
+        tops = [unit * sum(EARLY[:k]) for k in range(len(EARLY))]
+        early = [
+            lax.ppermute(h_core[t : t + unit * k].astype(BF16), "row", outward)
+            for t, k in zip(tops, EARLY)
+        ]
+    outgoing = (gather_blocks(density, picks[0], picks[1]) * DM_SCALE).astype(jnp.float16)
     incoming = lax.all_to_all(outgoing, ("row", "col"), split_axis=0, concat_axis=0, tiled=True)
 
     later, _ = lax.optimization_barrier((density, outgoing))
     dm_panel = lax.all_gather(later.astype(BF16), "col", axis=0, tiled=False)
 
     basis = split_basis(phi, my_counts)
+    if line:
+        incoming, early[0] = tie(incoming, early[0])
     returning = tile_ham(incoming.astype(F32), basis, v_ext, hold, my_counts)
+    if line:
+        returning, early[1] = tie(returning, early[1])
     arriving = lax.all_to_all(returning, ("row", "col"), split_axis=0, concat_axis=0, tiled=True)
-    where = (row_pick, col_pick, present)
-    parts = 2 if nrow == 4 else 1
-    low = assemble(h_core, arriving, *where, BF16, parts)
-    (hamiltonian,) = assemble(h_core, arriving, *where, F32, 1)
-
-    total = None
-    if nrow == 4:
-        swap = [(0, 1), (1, 0), (2, 3), (3, 2)]
-        cross = [(1, 2), (2, 1)]
-        outward = [(1, 0), (2, 3)]
-        partner = [lax.ppermute(x, "row", swap) for x in low]
-        near_mid = [lax.ppermute(x, "row", cross) for x in low]
-        far_mid = [lax.ppermute(x, "row", cross) for x in partner]
-        near_end = [lax.ppermute(x, "row", outward) for x in near_mid]
-        far_end = [lax.ppermute(x, "row", outward) for x in far_mid]
+    if line:
+        arriving, early[2] = tie(arriving, early[2])
+    low = assemble([h_core], arriving, picks, BF16, PARTS if line else 1)
+    (hamiltonian,) = assemble([h_core], arriving, picks, F32, 1)
+
+    if line:
+        pair_idx = row_idx + 1 - 2 * (row_idx % 2)
         is_low = row_idx < 2
         is_end = ((row_idx == 0) | (row_idx == 3)).astype(jnp.int32)
-        pair_idx = row_idx + 1 - 2 * (row_idx % 2)
         near_idx = jnp.where(is_low, 2, 1)
         far_idx = jnp.where(is_low, 3, 0)
-        for p in range(parts):
-            pieces = [((low[p],), 0, row_idx), ((partner[p],), 0, pair_idx)]
-            total = product(total, p, cols_loc, dm_panel, pieces, True)
-        for p in range(parts):
-            pieces = [((near_mid[p], near_end[p]), is_end, near_idx)]
-            total = product(total, p, cols_loc, dm_panel, pieces, False)
-        for p in range(parts):
-            pieces = [((far_mid[p], far_end[p]), is_end, far_idx)]
-            total = product(total, p, cols_loc, dm_panel, pieces, False)
+        pair_blocks = lax.ppermute(arriving, "row", outward)
+        low, early[3] = tie(low, early[3])
+        near_mid = [lax.ppermute(x, "row", cross) for x in low]
+        pair_mid = []
+        for p in range(PARTS):
+            ready = low[p] if p == 0 else tie(low[p], near_mid[p - 1])[0]
+            pair_mid.append(lax.ppermute(ready, "row", inward))
+        ready, (pair_blocks, early[4]) = tie(near_mid[0], (pair_blocks, early[4]))
+        near_end = [lax.ppermute(x, "row", outward) for x in [ready] + near_mid[1:]]
+        far_mid = [lax.ppermute(pair_mid[0], "row", cross)]
+        for p in range(1, PARTS):
+            ready, near_end[p - 1] = tie(pair_mid[p], near_end[p - 1])
+            far_mid.append(lax.ppermute(ready, "row", cross))
+        ready, near_end[-1] = tie(far_mid[0], near_end[-1])
+        far_end = [lax.ppermute(x, "row", outward) for x in [ready] + far_mid[1:]]
+        pair_end = assemble(early, pair_blocks, picks_of(pair_idx), BF16, 1)
+        total = product(
+            cols_loc,
+            dm_panel,
+            [
+                ((low,), 0, row_idx),
+                ((pair_mid, pair_end), is_end, pair_idx),
+                ((near_mid, near_end), is_end, near_idx),
+            ],
+        )
+        for p in range(PARTS):
+            total = product_add(
+                total, p, dm_panel, (far_mid[p], far_end[p]), is_end, far_idx
+            )
     else:
         ham_panel = lax.all_gather(low[0], "row", axis=0, tiled=False)
-        for k in range(nrow):
-            total = product(total, 0, cols_loc, dm_panel, [((ham_panel[k],), 0, k)], k == 0)
+        total = product(cols_loc, dm_panel, [(((ham_panel[0],),), 0, 0)])
+        for k in range(1, nrow):
+            total = product_add(total, 0, dm_panel, (ham_panel[k],), 0, k)
     return hamiltonian, total
 
 

time: 408 us -> 401 us (0.983)
  waiting for transfers between devices: 226 us -> 208 us
  starting transfers between devices: 25.3 us -> 42.4 us
  Pallas kernels: 117 us -> 100 us
  other arithmetic: 14.6 us -> 20 us
  local copies, waits for them, and re-layouts: 9.57 us -> 14.8 us
    pallas_call x6 -> x1, Pallas kernels: 79 us -> 37.3 us  [product(): pl.pallas_call(kernel, grid_spec=pltpu.PrefetchScalarGridSpec(num_scalar_...]
    all_to_all x1, waiting for transfers between devices: 25.6 us -> 0.01 us  [body(): lax.all_to_all(returning, ('row', 'col'), split_axis=0, concat_axis=0, ti...]
    ppermute x8 -> x14, waiting for transfers between devices: 185 us -> 208 us  [the longest x5 81.7 us: body(): lax.ppermute(h_core[t:t + unit * k].astype(BF16), 'row', outward)]
    pallas_call x0 -> x2, Pallas kernels: none -> 22.9 us  [product_add(): pl.pallas_call(kernel, grid_spec=pltpu.PrefetchScalarGridSpec(num_scalar_...]
    ppermute x8 -> x14, starting transfers between devices: 10.1 us -> 28 us  [the longest x2 12 us: body(): pair_mid.append(lax.ppermute(ready, 'row', inward))]
    all_to_all x1, waiting for transfers between devices: 16 us -> 0.01 us  [body(): lax.all_to_all(outgoing, ('row', 'col'), split_axis=0, concat_axis=0, til...]
    pallas_call x2 -> x3, Pallas kernels: 19.7 us -> 21.8 us  [assemble(): pl.pallas_call(kernel, grid_spec=pltpu.PrefetchScalarGridSpec(num_scalar_...]
    unnamed x21 -> x43, local copies, waits for them, and re-layouts: 8.68 us -> 9.11 us
  transfers between devices with their start and end apart: 13 -> 19, of which waited for: 8 -> 9; matrix products, arithmetic and copies ran while one was open for 1% -> 4% of each run, Pallas kernels for 25% -> 21%
where the time goes in v3:
time: 401 us; the launch traced here: 400 us
  waiting for transfers between devices  208 us (52%)
  Pallas kernels  100 us (25%)
  starting transfers between devices  42.4 us (11%)
  other arithmetic  20 us (5%)
  local copies, waits for them, and re-layouts  14.8 us (4%)
  between operations  14.5 us (4%)
    ppermute x5, waiting for transfers between devices, body(): lax.ppermute(h_core[t:t + unit * k].astype(BF16), 'row', outward)  81.7 us
    ppermute x2, waiting for transfers between devices, body(): near_end = [lax.ppermute(x, 'row', outward) for x in [ready] + near_mid[1:]]  64.5 us
    ppermute x2, waiting for transfers between devices, body(): far_end = [lax.ppermute(x, 'row', outward) for x in [ready] + far_mid[1:]]  40.9 us
    pallas_call x1, Pallas kernels, product(): pl.pallas_call(kernel, grid_spec=pltpu.PrefetchScalarGridSpec(num_scalar_...  37.3 us
    pallas_call x2, Pallas kernels, product_add(): pl.pallas_call(kernel, grid_spec=pltpu.PrefetchScalarGridSpec(num_scalar_...  22.9 us
    pallas_call x3, Pallas kernels, assemble(): pl.pallas_call(kernel, grid_spec=pltpu.PrefetchScalarGridSpec(num_scalar_...  21.8 us
    ppermute x1, waiting for transfers between devices, body(): pair_blocks = lax.ppermute(arriving, 'row', outward)  21.2 us
    ppermute x2, starting transfers between devices, body(): pair_mid.append(lax.ppermute(ready, 'row', inward))  12 us
  transfers between devices with their start and end apart: 19, of which 9 were waited for; matrix products, arithmetic and copies ran while one was open for 4% of the time, Pallas kernels for 21%

profile of v3, /device:TPU:0, one launch (start us, length us, event | category | flops | bytes accessed | tf_op | source)
XLA Modules:
  0.0 400.1 jit_solution(5486310510886280574)
XLA Ops:
  10.0 4.4 %gather_blocks.1 = f32[32,128,128]{2,1,0:T(8,128)} custom-call(s32[32]{0:T(128)} %get-tuple-element.52.row_ref, s32[32]{0:T(128)} %get-tuple-element.51.col_ref, f32[2048,1024]{1,0:T(8,128)} %dens_ref.1), custom_call_target="tpu_custom_call" | custom-call | bytes 4194304 | tf_op jit(solution)/shard_map/gather_blocks/pallas_call | solution.py:43
  14.4 2.9 multiply_convert_fusion
  17.3 6.1 %convert_element_type.24 = bf16[2048,1024]{1,0:T(8,128)(2,1)} convert(f32[2048,1024]{1,0:T(8,128)} %dens_ref.1) | non-fusion elementwise | flops 2097152 | bytes 12582912 | tf_op jit(solution)/shard_map/convert_element_type | solution.py:482
  23.4 7.1 %all-to-all-start = ((f16[32,128,128]{2,1,0:T(8,128)(2,1)}), f16[32,128,128]{2,1,0:T(8,128)(2,1)}, u32[]{:S(2)}, u32[]{:S(2)}) async-start(f16[32,128,128]{2,1,0:T(8,128)(2,1)} %multiply_convert_fusion), calls=%async_computation | async-start | bytes 2097152 | tf_op jit(solution)/shard_map/all_to_all | solution.py:479
  30.5 5.3 %convert.8 = bf16[2048,1024]{1,0:T(8,128)(2,1)S(1)} convert(f32[2048,1024]{1,0:T(8,128)} %rest_0_.3) | non-fusion elementwise | flops 2097152 | bytes 12582912 | tf_op jit(solution)/shard_map/convert.5
  37.0 1.4 collective-permute-start
  41.8 2.2 copy-done
  44.0 2.2 split_basis.1
  50.2 22.9 %collective-permute-done.rest_0_ = bf16[512,1024]{1,0:T(8,128)(2,1)} collective-permute-done((bf16[512,1024]{1,0:T(8,128)(2,1)}, bf16[512,1024]{1,0:T(8,128)(2,1)}, u32[]{:S(2)}, u32[]{:S(2)}) %collective-permute-start) | collective-permute-done | bytes 1048608 | tf_op jit(solution)/shard_map/ppermute | solution.py:475
  73.1 1.5 convert_element_type.23.in_ref
  75.0 11.3 %tile_ham.1 = bf16[32,128,128]{2,1,0:T(8,128)(2,1)} custom-call(s32[2,16]{1,0:T(2,128)S(1)} %add.56.hold_ref, s32[2]{0:T(128)S(1)} %dynamic-slice_bitcast_fusion.count_ref, f32[32,128,128]{2,1,0:T(8,128)S(1)} %convert_element_type.23.in_ref, bf16[2,1024,512]{2,1,0:T(8,128)(2,1)S(1)} %get-tuple-element.27.hi_ref, bf16[2,1024,512]{2,1,0:T(8,128)(2,1)S(1)} %copy-done.2, ...), custom_call_target="tpu_custom_call" | custom-call | flops 6442450944 | bytes 8388608 | tf_op jit(solution)/shard_map/tile_ham/pallas_call | solution.py:140
  86.4 4.4 %all-to-all-start.1 = ((bf16[32,128,128]{2,1,0:T(8,128)(2,1)}), bf16[32,128,128]{2,1,0:T(8,128)(2,1)S(1)}, u32[]{:S(2)}, u32[]{:S(2)}) async-start(bf16[32,128,128]{2,1,0:T(8,128)(2,1)} %tile_ham.1), calls=%async_computation.1 | async-start | bytes 2097152 | tf_op jit(solution)/shard_map/all_to_all | solution.py:490
  94.1 28.2 %collective-permute-done.2.rest_2_ = bf16[256,1024]{1,0:T(8,128)(2,1)S(1)} collective-permute-done((bf16[256,1024]{1,0:T(8,128)(2,1)S(1)}, bf16[256,1024]{1,0:T(8,128)(2,1)S(1)}, u32[]{:S(2)}, u32[]{:S(2)}) %collective-permute-start.2) | collective-permute-done | bytes 524320 | tf_op jit(solution)/shard_map/ppermute | solution.py:475
  123.3 7.6 %assemble.4 = (bf16[2048,512]{1,0:T(8,128)(2,1)}, bf16[2048,512]{1,0:T(8,128)(2,1)}) custom-call(s32[32]{0:T(128)} %get-tuple-element.52.row_ref, s32[32]{0:T(128)} %get-tuple-element.51.col_ref, s32[32]{0:T(128)} %convert_element_type.10.present_ref, bf16[32,128,128]{2,1,0:T(8,128)(2,1)} %copy-done.6, f32[2048,1024]{1,0:T(8,128)} %rest_0_.3), custom_call_target="tpu_custom_call" | custom-call | flops 2097152 | bytes 12582912 | tf_op jit(solution)/shard_map/assemble/pallas_call | solution.py:253
  130.9 2.1 collective-permute-done.3.rest_3_
  133.8 1.5 slice.29
  138.0 6.0 %collective-permute-start.11 = (bf16[2048,512]{1,0:T(8,128)(2,1)S(1)}, bf16[2048,512]{1,0:T(8,128)(2,1)}, u32[]{:S(2)}, u32[]{:S(2)}) collective-permute-start(bf16[2048,512]{1,0:T(8,128)(2,1)S(1)} %copy-done.9), channel_id=1, source_target_pairs={{0,8},{24,16},{1,9},{25,17},{2,10},{26,18},{3,11},{27,19},{4,12},{... | collective-permute-start | bytes 6291464 | tf_op jit(solution)/shard_map/ppermute | solution.py:508
  144.0 2.0 collective-permute-start.13
  146.0 28.5 %collective-permute-done.7.rest_4_ = bf16[768,1024]{1,0:T(8,128)(2,1)S(1)} collective-permute-done((bf16[768,1024]{1,0:T(8,128)(2,1)S(1)}, bf16[768,1024]{1,0:T(8,128)(2,1)S(1)}, u32[]{:S(2)}, u32[]{:S(2)}) %collective-permute-start.7) | collective-permute-done | bytes 1572896 | tf_op jit(solution)/shard_map/ppermute | solution.py:475
  174.5 21.2 %collective-permute-done.6.in_ref = bf16[32,128,128]{2,1,0:T(8,128)(2,1)S(1)} collective-permute-done((bf16[32,128,128]{2,1,0:T(8,128)(2,1)S(1)}, bf16[32,128,128]{2,1,0:T(8,128)(2,1)S(1)}, u32[]{:S(2)}, u32[]{:S(2)}) %collective-permute-start.6) | collective-permute-done | bytes 1048608 | tf_op jit(solution)/shard_map/ppermute | solution.py:502
  197.1 6.0 %collective-permute-start.5 = (bf16[2048,512]{1,0:T(8,128)(2,1)}, bf16[2048,512]{1,0:T(8,128)(2,1)}, u32[]{:S(2)}, u32[]{:S(2)}) collective-permute-start(bf16[2048,512]{1,0:T(8,128)(2,1)} %get-tuple-element.37.refs_1_), channel_id=1, source_target_pairs={{0,8},{24,16},{1,9},{25,17},{2,10},{26,18},{3,11},{27,19},{4,12},{... | collective-permute-start | bytes 6291464 | tf_op jit(solution)/shard_map/ppermute | solution.py:508
  205.2 41.0 %collective-permute-done.8.refs_7_ = bf16[2048,512]{1,0:T(8,128)(2,1)S(1)} collective-permute-done((bf16[2048,512]{1,0:T(8,128)(2,1)S(1)}, bf16[2048,512]{1,0:T(8,128)(2,1)S(1)}, u32[]{:S(2)}, u32[]{:S(2)}) %collective-permute-start.8) | collective-permute-done | bytes 2097184 | tf_op jit(solution)/shard_map/ppermute | solution.py:510
  247.6 2.0 collective-permute-start.9
  251.5 8.7 %assemble.3 = f32[2048,1024]{1,0:T(8,128)} custom-call(s32[32]{0:T(128)} %get-tuple-element.52.row_ref, s32[32]{0:T(128)} %get-tuple-element.51.col_ref, s32[32]{0:T(128)} %convert_element_type.10.present_ref, bf16[32,128,128]{2,1,0:T(8,128)(2,1)} %copy-done.6, f32[2048,1024]{1,0:T(8,128)} %rest_0_.3), custom_call_target="tpu_custom_call" | custom-call | flops 2097152 | bytes 12582912 | tf_op jit(solution)/shard_map/assemble/pallas_call | solution.py:253
  260.2 5.6 %assemble.5.refs_4_ = bf16[2048,1024]{1,0:T(8,128)(2,1)} custom-call(s32[32]{0:T(128)} %get-tuple-element.53.row_ref, s32[32]{0:T(128)} %get-tuple-element.50.col_ref, s32[32]{0:T(128)} %convert_element_type.25.present_ref, bf16[32,128,128]{2,1,0:T(8,128)(2,1)} %copy-done.13, bf16[512,1024]{1,0:T(8,128)(2,1)} %collective-permute-done.rest_0_, ...), custom_call_target="tpu_custom_call" | custom-call | flops 2097152 | bytes 12582912 | tf_op jit(solution)/shard_map/assemble/pallas_call | solution.py:253
  265.8 23.4 %collective-permute-done.14.refs_8_ = bf16[2048,512]{1,0:T(8,128)(2,1)} collective-permute-done((bf16[2048,512]{1,0:T(8,128)(2,1)}, bf16[2048,512]{1,0:T(8,128)(2,1)}, u32[]{:S(2)}, u32[]{:S(2)}) %collective-permute-start.14) | collective-permute-done | bytes 2097184 | tf_op jit(solution)/shard_map/ppermute | solution.py:510
  290.5 1.5 collective-permute-start.10
  292.0 37.3 %product.1.refs_3_ = f32[2048,1024]{1,0:T(8,128)} custom-call(s32[6]{0:T(128)} %stack.36.sc_ref, bf16[2048,512]{1,0:T(8,128)(2,1)} %get-tuple-element.36.refs_0_, bf16[2048,512]{1,0:T(8,128)(2,1)} %get-tuple-element.37.refs_1_, bf16[2048,512]{1,0:T(8,128)(2,1)} %collective-permute-done.11.refs_2_, bf16[2048,512]{1,0:T(8,128)(2,1)} %collective-permute-done.5.refs_3_, ...), custom_call_target="tpu_custom_call" | custom-call | flops 25769803776 | bytes 46137344 | tf_op jit(solution)/shard_map/product/pallas_call | solution.py:324
  329.3 10.5 %collective-permute-done.15.refs_1_ = bf16[2048,512]{1,0:T(8,128)(2,1)} collective-permute-done((bf16[2048,512]{1,0:T(8,128)(2,1)S(1)}, bf16[2048,512]{1,0:T(8,128)(2,1)}, u32[]{:S(2)}, u32[]{:S(2)}) %collective-permute-start.15) | collective-permute-done | bytes 2097184 | tf_op jit(solution)/shard_map/ppermute | solution.py:516
  339.8 11.5 %product_add.2.refs_3_ = f32[2048,1024]{1,0:T(8,128)} custom-call(s32[2]{0:T(128)} %pad_add_fusion.sc_ref, bf16[2048,512]{1,0:T(8,128)(2,1)} %copy-done.8, bf16[2048,512]{1,0:T(8,128)(2,1)} %collective-permute-done.15.refs_1_, bf16[8,2048,1024]{2,1,0:T(8,128)(2,1)} %bitcast.31, f32[2048,1024]{1,0:T(8,128)} %product.1.refs_3_), custom_call_target="tpu_custom_call", output_to_operand_aliasing={{}: (4, {})} | custom-call | flops 4294967296 | bytes 18874368 | tf_op jit(solution)/shard_map/product_add/pallas_call | solution.py:397
  351.3 30.5 %collective-permute-done.10.refs_1_ = bf16[2048,512]{1,0:T(8,128)(2,1)} collective-permute-done((bf16[2048,512]{1,0:T(8,128)(2,1)}, bf16[2048,512]{1,0:T(8,128)(2,1)}, u32[]{:S(2)}, u32[]{:S(2)}) %collective-permute-start.10) | collective-permute-done | bytes 2097184 | tf_op jit(solution)/shard_map/ppermute | solution.py:516
  381.7 11.5 %product_add.3 = f32[2048,1024]{1,0:T(8,128)} custom-call(s32[2]{0:T(128)} %pad_add_fusion.sc_ref, bf16[2048,512]{1,0:T(8,128)(2,1)} %collective-permute-done.9.refs_0_, bf16[2048,512]{1,0:T(8,128)(2,1)} %collective-permute-done.10.refs_1_, bf16[8,2048,1024]{2,1,0:T(8,128)(2,1)} %bitcast.32, ...), custom_call_target="tpu_custom_call", output_to_operand_aliasing={{}: (4, {})} | custom-call | flops 4294967296 | bytes 18874368 | tf_op jit(solution)/shard_map/product_add/pallas_call | solution.py:397
  (89 shorter events, 27.2 us)
Async XLA Ops:
  7.2 284.9 %all-gather.3.cloned.1.call-start = ((), (), s32[]{:S(2)}) async-start(), calls=%async_computation.2 | async-start | bytes 37748736 | tf_op jit(solution)/shard_map/all_gather | solution.py:482
  23.4 49.8 %all-to-all-start = ((f16[32,128,128]{2,1,0:T(8,128)(2,1)}), f16[32,128,128]{2,1,0:T(8,128)(2,1)}, u32[]{:S(2)}, u32[]{:S(2)}) async-start(f16[32,128,128]{2,1,0:T(8,128)(2,1)} %multiply_convert_fusion), calls=%async_computation | async-start | bytes 2097152 | tf_op jit(solution)/shard_map/all_to_all | solution.py:479
  37.0 4.0 %copy-start.18 = (s32[64,4]{0,1:T(4,128)S(1)}, s32[64,4]{0,1:T(4,128)}, u32[]{:S(2)}) copy-start(s32[64,4]{0,1:T(4,128)} %param.10) | copy-start | bytes 3076
  37.0 4.1 %copy-start.20 = (s32[64]{0:T(128)S(1)}, s32[64]{0:T(128)}, u32[]{:S(2)}) copy-start(s32[64]{0:T(128)} %param.11) | copy-start | bytes 772
  37.0 4.4 %copy-start.19 = (f32[2,1024]{1,0:T(2,128)S(1)}, f32[2,1024]{1,0:T(2,128)}, u32[]{:S(2)}) copy-start(f32[2,1024]{1,0:T(2,128)} %param.9) | copy-start | bytes 24580
  37.0 36.2 %collective-permute-start = (bf16[512,1024]{1,0:T(8,128)(2,1)}, bf16[512,1024]{1,0:T(8,128)(2,1)}, u32[]{:S(2)}, u32[]{:S(2)}) collective-permute-start(bf16[512,1024]{1,0:T(8,128)(2,1)} %slice.25), channel_id=1, source_target_pairs={{8,0},{16,24},{9,1},{17,25},{10,2},{18,26},{11,3},{19,27},{12,4},{... | collective-permute-start | bytes 3145736 | tf_op jit(solution)/shard_map/ppermute | solution.py:475
  39.7 46.7 %collective-permute-start.1 = (bf16[256,1024]{1,0:T(8,128)(2,1)}, bf16[256,1024]{1,0:T(8,128)(2,1)}, u32[]{:S(2)}, u32[]{:S(2)}) collective-permute-start(bf16[256,1024]{1,0:T(8,128)(2,1)} %get-tuple-element.63), channel_id=1, source_target_pairs={{8,0},{16,24},{9,1},{17,25},{10,2},{18,26},{11,3},{19,27},{12,4},{... | collective-permute-start | bytes 1572872 | tf_op jit(solution)/shard_map/ppermute | solution.py:475
  86.4 4.5 %copy-start.17 = (bf16[256,1024]{1,0:T(8,128)(2,1)S(1)}, bf16[256,1024]{1,0:T(8,128)(2,1)}, u32[]{:S(2)}) copy-start(bf16[256,1024]{1,0:T(8,128)(2,1)} %get-tuple-element.62) | copy-start | bytes 1572868
  86.4 5.8 %copy-start.16 = (bf16[256,1024]{1,0:T(8,128)(2,1)S(1)}, bf16[256,1024]{1,0:T(8,128)(2,1)}, u32[]{:S(2)}) copy-start(bf16[256,1024]{1,0:T(8,128)(2,1)} %get-tuple-element.61) | copy-start | bytes 1572868
  86.4 35.9 %all-to-all-start.1 = ((bf16[32,128,128]{2,1,0:T(8,128)(2,1)}), bf16[32,128,128]{2,1,0:T(8,128)(2,1)S(1)}, u32[]{:S(2)}, u32[]{:S(2)}) async-start(bf16[32,128,128]{2,1,0:T(8,128)(2,1)} %tile_ham.1), calls=%async_computation.1 | async-start | bytes 2097152 | tf_op jit(solution)/shard_map/all_to_all | solution.py:490
  90.8 31.4 %collective-permute-start.2 = (bf16[256,1024]{1,0:T(8,128)(2,1)S(1)}, bf16[256,1024]{1,0:T(8,128)(2,1)S(1)}, u32[]{:S(2)}, u32[]{:S(2)}) collective-permute-start(bf16[256,1024]{1,0:T(8,128)(2,1)S(1)} %copy-done.17), channel_id=1, source_target_pairs={{8,0},{16,24},{9,1},{17,25},{10,2},{18,26},{11,3},{19,27},{12,4},{... | collective-permute-start | bytes 1572872 | tf_op jit(solution)/shard_map/ppermute | solution.py:475
  92.2 40.9 %collective-permute-start.3 = (bf16[256,1024]{1,0:T(8,128)(2,1)S(1)}, bf16[256,1024]{1,0:T(8,128)(2,1)S(1)}, u32[]{:S(2)}, u32[]{:S(2)}) collective-permute-start(bf16[256,1024]{1,0:T(8,128)(2,1)S(1)} %copy-done.16), channel_id=1, source_target_pairs={{8,0},{16,24},{9,1},{17,25},{10,2},{18,26},{11,3},{19,27},{12,4},{... | collective-permute-start | bytes 1572872 | tf_op jit(solution)/shard_map/ppermute | solution.py:475
  122.3 13.1 %copy-start.14 = (bf16[256,1024]{1,0:T(8,128)(2,1)}, bf16[256,1024]{1,0:T(8,128)(2,1)S(1)}, u32[]{:S(2)}) copy-start(bf16[256,1024]{1,0:T(8,128)(2,1)S(1)} %collective-permute-done.2.rest_2_) | copy-start | bytes 1572868
  130.9 5.8 %copy-start.7 = (bf16[32,128,128]{2,1,0:T(8,128)(2,1)S(1)}, bf16[32,128,128]{2,1,0:T(8,128)(2,1)}, u32[]{:S(2)}) copy-start(bf16[32,128,128]{2,1,0:T(8,128)(2,1)} %copy-done.6) | copy-start | bytes 3145732
  130.9 7.1 %copy-start.9 = (bf16[2048,512]{1,0:T(8,128)(2,1)S(1)}, bf16[2048,512]{1,0:T(8,128)(2,1)}, u32[]{:S(2)}) copy-start(bf16[2048,512]{1,0:T(8,128)(2,1)} %get-tuple-element.36.refs_0_) | copy-start | bytes 6291460
  133.0 70.1 %copy-start.15 = (bf16[256,1024]{1,0:T(8,128)(2,1)}, bf16[256,1024]{1,0:T(8,128)(2,1)S(1)}, u32[]{:S(2)}) copy-start(bf16[256,1024]{1,0:T(8,128)(2,1)S(1)} %collective-permute-done.3.rest_3_) | copy-start | bytes 1572868
  133.0 62.8 %collective-permute-start.4 = (bf16[2048,512]{1,0:T(8,128)(2,1)}, bf16[2048,512]{1,0:T(8,128)(2,1)S(1)}, u32[]{:S(2)}, u32[]{:S(2)}) collective-permute-start(bf16[2048,512]{1,0:T(8,128)(2,1)} %get-tuple-element.36.refs_0_), channel_id=1, source_target_pairs={{8,16},{16,8},{9,17},{17,9},{10,18},{18,10},{11,19},{19,11},{12,20... | collective-permute-start | bytes 6291464 | tf_op jit(solution)/shard_map/ppermute | solution.py:504
  135.4 39.2 %collective-permute-start.7 = (bf16[768,1024]{1,0:T(8,128)(2,1)S(1)}, bf16[768,1024]{1,0:T(8,128)(2,1)S(1)}, u32[]{:S(2)}, u32[]{:S(2)}) collective-permute-start(bf16[768,1024]{1,0:T(8,128)(2,1)S(1)} %slice.29), channel_id=1, source_target_pairs={{8,0},{16,24},{9,1},{17,25},{10,2},{18,26},{11,3},{19,27},{12,4},{... | collective-permute-start | bytes 4718600 | tf_op jit(solution)/shard_map/ppermute | solution.py:475
  136.7 59.1 %collective-permute-start.6 = (bf16[32,128,128]{2,1,0:T(8,128)(2,1)S(1)}, bf16[32,128,128]{2,1,0:T(8,128)(2,1)S(1)}, u32[]{:S(2)}, u32[]{:S(2)}) collective-permute-start(bf16[32,128,128]{2,1,0:T(8,128)(2,1)S(1)} %copy-done.7), channel_id=1, source_target_pairs={{8,0},{16,24},{9,1},{17,25},{10,2},{18,26},{11,3},{19,27},{12,4},{... | collective-permute-start | bytes 3145736 | tf_op jit(solution)/shard_map/ppermute | solution.py:502
  138.0 65.1 %collective-permute-start.11 = (bf16[2048,512]{1,0:T(8,128)(2,1)S(1)}, bf16[2048,512]{1,0:T(8,128)(2,1)}, u32[]{:S(2)}, u32[]{:S(2)}) collective-permute-start(bf16[2048,512]{1,0:T(8,128)(2,1)S(1)} %copy-done.9), channel_id=1, source_target_pairs={{0,8},{24,16},{1,9},{25,17},{2,10},{26,18},{3,11},{27,19},{4,12},{... | collective-permute-start | bytes 6291464 | tf_op jit(solution)/shard_map/ppermute | solution.py:508
  144.0 59.9 %collective-permute-start.13 = (bf16[2048,512]{1,0:T(8,128)(2,1)}, bf16[2048,512]{1,0:T(8,128)(2,1)}, u32[]{:S(2)}, u32[]{:S(2)}) collective-permute-start(bf16[2048,512]{1,0:T(8,128)(2,1)} %get-tuple-element.37.refs_1_), channel_id=1, source_target_pairs={{8,16},{16,8},{9,17},{17,9},{10,18},{18,10},{11,19},{19,11},{12,20... | collective-permute-start | bytes 6291464 | tf_op jit(solution)/shard_map/ppermute | solution.py:504
  174.5 21.2 %copy-start.12 = (bf16[768,1024]{1,0:T(8,128)(2,1)}, bf16[768,1024]{1,0:T(8,128)(2,1)S(1)}, u32[]{:S(2)}) copy-start(bf16[768,1024]{1,0:T(8,128)(2,1)S(1)} %collective-permute-done.7.rest_4_) | copy-start | bytes 4718596
  195.8 64.4 %copy-start.13 = (bf16[32,128,128]{2,1,0:T(8,128)(2,1)}, bf16[32,128,128]{2,1,0:T(8,128)(2,1)S(1)}, u32[]{:S(2)}) copy-start(bf16[32,128,128]{2,1,0:T(8,128)(2,1)S(1)} %collective-permute-done.6.in_ref) | copy-start | bytes 3145732
  195.8 7.3 %copy-start.10 = (bf16[2048,512]{1,0:T(8,128)(2,1)}, bf16[2048,512]{1,0:T(8,128)(2,1)S(1)}, u32[]{:S(2)}) copy-start(bf16[2048,512]{1,0:T(8,128)(2,1)S(1)} %collective-permute-done.4.refs_5_) | copy-start | bytes 6291460
  195.8 50.5 %collective-permute-start.8 = (bf16[2048,512]{1,0:T(8,128)(2,1)S(1)}, bf16[2048,512]{1,0:T(8,128)(2,1)S(1)}, u32[]{:S(2)}, u32[]{:S(2)}) collective-permute-start(bf16[2048,512]{1,0:T(8,128)(2,1)S(1)} %collective-permute-done.4.refs_5_), channel_id=1, source_target_pairs={{8,0},{16,24},{9,1},{17,25},{10,2},{18,26},{11,3},{19,27},{12,4},{... | collective-permute-start | bytes 6291464 | tf_op jit(solution)/shard_map/ppermute | solution.py:510
  197.1 50.5 %collective-permute-start.5 = (bf16[2048,512]{1,0:T(8,128)(2,1)}, bf16[2048,512]{1,0:T(8,128)(2,1)}, u32[]{:S(2)}, u32[]{:S(2)}) collective-permute-start(bf16[2048,512]{1,0:T(8,128)(2,1)} %get-tuple-element.37.refs_1_), channel_id=1, source_target_pairs={{0,8},{24,16},{1,9},{25,17},{2,10},{26,18},{3,11},{27,19},{4,12},{... | collective-permute-start | bytes 6291464 | tf_op jit(solution)/shard_map/ppermute | solution.py:508
  203.1 62.7 %collective-permute-start.12 = (bf16[2048,512]{1,0:T(8,128)(2,1)}, bf16[2048,512]{1,0:T(8,128)(2,1)S(1)}, u32[]{:S(2)}, u32[]{:S(2)}) collective-permute-start(bf16[2048,512]{1,0:T(8,128)(2,1)} %collective-permute-done.11.refs_2_), channel_id=1, source_target_pairs={{8,16},{16,8},{9,17},{17,9},{10,18},{18,10},{11,19},{19,11},{12,20... | collective-permute-start | bytes 6291464 | tf_op jit(solution)/shard_map/ppermute | solution.py:511
  203.9 85.3 %collective-permute-start.14 = (bf16[2048,512]{1,0:T(8,128)(2,1)}, bf16[2048,512]{1,0:T(8,128)(2,1)}, u32[]{:S(2)}, u32[]{:S(2)}) collective-permute-start(bf16[2048,512]{1,0:T(8,128)(2,1)} %collective-permute-done.13.refs_6_), channel_id=1, source_target_pairs={{8,0},{16,24},{9,1},{17,25},{10,2},{18,26},{11,3},{19,27},{12,4},{... | collective-permute-start | bytes 6291464 | tf_op jit(solution)/shard_map/ppermute | solution.py:510
  247.6 42.9 %collective-permute-start.9 = (bf16[2048,512]{1,0:T(8,128)(2,1)}, bf16[2048,512]{1,0:T(8,128)(2,1)}, u32[]{:S(2)}, u32[]{:S(2)}) collective-permute-start(bf16[2048,512]{1,0:T(8,128)(2,1)} %collective-permute-done.5.refs_3_), channel_id=1, source_target_pairs={{8,16},{16,8},{9,17},{17,9},{10,18},{18,10},{11,19},{19,11},{12,20... | collective-permute-start | bytes 6291464 | tf_op jit(solution)/shard_map/ppermute | solution.py:514
  265.8 63.5 %copy-start.8 = (bf16[2048,512]{1,0:T(8,128)(2,1)}, bf16[2048,512]{1,0:T(8,128)(2,1)S(1)}, u32[]{:S(2)}) copy-start(bf16[2048,512]{1,0:T(8,128)(2,1)S(1)} %collective-permute-done.12.refs_0_) | copy-start | bytes 6291460
  289.2 50.6 %collective-permute-start.15 = (bf16[2048,512]{1,0:T(8,128)(2,1)S(1)}, bf16[2048,512]{1,0:T(8,128)(2,1)}, u32[]{:S(2)}, u32[]{:S(2)}) collective-permute-start(bf16[2048,512]{1,0:T(8,128)(2,1)S(1)} %collective-permute-done.12.refs_0_), channel_id=1, source_target_pairs={{8,0},{16,24},{9,1},{17,25},{10,2},{18,26},{11,3},{19,27},{12,4},{... | collective-permute-start | bytes 6291464 | tf_op jit(solution)/shard_map/ppermute | solution.py:516
  290.5 91.2 %collective-permute-start.10 = (bf16[2048,512]{1,0:T(8,128)(2,1)}, bf16[2048,512]{1,0:T(8,128)(2,1)}, u32[]{:S(2)}, u32[]{:S(2)}) collective-permute-start(bf16[2048,512]{1,0:T(8,128)(2,1)} %collective-permute-done.9.refs_0_), channel_id=1, source_target_pairs={{8,0},{16,24},{9,1},{17,25},{10,2},{18,26},{11,3},{19,27},{12,4},{... | collective-permute-start | bytes 6291464 | tf_op jit(solution)/shard_map/ppermute | solution.py:516
  (8 other events, 14.4 us)
Sparse Core Ops, SparseCore 0:
  23.5 175.4 all-gather.2

commit v4 on v3

--- a/solution.py
+++ b/solution.py
@@ -14,6 +14,7 @@
 F32 = jnp.float32
 BF16 = jnp.bfloat16
 MIB = 1 << 20
+AHEAD = 3
 
 
 def gather_kernel(row_ref, col_ref, dens_ref, out_ref, sems):
@@ -56,6 +57,58 @@
         ),
         name="gather_blocks",
     )(row_pick, col_pick, density)
+
+
+def round_bands(x, top, sizes):
+    cols = x.shape[1]
+    bm = min(256, min(sizes))
+    source = [(k, g) for k, size in enumerate(sizes) for g in range(size // bm)]
+    steps = len(source)
+
+    def kernel(x_ref, *rest):
+        outs = rest[: len(sizes)]
+        raw_ref, low_ref, in_sems, out_sems = rest[len(sizes) :]
+
+        def read(g):
+            return pltpu.make_async_copy(
+                x_ref.at[pl.ds(top + g * bm, bm)], raw_ref.at[g], in_sems.at[g]
+            )
+
+        def write(g):
+            k, at = source[g]
+            return pltpu.make_async_copy(
+                low_ref.at[g], outs[k].at[pl.ds(at * bm, bm)], out_sems.at[g]
+            )
+
+        for g in range(min(AHEAD, steps)):
+            read(g).start()
+        for g in range(steps):
+            read(g).wait()
+            if g + AHEAD < steps:
+                read(g + AHEAD).start()
+            low_ref[g] = raw_ref[g].astype(BF16)
+            write(g).start()
+        for g in range(steps):
+            write(g).wait()
+
+    return pl.pallas_call(
+        kernel,
+        grid=(1,),
+        in_specs=[pl.BlockSpec(memory_space=pl.ANY)],
+        out_specs=[pl.BlockSpec(memory_space=pl.ANY)] * len(sizes),
+        scratch_shapes=[
+            pltpu.VMEM((steps, bm, cols), F32),
+            pltpu.VMEM((steps, bm, cols), BF16),
+            pltpu.SemaphoreType.DMA((steps,)),
+            pltpu.SemaphoreType.DMA((steps,)),
+        ],
+        out_shape=[jax.ShapeDtypeStruct((size, cols), BF16) for size in sizes],
+        compiler_params=pltpu.CompilerParams(vmem_limit_bytes=56 * MIB),
+        cost_estimate=pl.CostEstimate(
+            flops=sum(sizes) * cols, bytes_accessed=sum(sizes) * cols * 6, transcendentals=0
+        ),
+        name="round_bands",
+    )(x)
 
 
 def split(x):
@@ -101,9 +154,22 @@
 
 
 def tile_kernel(
-    hold_ref, count_ref, in_ref, hi_ref, lo_ref, hit_ref, lot_ref, v_ref, out_ref, dh_ref, dl_ref
+    hold_ref,
+    count_ref,
+    in_ref,
+    hi_ref,
+    lo_ref,
+    hit_ref,
+    lot_ref,
+    v_ref,
+    dens_ref,
+    out_ref,
+    dens_low_ref,
+    dh_ref,
+    dl_ref,
 ):
     t = pl.program_id(0)
+    dens_low_ref[...] = dens_ref[...].astype(BF16)
     maxb = hi_ref.shape[2] // BLK
     for i in range(maxb):
         for j in range(maxb):
@@ -131,8 +197,10 @@
                 ]
 
 
-def tile_ham(incoming, basis, v_ext, hold, counts):
+def tile_ham(incoming, basis, v_ext, hold, counts, density):
     n = incoming.shape[0]
+    rows, cols = density.shape
+    band = pl.BlockSpec((rows // basis[0].shape[0], cols), lambda t, *_: (t, 0))
     tdev, npts, local = basis[0].shape
     flops = tdev * 3 * 2 * 2 * npts * local * local
     spec = pl.BlockSpec((1, npts, local), lambda t, *_: (t, 0, 0))
@@ -149,20 +217,24 @@
                 spec_t,
                 spec_t,
                 pl.BlockSpec((1, npts, 1), lambda t, *_: (t, 0, 0)),
+                band,
             ],
-            out_specs=pl.BlockSpec((n, BLK, BLK), lambda t, *_: (0, 0, 0)),
+            out_specs=[pl.BlockSpec((n, BLK, BLK), lambda t, *_: (0, 0, 0)), band],
             scratch_shapes=[
                 pltpu.VMEM((local, local), BF16),
                 pltpu.VMEM((local, local), BF16),
             ],
         ),
-        out_shape=jax.ShapeDtypeStruct((n, BLK, BLK), BF16),
-        compiler_params=pltpu.CompilerParams(vmem_limit_bytes=44 * MIB),
+        out_shape=[
+            jax.ShapeDtypeStruct((n, BLK, BLK), BF16),
+            jax.ShapeDtypeStruct((rows, cols), BF16),
+        ],
+        compiler_params=pltpu.CompilerParams(vmem_limit_bytes=52 * MIB),
         cost_estimate=pl.CostEstimate(
             flops=flops, bytes_accessed=tdev * npts * local * 8, transcendentals=0
         ),
         name="tile_ham",
-    )(hold, counts, incoming, *basis, v_ext[:, :, None])
+    )(hold, counts, incoming, *basis, v_ext[:, :, None], density)
 
 
 def assemble(h_core, arriving, picks, dtype, parts):
@@ -200,8 +272,9 @@
                 low_refs[p].at[band(g)], outs[p].at[band(g)], out_sems.at[g, p]
             )
 
+        for g in range(min(AHEAD, steps)):
+            read(g).start()
         for g in range(steps):
-            read(g).start()
             num_ref[g] = 0
 
         def note(s, carry):
@@ -218,6 +291,8 @@
 
         for g in range(steps):
             read(g).wait()
+            if g + AHEAD < steps:
+                read(g + AHEAD).start()
             if widen:
                 work_ref[band(g), :] = raw_ref[band(g), :].astype(F32)
 
@@ -380,15 +455,20 @@
             def _(k=k):
                 pltpu.make_async_copy(h_refs[k], held, h_sem.at[0]).start()
 
-        for i in range(steps):
+        def start(i):
             for q in range(per):
                 read_d(i, q).start()
             read_c(i).start()
+
+        for i in range(min(2, steps)):
+            start(i)
         pltpu.make_async_copy(h_refs[0], held, h_sem.at[0]).wait()
         for i in range(steps):
             for q in range(per):
                 read_d(i, q).wait()
             read_c(i).wait()
+            if i + 2 < steps:
+                start(i + 2)
             c_ref[i] = c_ref[i] + mm(d_ref[i], held[...])
             write(i).start()
         for i in range(steps):
@@ -424,7 +504,7 @@
 
 
 PARTS = 2
-EARLY = (2, 1, 1, 1, 3)
+EARLY = (3, 2, 3)
 
 
 def tie(x, y):
@@ -470,26 +550,22 @@
 
     if line:
         unit = rows_loc // sum(EARLY)
-        tops = [unit * sum(EARLY[:k]) for k in range(len(EARLY))]
-        early = [
-            lax.ppermute(h_core[t : t + unit * k].astype(BF16), "row", outward)
-            for t, k in zip(tops, EARLY)
-        ]
+        sizes = [unit * k for k in EARLY]
+        first = round_bands(h_core, 0, sizes[:1])
+        density, first = tie(density, first)
+        rest = round_bands(h_core, sizes[0], sizes[1:])
+        early = [lax.ppermute(x, "row", outward) for x in first + rest]
     outgoing = (gather_blocks(density, picks[0], picks[1]) * DM_SCALE).astype(jnp.float16)
     incoming = lax.all_to_all(outgoing, ("row", "col"), split_axis=0, concat_axis=0, tiled=True)
 
-    later, _ = lax.optimization_barrier((density, outgoing))
-    dm_panel = lax.all_gather(later.astype(BF16), "col", axis=0, tiled=False)
-
     basis = split_basis(phi, my_counts)
     if line:
-        incoming, early[0] = tie(incoming, early[0])
-    returning = tile_ham(incoming.astype(F32), basis, v_ext, hold, my_counts)
-    if line:
-        returning, early[1] = tie(returning, early[1])
+        incoming, (early[0], _) = tie(incoming, (early[0], rest))
+    returning, dm_low = tile_ham(incoming.astype(F32), basis, v_ext, hold, my_counts, density)
+    dm_panel = lax.all_gather(dm_low, "col", axis=0, tiled=False)
     arriving = lax.all_to_all(returning, ("row", "col"), split_axis=0, concat_axis=0, tiled=True)
     if line:
-        arriving, early[2] = tie(arriving, early[2])
+        arriving, early[1] = tie(arriving, early[1])
     low = assemble([h_core], arriving, picks, BF16, PARTS if line else 1)
     (hamiltonian,) = assemble([h_core], arriving, picks, F32, 1)
 
@@ -500,20 +576,24 @@
         near_idx = jnp.where(is_low, 2, 1)
         far_idx = jnp.where(is_low, 3, 0)
         pair_blocks = lax.ppermute(arriving, "row", outward)
-        low, early[3] = tie(low, early[3])
-        near_mid = [lax.ppermute(x, "row", cross) for x in low]
+        near_mid = []
+        for p in range(PARTS):
+            ready = low[p]
+            if p == 1:
+                ready, (pair_blocks, early[2]) = tie(ready, (pair_blocks, early[2]))
+            near_mid.append(lax.ppermute(ready, "row", cross))
+        near_end = [lax.ppermute(x, "row", outward) for x in near_mid]
         pair_mid = []
         for p in range(PARTS):
             ready = low[p] if p == 0 else tie(low[p], near_mid[p - 1])[0]
             pair_mid.append(lax.ppermute(ready, "row", inward))
-        ready, (pair_blocks, early[4]) = tie(near_mid[0], (pair_blocks, early[4]))
-        near_end = [lax.ppermute(x, "row", outward) for x in [ready] + near_mid[1:]]
         far_mid = [lax.ppermute(pair_mid[0], "row", cross)]
         for p in range(1, PARTS):
             ready, near_end[p - 1] = tie(pair_mid[p], near_end[p - 1])
             far_mid.append(lax.ppermute(ready, "row", cross))
-        ready, near_end[-1] = tie(far_mid[0], near_end[-1])
-        far_end = [lax.ppermute(x, "row", outward) for x in [ready] + far_mid[1:]]
+        far_end = [lax.ppermute(x, "row", outward) for x in far_mid[:-1]]
+        ready, near_end[-1] = tie(far_mid[-1], near_end[-1])
+        far_end.append(lax.ppermute(ready, "row", outward))
         pair_end = assemble(early, pair_blocks, picks_of(pair_idx), BF16, 1)
         total = product(
             cols_loc,

time: 401 us -> 423 us (1.055)
  waiting for transfers between devices: 208 us -> 239 us
  other arithmetic: 20 us -> 8.6 us
  Pallas kernels: 100 us -> 111 us
  local copies, waits for them, and re-layouts: 14.8 us -> 10.5 us
    ppermute x2, waiting for transfers between devices: 0.01 us -> 39.6 us  [body(): pair_mid.append(lax.ppermute(ready, 'row', inward))]
    ppermute x11 -> x9, waiting for transfers between devices: 187 us -> 178 us  [the longest x3 109 us: body(): early = [lax.ppermute(x, 'row', outward) for x in first + rest]]
    pallas_call x0 -> x2, Pallas kernels: none -> 7.29 us  [round_bands(): pl.pallas_call(kernel, grid=(1,), in_specs=[pl.BlockSpec(memory_space=pl....]
    convert_element_type x2 -> x1, other arithmetic: 7.59 us -> 1.61 us  [body(): incoming.astype(F32)]
    another operation x1 -> x0, other arithmetic: 5.31 us -> none
    pallas_call x1, Pallas kernels: 11.3 us -> 16.3 us  [tile_ham(): pl.pallas_call(tile_kernel, grid_spec=pltpu.PrefetchScalarGridSpec(num_sc...]
    ppermute x11 -> x9, starting transfers between devices: 14.7 us -> 12 us  [the longest x3 3.88 us: body(): early = [lax.ppermute(x, 'row', outward) for x in first + rest]]
    unnamed x43 -> x35, local copies, waits for them, and re-layouts: 9.11 us -> 7.83 us
  transfers between devices with their start and end apart: 19 -> 17, of which waited for: 9 -> 9; matrix products, arithmetic and copies ran while one was open for 4% -> 1% of each run, Pallas kernels for 21% -> 18%
where the time goes in v4:
time: 423 us; the launch traced here: 422 us
  waiting for transfers between devices  239 us (57%)
  Pallas kernels  111 us (26%)
  starting transfers between devices  38.4 us (9%)
  between operations  14.5 us (3%)
  local copies, waits for them, and re-layouts  10.5 us (2%)
  other arithmetic  8.6 us (2%)
    ppermute x3, waiting for transfers between devices, body(): early = [lax.ppermute(x, 'row', outward) for x in first + rest]  109 us
    ppermute x2, waiting for transfers between devices, body(): pair_mid.append(lax.ppermute(ready, 'row', inward))  39.6 us
    pallas_call x1, Pallas kernels, product(): pl.pallas_call(kernel, grid_spec=pltpu.PrefetchScalarGridSpec(num_scalar_...  37.3 us
    ppermute x1, waiting for transfers between devices, body(): far_end.append(lax.ppermute(ready, 'row', outward))  33 us
    ppermute x2, waiting for transfers between devices, body(): near_end = [lax.ppermute(x, 'row', outward) for x in near_mid]  30 us
    pallas_call x3, Pallas kernels, assemble(): pl.pallas_call(kernel, grid_spec=pltpu.PrefetchScalarGridSpec(num_scalar_...  24.2 us
    ppermute x1, waiting for transfers between devices, body(): pair_blocks = lax.ppermute(arriving, 'row', outward)  21.4 us
    pallas_call x2, Pallas kernels, product_add(): pl.pallas_call(kernel, grid_spec=pltpu.PrefetchScalarGridSpec(num_scalar_...  19.4 us
  transfers between devices with their start and end apart: 17, of which 9 were waited for; matrix products, arithmetic and copies ran while one was open for 1% of the time, Pallas kernels for 18%

profile of v4, /device:TPU:0, one launch (start us, length us, event | category | flops | bytes accessed | tf_op | source)
XLA Modules:
  0.0 422.3 jit_solution(390412545913836990)
XLA Ops:
  9.2 2.8 round_bands.2
  12.7 4.5 %gather_blocks.1 = f32[32,128,128]{2,1,0:T(8,128)} custom-call(s32[32]{0:T(128)} %get-tuple-element.52.row_ref, s32[32]{0:T(128)} %get-tuple-element.51.col_ref, f32[2048,1024]{1,0:T(8,128)} %dens_ref.1), custom_call_target="tpu_custom_call" | custom-call | bytes 4194304 | tf_op jit(solution)/shard_map/gather_blocks/pallas_call | solution.py:44
  17.2 2.9 multiply_convert_fusion
  20.1 7.4 %all-to-all-start = ((f16[32,128,128]{2,1,0:T(8,128)(2,1)}), f16[32,128,128]{2,1,0:T(8,128)(2,1)S(1)}, u32[]{:S(2)}, u32[]{:S(2)}) async-start(f16[32,128,128]{2,1,0:T(8,128)(2,1)} %multiply_convert_fusion), calls=%async_computation | async-start | bytes 2097152 | tf_op jit(solution)/shard_map/all_to_all | solution.py:559
  29.2 1.4 copy.12.v_ref
  30.6 4.5 %round_bands.3 = (bf16[512,1024]{1,0:T(8,128)(2,1)}, bf16[768,1024]{1,0:T(8,128)(2,1)}) custom-call(f32[2048,1024]{1,0:T(8,128)} %rest_0_.3), custom_call_target="tpu_custom_call" | custom-call | flops 1310720 | bytes 7864320 | tf_op jit(solution)/shard_map/round_bands/pallas_call | solution.py:94
  35.2 2.2 split_basis.1
  41.4 1.3 copy-done.4
  42.7 38.2 %collective-permute-done.rest_0_ = bf16[768,1024]{1,0:T(8,128)(2,1)S(1)} collective-permute-done((bf16[768,1024]{1,0:T(8,128)(2,1)}, bf16[768,1024]{1,0:T(8,128)(2,1)S(1)}, u32[]{:S(2)}, u32[]{:S(2)}) %collective-permute-start) | collective-permute-done | bytes 1572896 | tf_op jit(solution)/shard_map/ppermute | solution.py:557
  80.9 1.6 convert_element_type.15.in_ref
  82.5 16.3 %tile_ham.1 = (bf16[32,128,128]{2,1,0:T(8,128)(2,1)}, bf16[2048,1024]{1,0:T(8,128)(2,1)}) custom-call(s32[2,16]{1,0:T(2,128)S(1)} %add.56.hold_ref, s32[2]{0:T(128)S(1)} %dynamic-slice_bitcast_fusion.count_ref, f32[32,128,128]{2,1,0:T(8,128)} %convert_element_type.15.in_ref, bf16[2,1024,512]{2,1,0:T(8,128)(2,1)} %copy-done.1, ...), custom_call_target="tpu_custom_call" | custom-call | flops 6442450944 | bytes 8388608 | tf_op jit(solution)/shard_map/tile_ham/pallas_call | solution.py:208
  98.8 4.6 %all-to-all-start.1 = ((bf16[32,128,128]{2,1,0:T(8,128)(2,1)}), bf16[32,128,128]{2,1,0:T(8,128)(2,1)S(1)}, u32[]{:S(2)}, u32[]{:S(2)}) async-start(bf16[32,128,128]{2,1,0:T(8,128)(2,1)} %get-tuple-element.35), calls=%async_computation.1 | async-start | bytes 2097152 | tf_op jit(solution)/shard_map/all_to_all | solution.py:566
  105.4 40.2 %collective-permute-done.1.rest_1_ = bf16[512,1024]{1,0:T(8,128)(2,1)S(1)} collective-permute-done((bf16[512,1024]{1,0:T(8,128)(2,1)}, bf16[512,1024]{1,0:T(8,128)(2,1)S(1)}, u32[]{:S(2)}, u32[]{:S(2)}) %collective-permute-start.1) | collective-permute-done | bytes 1048608 | tf_op jit(solution)/shard_map/ppermute | solution.py:557
  146.6 8.2 %assemble.4 = (bf16[2048,512]{1,0:T(8,128)(2,1)}, bf16[2048,512]{1,0:T(8,128)(2,1)}) custom-call(s32[32]{0:T(128)} %get-tuple-element.52.row_ref, s32[32]{0:T(128)} %get-tuple-element.51.col_ref, s32[32]{0:T(128)} %convert_element_type.13.present_ref, bf16[32,128,128]{2,1,0:T(8,128)(2,1)} %copy-done.5, f32[2048,1024]{1,0:T(8,128)} %rest_0_.3), custom_call_target="tpu_custom_call" | custom-call | flops 2097152 | bytes 12582912 | tf_op jit(solution)/shard_map/assemble/pallas_call | solution.py:328
  158.3 6.0 %collective-permute-start.11 = (bf16[2048,512]{1,0:T(8,128)(2,1)}, bf16[2048,512]{1,0:T(8,128)(2,1)}, u32[]{:S(2)}, u32[]{:S(2)}) collective-permute-start(bf16[2048,512]{1,0:T(8,128)(2,1)} %get-tuple-element.38.refs_0_), channel_id=1, source_target_pairs={{0,8},{24,16},{1,9},{25,17},{2,10},{26,18},{3,11},{27,19},{4,12},{... | collective-permute-start | bytes 6291464 | tf_op jit(solution)/shard_map/ppermute | solution.py:589
  164.3 30.5 %collective-permute-done.7.rest_2_ = bf16[768,1024]{1,0:T(8,128)(2,1)S(1)} collective-permute-done((bf16[768,1024]{1,0:T(8,128)(2,1)S(1)}, bf16[768,1024]{1,0:T(8,128)(2,1)S(1)}, u32[]{:S(2)}, u32[]{:S(2)}) %collective-permute-start.7) | collective-permute-done | bytes 1572896 | tf_op jit(solution)/shard_map/ppermute | solution.py:557
  194.8 21.4 %collective-permute-done.6.in_ref = bf16[32,128,128]{2,1,0:T(8,128)(2,1)S(1)} collective-permute-done((bf16[32,128,128]{2,1,0:T(8,128)(2,1)}, bf16[32,128,128]{2,1,0:T(8,128)(2,1)S(1)}, u32[]{:S(2)}, u32[]{:S(2)}) %collective-permute-start.6) | collective-permute-done | bytes 1048608 | tf_op jit(solution)/shard_map/ppermute | solution.py:578
  216.2 2.0 collective-permute-start.8
  218.3 4.4 %collective-permute-start.3 = (bf16[2048,512]{1,0:T(8,128)(2,1)}, bf16[2048,512]{1,0:T(8,128)(2,1)}, u32[]{:S(2)}, u32[]{:S(2)}) collective-permute-start(bf16[2048,512]{1,0:T(8,128)(2,1)} %get-tuple-element.41.refs_1_), channel_id=1, source_target_pairs={{0,8},{24,16},{1,9},{25,17},{2,10},{26,18},{3,11},{27,19},{4,12},{... | collective-permute-start | bytes 6291464 | tf_op jit(solution)/shard_map/ppermute | solution.py:589
  226.0 39.6 %collective-permute-done.3.refs_3_ = bf16[2048,512]{1,0:T(8,128)(2,1)} collective-permute-done((bf16[2048,512]{1,0:T(8,128)(2,1)}, bf16[2048,512]{1,0:T(8,128)(2,1)}, u32[]{:S(2)}, u32[]{:S(2)}) %collective-permute-start.3) | collective-permute-done | bytes 2097184 | tf_op jit(solution)/shard_map/ppermute | solution.py:589
  265.7 7.4 %collective-permute-done.4.refs_7_ = bf16[2048,512]{1,0:T(8,128)(2,1)S(1)} collective-permute-done((bf16[2048,512]{1,0:T(8,128)(2,1)S(1)}, bf16[2048,512]{1,0:T(8,128)(2,1)S(1)}, u32[]{:S(2)}, u32[]{:S(2)}) %collective-permute-start.4) | collective-permute-done | bytes 2097184 | tf_op jit(solution)/shard_map/ppermute | solution.py:585
  273.1 1.4 copy-done.8
  274.4 2.0 collective-permute-start.5
  278.2 9.2 %assemble.3 = f32[2048,1024]{1,0:T(8,128)} custom-call(s32[32]{0:T(128)} %get-tuple-element.52.row_ref, s32[32]{0:T(128)} %get-tuple-element.51.col_ref, s32[32]{0:T(128)} %convert_element_type.13.present_ref, bf16[32,128,128]{2,1,0:T(8,128)(2,1)} %copy-done.5, f32[2048,1024]{1,0:T(8,128)} %rest_0_.3), custom_call_target="tpu_custom_call" | custom-call | flops 2097152 | bytes 12582912 | tf_op jit(solution)/shard_map/assemble/pallas_call | solution.py:328
  287.4 6.8 %assemble.5.refs_4_ = bf16[2048,1024]{1,0:T(8,128)(2,1)} custom-call(s32[32]{0:T(128)} %get-tuple-element.53.row_ref, s32[32]{0:T(128)} %get-tuple-element.50.col_ref, s32[32]{0:T(128)} %convert_element_type.16.present_ref, bf16[32,128,128]{2,1,0:T(8,128)(2,1)} %copy-done.12, bf16[768,1024]{1,0:T(8,128)(2,1)} %copy-done.9, bf16[512,1024]{1,0:T(8,128)(2,1)} %copy-done.11, ...), custom_call_target="tpu_custom_call" | custom-call | flops 2097152 | bytes 12582912 | tf_op jit(solution)/shard_map/assemble/pallas_call | solution.py:328
  295.6 22.5 %collective-permute-done.9.refs_8_ = bf16[2048,512]{1,0:T(8,128)(2,1)} collective-permute-done((bf16[2048,512]{1,0:T(8,128)(2,1)}, bf16[2048,512]{1,0:T(8,128)(2,1)}, u32[]{:S(2)}, u32[]{:S(2)}) %collective-permute-start.9) | collective-permute-done | bytes 2097184 | tf_op jit(solution)/shard_map/ppermute | solution.py:585
  318.1 1.5 collective-permute-start.10
  319.6 37.3 %product.1.refs_3_ = f32[2048,1024]{1,0:T(8,128)} custom-call(s32[6]{0:T(128)} %stack.36.sc_ref, bf16[2048,512]{1,0:T(8,128)(2,1)} %get-tuple-element.38.refs_0_, bf16[2048,512]{1,0:T(8,128)(2,1)} %get-tuple-element.41.refs_1_, bf16[2048,512]{1,0:T(8,128)(2,1)} %collective-permute-done.11.refs_2_, bf16[2048,512]{1,0:T(8,128)(2,1)} %collective-permute-done.3.refs_3_, ...), custom_call_target="tpu_custom_call" | custom-call | flops 25769803776 | bytes 46137344 | tf_op jit(solution)/shard_map/product/pallas_call | solution.py:399
  356.9 6.1 %collective-permute-done.13.refs_1_ = bf16[2048,512]{1,0:T(8,128)(2,1)} collective-permute-done((bf16[2048,512]{1,0:T(8,128)(2,1)S(1)}, bf16[2048,512]{1,0:T(8,128)(2,1)}, u32[]{:S(2)}, u32[]{:S(2)}) %collective-permute-start.13) | collective-permute-done | bytes 2097184 | tf_op jit(solution)/shard_map/ppermute | solution.py:594
  363.1 9.7 %product_add.2.refs_3_ = f32[2048,1024]{1,0:T(8,128)} custom-call(s32[2]{0:T(128)} %pad_add_fusion.sc_ref, bf16[2048,512]{1,0:T(8,128)(2,1)} %copy-done.6, bf16[2048,512]{1,0:T(8,128)(2,1)} %collective-permute-done.13.refs_1_, bf16[8,2048,1024]{2,1,0:T(8,128)(2,1)} %bitcast.31, f32[2048,1024]{1,0:T(8,128)} %product.1.refs_3_), custom_call_target="tpu_custom_call", output_to_operand_aliasing={{}: (4, {})} | custom-call | flops 4294967296 | bytes 18874368 | tf_op jit(solution)/shard_map/product_add/pallas_call | solution.py:477
  372.8 33.0 %collective-permute-done.10.refs_1_ = bf16[2048,512]{1,0:T(8,128)(2,1)} collective-permute-done((bf16[2048,512]{1,0:T(8,128)(2,1)}, bf16[2048,512]{1,0:T(8,128)(2,1)}, u32[]{:S(2)}, u32[]{:S(2)}) %collective-permute-start.10) | collective-permute-done | bytes 2097184 | tf_op jit(solution)/shard_map/ppermute | solution.py:596
  405.7 9.7 %product_add.3 = f32[2048,1024]{1,0:T(8,128)} custom-call(s32[2]{0:T(128)} %pad_add_fusion.sc_ref, bf16[2048,512]{1,0:T(8,128)(2,1)} %collective-permute-done.5.refs_0_, bf16[2048,512]{1,0:T(8,128)(2,1)} %collective-permute-done.10.refs_1_, bf16[8,2048,1024]{2,1,0:T(8,128)(2,1)} %bitcast.32, ...), custom_call_target="tpu_custom_call", output_to_operand_aliasing={{}: (4, {})} | custom-call | flops 4294967296 | bytes 18874368 | tf_op jit(solution)/shard_map/product_add/pallas_call | solution.py:477
  (74 shorter events, 21.2 us)
Async XLA Ops:
  17.2 11.6 %copy-start.13 = (s32[64,4]{0,1:T(4,128)S(1)}, s32[64,4]{0,1:T(4,128)}, u32[]{:S(2)}) copy-start(s32[64,4]{0,1:T(4,128)} %param.10) | copy-start | bytes 3076
  17.2 11.7 %copy-start.15 = (s32[64]{0:T(128)S(1)}, s32[64]{0:T(128)}, u32[]{:S(2)}) copy-start(s32[64]{0:T(128)} %param.11) | copy-start | bytes 772
  17.2 12.0 %copy-start.14 = (f32[2,1024]{1,0:T(2,128)S(1)}, f32[2,1024]{1,0:T(2,128)}, u32[]{:S(2)}) copy-start(f32[2,1024]{1,0:T(2,128)} %param.9) | copy-start | bytes 24580
  20.1 60.8 %all-to-all-start = ((f16[32,128,128]{2,1,0:T(8,128)(2,1)}), f16[32,128,128]{2,1,0:T(8,128)(2,1)S(1)}, u32[]{:S(2)}, u32[]{:S(2)}) async-start(f16[32,128,128]{2,1,0:T(8,128)(2,1)} %multiply_convert_fusion), calls=%async_computation | async-start | bytes 2097152 | tf_op jit(solution)/shard_map/all_to_all | solution.py:559
  27.5 292.1 %all-gather.3.cloned.1.call-start = ((), (), s32[]{:S(2)}) async-start(), calls=%async_computation.2 | async-start | bytes 37748736 | tf_op jit(solution)/shard_map/all_gather | solution.py:565
  27.5 53.4 %collective-permute-start = (bf16[768,1024]{1,0:T(8,128)(2,1)}, bf16[768,1024]{1,0:T(8,128)(2,1)S(1)}, u32[]{:S(2)}, u32[]{:S(2)}) collective-permute-start(bf16[768,1024]{1,0:T(8,128)(2,1)} %round_bands.2), channel_id=1, source_target_pairs={{8,0},{16,24},{9,1},{17,25},{10,2},{18,26},{11,3},{19,27},{12,4},{... | collective-permute-start | bytes 4718600 | tf_op jit(solution)/shard_map/ppermute | solution.py:557
  30.6 4.6 %copy-start = (f32[2,1024,512]{2,1,0:T(8,128)S(1)}, f32[2,1024,512]{2,1,0:T(8,128)}, u32[]{:S(2)}) copy-start(f32[2,1024,512]{2,1,0:T(8,128)} %phi_ref.1) | copy-start | bytes 12582916
  37.4 1.3 copy-start.1
  40.0 1.3 copy-start.3
  41.4 1.3 copy-start.4
  80.9 17.9 %copy-start.9 = (bf16[768,1024]{1,0:T(8,128)(2,1)}, bf16[768,1024]{1,0:T(8,128)(2,1)S(1)}, u32[]{:S(2)}) copy-start(bf16[768,1024]{1,0:T(8,128)(2,1)S(1)} %collective-permute-done.rest_0_) | copy-start | bytes 4718596
  98.8 46.8 %all-to-all-start.1 = ((bf16[32,128,128]{2,1,0:T(8,128)(2,1)}), bf16[32,128,128]{2,1,0:T(8,128)(2,1)S(1)}, u32[]{:S(2)}, u32[]{:S(2)}) async-start(bf16[32,128,128]{2,1,0:T(8,128)(2,1)} %get-tuple-element.35), calls=%async_computation.1 | async-start | bytes 2097152 | tf_op jit(solution)/shard_map/all_to_all | solution.py:566
  103.4 42.2 %collective-permute-start.1 = (bf16[512,1024]{1,0:T(8,128)(2,1)}, bf16[512,1024]{1,0:T(8,128)(2,1)S(1)}, u32[]{:S(2)}, u32[]{:S(2)}) collective-permute-start(bf16[512,1024]{1,0:T(8,128)(2,1)} %get-tuple-element.28), channel_id=1, source_target_pairs={{8,0},{16,24},{9,1},{17,25},{10,2},{18,26},{11,3},{19,27},{12,4},{... | collective-permute-start | bytes 3145736 | tf_op jit(solution)/shard_map/ppermute | solution.py:557
  145.6 141.8 %copy-start.11 = (bf16[512,1024]{1,0:T(8,128)(2,1)}, bf16[512,1024]{1,0:T(8,128)(2,1)S(1)}, u32[]{:S(2)}) copy-start(bf16[512,1024]{1,0:T(8,128)(2,1)S(1)} %collective-permute-done.1.rest_1_) | copy-start | bytes 3145732
  146.6 9.1 %copy-start.16 = (bf16[768,1024]{1,0:T(8,128)(2,1)S(1)}, bf16[768,1024]{1,0:T(8,128)(2,1)}, u32[]{:S(2)}) copy-start(bf16[768,1024]{1,0:T(8,128)(2,1)} %get-tuple-element.29) | copy-start | bytes 4718596
  154.9 63.4 %collective-permute-start.2 = (bf16[2048,512]{1,0:T(8,128)(2,1)}, bf16[2048,512]{1,0:T(8,128)(2,1)S(1)}, u32[]{:S(2)}, u32[]{:S(2)}) collective-permute-start(bf16[2048,512]{1,0:T(8,128)(2,1)} %get-tuple-element.38.refs_0_), channel_id=1, source_target_pairs={{8,16},{16,8},{9,17},{17,9},{10,18},{18,10},{11,19},{19,11},{12,20... | collective-permute-start | bytes 6291464 | tf_op jit(solution)/shard_map/ppermute | solution.py:584
  155.7 39.2 %collective-permute-start.7 = (bf16[768,1024]{1,0:T(8,128)(2,1)S(1)}, bf16[768,1024]{1,0:T(8,128)(2,1)S(1)}, u32[]{:S(2)}, u32[]{:S(2)}) collective-permute-start(bf16[768,1024]{1,0:T(8,128)(2,1)S(1)} %copy-done.16), channel_id=1, source_target_pairs={{8,0},{16,24},{9,1},{17,25},{10,2},{18,26},{11,3},{19,27},{12,4},{... | collective-permute-start | bytes 4718600 | tf_op jit(solution)/shard_map/ppermute | solution.py:557
  157.0 59.3 %collective-permute-start.6 = (bf16[32,128,128]{2,1,0:T(8,128)(2,1)}, bf16[32,128,128]{2,1,0:T(8,128)(2,1)S(1)}, u32[]{:S(2)}, u32[]{:S(2)}) collective-permute-start(bf16[32,128,128]{2,1,0:T(8,128)(2,1)} %copy-done.5), channel_id=1, source_target_pairs={{8,0},{16,24},{9,1},{17,25},{10,2},{18,26},{11,3},{19,27},{12,4},{... | collective-permute-start | bytes 3145736 | tf_op jit(solution)/shard_map/ppermute | solution.py:578
  158.3 65.6 %collective-permute-start.11 = (bf16[2048,512]{1,0:T(8,128)(2,1)}, bf16[2048,512]{1,0:T(8,128)(2,1)}, u32[]{:S(2)}, u32[]{:S(2)}) collective-permute-start(bf16[2048,512]{1,0:T(8,128)(2,1)} %get-tuple-element.38.refs_0_), channel_id=1, source_target_pairs={{0,8},{24,16},{1,9},{25,17},{2,10},{26,18},{3,11},{27,19},{4,12},{... | collective-permute-start | bytes 6291464 | tf_op jit(solution)/shard_map/ppermute | solution.py:589
  194.8 23.4 %copy-start.10 = (bf16[768,1024]{1,0:T(8,128)(2,1)}, bf16[768,1024]{1,0:T(8,128)(2,1)S(1)}, u32[]{:S(2)}) copy-start(bf16[768,1024]{1,0:T(8,128)(2,1)S(1)} %collective-permute-done.7.rest_2_) | copy-start | bytes 4718596
  216.2 2.0 copy-start.12
  216.2 8.5 %collective-permute-start.8 = (bf16[2048,512]{1,0:T(8,128)(2,1)}, bf16[2048,512]{1,0:T(8,128)(2,1)}, u32[]{:S(2)}, u32[]{:S(2)}) collective-permute-start(bf16[2048,512]{1,0:T(8,128)(2,1)} %get-tuple-element.41.refs_1_), channel_id=1, source_target_pairs={{8,16},{16,8},{9,17},{17,9},{10,18},{18,10},{11,19},{19,11},{12,20... | collective-permute-start | bytes 6291464 | tf_op jit(solution)/shard_map/ppermute | solution.py:584
  218.2 5.7 %copy-start.7 = (bf16[2048,512]{1,0:T(8,128)(2,1)}, bf16[2048,512]{1,0:T(8,128)(2,1)S(1)}, u32[]{:S(2)}) copy-start(bf16[2048,512]{1,0:T(8,128)(2,1)S(1)} %collective-permute-done.2.refs_5_) | copy-start | bytes 6291460
  218.3 47.4 %collective-permute-start.3 = (bf16[2048,512]{1,0:T(8,128)(2,1)}, bf16[2048,512]{1,0:T(8,128)(2,1)}, u32[]{:S(2)}, u32[]{:S(2)}) collective-permute-start(bf16[2048,512]{1,0:T(8,128)(2,1)} %get-tuple-element.41.refs_1_), channel_id=1, source_target_pairs={{0,8},{24,16},{1,9},{25,17},{2,10},{26,18},{3,11},{27,19},{4,12},{... | collective-permute-start | bytes 6291464 | tf_op jit(solution)/shard_map/ppermute | solution.py:589
  222.6 50.4 %collective-permute-start.4 = (bf16[2048,512]{1,0:T(8,128)(2,1)S(1)}, bf16[2048,512]{1,0:T(8,128)(2,1)S(1)}, u32[]{:S(2)}, u32[]{:S(2)}) collective-permute-start(bf16[2048,512]{1,0:T(8,128)(2,1)S(1)} %collective-permute-done.2.refs_5_), channel_id=1, source_target_pairs={{8,0},{16,24},{9,1},{17,25},{10,2},{18,26},{11,3},{19,27},{12,4},{... | collective-permute-start | bytes 6291464 | tf_op jit(solution)/shard_map/ppermute | solution.py:585
  223.9 70.3 %collective-permute-start.12 = (bf16[2048,512]{1,0:T(8,128)(2,1)}, bf16[2048,512]{1,0:T(8,128)(2,1)S(1)}, u32[]{:S(2)}, u32[]{:S(2)}) collective-permute-start(bf16[2048,512]{1,0:T(8,128)(2,1)} %collective-permute-done.11.refs_2_), channel_id=1, source_target_pairs={{8,16},{16,8},{9,17},{17,9},{10,18},{18,10},{11,19},{19,11},{12,20... | collective-permute-start | bytes 6291464 | tf_op jit(solution)/shard_map/ppermute | solution.py:590
  224.7 93.4 %collective-permute-start.9 = (bf16[2048,512]{1,0:T(8,128)(2,1)}, bf16[2048,512]{1,0:T(8,128)(2,1)}, u32[]{:S(2)}, u32[]{:S(2)}) collective-permute-start(bf16[2048,512]{1,0:T(8,128)(2,1)} %collective-permute-done.8.refs_6_), channel_id=1, source_target_pairs={{8,0},{16,24},{9,1},{17,25},{10,2},{18,26},{11,3},{19,27},{12,4},{... | collective-permute-start | bytes 6291464 | tf_op jit(solution)/shard_map/ppermute | solution.py:585
  273.1 1.4 copy-start.8
  274.4 43.7 %collective-permute-start.5 = (bf16[2048,512]{1,0:T(8,128)(2,1)}, bf16[2048,512]{1,0:T(8,128)(2,1)}, u32[]{:S(2)}, u32[]{:S(2)}) collective-permute-start(bf16[2048,512]{1,0:T(8,128)(2,1)} %collective-permute-done.3.refs_3_), channel_id=1, source_target_pairs={{8,16},{16,8},{9,17},{17,9},{10,18},{18,10},{11,19},{19,11},{12,20... | collective-permute-start | bytes 6291464 | tf_op jit(solution)/shard_map/ppermute | solution.py:593
  294.3 62.6 %copy-start.6 = (bf16[2048,512]{1,0:T(8,128)(2,1)}, bf16[2048,512]{1,0:T(8,128)(2,1)S(1)}, u32[]{:S(2)}) copy-start(bf16[2048,512]{1,0:T(8,128)(2,1)S(1)} %collective-permute-done.12.refs_0_) | copy-start | bytes 6291460
  294.3 68.8 %collective-permute-start.13 = (bf16[2048,512]{1,0:T(8,128)(2,1)S(1)}, bf16[2048,512]{1,0:T(8,128)(2,1)}, u32[]{:S(2)}, u32[]{:S(2)}) collective-permute-start(bf16[2048,512]{1,0:T(8,128)(2,1)S(1)} %collective-permute-done.12.refs_0_), channel_id=1, source_target_pairs={{8,0},{16,24},{9,1},{17,25},{10,2},{18,26},{11,3},{19,27},{12,4},{... | collective-permute-start | bytes 6291464 | tf_op jit(solution)/shard_map/ppermute | solution.py:594
  318.1 87.6 %collective-permute-start.10 = (bf16[2048,512]{1,0:T(8,128)(2,1)}, bf16[2048,512]{1,0:T(8,128)(2,1)}, u32[]{:S(2)}, u32[]{:S(2)}) collective-permute-start(bf16[2048,512]{1,0:T(8,128)(2,1)} %collective-permute-done.5.refs_0_), channel_id=1, source_target_pairs={{8,0},{16,24},{9,1},{17,25},{10,2},{18,26},{11,3},{19,27},{12,4},{... | collective-permute-start | bytes 6291464 | tf_op jit(solution)/shard_map/ppermute | solution.py:596
  (2 other events, 2.3 us)
Sparse Core Ops, SparseCore 0:
  98.9 165.3 all-gather.2

commit v5 on v4

--- a/solution.py
+++ b/solution.py
@@ -162,14 +162,11 @@
     hit_ref,
     lot_ref,
     v_ref,
-    dens_ref,
     out_ref,
-    dens_low_ref,
     dh_ref,
     dl_ref,
 ):
     t = pl.program_id(0)
-    dens_low_ref[...] = dens_ref[...].astype(BF16)
     maxb = hi_ref.shape[2] // BLK
     for i in range(maxb):
         for j in range(maxb):
@@ -197,10 +194,8 @@
                 ]
 
 
-def tile_ham(incoming, basis, v_ext, hold, counts, density):
+def tile_ham(incoming, basis, v_ext, hold, counts):
     n = incoming.shape[0]
-    rows, cols = density.shape
-    band = pl.BlockSpec((rows // basis[0].shape[0], cols), lambda t, *_: (t, 0))
     tdev, npts, local = basis[0].shape
     flops = tdev * 3 * 2 * 2 * npts * local * local
     spec = pl.BlockSpec((1, npts, local), lambda t, *_: (t, 0, 0))
@@ -217,24 +212,20 @@
                 spec_t,
                 spec_t,
                 pl.BlockSpec((1, npts, 1), lambda t, *_: (t, 0, 0)),
-                band,
             ],
-            out_specs=[pl.BlockSpec((n, BLK, BLK), lambda t, *_: (0, 0, 0)), band],
+            out_specs=pl.BlockSpec((n, BLK, BLK), lambda t, *_: (0, 0, 0)),
             scratch_shapes=[
                 pltpu.VMEM((local, local), BF16),
                 pltpu.VMEM((local, local), BF16),
             ],
         ),
-        out_shape=[
-            jax.ShapeDtypeStruct((n, BLK, BLK), BF16),
-            jax.ShapeDtypeStruct((rows, cols), BF16),
-        ],
-        compiler_params=pltpu.CompilerParams(vmem_limit_bytes=52 * MIB),
+        out_shape=jax.ShapeDtypeStruct((n, BLK, BLK), BF16),
+        compiler_params=pltpu.CompilerParams(vmem_limit_bytes=44 * MIB),
         cost_estimate=pl.CostEstimate(
             flops=flops, bytes_accessed=tdev * npts * local * 8, transcendentals=0
         ),
         name="tile_ham",
-    )(hold, counts, incoming, *basis, v_ext[:, :, None], density)
+    )(hold, counts, incoming, *basis, v_ext[:, :, None])
 
 
 def assemble(h_core, arriving, picks, dtype, parts):
@@ -504,7 +495,6 @@
 
 
 PARTS = 2
-EARLY = (3, 2, 3)
 
 
 def tie(x, y):
@@ -525,7 +515,7 @@
     maxb = tile_blocks.shape[1]
     line = nrow == 4
 
-    inward = [(0, 1), (3, 2)]
+    swap = [(0, 1), (1, 0), (2, 3), (3, 2)]
     cross = [(1, 2), (2, 1)]
     outward = [(1, 0), (2, 3)]
 
@@ -548,24 +538,15 @@
     my_counts = lax.dynamic_index_in_dim(counts, myself, 0, keepdims=False)
     hold = ((mine // rowb)[:, :, None] * ncol + (mine // colb)[:, None, :]).reshape(tdev, -1)
 
-    if line:
-        unit = rows_loc // sum(EARLY)
-        sizes = [unit * k for k in EARLY]
-        first = round_bands(h_core, 0, sizes[:1])
-        density, first = tie(density, first)
-        rest = round_bands(h_core, sizes[0], sizes[1:])
-        early = [lax.ppermute(x, "row", outward) for x in first + rest]
     outgoing = (gather_blocks(density, picks[0], picks[1]) * DM_SCALE).astype(jnp.float16)
     incoming = lax.all_to_all(outgoing, ("row", "col"), split_axis=0, concat_axis=0, tiled=True)
-
     basis = split_basis(phi, my_counts)
-    if line:
-        incoming, (early[0], _) = tie(incoming, (early[0], rest))
-    returning, dm_low = tile_ham(incoming.astype(F32), basis, v_ext, hold, my_counts, density)
+    (dm_low,) = round_bands(density, 0, [rows_loc])
+    incoming, dm_low = tie(incoming, dm_low)
     dm_panel = lax.all_gather(dm_low, "col", axis=0, tiled=False)
+
+    returning = tile_ham(incoming.astype(F32), basis, v_ext, hold, my_counts)
     arriving = lax.all_to_all(returning, ("row", "col"), split_axis=0, concat_axis=0, tiled=True)
-    if line:
-        arriving, early[1] = tie(arriving, early[1])
     low = assemble([h_core], arriving, picks, BF16, PARTS if line else 1)
     (hamiltonian,) = assemble([h_core], arriving, picks, F32, 1)
 
@@ -575,32 +556,22 @@
         is_end = ((row_idx == 0) | (row_idx == 3)).astype(jnp.int32)
         near_idx = jnp.where(is_low, 2, 1)
         far_idx = jnp.where(is_low, 3, 0)
-        pair_blocks = lax.ppermute(arriving, "row", outward)
-        near_mid = []
-        for p in range(PARTS):
-            ready = low[p]
-            if p == 1:
-                ready, (pair_blocks, early[2]) = tie(ready, (pair_blocks, early[2]))
-            near_mid.append(lax.ppermute(ready, "row", cross))
+        pair = [lax.ppermute(x, "row", swap) for x in low]
+        near_mid = [lax.ppermute(x, "row", cross) for x in low]
         near_end = [lax.ppermute(x, "row", outward) for x in near_mid]
-        pair_mid = []
-        for p in range(PARTS):
-            ready = low[p] if p == 0 else tie(low[p], near_mid[p - 1])[0]
-            pair_mid.append(lax.ppermute(ready, "row", inward))
-        far_mid = [lax.ppermute(pair_mid[0], "row", cross)]
+        far_mid = [lax.ppermute(pair[0], "row", cross)]
         for p in range(1, PARTS):
-            ready, near_end[p - 1] = tie(pair_mid[p], near_end[p - 1])
+            ready, near_end[p - 1] = tie(pair[p], near_end[p - 1])
             far_mid.append(lax.ppermute(ready, "row", cross))
         far_end = [lax.ppermute(x, "row", outward) for x in far_mid[:-1]]
         ready, near_end[-1] = tie(far_mid[-1], near_end[-1])
         far_end.append(lax.ppermute(ready, "row", outward))
-        pair_end = assemble(early, pair_blocks, picks_of(pair_idx), BF16, 1)
         total = product(
             cols_loc,
             dm_panel,
             [
                 ((low,), 0, row_idx),
-                ((pair_mid, pair_end), is_end, pair_idx),
+                ((pair,), 0, pair_idx),
                 ((near_mid, near_end), is_end, near_idx),
             ],
         )

time: 423 us -> 404 us (0.955)
  Pallas kernels: 111 us -> 98.7 us
  starting transfers between devices: 38.4 us -> 27.1 us
  waiting for transfers between devices: 239 us -> 247 us
    ppermute x9 -> x5, waiting for transfers between devices: 170 us -> 87 us  [the longest x2 87 us: body(): pair = [lax.ppermute(x, 'row', swap) for x in low]]
    ppermute x2, waiting for transfers between devices: 30 us -> 74.9 us  [body(): near_end = [lax.ppermute(x, 'row', outward) for x in near_mid]]
    all_to_all x1, waiting for transfers between devices: 0.01 us -> 25.6 us  [body(): lax.all_to_all(returning, ('row', 'col'), split_axis=0, concat_axis=0, ti...]
    all_to_all x1, waiting for transfers between devices: 0.01 us -> 20 us  [body(): lax.all_to_all(outgoing, ('row', 'col'), split_axis=0, concat_axis=0, til...]
    ppermute x9 -> x5, starting transfers between devices: 19.2 us -> 8.87 us  [the longest x2 4.07 us: body(): pair = [lax.ppermute(x, 'row', swap) for x in low]]
    pallas_call x3 -> x2, Pallas kernels: 24.2 us -> 17.2 us  [assemble(): pl.pallas_call(kernel, grid_spec=pltpu.PrefetchScalarGridSpec(num_scalar_...]
    pallas_call x1, Pallas kernels: 16.3 us -> 11.8 us  [tile_ham(): pl.pallas_call(tile_kernel, grid_spec=pltpu.PrefetchScalarGridSpec(num_sc...]
    unnamed x35 -> x21, local copies, waits for them, and re-layouts: 7.83 us -> 8.61 us
  transfers between devices with their start and end apart: 17 -> 13, of which waited for: 9 -> 8; matrix products, arithmetic and copies ran while one was open for 1% -> 1% of each run, Pallas kernels for 18% -> 21%
where the time goes in v5:
time: 404 us; the launch traced here: 403 us
  waiting for transfers between devices  247 us (61%)
  Pallas kernels  98.7 us (24%)
  starting transfers between devices  27.1 us (7%)
  between operations  14.3 us (4%)
  local copies, waits for them, and re-layouts  10.1 us (2%)
  other arithmetic  5.77 us (1%)
    ppermute x2, waiting for transfers between devices, body(): pair = [lax.ppermute(x, 'row', swap) for x in low]  87 us
    ppermute x2, waiting for transfers between devices, body(): near_end = [lax.ppermute(x, 'row', outward) for x in near_mid]  74.9 us
    pallas_call x1, Pallas kernels, product(): pl.pallas_call(kernel, grid_spec=pltpu.PrefetchScalarGridSpec(num_scalar_...  37.3 us
    ppermute x1, waiting for transfers between devices, body(): far_end.append(lax.ppermute(ready, 'row', outward))  33.1 us
    all_to_all x1, waiting for transfers between devices, body(): lax.all_to_all(returning, ('row', 'col'), split_axis=0, concat_axis=0, ti...  25.6 us
    all_to_all x1, waiting for transfers between devices, body(): lax.all_to_all(outgoing, ('row', 'col'), split_axis=0, concat_axis=0, til...  20 us
    pallas_call x2, Pallas kernels, product_add(): pl.pallas_call(kernel, grid_spec=pltpu.PrefetchScalarGridSpec(num_scalar_...  19.4 us
    pallas_call x2, Pallas kernels, assemble(): pl.pallas_call(kernel, grid_spec=pltpu.PrefetchScalarGridSpec(num_scalar_...  17.2 us
  transfers between devices with their start and end apart: 13, of which 8 were waited for; matrix products, arithmetic and copies ran while one was open for 1% of the time, Pallas kernels for 21%

profile of v5, /device:TPU:0, one launch (start us, length us, event | category | flops | bytes accessed | tf_op | source)
XLA Modules:
  0.0 402.6 jit_solution(16228410516673484363)
XLA Ops:
  9.0 4.6 %gather_blocks.1 = f32[32,128,128]{2,1,0:T(8,128)} custom-call(s32[32]{0:T(128)} %get-tuple-element.27.row_ref, s32[32]{0:T(128)} %get-tuple-element.26.col_ref, f32[2048,1024]{1,0:T(8,128)} %x_ref.1), custom_call_target="tpu_custom_call" | custom-call | bytes 4194304 | tf_op jit(solution)/shard_map/gather_blocks/pallas_call | solution.py:44
  13.6 2.9 multiply_convert_fusion
  16.5 7.1 %all-to-all-start = ((f16[32,128,128]{2,1,0:T(8,128)(2,1)}), f16[32,128,128]{2,1,0:T(8,128)(2,1)S(1)}, u32[]{:S(2)}, u32[]{:S(2)}) async-start(f16[32,128,128]{2,1,0:T(8,128)(2,1)} %multiply_convert_fusion), calls=%async_computation | async-start | bytes 2097152 | tf_op jit(solution)/shard_map/all_to_all | solution.py:542
  23.6 6.2 %round_bands.1 = bf16[2048,1024]{1,0:T(8,128)(2,1)} custom-call(f32[2048,1024]{1,0:T(8,128)} %x_ref.1), custom_call_target="tpu_custom_call" | custom-call | flops 2097152 | bytes 12582912 | tf_op jit(solution)/shard_map/round_bands/pallas_call | solution.py:94
  29.8 20.0 %all-to-all-done = f16[32,128,128]{2,1,0:T(8,128)(2,1)S(1)} async-done(((f16[32,128,128]{2,1,0:T(8,128)(2,1)}), f16[32,128,128]{2,1,0:T(8,128)(2,1)S(1)}, u32[]{:S(2)}, u32[]{:S(2)}) %all-to-all-start) | async-done | bytes 1048608 | tf_op jit(solution)/shard_map/all_to_all | solution.py:542
  50.6 2.2 copy-done
  52.8 2.2 split_basis.1
  55.0 1.3 copy-done.1
  56.3 1.3 copy-done.2
  57.8 11.8 %tile_ham.1 = bf16[32,128,128]{2,1,0:T(8,128)(2,1)} custom-call(s32[2,16]{1,0:T(2,128)S(1)} %add.54.hold_ref, s32[2]{0:T(128)S(1)} %dynamic-slice_bitcast_fusion.count_ref, f32[32,128,128]{2,1,0:T(8,128)S(1)} %convert_element_type.12.in_ref, bf16[2,1024,512]{2,1,0:T(8,128)(2,1)S(1)} %get-tuple-element.15.hi_ref, ...), custom_call_target="tpu_custom_call" | custom-call | flops 6442450944 | bytes 8388608 | tf_op jit(solution)/shard_map/tile_ham/pallas_call | solution.py:203
  69.6 3.7 all-to-all-start.1
  74.0 25.6 %all-to-all-done.1.in_ref = bf16[32,128,128]{2,1,0:T(8,128)(2,1)S(1)} async-done(((bf16[32,128,128]{2,1,0:T(8,128)(2,1)}), bf16[32,128,128]{2,1,0:T(8,128)(2,1)S(1)}, u32[]{:S(2)}, u32[]{:S(2)}) %all-to-all-start.1) | async-done | bytes 1048608 | tf_op jit(solution)/shard_map/all_to_all | solution.py:549
  100.6 8.1 %assemble.3 = (bf16[2048,512]{1,0:T(8,128)(2,1)}, bf16[2048,512]{1,0:T(8,128)(2,1)}) custom-call(s32[32]{0:T(128)} %get-tuple-element.27.row_ref, s32[32]{0:T(128)} %get-tuple-element.26.col_ref, s32[32]{0:T(128)} %convert_element_type.10.present_ref, bf16[32,128,128]{2,1,0:T(8,128)(2,1)} %copy-done.3, f32[2048,1024]{1,0:T(8,128)} %rest_0_.3), custom_call_target="tpu_custom_call" | custom-call | flops 2097152 | bytes 12582912 | tf_op jit(solution)/shard_map/assemble/pallas_call | solution.py:319
  109.5 2.0 collective-permute-start.4
  111.5 4.0 collective-permute-start.7
  116.9 1.3 collective-permute-start.5
  118.2 44.1 %collective-permute-done.7.refs_2_ = bf16[2048,512]{1,0:T(8,128)(2,1)} collective-permute-done((bf16[2048,512]{1,0:T(8,128)(2,1)}, bf16[2048,512]{1,0:T(8,128)(2,1)}, u32[]{:S(2)}, u32[]{:S(2)}) %collective-permute-start.7) | collective-permute-done | bytes 2097184 | tf_op jit(solution)/shard_map/ppermute | solution.py:559
  162.3 2.0 collective-permute-start.8
  164.3 42.9 %collective-permute-done.refs_3_ = bf16[2048,512]{1,0:T(8,128)(2,1)} collective-permute-done((bf16[2048,512]{1,0:T(8,128)(2,1)}, bf16[2048,512]{1,0:T(8,128)(2,1)}, u32[]{:S(2)}, u32[]{:S(2)}) %collective-permute-start) | collective-permute-done | bytes 2097184 | tf_op jit(solution)/shard_map/ppermute | solution.py:559
  207.2 44.8 %collective-permute-done.2.refs_6_ = bf16[2048,512]{1,0:T(8,128)(2,1)S(1)} collective-permute-done((bf16[2048,512]{1,0:T(8,128)(2,1)S(1)}, bf16[2048,512]{1,0:T(8,128)(2,1)S(1)}, u32[]{:S(2)}, u32[]{:S(2)}) %collective-permute-start.2) | collective-permute-done | bytes 2097184 | tf_op jit(solution)/shard_map/ppermute | solution.py:561
  252.1 1.4 copy-done.5
  253.5 2.0 collective-permute-start.3
  256.6 9.1 %assemble.2 = f32[2048,1024]{1,0:T(8,128)} custom-call(s32[32]{0:T(128)} %get-tuple-element.27.row_ref, s32[32]{0:T(128)} %get-tuple-element.26.col_ref, s32[32]{0:T(128)} %convert_element_type.10.present_ref, bf16[32,128,128]{2,1,0:T(8,128)(2,1)} %copy-done.3, f32[2048,1024]{1,0:T(8,128)} %rest_0_.3), custom_call_target="tpu_custom_call" | custom-call | flops 2097152 | bytes 12582912 | tf_op jit(solution)/shard_map/assemble/pallas_call | solution.py:319
  265.8 1.3 collective-permute-start.9
  267.1 30.1 %collective-permute-done.5.refs_7_ = bf16[2048,512]{1,0:T(8,128)(2,1)} collective-permute-done((bf16[2048,512]{1,0:T(8,128)(2,1)}, bf16[2048,512]{1,0:T(8,128)(2,1)}, u32[]{:S(2)}, u32[]{:S(2)}) %collective-permute-start.5) | collective-permute-done | bytes 2097184 | tf_op jit(solution)/shard_map/ppermute | solution.py:561
  297.1 1.5 collective-permute-start.6
  298.6 37.3 %product.1.refs_3_ = f32[2048,1024]{1,0:T(8,128)} custom-call(s32[6]{0:T(128)} %stack.35.sc_ref, bf16[2048,512]{1,0:T(8,128)(2,1)} %get-tuple-element.20.refs_0_, bf16[2048,512]{1,0:T(8,128)(2,1)} %get-tuple-element.19.refs_1_, bf16[2048,512]{1,0:T(8,128)(2,1)} %collective-permute-done.7.refs_2_, bf16[2048,512]{1,0:T(8,128)(2,1)} %collective-permute-done.refs_3_, ...), custom_call_target="tpu_custom_call" | custom-call | flops 25769803776 | bytes 46137344 | tf_op jit(solution)/shard_map/product/pallas_call | solution.py:390
  335.9 6.1 %collective-permute-done.9.refs_1_ = bf16[2048,512]{1,0:T(8,128)(2,1)S(1)} collective-permute-done((bf16[2048,512]{1,0:T(8,128)(2,1)}, bf16[2048,512]{1,0:T(8,128)(2,1)S(1)}, u32[]{:S(2)}, u32[]{:S(2)}) %collective-permute-start.9) | collective-permute-done | bytes 2097184 | tf_op jit(solution)/shard_map/ppermute | solution.py:566
  342.0 1.3 copy-done.6
  343.3 9.7 %product_add.2.refs_3_ = f32[2048,1024]{1,0:T(8,128)} custom-call(s32[2]{0:T(128)} %pad_add_fusion.sc_ref, bf16[2048,512]{1,0:T(8,128)(2,1)} %collective-permute-done.8.refs_0_, bf16[2048,512]{1,0:T(8,128)(2,1)} %copy-done.6, bf16[8,2048,1024]{2,1,0:T(8,128)(2,1)} %bitcast.31, f32[2048,1024]{1,0:T(8,128)} %product.1.refs_3_), custom_call_target="tpu_custom_call", output_to_operand_aliasing={{}: (4, {})} | custom-call | flops 4294967296 | bytes 18874368 | tf_op jit(solution)/shard_map/product_add/pallas_call | solution.py:468
  353.0 33.1 %collective-permute-done.6.refs_1_ = bf16[2048,512]{1,0:T(8,128)(2,1)} collective-permute-done((bf16[2048,512]{1,0:T(8,128)(2,1)}, bf16[2048,512]{1,0:T(8,128)(2,1)}, u32[]{:S(2)}, u32[]{:S(2)}) %collective-permute-start.6) | collective-permute-done | bytes 2097184 | tf_op jit(solution)/shard_map/ppermute | solution.py:568
  386.0 9.7 %product_add.3 = f32[2048,1024]{1,0:T(8,128)} custom-call(s32[2]{0:T(128)} %pad_add_fusion.sc_ref, bf16[2048,512]{1,0:T(8,128)(2,1)} %collective-permute-done.3.refs_0_, bf16[2048,512]{1,0:T(8,128)(2,1)} %collective-permute-done.6.refs_1_, bf16[8,2048,1024]{2,1,0:T(8,128)(2,1)} %bitcast.32, ...), custom_call_target="tpu_custom_call", output_to_operand_aliasing={{}: (4, {})} | custom-call | flops 4294967296 | bytes 18874368 | tf_op jit(solution)/shard_map/product_add/pallas_call | solution.py:468
  (46 shorter events, 7.8 us)
Async XLA Ops:
  16.5 33.3 %all-to-all-start = ((f16[32,128,128]{2,1,0:T(8,128)(2,1)}), f16[32,128,128]{2,1,0:T(8,128)(2,1)S(1)}, u32[]{:S(2)}, u32[]{:S(2)}) async-start(f16[32,128,128]{2,1,0:T(8,128)(2,1)} %multiply_convert_fusion), calls=%async_computation | async-start | bytes 2097152 | tf_op jit(solution)/shard_map/all_to_all | solution.py:542
  23.6 275.1 %all-gather.3.cloned.1.call-start = ((), (), s32[]{:S(2)}) async-start(), calls=%async_computation.2 | async-start | bytes 37748736 | tf_op jit(solution)/shard_map/all_gather | solution.py:546
  29.8 20.0 %copy-start.8 = (s32[64,4]{0,1:T(4,128)S(1)}, s32[64,4]{0,1:T(4,128)}, u32[]{:S(2)}) copy-start(s32[64,4]{0,1:T(4,128)} %param.10) | copy-start | bytes 3076
  29.8 20.1 %copy-start.9 = (s32[64]{0:T(128)S(1)}, s32[64]{0:T(128)}, u32[]{:S(2)}) copy-start(s32[64]{0:T(128)} %param.11) | copy-start | bytes 772
  29.8 20.4 %copy-start.7 = (f32[2,1024]{1,0:T(2,128)S(1)}, f32[2,1024]{1,0:T(2,128)}, u32[]{:S(2)}) copy-start(f32[2,1024]{1,0:T(2,128)} %param.9) | copy-start | bytes 24580
  50.6 2.2 copy-start
  55.0 1.3 copy-start.1
  56.3 1.3 copy-start.2
  69.6 30.0 %all-to-all-start.1 = ((bf16[32,128,128]{2,1,0:T(8,128)(2,1)}), bf16[32,128,128]{2,1,0:T(8,128)(2,1)S(1)}, u32[]{:S(2)}, u32[]{:S(2)}) async-start(bf16[32,128,128]{2,1,0:T(8,128)(2,1)} %tile_ham.1), calls=%async_computation.1 | async-start | bytes 2097152 | tf_op jit(solution)/shard_map/all_to_all | solution.py:549
  99.6 1.0 copy-start.3
  108.7 6.8 %collective-permute-start.1 = (bf16[2048,512]{1,0:T(8,128)(2,1)}, bf16[2048,512]{1,0:T(8,128)(2,1)S(1)}, u32[]{:S(2)}, u32[]{:S(2)}) collective-permute-start(bf16[2048,512]{1,0:T(8,128)(2,1)} %get-tuple-element.20.refs_0_), channel_id=1, source_target_pairs={{8,16},{16,8},{9,17},{17,9},{10,18},{18,10},{11,19},{19,11},{12,20... | collective-permute-start | bytes 6291464 | tf_op jit(solution)/shard_map/ppermute | solution.py:560
  109.5 7.3 %collective-permute-start.4 = (bf16[2048,512]{1,0:T(8,128)(2,1)}, bf16[2048,512]{1,0:T(8,128)(2,1)}, u32[]{:S(2)}, u32[]{:S(2)}) collective-permute-start(bf16[2048,512]{1,0:T(8,128)(2,1)} %get-tuple-element.19.refs_1_), channel_id=1, source_target_pairs={{8,16},{16,8},{9,17},{17,9},{10,18},{18,10},{11,19},{19,11},{12,20... | collective-permute-start | bytes 6291464 | tf_op jit(solution)/shard_map/ppermute | solution.py:560
  111.5 50.8 %collective-permute-start.7 = (bf16[2048,512]{1,0:T(8,128)(2,1)}, bf16[2048,512]{1,0:T(8,128)(2,1)}, u32[]{:S(2)}, u32[]{:S(2)}) collective-permute-start(bf16[2048,512]{1,0:T(8,128)(2,1)} %get-tuple-element.20.refs_0_), channel_id=1, source_target_pairs={{0,8},{8,0},{16,24},{24,16},{1,9},{9,1},{17,25},{25,17},{2,10},{10... | collective-permute-start | bytes 6291464 | tf_op jit(solution)/shard_map/ppermute | solution.py:559
  115.5 91.7 %collective-permute-start = (bf16[2048,512]{1,0:T(8,128)(2,1)}, bf16[2048,512]{1,0:T(8,128)(2,1)}, u32[]{:S(2)}, u32[]{:S(2)}) collective-permute-start(bf16[2048,512]{1,0:T(8,128)(2,1)} %get-tuple-element.19.refs_1_), channel_id=1, source_target_pairs={{0,8},{8,0},{16,24},{24,16},{1,9},{9,1},{17,25},{25,17},{2,10},{10... | collective-permute-start | bytes 6291464 | tf_op jit(solution)/shard_map/ppermute | solution.py:559
  115.6 150.2 %copy-start.4 = (bf16[2048,512]{1,0:T(8,128)(2,1)}, bf16[2048,512]{1,0:T(8,128)(2,1)S(1)}, u32[]{:S(2)}) copy-start(bf16[2048,512]{1,0:T(8,128)(2,1)S(1)} %collective-permute-done.1.refs_4_) | copy-start | bytes 6291460
  115.6 136.5 %collective-permute-start.2 = (bf16[2048,512]{1,0:T(8,128)(2,1)S(1)}, bf16[2048,512]{1,0:T(8,128)(2,1)S(1)}, u32[]{:S(2)}, u32[]{:S(2)}) collective-permute-start(bf16[2048,512]{1,0:T(8,128)(2,1)S(1)} %collective-permute-done.1.refs_4_), channel_id=1, source_target_pairs={{8,0},{16,24},{9,1},{17,25},{10,2},{18,26},{11,3},{19,27},{12,4},{... | collective-permute-start | bytes 6291464 | tf_op jit(solution)/shard_map/ppermute | solution.py:561
  116.9 180.2 %collective-permute-start.5 = (bf16[2048,512]{1,0:T(8,128)(2,1)}, bf16[2048,512]{1,0:T(8,128)(2,1)}, u32[]{:S(2)}, u32[]{:S(2)}) collective-permute-start(bf16[2048,512]{1,0:T(8,128)(2,1)} %collective-permute-done.4.refs_5_), channel_id=1, source_target_pairs={{8,0},{16,24},{9,1},{17,25},{10,2},{18,26},{11,3},{19,27},{12,4},{... | collective-permute-start | bytes 6291464 | tf_op jit(solution)/shard_map/ppermute | solution.py:561
  162.3 103.5 %collective-permute-start.8 = (bf16[2048,512]{1,0:T(8,128)(2,1)}, bf16[2048,512]{1,0:T(8,128)(2,1)}, u32[]{:S(2)}, u32[]{:S(2)}) collective-permute-start(bf16[2048,512]{1,0:T(8,128)(2,1)} %collective-permute-done.7.refs_2_), channel_id=1, source_target_pairs={{8,16},{16,8},{9,17},{17,9},{10,18},{18,10},{11,19},{19,11},{12,20... | collective-permute-start | bytes 6291464 | tf_op jit(solution)/shard_map/ppermute | solution.py:562
  252.1 1.4 copy-start.5
  253.5 43.7 %collective-permute-start.3 = (bf16[2048,512]{1,0:T(8,128)(2,1)}, bf16[2048,512]{1,0:T(8,128)(2,1)}, u32[]{:S(2)}, u32[]{:S(2)}) collective-permute-start(bf16[2048,512]{1,0:T(8,128)(2,1)} %collective-permute-done.refs_3_), channel_id=1, source_target_pairs={{8,16},{16,8},{9,17},{17,9},{10,18},{18,10},{11,19},{19,11},{12,20... | collective-permute-start | bytes 6291464 | tf_op jit(solution)/shard_map/ppermute | solution.py:565
  265.8 76.2 %collective-permute-start.9 = (bf16[2048,512]{1,0:T(8,128)(2,1)}, bf16[2048,512]{1,0:T(8,128)(2,1)S(1)}, u32[]{:S(2)}, u32[]{:S(2)}) collective-permute-start(bf16[2048,512]{1,0:T(8,128)(2,1)} %collective-permute-done.8.refs_0_), channel_id=1, source_target_pairs={{8,0},{16,24},{9,1},{17,25},{10,2},{18,26},{11,3},{19,27},{12,4},{... | collective-permute-start | bytes 6291464 | tf_op jit(solution)/shard_map/ppermute | solution.py:566
  297.1 88.9 %collective-permute-start.6 = (bf16[2048,512]{1,0:T(8,128)(2,1)}, bf16[2048,512]{1,0:T(8,128)(2,1)}, u32[]{:S(2)}, u32[]{:S(2)}) collective-permute-start(bf16[2048,512]{1,0:T(8,128)(2,1)} %collective-permute-done.3.refs_0_), channel_id=1, source_target_pairs={{8,0},{16,24},{9,1},{17,25},{10,2},{18,26},{11,3},{19,27},{12,4},{... | collective-permute-start | bytes 6291464 | tf_op jit(solution)/shard_map/ppermute | solution.py:568
  342.0 1.3 copy-start.6
Sparse Core Ops, SparseCore 0:
  49.9 171.0 all-gather.2

commit v6 on v5

--- a/solution.py
+++ b/solution.py
@@ -228,34 +228,25 @@
     )(hold, counts, incoming, *basis, v_ext[:, :, None])
 
 
-def assemble(h_core, arriving, picks, dtype, parts):
-    nband = len(h_core)
-    rows, cols = sum(x.shape[0] for x in h_core), h_core[0].shape[1]
+def assemble(h_core, arriving, picks, dtype, first, parts, wide):
+    rows, cols = h_core.shape[0], parts * wide
     n = arriving.shape[0]
     per = 2
     bm = per * BLK
     steps = rows // bm
-    wide = cols // parts
-    widen = h_core[0].dtype != F32
     narrow = dtype != F32
-    source = [(k, g) for k, x in enumerate(h_core) for g in range(x.shape[0] // bm)]
-
-    def kernel(row_ref, col_ref, present_ref, in_ref, *rest):
-        h_refs, outs, rest = rest[:nband], rest[nband : nband + parts], rest[nband + parts :]
+
+    def kernel(row_ref, col_ref, present_ref, in_ref, h_ref, *rest):
+        outs, rest = rest[:parts], rest[parts:]
         work_ref, in_sems, out_sems, num_ref, list_ref = rest[:5]
-        rest = rest[5:]
-        raw_ref = work_ref
-        if widen:
-            raw_ref, rest = rest[0], rest[1:]
-        low_refs = rest if narrow else (work_ref,)
+        low_refs = rest[5:] if narrow else (work_ref,)
 
         def band(g):
             return pl.ds(g * bm, bm)
 
         def read(g):
-            k, at = source[g]
             return pltpu.make_async_copy(
-                h_refs[k].at[band(at)], raw_ref.at[band(g)], in_sems.at[g]
+                h_ref.at[band(g), pl.ds(first, cols)], work_ref.at[band(g)], in_sems.at[g]
             )
 
         def write(g, p):
@@ -269,7 +260,9 @@
             num_ref[g] = 0
 
         def note(s, carry):
-            @pl.when(present_ref[s] > 0)
+            c = col_ref[s] * BLK
+
+            @pl.when((present_ref[s] > 0) & (c >= first) & (c < first + cols))
             def _():
                 g = row_ref[s] // per
                 k = num_ref[g]
@@ -284,13 +277,11 @@
             read(g).wait()
             if g + AHEAD < steps:
                 read(g + AHEAD).start()
-            if widen:
-                work_ref[band(g), :] = raw_ref[band(g), :].astype(F32)
 
             def add(k, carry, g=g):
                 s = list_ref[g * n + k]
                 top = pl.ds(pl.multiple_of(row_ref[s] * BLK, BLK), BLK)
-                left = pl.ds(pl.multiple_of(col_ref[s] * BLK, BLK), BLK)
+                left = pl.ds(pl.multiple_of(col_ref[s] * BLK - first, BLK), BLK)
                 work_ref[top, left] = work_ref[top, left] + in_ref[s].astype(F32)
                 return carry
 
@@ -312,8 +303,6 @@
         pltpu.SMEM((steps,), jnp.int32),
         pltpu.SMEM((steps * n,), jnp.int32),
     ]
-    if widen:
-        scratch.append(pltpu.VMEM((rows, cols), h_core[0].dtype))
     if narrow:
         scratch.extend([pltpu.VMEM((rows, wide), dtype)] * parts)
     return pl.pallas_call(
@@ -323,8 +312,8 @@
             grid=(1,),
             in_specs=[
                 pl.BlockSpec((n, BLK, BLK), lambda i, *_: (0, 0, 0)),
-            ]
-            + [pl.BlockSpec(memory_space=pl.ANY)] * nband,
+                pl.BlockSpec(memory_space=pl.ANY),
+            ],
             out_specs=[pl.BlockSpec(memory_space=pl.ANY)] * parts,
             scratch_shapes=scratch,
         ),
@@ -334,7 +323,7 @@
             flops=rows * cols, bytes_accessed=rows * cols * 6, transcendentals=0
         ),
         name="assemble",
-    )(*picks, arriving, *h_core)
+    )(*picks, arriving, h_core)
 
 
 def product(cols, dm_panel, pieces):
@@ -494,7 +483,7 @@
     )(scalars, *candidates, dm_panel, total)
 
 
-PARTS = 2
+PARTS = 4
 
 
 def tie(x, y):
@@ -542,13 +531,17 @@
     incoming = lax.all_to_all(outgoing, ("row", "col"), split_axis=0, concat_axis=0, tiled=True)
     basis = split_basis(phi, my_counts)
     (dm_low,) = round_bands(density, 0, [rows_loc])
-    incoming, dm_low = tie(incoming, dm_low)
+    incoming, (dm_low, basis) = tie(incoming, (dm_low, basis))
     dm_panel = lax.all_gather(dm_low, "col", axis=0, tiled=False)
 
     returning = tile_ham(incoming.astype(F32), basis, v_ext, hold, my_counts)
     arriving = lax.all_to_all(returning, ("row", "col"), split_axis=0, concat_axis=0, tiled=True)
-    low = assemble([h_core], arriving, picks, BF16, PARTS if line else 1)
-    (hamiltonian,) = assemble([h_core], arriving, picks, F32, 1)
+    parts = PARTS if line and cols_loc % (PARTS * BLK) == 0 else 1
+    wide = cols_loc // parts
+    low = assemble(h_core, arriving, picks, BF16, 0, 1, wide)
+    if parts > 1:
+        low = low + assemble(h_core, arriving, picks, BF16, wide, parts - 1, wide)
+    (hamiltonian,) = assemble(h_core, arriving, picks, F32, 0, 1, cols_loc)
 
     if line:
         pair_idx = row_idx + 1 - 2 * (row_idx % 2)
@@ -556,16 +549,24 @@
         is_end = ((row_idx == 0) | (row_idx == 3)).astype(jnp.int32)
         near_idx = jnp.where(is_low, 2, 1)
         far_idx = jnp.where(is_low, 3, 0)
-        pair = [lax.ppermute(x, "row", swap) for x in low]
-        near_mid = [lax.ppermute(x, "row", cross) for x in low]
+        pair, near_mid = [], []
+        for p in range(parts):
+            ready = low[p] if p < 2 else tie(low[p], near_mid[p - 2])[0]
+            pair.append(lax.ppermute(ready, "row", swap))
+            near_mid.append(lax.ppermute(ready, "row", cross))
         near_end = [lax.ppermute(x, "row", outward) for x in near_mid]
-        far_mid = [lax.ppermute(pair[0], "row", cross)]
-        for p in range(1, PARTS):
-            ready, near_end[p - 1] = tie(pair[p], near_end[p - 1])
+        far_mid = []
+        for p in range(parts):
+            ready = pair[p]
+            if p > 0:
+                ready, near_end[p - 1] = tie(ready, near_end[p - 1])
             far_mid.append(lax.ppermute(ready, "row", cross))
-        far_end = [lax.ppermute(x, "row", outward) for x in far_mid[:-1]]
-        ready, near_end[-1] = tie(far_mid[-1], near_end[-1])
-        far_end.append(lax.ppermute(ready, "row", outward))
+        far_end = []
+        for p in range(parts):
+            ready = far_mid[p]
+            if p == parts - 1:
+                ready, near_end[p] = tie(ready, near_end[p])
+            far_end.append(lax.ppermute(ready, "row", outward))
         total = product(
             cols_loc,
             dm_panel,
@@ -575,7 +576,7 @@
                 ((near_mid, near_end), is_end, near_idx),
             ],
         )
-        for p in range(PARTS):
+        for p in range(parts):
             total = product_add(
                 total, p, dm_panel, (far_mid[p], far_end[p]), is_end, far_idx
             )

time: 404 us -> 402 us (level)
  waiting for transfers between devices: 247 us -> 203 us
  Pallas kernels: 98.7 us -> 120 us
  starting transfers between devices: 27.1 us -> 40.8 us
  local copies, waits for them, and re-layouts: 10.1 us -> 15.2 us
    pallas_call x2 -> x4, Pallas kernels: 19.4 us -> 35.5 us  [product_add(): pl.pallas_call(kernel, grid_spec=pltpu.PrefetchScalarGridSpec(num_scalar_...]
    ppermute x6 -> x8, waiting for transfers between devices: 93.1 us -> 78.5 us  [the longest x4 78.5 us: body(): pair.append(lax.ppermute(ready, 'row', swap))]
    ppermute x1 -> x4, waiting for transfers between devices: 33.1 us -> 21.5 us  [body(): far_end.append(lax.ppermute(ready, 'row', outward))]
    ppermute x2 -> x4, waiting for transfers between devices: 74.9 us -> 66 us  [body(): near_end = [lax.ppermute(x, 'row', outward) for x in near_mid]]
    all_to_all x1, waiting for transfers between devices: 20 us -> 11.5 us  [body(): lax.all_to_all(outgoing, ('row', 'col'), split_axis=0, concat_axis=0, til...]
    pallas_call x2 -> x3, Pallas kernels: 17.2 us -> 22.6 us  [assemble(): pl.pallas_call(kernel, grid_spec=pltpu.PrefetchScalarGridSpec(num_scalar_...]
    unnamed x21 -> x43, local copies, waits for them, and re-layouts: 8.61 us -> 13.6 us
    ppermute x1 -> x4, starting transfers between devices: 1.99 us -> 6.57 us  [body(): far_mid.append(lax.ppermute(ready, 'row', cross))]
  transfers between devices with their start and end apart: 13 -> 23, of which waited for: 8 -> 12; matrix products, arithmetic and copies ran while one was open for 1% -> 1% of each run, Pallas kernels for 21% -> 27%
where the time goes in v6:
time: 402 us; the launch traced here: 401 us
  waiting for transfers between devices  203 us (50%)
  Pallas kernels  120 us (30%)
  starting transfers between devices  40.8 us (10%)
  local copies, waits for them, and re-layouts  15.2 us (4%)
  between operations  14.5 us (4%)
  other arithmetic  7.14 us (2%)
    ppermute x4, waiting for transfers between devices, body(): pair.append(lax.ppermute(ready, 'row', swap))  78.5 us
    ppermute x4, waiting for transfers between devices, body(): near_end = [lax.ppermute(x, 'row', outward) for x in near_mid]  66 us
    pallas_call x1, Pallas kernels, product(): pl.pallas_call(kernel, grid_spec=pltpu.PrefetchScalarGridSpec(num_scalar_...  37.2 us
    pallas_call x4, Pallas kernels, product_add(): pl.pallas_call(kernel, grid_spec=pltpu.PrefetchScalarGridSpec(num_scalar_...  35.5 us
    all_to_all x1, waiting for transfers between devices, body(): lax.all_to_all(returning, ('row', 'col'), split_axis=0, concat_axis=0, ti...  25.5 us
    pallas_call x3, Pallas kernels, assemble(): pl.pallas_call(kernel, grid_spec=pltpu.PrefetchScalarGridSpec(num_scalar_...  22.6 us
    ppermute x4, waiting for transfers between devices, body(): far_end.append(lax.ppermute(ready, 'row', outward))  21.5 us
    unnamed x43, local copies, waits for them, and re-layouts  13.6 us
  transfers between devices with their start and end apart: 23, of which 12 were waited for; matrix products, arithmetic and copies ran while one was open for 1% of the time, Pallas kernels for 27%

profile of v6, /device:TPU:0, one launch (start us, length us, event | category | flops | bytes accessed | tf_op | source)
XLA Modules:
  0.0 400.5 jit_solution(14446067196543724886)
XLA Ops:
  9.0 4.3 %gather_blocks.1 = f32[32,128,128]{2,1,0:T(8,128)} custom-call(s32[32]{0:T(128)} %get-tuple-element.49.row_ref, s32[32]{0:T(128)} %get-tuple-element.48.col_ref, f32[2048,1024]{1,0:T(8,128)} %x_ref.1), custom_call_target="tpu_custom_call" | custom-call | bytes 4194304 | tf_op jit(solution)/shard_map/gather_blocks/pallas_call | solution.py:44
  13.3 2.9 multiply_convert_fusion
  16.1 7.4 %all-to-all-start = ((f16[32,128,128]{2,1,0:T(8,128)(2,1)}), f16[32,128,128]{2,1,0:T(8,128)(2,1)S(1)}, u32[]{:S(2)}, u32[]{:S(2)}) async-start(f16[32,128,128]{2,1,0:T(8,128)(2,1)} %multiply_convert_fusion), calls=%async_computation | async-start | bytes 2097152 | tf_op jit(solution)/shard_map/all_to_all | solution.py:531
  23.7 6.2 %round_bands.1 = bf16[2048,1024]{1,0:T(8,128)(2,1)} custom-call(f32[2048,1024]{1,0:T(8,128)} %x_ref.1), custom_call_target="tpu_custom_call" | custom-call | flops 2097152 | bytes 12582912 | tf_op jit(solution)/shard_map/round_bands/pallas_call | solution.py:94
  29.9 2.2 copy-done
  32.1 2.2 split_basis.1
  38.3 11.5 %all-to-all-done = f16[32,128,128]{2,1,0:T(8,128)(2,1)S(1)} async-done(((f16[32,128,128]{2,1,0:T(8,128)(2,1)}), f16[32,128,128]{2,1,0:T(8,128)(2,1)S(1)}, u32[]{:S(2)}, u32[]{:S(2)}) %all-to-all-start) | async-done | bytes 1048608 | tf_op jit(solution)/shard_map/all_to_all | solution.py:531
  54.3 11.8 %tile_ham.1 = bf16[32,128,128]{2,1,0:T(8,128)(2,1)} custom-call(s32[2,16]{1,0:T(2,128)S(1)} %add.54.hold_ref, s32[2]{0:T(128)S(1)} %dynamic-slice_bitcast_fusion.count_ref, f32[32,128,128]{2,1,0:T(8,128)S(1)} %convert_element_type.12.in_ref, bf16[2,1024,512]{2,1,0:T(8,128)(2,1)S(1)} %get-tuple-element.30.hi_ref, bf16[2,1024,512]{2,1,0:T(8,128)(2,1)S(1)} %copy-done.2, ...), custom_call_target="tpu_custom_call" | custom-call | flops 6442450944 | bytes 8388608 | tf_op jit(solution)/shard_map/tile_ham/pallas_call | solution.py:203
  66.1 3.1 all-to-all-start.1
  69.9 25.5 %all-to-all-done.1.in_ref = bf16[32,128,128]{2,1,0:T(8,128)(2,1)S(1)} async-done(((bf16[32,128,128]{2,1,0:T(8,128)(2,1)}), bf16[32,128,128]{2,1,0:T(8,128)(2,1)S(1)}, u32[]{:S(2)}, u32[]{:S(2)}) %all-to-all-start.1) | async-done | bytes 1048608 | tf_op jit(solution)/shard_map/all_to_all | solution.py:538
  96.5 6.0 %assemble.5.refs_0_ = bf16[2048,256]{1,0:T(8,128)(2,1)} custom-call(s32[32]{0:T(128)} %get-tuple-element.49.row_ref, s32[32]{0:T(128)} %get-tuple-element.48.col_ref, s32[32]{0:T(128)} %convert_element_type.10.present_ref, bf16[32,128,128]{2,1,0:T(8,128)(2,1)} %copy-done.5, f32[2048,1024]{1,0:T(8,128)} %h_ref.5), custom_call_target="tpu_custom_call" | custom-call | flops 524288 | bytes 3145728 | tf_op jit(solution)/shard_map/assemble/pallas_call | solution.py:308
  103.3 7.5 %assemble.4 = (bf16[2048,256]{1,0:T(8,128)(2,1)}, bf16[2048,256]{1,0:T(8,128)(2,1)}, bf16[2048,256]{1,0:T(8,128)(2,1)}) custom-call(s32[32]{0:T(128)} %get-tuple-element.49.row_ref, s32[32]{0:T(128)} %get-tuple-element.48.col_ref, s32[32]{0:T(128)} %convert_element_type.10.present_ref, bf16[32,128,128]{2,1,0:T(8,128)(2,1)} %copy-done.5, f32[2048,1024]{1,0:T(8,128)} %h_ref.5), custom_call_target="tpu_custom_call" | custom-call | flops 1572864 | bytes 9437184 | tf_op jit(solution)/shard_map/assemble/pallas_call | solution.py:308
  110.8 2.5 collective-permute-start.13
  114.1 2.9 collective-permute-start.17
  119.0 18.6 %collective-permute-done.13.refs_5_ = bf16[2048,256]{1,0:T(8,128)(2,1)S(1)} collective-permute-done((bf16[2048,256]{1,0:T(8,128)(2,1)}, bf16[2048,256]{1,0:T(8,128)(2,1)S(1)}, u32[]{:S(2)}, u32[]{:S(2)}) %collective-permute-start.13) | collective-permute-done | bytes 1048608 | tf_op jit(solution)/shard_map/ppermute | solution.py:555
  137.5 1.9 collective-permute-start.9
  140.8 19.4 %collective-permute-done.17.refs_4_ = bf16[2048,256]{1,0:T(8,128)(2,1)} collective-permute-done((bf16[2048,256]{1,0:T(8,128)(2,1)S(1)}, bf16[2048,256]{1,0:T(8,128)(2,1)}, u32[]{:S(2)}, u32[]{:S(2)}) %collective-permute-start.17) | collective-permute-done | bytes 1048608 | tf_op jit(solution)/shard_map/ppermute | solution.py:555
  160.1 1.9 collective-permute-start.1
  162.0 20.4 %collective-permute-done.14.refs_12_ = bf16[2048,256]{1,0:T(8,128)(2,1)S(1)} collective-permute-done((bf16[2048,256]{1,0:T(8,128)(2,1)S(1)}, bf16[2048,256]{1,0:T(8,128)(2,1)S(1)}, u32[]{:S(2)}, u32[]{:S(2)}) %collective-permute-start.14) | collective-permute-done | bytes 1048608 | tf_op jit(solution)/shard_map/ppermute | solution.py:557
  185.4 19.6 %collective-permute-done.9.refs_6_ = bf16[2048,256]{1,0:T(8,128)(2,1)} collective-permute-done((bf16[2048,256]{1,0:T(8,128)(2,1)}, bf16[2048,256]{1,0:T(8,128)(2,1)}, u32[]{:S(2)}, u32[]{:S(2)}) %collective-permute-start.9) | collective-permute-done | bytes 1048608 | tf_op jit(solution)/shard_map/ppermute | solution.py:555
  206.7 20.7 %collective-permute-done.10.refs_13_ = bf16[2048,256]{1,0:T(8,128)(2,1)S(1)} collective-permute-done((bf16[2048,256]{1,0:T(8,128)(2,1)S(1)}, bf16[2048,256]{1,0:T(8,128)(2,1)S(1)}, u32[]{:S(2)}, u32[]{:S(2)}) %collective-permute-start.10) | collective-permute-done | bytes 1048608 | tf_op jit(solution)/shard_map/ppermute | solution.py:557
  229.1 20.9 %collective-permute-done.1.refs_7_ = bf16[2048,256]{1,0:T(8,128)(2,1)} collective-permute-done((bf16[2048,256]{1,0:T(8,128)(2,1)}, bf16[2048,256]{1,0:T(8,128)(2,1)}, u32[]{:S(2)}, u32[]{:S(2)}) %collective-permute-start.1) | collective-permute-done | bytes 1048608 | tf_op jit(solution)/shard_map/ppermute | solution.py:555
  252.9 19.4 %collective-permute-done.4.refs_14_ = bf16[2048,256]{1,0:T(8,128)(2,1)S(1)} collective-permute-done((bf16[2048,256]{1,0:T(8,128)(2,1)S(1)}, bf16[2048,256]{1,0:T(8,128)(2,1)S(1)}, u32[]{:S(2)}, u32[]{:S(2)}) %collective-permute-start.4) | collective-permute-done | bytes 1048608 | tf_op jit(solution)/shard_map/ppermute | solution.py:557
  276.3 9.2 %assemble.3 = f32[2048,1024]{1,0:T(8,128)} custom-call(s32[32]{0:T(128)} %get-tuple-element.49.row_ref, s32[32]{0:T(128)} %get-tuple-element.48.col_ref, s32[32]{0:T(128)} %convert_element_type.10.present_ref, bf16[32,128,128]{2,1,0:T(8,128)(2,1)} %copy-done.5, f32[2048,1024]{1,0:T(8,128)} %h_ref.5), custom_call_target="tpu_custom_call" | custom-call | flops 2097152 | bytes 12582912 | tf_op jit(solution)/shard_map/assemble/pallas_call | solution.py:308
  289.5 5.5 %collective-permute-done.7.refs_15_ = bf16[2048,256]{1,0:T(8,128)(2,1)} collective-permute-done((bf16[2048,256]{1,0:T(8,128)(2,1)}, bf16[2048,256]{1,0:T(8,128)(2,1)}, u32[]{:S(2)}, u32[]{:S(2)}) %collective-permute-start.7) | collective-permute-done | bytes 1048608 | tf_op jit(solution)/shard_map/ppermute | solution.py:557
  296.4 37.2 %product.1.refs_3_ = f32[2048,1024]{1,0:T(8,128)} custom-call(s32[6]{0:T(128)} %stack.41.sc_ref, bf16[2048,256]{1,0:T(8,128)(2,1)} %assemble.5.refs_0_, bf16[2048,256]{1,0:T(8,128)(2,1)} %get-tuple-element.35.refs_1_, bf16[2048,256]{1,0:T(8,128)(2,1)} %get-tuple-element.38.refs_2_, bf16[2048,256]{1,0:T(8,128)(2,1)} %get-tuple-element.36.refs_3_, ...), custom_call_target="tpu_custom_call" | custom-call | flops 25769803776 | bytes 46137344 | tf_op jit(solution)/shard_map/product/pallas_call | solution.py:379
  334.7 8.9 %product_add.4.refs_3_ = f32[2048,1024]{1,0:T(8,128)} custom-call(s32[2]{0:T(128)} %pad_add_fusion.sc_ref, bf16[2048,256]{1,0:T(8,128)(2,1)} %collective-permute-done.18.refs_0_, bf16[2048,256]{1,0:T(8,128)(2,1)} %copy-done.15, bf16[8,2048,1024]{2,1,0:T(8,128)(2,1)} %bitcast.31, f32[2048,1024]{1,0:T(8,128)} %product.1.refs_3_), custom_call_target="tpu_custom_call", output_to_operand_aliasing={{}: (4, {})} | custom-call | flops 2147483648 | bytes 13631488 | tf_op jit(solution)/shard_map/product_add/pallas_call | solution.py:457
  344.6 8.9 %product_add.5.refs_3_ = f32[2048,1024]{1,0:T(8,128)} custom-call(s32[2]{0:T(128)} %pad_add_fusion.sc_ref, bf16[2048,256]{1,0:T(8,128)(2,1)} %collective-permute-done.15.refs_0_, bf16[2048,256]{1,0:T(8,128)(2,1)} %copy-done.16, bf16[8,2048,1024]{2,1,0:T(8,128)(2,1)} %bitcast.32, f32[2048,1024]{1,0:T(8,128)} %product_add.4.refs_3_), custom_call_target="tpu_custom_call", output_to_operand_aliasing={{}: (4, {})} | custom-call | flops 2147483648 | bytes 13631488 | tf_op jit(solution)/shard_map/product_add/pallas_call | solution.py:457
  353.4 8.8 %collective-permute-done.12.refs_1_ = bf16[2048,256]{1,0:T(8,128)(2,1)S(1)} collective-permute-done((bf16[2048,256]{1,0:T(8,128)(2,1)}, bf16[2048,256]{1,0:T(8,128)(2,1)S(1)}, u32[]{:S(2)}, u32[]{:S(2)}) %collective-permute-start.12) | collective-permute-done | bytes 1048608 | tf_op jit(solution)/shard_map/ppermute | solution.py:569
  363.2 8.9 %product_add.6.refs_3_ = f32[2048,1024]{1,0:T(8,128)} custom-call(s32[2]{0:T(128)} %pad_add_fusion.sc_ref, bf16[2048,256]{1,0:T(8,128)(2,1)} %collective-permute-done.11.refs_0_, bf16[2048,256]{1,0:T(8,128)(2,1)} %copy-done.17, bf16[8,2048,1024]{2,1,0:T(8,128)(2,1)} %bitcast.33, f32[2048,1024]{1,0:T(8,128)} %product_add.5.refs_3_), custom_call_target="tpu_custom_call", output_to_operand_aliasing={{}: (4, {})} | custom-call | flops 2147483648 | bytes 13631488 | tf_op jit(solution)/shard_map/product_add/pallas_call | solution.py:457
  372.1 12.6 %collective-permute-done.8.refs_1_ = bf16[2048,256]{1,0:T(8,128)(2,1)} collective-permute-done((bf16[2048,256]{1,0:T(8,128)(2,1)}, bf16[2048,256]{1,0:T(8,128)(2,1)}, u32[]{:S(2)}, u32[]{:S(2)}) %collective-permute-start.8) | collective-permute-done | bytes 1048608 | tf_op jit(solution)/shard_map/ppermute | solution.py:569
  384.8 8.9 %product_add.7 = f32[2048,1024]{1,0:T(8,128)} custom-call(s32[2]{0:T(128)} %pad_add_fusion.sc_ref, bf16[2048,256]{1,0:T(8,128)(2,1)} %collective-permute-done.5.refs_0_, bf16[2048,256]{1,0:T(8,128)(2,1)} %collective-permute-done.8.refs_1_, bf16[8,2048,1024]{2,1,0:T(8,128)(2,1)} %bitcast.34, ...), custom_call_target="tpu_custom_call", output_to_operand_aliasing={{}: (4, {})} | custom-call | flops 2147483648 | bytes 13631488 | tf_op jit(solution)/shard_map/product_add/pallas_call | solution.py:457
  (91 shorter events, 38.4 us)
Async XLA Ops:
  16.1 33.6 %all-to-all-start = ((f16[32,128,128]{2,1,0:T(8,128)(2,1)}), f16[32,128,128]{2,1,0:T(8,128)(2,1)S(1)}, u32[]{:S(2)}, u32[]{:S(2)}) async-start(f16[32,128,128]{2,1,0:T(8,128)(2,1)} %multiply_convert_fusion), calls=%async_computation | async-start | bytes 2097152 | tf_op jit(solution)/shard_map/all_to_all | solution.py:531
  23.5 272.9 %all-gather.3.cloned.1.call-start = ((), (), s32[]{:S(2)}) async-start(), calls=%async_computation.2 | async-start | bytes 37748736 | tf_op jit(solution)/shard_map/all_gather | solution.py:535
  32.1 17.7 %copy-start.19 = (s32[64,4]{0,1:T(4,128)S(1)}, s32[64,4]{0,1:T(4,128)}, u32[]{:S(2)}) copy-start(s32[64,4]{0,1:T(4,128)} %param.10) | copy-start | bytes 3076
  32.1 18.8 %copy-start.18 = (f32[2,1024]{1,0:T(2,128)S(1)}, f32[2,1024]{1,0:T(2,128)}, u32[]{:S(2)}) copy-start(f32[2,1024]{1,0:T(2,128)} %param.9) | copy-start | bytes 24580
  66.1 29.4 %all-to-all-start.1 = ((bf16[32,128,128]{2,1,0:T(8,128)(2,1)}), bf16[32,128,128]{2,1,0:T(8,128)(2,1)S(1)}, u32[]{:S(2)}, u32[]{:S(2)}) async-start(bf16[32,128,128]{2,1,0:T(8,128)(2,1)} %tile_ham.1), calls=%async_computation.1 | async-start | bytes 2097152 | tf_op jit(solution)/shard_map/all_to_all | solution.py:538
  102.4 11.6 %copy-start.6 = (bf16[2048,256]{1,0:T(8,128)(2,1)S(1)}, bf16[2048,256]{1,0:T(8,128)(2,1)}, u32[]{:S(2)}) copy-start(bf16[2048,256]{1,0:T(8,128)(2,1)} %assemble.5.refs_0_) | copy-start | bytes 3145732
  102.5 14.5 %collective-permute-start.2 = (bf16[2048,256]{1,0:T(8,128)(2,1)}, bf16[2048,256]{1,0:T(8,128)(2,1)S(1)}, u32[]{:S(2)}, u32[]{:S(2)}) collective-permute-start(bf16[2048,256]{1,0:T(8,128)(2,1)} %assemble.5.refs_0_), channel_id=1, source_target_pairs={{8,16},{16,8},{9,17},{17,9},{10,18},{18,10},{11,19},{19,11},{12,20... | collective-permute-start | bytes 3145736 | tf_op jit(solution)/shard_map/ppermute | solution.py:556
  110.8 26.7 %collective-permute-start.13 = (bf16[2048,256]{1,0:T(8,128)(2,1)}, bf16[2048,256]{1,0:T(8,128)(2,1)S(1)}, u32[]{:S(2)}, u32[]{:S(2)}) collective-permute-start(bf16[2048,256]{1,0:T(8,128)(2,1)} %get-tuple-element.35.refs_1_), channel_id=1, source_target_pairs={{0,8},{8,0},{16,24},{24,16},{1,9},{9,1},{17,25},{25,17},{2,10},{10... | collective-permute-start | bytes 3145736 | tf_op jit(solution)/shard_map/ppermute | solution.py:555
  113.3 26.2 %collective-permute-start = (bf16[2048,256]{1,0:T(8,128)(2,1)}, bf16[2048,256]{1,0:T(8,128)(2,1)S(1)}, u32[]{:S(2)}, u32[]{:S(2)}) collective-permute-start(bf16[2048,256]{1,0:T(8,128)(2,1)} %get-tuple-element.35.refs_1_), channel_id=1, source_target_pairs={{8,16},{16,8},{9,17},{17,9},{10,18},{18,10},{11,19},{19,11},{12,20... | collective-permute-start | bytes 3145736 | tf_op jit(solution)/shard_map/ppermute | solution.py:556
  114.1 46.1 %collective-permute-start.17 = (bf16[2048,256]{1,0:T(8,128)(2,1)S(1)}, bf16[2048,256]{1,0:T(8,128)(2,1)}, u32[]{:S(2)}, u32[]{:S(2)}) collective-permute-start(bf16[2048,256]{1,0:T(8,128)(2,1)S(1)} %copy-done.6), channel_id=1, source_target_pairs={{0,8},{8,0},{16,24},{24,16},{1,9},{9,1},{17,25},{25,17},{2,10},{10... | collective-permute-start | bytes 3145736 | tf_op jit(solution)/shard_map/ppermute | solution.py:555
  116.9 168.6 %copy-start.8 = (bf16[2048,256]{1,0:T(8,128)(2,1)}, bf16[2048,256]{1,0:T(8,128)(2,1)S(1)}, u32[]{:S(2)}) copy-start(bf16[2048,256]{1,0:T(8,128)(2,1)S(1)} %collective-permute-done.2.refs_8_) | copy-start | bytes 3145732
  116.9 65.5 %collective-permute-start.14 = (bf16[2048,256]{1,0:T(8,128)(2,1)S(1)}, bf16[2048,256]{1,0:T(8,128)(2,1)S(1)}, u32[]{:S(2)}, u32[]{:S(2)}) collective-permute-start(bf16[2048,256]{1,0:T(8,128)(2,1)S(1)} %collective-permute-done.2.refs_8_), channel_id=1, source_target_pairs={{8,0},{16,24},{9,1},{17,25},{10,2},{18,26},{11,3},{19,27},{12,4},{... | collective-permute-start | bytes 3145736 | tf_op jit(solution)/shard_map/ppermute | solution.py:557
  118.2 65.9 %collective-permute-start.3 = (bf16[2048,256]{1,0:T(8,128)(2,1)}, bf16[2048,256]{1,0:T(8,128)(2,1)S(1)}, u32[]{:S(2)}, u32[]{:S(2)}) collective-permute-start(bf16[2048,256]{1,0:T(8,128)(2,1)} %get-tuple-element.38.refs_2_), channel_id=1, source_target_pairs={{8,16},{16,8},{9,17},{17,9},{10,18},{18,10},{11,19},{19,11},{12,20... | collective-permute-start | bytes 3145736 | tf_op jit(solution)/shard_map/ppermute | solution.py:556
  137.5 148.0 %copy-start.9 = (bf16[2048,256]{1,0:T(8,128)(2,1)}, bf16[2048,256]{1,0:T(8,128)(2,1)S(1)}, u32[]{:S(2)}) copy-start(bf16[2048,256]{1,0:T(8,128)(2,1)S(1)} %collective-permute-done.13.refs_5_) | copy-start | bytes 3145732
  137.5 67.5 %collective-permute-start.9 = (bf16[2048,256]{1,0:T(8,128)(2,1)}, bf16[2048,256]{1,0:T(8,128)(2,1)}, u32[]{:S(2)}, u32[]{:S(2)}) collective-permute-start(bf16[2048,256]{1,0:T(8,128)(2,1)} %get-tuple-element.38.refs_2_), channel_id=1, source_target_pairs={{0,8},{8,0},{16,24},{24,16},{1,9},{9,1},{17,25},{25,17},{2,10},{10... | collective-permute-start | bytes 3145736 | tf_op jit(solution)/shard_map/ppermute | solution.py:555
  139.5 146.1 %copy-start.10 = (bf16[2048,256]{1,0:T(8,128)(2,1)}, bf16[2048,256]{1,0:T(8,128)(2,1)S(1)}, u32[]{:S(2)}) copy-start(bf16[2048,256]{1,0:T(8,128)(2,1)S(1)} %collective-permute-done.refs_9_) | copy-start | bytes 3145732
  139.5 87.9 %collective-permute-start.10 = (bf16[2048,256]{1,0:T(8,128)(2,1)S(1)}, bf16[2048,256]{1,0:T(8,128)(2,1)S(1)}, u32[]{:S(2)}, u32[]{:S(2)}) collective-permute-start(bf16[2048,256]{1,0:T(8,128)(2,1)S(1)} %collective-permute-done.refs_9_), channel_id=1, source_target_pairs={{8,0},{16,24},{9,1},{17,25},{10,2},{18,26},{11,3},{19,27},{12,4},{... | collective-permute-start | bytes 3145736 | tf_op jit(solution)/shard_map/ppermute | solution.py:557
  160.1 89.9 %collective-permute-start.1 = (bf16[2048,256]{1,0:T(8,128)(2,1)}, bf16[2048,256]{1,0:T(8,128)(2,1)}, u32[]{:S(2)}, u32[]{:S(2)}) collective-permute-start(bf16[2048,256]{1,0:T(8,128)(2,1)} %get-tuple-element.36.refs_3_), channel_id=1, source_target_pairs={{0,8},{8,0},{16,24},{24,16},{1,9},{9,1},{17,25},{25,17},{2,10},{10... | collective-permute-start | bytes 3145736 | tf_op jit(solution)/shard_map/ppermute | solution.py:555
  182.5 44.9 %copy-start.11 = (bf16[2048,256]{1,0:T(8,128)(2,1)}, bf16[2048,256]{1,0:T(8,128)(2,1)S(1)}, u32[]{:S(2)}) copy-start(bf16[2048,256]{1,0:T(8,128)(2,1)S(1)} %collective-permute-done.14.refs_12_) | copy-start | bytes 3145732
  182.5 69.2 %collective-permute-start.6 = (bf16[2048,256]{1,0:T(8,128)(2,1)}, bf16[2048,256]{1,0:T(8,128)(2,1)}, u32[]{:S(2)}, u32[]{:S(2)}) collective-permute-start(bf16[2048,256]{1,0:T(8,128)(2,1)} %get-tuple-element.36.refs_3_), channel_id=1, source_target_pairs={{8,16},{16,8},{9,17},{17,9},{10,18},{18,10},{11,19},{19,11},{12,20... | collective-permute-start | bytes 3145736 | tf_op jit(solution)/shard_map/ppermute | solution.py:556
  184.1 44.9 %copy-start.12 = (bf16[2048,256]{1,0:T(8,128)(2,1)}, bf16[2048,256]{1,0:T(8,128)(2,1)S(1)}, u32[]{:S(2)}) copy-start(bf16[2048,256]{1,0:T(8,128)(2,1)S(1)} %collective-permute-done.3.refs_10_) | copy-start | bytes 3145732
  184.1 88.2 %collective-permute-start.4 = (bf16[2048,256]{1,0:T(8,128)(2,1)S(1)}, bf16[2048,256]{1,0:T(8,128)(2,1)S(1)}, u32[]{:S(2)}, u32[]{:S(2)}) collective-permute-start(bf16[2048,256]{1,0:T(8,128)(2,1)S(1)} %collective-permute-done.3.refs_10_), channel_id=1, source_target_pairs={{8,0},{16,24},{9,1},{17,25},{10,2},{18,26},{11,3},{19,27},{12,4},{... | collective-permute-start | bytes 3145736 | tf_op jit(solution)/shard_map/ppermute | solution.py:557
  205.1 80.5 %collective-permute-start.18 = (bf16[2048,256]{1,0:T(8,128)(2,1)}, bf16[2048,256]{1,0:T(8,128)(2,1)}, u32[]{:S(2)}, u32[]{:S(2)}) collective-permute-start(bf16[2048,256]{1,0:T(8,128)(2,1)} %collective-permute-done.17.refs_4_), channel_id=1, source_target_pairs={{8,16},{16,8},{9,17},{17,9},{10,18},{18,10},{11,19},{19,11},{12,20... | collective-permute-start | bytes 3145736 | tf_op jit(solution)/shard_map/ppermute | solution.py:563
  227.4 44.9 %copy-start.13 = (bf16[2048,256]{1,0:T(8,128)(2,1)}, bf16[2048,256]{1,0:T(8,128)(2,1)S(1)}, u32[]{:S(2)}) copy-start(bf16[2048,256]{1,0:T(8,128)(2,1)S(1)} %collective-permute-done.10.refs_13_) | copy-start | bytes 3145732
  227.4 59.4 %collective-permute-start.15 = (bf16[2048,256]{1,0:T(8,128)(2,1)S(1)}, bf16[2048,256]{1,0:T(8,128)(2,1)}, u32[]{:S(2)}, u32[]{:S(2)}) collective-permute-start(bf16[2048,256]{1,0:T(8,128)(2,1)S(1)} %collective-permute-done.13.refs_5_), channel_id=1, source_target_pairs={{8,16},{16,8},{9,17},{17,9},{10,18},{18,10},{11,19},{19,11},{12,20... | collective-permute-start | bytes 3145736 | tf_op jit(solution)/shard_map/ppermute | solution.py:563
  250.0 38.2 %collective-permute-start.11 = (bf16[2048,256]{1,0:T(8,128)(2,1)}, bf16[2048,256]{1,0:T(8,128)(2,1)}, u32[]{:S(2)}, u32[]{:S(2)}) collective-permute-start(bf16[2048,256]{1,0:T(8,128)(2,1)} %collective-permute-done.9.refs_6_), channel_id=1, source_target_pairs={{8,16},{16,8},{9,17},{17,9},{10,18},{18,10},{11,19},{19,11},{12,20... | collective-permute-start | bytes 3145736 | tf_op jit(solution)/shard_map/ppermute | solution.py:563
  251.6 43.3 %collective-permute-start.7 = (bf16[2048,256]{1,0:T(8,128)(2,1)}, bf16[2048,256]{1,0:T(8,128)(2,1)}, u32[]{:S(2)}, u32[]{:S(2)}) collective-permute-start(bf16[2048,256]{1,0:T(8,128)(2,1)} %collective-permute-done.6.refs_11_), channel_id=1, source_target_pairs={{8,0},{16,24},{9,1},{17,25},{10,2},{18,26},{11,3},{19,27},{12,4},{... | collective-permute-start | bytes 3145736 | tf_op jit(solution)/shard_map/ppermute | solution.py:557
  273.4 21.6 %collective-permute-start.5 = (bf16[2048,256]{1,0:T(8,128)(2,1)}, bf16[2048,256]{1,0:T(8,128)(2,1)}, u32[]{:S(2)}, u32[]{:S(2)}) collective-permute-start(bf16[2048,256]{1,0:T(8,128)(2,1)} %collective-permute-done.1.refs_7_), channel_id=1, source_target_pairs={{8,16},{16,8},{9,17},{17,9},{10,18},{18,10},{11,19},{19,11},{12,20... | collective-permute-start | bytes 3145736 | tf_op jit(solution)/shard_map/ppermute | solution.py:563
  285.6 48.1 %collective-permute-start.19 = (bf16[2048,256]{1,0:T(8,128)(2,1)}, bf16[2048,256]{1,0:T(8,128)(2,1)S(1)}, u32[]{:S(2)}, u32[]{:S(2)}) collective-permute-start(bf16[2048,256]{1,0:T(8,128)(2,1)} %collective-permute-done.18.refs_0_), channel_id=1, source_target_pairs={{8,0},{16,24},{9,1},{17,25},{10,2},{18,26},{11,3},{19,27},{12,4},{... | collective-permute-start | bytes 3145736 | tf_op jit(solution)/shard_map/ppermute | solution.py:569
  286.9 56.7 %collective-permute-start.16 = (bf16[2048,256]{1,0:T(8,128)(2,1)}, bf16[2048,256]{1,0:T(8,128)(2,1)S(1)}, u32[]{:S(2)}, u32[]{:S(2)}) collective-permute-start(bf16[2048,256]{1,0:T(8,128)(2,1)} %collective-permute-done.15.refs_0_), channel_id=1, source_target_pairs={{8,0},{16,24},{9,1},{17,25},{10,2},{18,26},{11,3},{19,27},{12,4},{... | collective-permute-start | bytes 3145736 | tf_op jit(solution)/shard_map/ppermute | solution.py:569
  288.2 74.1 %collective-permute-start.12 = (bf16[2048,256]{1,0:T(8,128)(2,1)}, bf16[2048,256]{1,0:T(8,128)(2,1)S(1)}, u32[]{:S(2)}, u32[]{:S(2)}) collective-permute-start(bf16[2048,256]{1,0:T(8,128)(2,1)} %collective-permute-done.11.refs_0_), channel_id=1, source_target_pairs={{8,0},{16,24},{9,1},{17,25},{10,2},{18,26},{11,3},{19,27},{12,4},{... | collective-permute-start | bytes 3145736 | tf_op jit(solution)/shard_map/ppermute | solution.py:569
  294.9 89.8 %collective-permute-start.8 = (bf16[2048,256]{1,0:T(8,128)(2,1)}, bf16[2048,256]{1,0:T(8,128)(2,1)}, u32[]{:S(2)}, u32[]{:S(2)}) collective-permute-start(bf16[2048,256]{1,0:T(8,128)(2,1)} %collective-permute-done.5.refs_0_), channel_id=1, source_target_pairs={{8,0},{16,24},{9,1},{17,25},{10,2},{18,26},{11,3},{19,27},{12,4},{... | collective-permute-start | bytes 3145736 | tf_op jit(solution)/shard_map/ppermute | solution.py:569
  (12 other events, 24.0 us)
Sparse Core Ops, SparseCore 0:
  49.9 171.0 all-gather.2

commit v7 on v6

--- a/solution.py
+++ b/solution.py
@@ -59,25 +59,25 @@
     )(row_pick, col_pick, density)
 
 
-def round_bands(x, top, sizes):
-    cols = x.shape[1]
-    bm = min(256, min(sizes))
-    source = [(k, g) for k, size in enumerate(sizes) for g in range(size // bm)]
-    steps = len(source)
+def round_parts(x, parts):
+    rows, cols = x.shape
+    wide = cols // parts
+    bm = min(256, rows)
+    steps = rows // bm
 
     def kernel(x_ref, *rest):
-        outs = rest[: len(sizes)]
-        raw_ref, low_ref, in_sems, out_sems = rest[len(sizes) :]
+        outs, (raw_ref, low_ref, in_sems, out_sems) = rest[:parts], rest[parts:]
 
         def read(g):
             return pltpu.make_async_copy(
-                x_ref.at[pl.ds(top + g * bm, bm)], raw_ref.at[g], in_sems.at[g]
-            )
-
-        def write(g):
-            k, at = source[g]
+                x_ref.at[pl.ds(g * bm, bm)], raw_ref.at[g], in_sems.at[g]
+            )
+
+        def write(g, p):
             return pltpu.make_async_copy(
-                low_ref.at[g], outs[k].at[pl.ds(at * bm, bm)], out_sems.at[g]
+                low_ref.at[g, :, pl.ds(p * wide, wide)],
+                outs[p].at[pl.ds(g * bm, bm)],
+                out_sems.at[g, p],
             )
 
         for g in range(min(AHEAD, steps)):
@@ -87,28 +87,112 @@
             if g + AHEAD < steps:
                 read(g + AHEAD).start()
             low_ref[g] = raw_ref[g].astype(BF16)
-            write(g).start()
+            for p in range(parts):
+                write(g, p).start()
         for g in range(steps):
-            write(g).wait()
+            for p in range(parts):
+                write(g, p).wait()
 
     return pl.pallas_call(
         kernel,
         grid=(1,),
         in_specs=[pl.BlockSpec(memory_space=pl.ANY)],
-        out_specs=[pl.BlockSpec(memory_space=pl.ANY)] * len(sizes),
+        out_specs=[pl.BlockSpec(memory_space=pl.ANY)] * parts,
         scratch_shapes=[
             pltpu.VMEM((steps, bm, cols), F32),
             pltpu.VMEM((steps, bm, cols), BF16),
             pltpu.SemaphoreType.DMA((steps,)),
-            pltpu.SemaphoreType.DMA((steps,)),
+            pltpu.SemaphoreType.DMA((steps, parts)),
         ],
-        out_shape=[jax.ShapeDtypeStruct((size, cols), BF16) for size in sizes],
+        out_shape=[jax.ShapeDtypeStruct((rows, wide), BF16)] * parts,
         compiler_params=pltpu.CompilerParams(vmem_limit_bytes=56 * MIB),
         cost_estimate=pl.CostEstimate(
-            flops=sum(sizes) * cols, bytes_accessed=sum(sizes) * cols * 6, transcendentals=0
-        ),
-        name="round_bands",
+            flops=rows * cols, bytes_accessed=rows * cols * 6, transcendentals=0
+        ),
+        name="round_parts",
     )(x)
+
+
+def update_blocks(low, h_blocks, arriving, picks):
+    parts, wide = len(low), low[0].shape[1]
+    n = arriving.shape[0]
+    row_pick, col_pick, present = picks
+    order = jnp.arange(n, dtype=jnp.int32)
+    same = (
+        (row_pick[:, None] == row_pick[None, :])
+        & (col_pick[:, None] == col_pick[None, :])
+        & (present[:, None] * present[None, :] > 0)
+    )
+    leader = jnp.min(jnp.where(same, order[None, :], n), axis=1)
+
+    def kernel(row_ref, col_ref, lead_ref, in_ref, h_ref, *rest):
+        outs, (work_ref, low_ref, sems) = rest[parts : 2 * parts], rest[2 * parts :]
+
+        def add(s, carry):
+            first = lead_ref[s]
+
+            @pl.when(first == s)
+            def _():
+                work_ref[s] = h_ref[s] + in_ref[s].astype(F32)
+
+            @pl.when(first < s)
+            def _():
+                work_ref[first] = work_ref[first] + in_ref[s].astype(F32)
+
+            return carry
+
+        def write(s, carry):
+            @pl.when(lead_ref[s] == s)
+            def _():
+                low_ref[s] = work_ref[s].astype(BF16)
+                top = pl.ds(pl.multiple_of(row_ref[s] * BLK, BLK), BLK)
+                column = col_ref[s] * BLK
+                for p in range(parts):
+
+                    @pl.when((column >= p * wide) & (column < (p + 1) * wide))
+                    def _(p=p):
+                        left = pl.ds(pl.multiple_of(column - p * wide, BLK), BLK)
+                        pltpu.make_async_copy(
+                            low_ref.at[s], outs[p].at[top, left], sems.at[s]
+                        ).start()
+
+            return carry
+
+        def wait(s, carry):
+            @pl.when(lead_ref[s] == s)
+            def _():
+                pltpu.make_async_copy(
+                    low_ref.at[s], outs[0].at[pl.ds(0, BLK), pl.ds(0, BLK)], sems.at[s]
+                ).wait()
+
+            return carry
+
+        lax.fori_loop(0, n, add, 0)
+        lax.fori_loop(0, n, write, 0)
+        lax.fori_loop(0, n, wait, 0)
+
+    whole = pl.BlockSpec((n, BLK, BLK), lambda i, *_: (0, 0, 0))
+    return pl.pallas_call(
+        kernel,
+        grid_spec=pltpu.PrefetchScalarGridSpec(
+            num_scalar_prefetch=3,
+            grid=(1,),
+            in_specs=[whole, whole] + [pl.BlockSpec(memory_space=pl.ANY)] * parts,
+            out_specs=[pl.BlockSpec(memory_space=pl.ANY)] * parts,
+            scratch_shapes=[
+                pltpu.VMEM((n, BLK, BLK), F32),
+                pltpu.VMEM((n, BLK, BLK), BF16),
+                pltpu.SemaphoreType.DMA((n,)),
+            ],
+        ),
+        out_shape=[jax.ShapeDtypeStruct(x.shape, x.dtype) for x in low],
+        input_output_aliases={5 + p: p for p in range(parts)},
+        compiler_params=pltpu.CompilerParams(vmem_limit_bytes=40 * MIB),
+        cost_estimate=pl.CostEstimate(
+            flops=n * BLK * BLK, bytes_accessed=n * BLK * BLK * 8, transcendentals=0
+        ),
+        name="update_blocks",
+    )(row_pick, col_pick, leader, arriving, h_blocks, *low)
 
 
 def split(x):
@@ -530,7 +614,7 @@
     outgoing = (gather_blocks(density, picks[0], picks[1]) * DM_SCALE).astype(jnp.float16)
     incoming = lax.all_to_all(outgoing, ("row", "col"), split_axis=0, concat_axis=0, tiled=True)
     basis = split_basis(phi, my_counts)
-    (dm_low,) = round_bands(density, 0, [rows_loc])
+    (dm_low,) = round_parts(density, 1)
     incoming, (dm_low, basis) = tie(incoming, (dm_low, basis))
     dm_panel = lax.all_gather(dm_low, "col", axis=0, tiled=False)
 
@@ -538,9 +622,10 @@
     arriving = lax.all_to_all(returning, ("row", "col"), split_axis=0, concat_axis=0, tiled=True)
     parts = PARTS if line and cols_loc % (PARTS * BLK) == 0 else 1
     wide = cols_loc // parts
-    low = assemble(h_core, arriving, picks, BF16, 0, 1, wide)
-    if parts > 1:
-        low = low + assemble(h_core, arriving, picks, BF16, wide, parts - 1, wide)
+    low = round_parts(h_core, parts)
+    h_blocks = gather_blocks(h_core, picks[0], picks[1])
+    arriving, (low, h_blocks) = tie(arriving, (low, h_blocks))
+    low = update_blocks(low, h_blocks, arriving, picks)
     (hamiltonian,) = assemble(h_core, arriving, picks, F32, 0, 1, cols_loc)
 
     if line:

time: 402 us -> 395 us (0.983)
  waiting for transfers between devices: 203 us -> 188 us
  local copies, waits for them, and re-layouts: 15.2 us -> 19.5 us
    pallas_call x3 -> x1, Pallas kernels: 22.6 us -> 8.67 us  [assemble(): pl.pallas_call(kernel, grid_spec=pltpu.PrefetchScalarGridSpec(num_scalar_...]
    all_to_all x1, waiting for transfers between devices: 25.5 us -> 14.7 us  [body(): lax.all_to_all(returning, ('row', 'col'), split_axis=0, concat_axis=0, ti...]
    pallas_call x1 -> x3, Pallas kernels: 6.16 us -> 15.2 us  [the longest x2 12.7 us: round_parts(): pl.pallas_call(kernel, grid=(1,), in_specs=[pl.BlockSpec(memory_space=pl....]
    pallas_call x1 -> x2, Pallas kernels: 4.29 us -> 9.29 us  [gather_blocks(): pl.pallas_call(gather_kernel, grid_spec=pltpu.PrefetchScalarGridSpec(num_...]
    ppermute x4, starting transfers between devices: 9.24 us -> 13.9 us  [body(): pair.append(lax.ppermute(ready, 'row', swap))]
    unnamed x43 -> x65, local copies, waits for them, and re-layouts: 13.6 us -> 18 us
where the time goes in v7:
time: 395 us; the launch traced here: 394 us
  waiting for transfers between devices  188 us (48%)
  Pallas kernels  120 us (30%)
  starting transfers between devices  44.7 us (11%)
  local copies, waits for them, and re-layouts  19.5 us (5%)
  between operations  14.6 us (4%)
  other arithmetic  6.67 us (2%)
    ppermute x4, waiting for transfers between devices, body(): pair.append(lax.ppermute(ready, 'row', swap))  74.9 us
    ppermute x4, waiting for transfers between devices, body(): near_end = [lax.ppermute(x, 'row', outward) for x in near_mid]  65.7 us
    pallas_call x1, Pallas kernels, product(): pl.pallas_call(kernel, grid_spec=pltpu.PrefetchScalarGridSpec(num_scalar_...  37.2 us
    pallas_call x4, Pallas kernels, product_add(): pl.pallas_call(kernel, grid_spec=pltpu.PrefetchScalarGridSpec(num_scalar_...  35.5 us
    ppermute x4, waiting for transfers between devices, body(): far_end.append(lax.ppermute(ready, 'row', outward))  21.4 us
    unnamed x65, local copies, waits for them, and re-layouts  18 us
    all_to_all x1, waiting for transfers between devices, body(): lax.all_to_all(returning, ('row', 'col'), split_axis=0, concat_axis=0, ti...  14.7 us
    ppermute x4, starting transfers between devices, body(): pair.append(lax.ppermute(ready, 'row', swap))  13.9 us
  transfers between devices with their start and end apart: 23, of which 12 were waited for; matrix products, arithmetic and copies ran while one was open for 1% of the time, Pallas kernels for 27%

profile of v7, /device:TPU:0, one launch (start us, length us, event | category | flops | bytes accessed | tf_op | source)
XLA Modules:
  0.0 393.7 jit_solution(655427894746766808)
XLA Ops:
  8.9 4.7 %gather_blocks.2 = f32[32,128,128]{2,1,0:T(8,128)} custom-call(s32[32]{0:T(128)} %get-tuple-element.71.row_ref, s32[32]{0:T(128)} %get-tuple-element.70.col_ref, f32[2048,1024]{1,0:T(8,128)} %x_ref.2), custom_call_target="tpu_custom_call" | custom-call | bytes 4194304 | tf_op jit(solution)/shard_map/gather_blocks/pallas_call | solution.py:44
  13.7 2.9 multiply_convert_fusion
  16.5 6.9 %all-to-all-start = ((f16[32,128,128]{2,1,0:T(8,128)(2,1)}), f16[32,128,128]{2,1,0:T(8,128)(2,1)S(1)}, u32[]{:S(2)}, u32[]{:S(2)}) async-start(f16[32,128,128]{2,1,0:T(8,128)(2,1)} %multiply_convert_fusion), calls=%async_computation | async-start | bytes 2097152 | tf_op jit(solution)/shard_map/all_to_all | solution.py:615
  23.6 6.2 %round_parts.2 = bf16[2048,1024]{1,0:T(8,128)(2,1)} custom-call(f32[2048,1024]{1,0:T(8,128)} %x_ref.2), custom_call_target="tpu_custom_call" | custom-call | flops 2097152 | bytes 12582912 | tf_op jit(solution)/shard_map/round_parts/pallas_call | solution.py:96
  32.0 2.2 split_basis.1
  38.2 11.5 %all-to-all-done = f16[32,128,128]{2,1,0:T(8,128)(2,1)S(1)} async-done(((f16[32,128,128]{2,1,0:T(8,128)(2,1)}), f16[32,128,128]{2,1,0:T(8,128)(2,1)S(1)}, u32[]{:S(2)}, u32[]{:S(2)}) %all-to-all-start) | async-done | bytes 1048608 | tf_op jit(solution)/shard_map/all_to_all | solution.py:615
  54.1 11.8 %tile_ham.1 = bf16[32,128,128]{2,1,0:T(8,128)(2,1)} custom-call(s32[2,16]{1,0:T(2,128)S(1)} %add.54.hold_ref, s32[2]{0:T(128)S(1)} %dynamic-slice_bitcast_fusion.count_ref, f32[32,128,128]{2,1,0:T(8,128)S(1)} %convert_element_type.12.in_ref, bf16[2,1024,512]{2,1,0:T(8,128)(2,1)S(1)} %get-tuple-element.41.hi_ref, bf16[2,1024,512]{2,1,0:T(8,128)(2,1)S(1)} %copy-done.14, ...), custom_call_target="tpu_custom_call" | custom-call | flops 6442450944 | bytes 8388608 | tf_op jit(solution)/shard_map/tile_ham/pallas_call | solution.py:287
  66.0 3.1 all-to-all-start.1
  69.2 4.6 %gather_blocks.3.h_ref = f32[32,128,128]{2,1,0:T(8,128)} custom-call(s32[32]{0:T(128)} %get-tuple-element.71.row_ref, s32[32]{0:T(128)} %get-tuple-element.70.col_ref, f32[2048,1024]{1,0:T(8,128)} %h_ref.1), custom_call_target="tpu_custom_call" | custom-call | bytes 4194304 | tf_op jit(solution)/shard_map/gather_blocks/pallas_call | solution.py:44
  73.8 6.5 %round_parts.3 = (bf16[2048,256]{1,0:T(8,128)(2,1)}, bf16[2048,256]{1,0:T(8,128)(2,1)}, bf16[2048,256]{1,0:T(8,128)(2,1)}, bf16[2048,256]{1,0:T(8,128)(2,1)}) custom-call(f32[2048,1024]{1,0:T(8,128)} %h_ref.1), custom_call_target="tpu_custom_call" | custom-call | flops 2097152 | bytes 12582912 | tf_op jit(solution)/shard_map/round_parts/pallas_call | solution.py:96
  80.6 14.7 %all-to-all-done.1.in_ref = bf16[32,128,128]{2,1,0:T(8,128)(2,1)S(1)} async-done(((bf16[32,128,128]{2,1,0:T(8,128)(2,1)}), bf16[32,128,128]{2,1,0:T(8,128)(2,1)S(1)}, u32[]{:S(2)}, u32[]{:S(2)}) %all-to-all-start.1) | async-done | bytes 1048608 | tf_op jit(solution)/shard_map/all_to_all | solution.py:622
  100.6 2.5 update_blocks.1
  103.9 2.9 collective-permute-start.13
  107.5 2.9 collective-permute-start.17
  112.4 18.3 %collective-permute-done.13.refs_5_ = bf16[2048,256]{1,0:T(8,128)(2,1)S(1)} collective-permute-done((bf16[2048,256]{1,0:T(8,128)(2,1)S(1)}, bf16[2048,256]{1,0:T(8,128)(2,1)S(1)}, u32[]{:S(2)}, u32[]{:S(2)}) %collective-permute-start.13) | collective-permute-done | bytes 1048608 | tf_op jit(solution)/shard_map/ppermute | solution.py:640
  130.8 5.3 %collective-permute-start.9 = (bf16[2048,256]{1,0:T(8,128)(2,1)S(1)}, bf16[2048,256]{1,0:T(8,128)(2,1)}, u32[]{:S(2)}, u32[]{:S(2)}) collective-permute-start(bf16[2048,256]{1,0:T(8,128)(2,1)S(1)} %get-tuple-element.60.refs_2_), channel_id=1, source_target_pairs={{0,8},{8,0},{16,24},{24,16},{1,9},{9,1},{17,25},{25,17},{2,10},{10... | collective-permute-start | bytes 3145736 | tf_op jit(solution)/shard_map/ppermute | solution.py:640
  137.4 16.0 %collective-permute-done.17.refs_4_ = bf16[2048,256]{1,0:T(8,128)(2,1)} collective-permute-done((bf16[2048,256]{1,0:T(8,128)(2,1)S(1)}, bf16[2048,256]{1,0:T(8,128)(2,1)}, u32[]{:S(2)}, u32[]{:S(2)}) %collective-permute-start.17) | collective-permute-done | bytes 1048608 | tf_op jit(solution)/shard_map/ppermute | solution.py:640
  153.4 2.8 collective-permute-start.1
  156.2 19.5 %collective-permute-done.14.refs_12_ = bf16[2048,256]{1,0:T(8,128)(2,1)S(1)} collective-permute-done((bf16[2048,256]{1,0:T(8,128)(2,1)S(1)}, bf16[2048,256]{1,0:T(8,128)(2,1)S(1)}, u32[]{:S(2)}, u32[]{:S(2)}) %collective-permute-start.14) | collective-permute-done | bytes 1048608 | tf_op jit(solution)/shard_map/ppermute | solution.py:642
  178.7 19.6 %collective-permute-done.9.refs_6_ = bf16[2048,256]{1,0:T(8,128)(2,1)} collective-permute-done((bf16[2048,256]{1,0:T(8,128)(2,1)S(1)}, bf16[2048,256]{1,0:T(8,128)(2,1)}, u32[]{:S(2)}, u32[]{:S(2)}) %collective-permute-start.9) | collective-permute-done | bytes 1048608 | tf_op jit(solution)/shard_map/ppermute | solution.py:640
  200.0 20.7 %collective-permute-done.10.refs_13_ = bf16[2048,256]{1,0:T(8,128)(2,1)S(1)} collective-permute-done((bf16[2048,256]{1,0:T(8,128)(2,1)S(1)}, bf16[2048,256]{1,0:T(8,128)(2,1)S(1)}, u32[]{:S(2)}, u32[]{:S(2)}) %collective-permute-start.10) | collective-permute-done | bytes 1048608 | tf_op jit(solution)/shard_map/ppermute | solution.py:642
  222.3 21.0 %collective-permute-done.1.refs_7_ = bf16[2048,256]{1,0:T(8,128)(2,1)} collective-permute-done((bf16[2048,256]{1,0:T(8,128)(2,1)S(1)}, bf16[2048,256]{1,0:T(8,128)(2,1)}, u32[]{:S(2)}, u32[]{:S(2)}) %collective-permute-start.1) | collective-permute-done | bytes 1048608 | tf_op jit(solution)/shard_map/ppermute | solution.py:640
  246.2 19.4 %collective-permute-done.4.refs_14_ = bf16[2048,256]{1,0:T(8,128)(2,1)S(1)} collective-permute-done((bf16[2048,256]{1,0:T(8,128)(2,1)S(1)}, bf16[2048,256]{1,0:T(8,128)(2,1)S(1)}, u32[]{:S(2)}, u32[]{:S(2)}) %collective-permute-start.4) | collective-permute-done | bytes 1048608 | tf_op jit(solution)/shard_map/ppermute | solution.py:642
  269.5 8.7 %assemble.1 = f32[2048,1024]{1,0:T(8,128)} custom-call(s32[32]{0:T(128)} %get-tuple-element.71.row_ref, s32[32]{0:T(128)} %get-tuple-element.70.col_ref, s32[32]{0:T(128)} %copy-done.30, bf16[32,128,128]{2,1,0:T(8,128)(2,1)} %copy-done, f32[2048,1024]{1,0:T(8,128)} %h_ref.1), custom_call_target="tpu_custom_call" | custom-call | flops 2097152 | bytes 12582912 | tf_op jit(solution)/shard_map/assemble/pallas_call | solution.py:392
  282.2 6.0 %collective-permute-done.7.refs_15_ = bf16[2048,256]{1,0:T(8,128)(2,1)} collective-permute-done((bf16[2048,256]{1,0:T(8,128)(2,1)}, bf16[2048,256]{1,0:T(8,128)(2,1)}, u32[]{:S(2)}, u32[]{:S(2)}) %collective-permute-start.7) | collective-permute-done | bytes 1048608 | tf_op jit(solution)/shard_map/ppermute | solution.py:642
  289.7 37.2 %product.1.refs_3_ = f32[2048,1024]{1,0:T(8,128)} custom-call(s32[6]{0:T(128)} %stack.41.sc_ref, bf16[2048,256]{1,0:T(8,128)(2,1)} %copy-done.3, bf16[2048,256]{1,0:T(8,128)(2,1)} %copy-done.5, bf16[2048,256]{1,0:T(8,128)(2,1)} %copy-done.7, bf16[2048,256]{1,0:T(8,128)(2,1)} %copy-done.9, bf16[2048,256]{1,0:T(8,128)(2,1)} %collective-permute-done.17.refs_4_, ...), custom_call_target="tpu_custom_call" | custom-call | flops 25769803776 | bytes 46137344 | tf_op jit(solution)/shard_map/product/pallas_call | solution.py:463
  327.9 8.9 %product_add.4.refs_3_ = f32[2048,1024]{1,0:T(8,128)} custom-call(s32[2]{0:T(128)} %pad_add_fusion.sc_ref, bf16[2048,256]{1,0:T(8,128)(2,1)} %collective-permute-done.18.refs_0_, bf16[2048,256]{1,0:T(8,128)(2,1)} %copy-done.25, bf16[8,2048,1024]{2,1,0:T(8,128)(2,1)} %bitcast.31, f32[2048,1024]{1,0:T(8,128)} %product.1.refs_3_), custom_call_target="tpu_custom_call", output_to_operand_aliasing={{}: (4, {})} | custom-call | flops 2147483648 | bytes 13631488 | tf_op jit(solution)/shard_map/product_add/pallas_call | solution.py:541
  337.8 8.9 %product_add.5.refs_3_ = f32[2048,1024]{1,0:T(8,128)} custom-call(s32[2]{0:T(128)} %pad_add_fusion.sc_ref, bf16[2048,256]{1,0:T(8,128)(2,1)} %collective-permute-done.15.refs_0_, bf16[2048,256]{1,0:T(8,128)(2,1)} %copy-done.26, bf16[8,2048,1024]{2,1,0:T(8,128)(2,1)} %bitcast.32, f32[2048,1024]{1,0:T(8,128)} %product_add.4.refs_3_), custom_call_target="tpu_custom_call", output_to_operand_aliasing={{}: (4, {})} | custom-call | flops 2147483648 | bytes 13631488 | tf_op jit(solution)/shard_map/product_add/pallas_call | solution.py:541
  346.7 8.8 %collective-permute-done.12.refs_1_ = bf16[2048,256]{1,0:T(8,128)(2,1)S(1)} collective-permute-done((bf16[2048,256]{1,0:T(8,128)(2,1)}, bf16[2048,256]{1,0:T(8,128)(2,1)S(1)}, u32[]{:S(2)}, u32[]{:S(2)}) %collective-permute-start.12) | collective-permute-done | bytes 1048608 | tf_op jit(solution)/shard_map/ppermute | solution.py:654
  356.5 8.9 %product_add.6.refs_3_ = f32[2048,1024]{1,0:T(8,128)} custom-call(s32[2]{0:T(128)} %pad_add_fusion.sc_ref, bf16[2048,256]{1,0:T(8,128)(2,1)} %collective-permute-done.11.refs_0_, bf16[2048,256]{1,0:T(8,128)(2,1)} %copy-done.27, bf16[8,2048,1024]{2,1,0:T(8,128)(2,1)} %bitcast.33, f32[2048,1024]{1,0:T(8,128)} %product_add.5.refs_3_), custom_call_target="tpu_custom_call", output_to_operand_aliasing={{}: (4, {})} | custom-call | flops 2147483648 | bytes 13631488 | tf_op jit(solution)/shard_map/product_add/pallas_call | solution.py:541
  365.3 12.6 %collective-permute-done.8.refs_1_ = bf16[2048,256]{1,0:T(8,128)(2,1)} collective-permute-done((bf16[2048,256]{1,0:T(8,128)(2,1)}, bf16[2048,256]{1,0:T(8,128)(2,1)}, u32[]{:S(2)}, u32[]{:S(2)}) %collective-permute-start.8) | collective-permute-done | bytes 1048608 | tf_op jit(solution)/shard_map/ppermute | solution.py:654
  378.0 8.9 %product_add.7 = f32[2048,1024]{1,0:T(8,128)} custom-call(s32[2]{0:T(128)} %pad_add_fusion.sc_ref, bf16[2048,256]{1,0:T(8,128)(2,1)} %collective-permute-done.5.refs_0_, bf16[2048,256]{1,0:T(8,128)(2,1)} %collective-permute-done.8.refs_1_, bf16[8,2048,1024]{2,1,0:T(8,128)(2,1)} %bitcast.34, ...), custom_call_target="tpu_custom_call", output_to_operand_aliasing={{}: (4, {})} | custom-call | flops 2147483648 | bytes 13631488 | tf_op jit(solution)/shard_map/product_add/pallas_call | solution.py:541
  (115 shorter events, 44.2 us)
Async XLA Ops:
  16.5 33.1 %all-to-all-start = ((f16[32,128,128]{2,1,0:T(8,128)(2,1)}), f16[32,128,128]{2,1,0:T(8,128)(2,1)S(1)}, u32[]{:S(2)}, u32[]{:S(2)}) async-start(f16[32,128,128]{2,1,0:T(8,128)(2,1)} %multiply_convert_fusion), calls=%async_computation | async-start | bytes 2097152 | tf_op jit(solution)/shard_map/all_to_all | solution.py:615
  23.4 266.3 %all-gather.3.cloned.1.call-start = ((), (), s32[]{:S(2)}) async-start(), calls=%async_computation.2 | async-start | bytes 37748736 | tf_op jit(solution)/shard_map/all_gather | solution.py:619
  66.0 29.3 %all-to-all-start.1 = ((bf16[32,128,128]{2,1,0:T(8,128)(2,1)}), bf16[32,128,128]{2,1,0:T(8,128)(2,1)S(1)}, u32[]{:S(2)}, u32[]{:S(2)}) async-start(bf16[32,128,128]{2,1,0:T(8,128)(2,1)} %tile_ham.1), calls=%async_computation.1 | async-start | bytes 2097152 | tf_op jit(solution)/shard_map/all_to_all | solution.py:622
  95.3 174.2 %copy-start = (bf16[32,128,128]{2,1,0:T(8,128)(2,1)}, bf16[32,128,128]{2,1,0:T(8,128)(2,1)S(1)}, u32[]{:S(2)}) copy-start(bf16[32,128,128]{2,1,0:T(8,128)(2,1)S(1)} %all-to-all-done.1.in_ref) | copy-start | bytes 3145732
  103.2 50.2 %copy-start.5 = (bf16[2048,256]{1,0:T(8,128)(2,1)}, bf16[2048,256]{1,0:T(8,128)(2,1)S(1)}, u32[]{:S(2)}) copy-start(bf16[2048,256]{1,0:T(8,128)(2,1)S(1)} %get-tuple-element.56.refs_1_) | copy-start | bytes 3145732
  103.2 53.0 %copy-start.7 = (bf16[2048,256]{1,0:T(8,128)(2,1)}, bf16[2048,256]{1,0:T(8,128)(2,1)S(1)}, u32[]{:S(2)}) copy-start(bf16[2048,256]{1,0:T(8,128)(2,1)S(1)} %get-tuple-element.60.refs_2_) | copy-start | bytes 3145732
  103.2 95.1 %copy-start.9 = (bf16[2048,256]{1,0:T(8,128)(2,1)}, bf16[2048,256]{1,0:T(8,128)(2,1)S(1)}, u32[]{:S(2)}) copy-start(bf16[2048,256]{1,0:T(8,128)(2,1)S(1)} %get-tuple-element.57.refs_3_) | copy-start | bytes 3145732
  103.2 7.2 %collective-permute-start.2 = (bf16[2048,256]{1,0:T(8,128)(2,1)S(1)}, bf16[2048,256]{1,0:T(8,128)(2,1)S(1)}, u32[]{:S(2)}, u32[]{:S(2)}) collective-permute-start(bf16[2048,256]{1,0:T(8,128)(2,1)S(1)} %get-tuple-element.59.refs_0_), channel_id=1, source_target_pairs={{8,16},{16,8},{9,17},{17,9},{10,18},{18,10},{11,19},{19,11},{12,20... | collective-permute-start | bytes 3145736 | tf_op jit(solution)/shard_map/ppermute | solution.py:641
  103.9 26.9 %collective-permute-start.13 = (bf16[2048,256]{1,0:T(8,128)(2,1)S(1)}, bf16[2048,256]{1,0:T(8,128)(2,1)S(1)}, u32[]{:S(2)}, u32[]{:S(2)}) collective-permute-start(bf16[2048,256]{1,0:T(8,128)(2,1)S(1)} %get-tuple-element.56.refs_1_), channel_id=1, source_target_pairs={{0,8},{8,0},{16,24},{24,16},{1,9},{9,1},{17,25},{25,17},{2,10},{10... | collective-permute-start | bytes 3145736 | tf_op jit(solution)/shard_map/ppermute | solution.py:640
  106.8 29.3 %collective-permute-start = (bf16[2048,256]{1,0:T(8,128)(2,1)S(1)}, bf16[2048,256]{1,0:T(8,128)(2,1)S(1)}, u32[]{:S(2)}, u32[]{:S(2)}) collective-permute-start(bf16[2048,256]{1,0:T(8,128)(2,1)S(1)} %get-tuple-element.56.refs_1_), channel_id=1, source_target_pairs={{8,16},{16,8},{9,17},{17,9},{10,18},{18,10},{11,19},{19,11},{12,20... | collective-permute-start | bytes 3145736 | tf_op jit(solution)/shard_map/ppermute | solution.py:641
  107.5 45.9 %collective-permute-start.17 = (bf16[2048,256]{1,0:T(8,128)(2,1)S(1)}, bf16[2048,256]{1,0:T(8,128)(2,1)}, u32[]{:S(2)}, u32[]{:S(2)}) collective-permute-start(bf16[2048,256]{1,0:T(8,128)(2,1)S(1)} %get-tuple-element.59.refs_0_), channel_id=1, source_target_pairs={{0,8},{8,0},{16,24},{24,16},{1,9},{9,1},{17,25},{25,17},{2,10},{10... | collective-permute-start | bytes 3145736 | tf_op jit(solution)/shard_map/ppermute | solution.py:640
  110.4 167.8 %copy-start.18 = (bf16[2048,256]{1,0:T(8,128)(2,1)}, bf16[2048,256]{1,0:T(8,128)(2,1)S(1)}, u32[]{:S(2)}) copy-start(bf16[2048,256]{1,0:T(8,128)(2,1)S(1)} %collective-permute-done.2.refs_8_) | copy-start | bytes 3145732
  110.4 65.3 %collective-permute-start.14 = (bf16[2048,256]{1,0:T(8,128)(2,1)S(1)}, bf16[2048,256]{1,0:T(8,128)(2,1)S(1)}, u32[]{:S(2)}, u32[]{:S(2)}) collective-permute-start(bf16[2048,256]{1,0:T(8,128)(2,1)S(1)} %collective-permute-done.2.refs_8_), channel_id=1, source_target_pairs={{8,0},{16,24},{9,1},{17,25},{10,2},{18,26},{11,3},{19,27},{12,4},{... | collective-permute-start | bytes 3145736 | tf_op jit(solution)/shard_map/ppermute | solution.py:642
  111.7 65.7 %collective-permute-start.3 = (bf16[2048,256]{1,0:T(8,128)(2,1)S(1)}, bf16[2048,256]{1,0:T(8,128)(2,1)S(1)}, u32[]{:S(2)}, u32[]{:S(2)}) collective-permute-start(bf16[2048,256]{1,0:T(8,128)(2,1)S(1)} %get-tuple-element.60.refs_2_), channel_id=1, source_target_pairs={{8,16},{16,8},{9,17},{17,9},{10,18},{18,10},{11,19},{19,11},{12,20... | collective-permute-start | bytes 3145736 | tf_op jit(solution)/shard_map/ppermute | solution.py:641
  130.8 147.4 %copy-start.19 = (bf16[2048,256]{1,0:T(8,128)(2,1)}, bf16[2048,256]{1,0:T(8,128)(2,1)S(1)}, u32[]{:S(2)}) copy-start(bf16[2048,256]{1,0:T(8,128)(2,1)S(1)} %collective-permute-done.13.refs_5_) | copy-start | bytes 3145732
  130.8 67.5 %collective-permute-start.9 = (bf16[2048,256]{1,0:T(8,128)(2,1)S(1)}, bf16[2048,256]{1,0:T(8,128)(2,1)}, u32[]{:S(2)}, u32[]{:S(2)}) collective-permute-start(bf16[2048,256]{1,0:T(8,128)(2,1)S(1)} %get-tuple-element.60.refs_2_), channel_id=1, source_target_pairs={{0,8},{8,0},{16,24},{24,16},{1,9},{9,1},{17,25},{25,17},{2,10},{10... | collective-permute-start | bytes 3145736 | tf_op jit(solution)/shard_map/ppermute | solution.py:640
  136.1 108.8 %copy-start.20 = (bf16[2048,256]{1,0:T(8,128)(2,1)}, bf16[2048,256]{1,0:T(8,128)(2,1)S(1)}, u32[]{:S(2)}) copy-start(bf16[2048,256]{1,0:T(8,128)(2,1)S(1)} %collective-permute-done.refs_9_) | copy-start | bytes 3145732
  136.1 84.6 %collective-permute-start.10 = (bf16[2048,256]{1,0:T(8,128)(2,1)S(1)}, bf16[2048,256]{1,0:T(8,128)(2,1)S(1)}, u32[]{:S(2)}, u32[]{:S(2)}) collective-permute-start(bf16[2048,256]{1,0:T(8,128)(2,1)S(1)} %collective-permute-done.refs_9_), channel_id=1, source_target_pairs={{8,0},{16,24},{9,1},{17,25},{10,2},{18,26},{11,3},{19,27},{12,4},{... | collective-permute-start | bytes 3145736 | tf_op jit(solution)/shard_map/ppermute | solution.py:642
  153.4 89.9 %collective-permute-start.1 = (bf16[2048,256]{1,0:T(8,128)(2,1)S(1)}, bf16[2048,256]{1,0:T(8,128)(2,1)}, u32[]{:S(2)}, u32[]{:S(2)}) collective-permute-start(bf16[2048,256]{1,0:T(8,128)(2,1)S(1)} %get-tuple-element.57.refs_3_), channel_id=1, source_target_pairs={{0,8},{8,0},{16,24},{24,16},{1,9},{9,1},{17,25},{25,17},{2,10},{10... | collective-permute-start | bytes 3145736 | tf_op jit(solution)/shard_map/ppermute | solution.py:640
  175.7 70.4 %copy-start.21 = (bf16[2048,256]{1,0:T(8,128)(2,1)}, bf16[2048,256]{1,0:T(8,128)(2,1)S(1)}, u32[]{:S(2)}) copy-start(bf16[2048,256]{1,0:T(8,128)(2,1)S(1)} %collective-permute-done.14.refs_12_) | copy-start | bytes 3145732
  175.7 69.2 %collective-permute-start.6 = (bf16[2048,256]{1,0:T(8,128)(2,1)S(1)}, bf16[2048,256]{1,0:T(8,128)(2,1)}, u32[]{:S(2)}, u32[]{:S(2)}) collective-permute-start(bf16[2048,256]{1,0:T(8,128)(2,1)S(1)} %get-tuple-element.57.refs_3_), channel_id=1, source_target_pairs={{8,16},{16,8},{9,17},{17,9},{10,18},{18,10},{11,19},{19,11},{12,20... | collective-permute-start | bytes 3145736 | tf_op jit(solution)/shard_map/ppermute | solution.py:641
  177.4 88.2 %copy-start.22 = (bf16[2048,256]{1,0:T(8,128)(2,1)}, bf16[2048,256]{1,0:T(8,128)(2,1)S(1)}, u32[]{:S(2)}) copy-start(bf16[2048,256]{1,0:T(8,128)(2,1)S(1)} %collective-permute-done.3.refs_10_) | copy-start | bytes 3145732
  177.4 88.2 %collective-permute-start.4 = (bf16[2048,256]{1,0:T(8,128)(2,1)S(1)}, bf16[2048,256]{1,0:T(8,128)(2,1)S(1)}, u32[]{:S(2)}, u32[]{:S(2)}) collective-permute-start(bf16[2048,256]{1,0:T(8,128)(2,1)S(1)} %collective-permute-done.3.refs_10_), channel_id=1, source_target_pairs={{8,0},{16,24},{9,1},{17,25},{10,2},{18,26},{11,3},{19,27},{12,4},{... | collective-permute-start | bytes 3145736 | tf_op jit(solution)/shard_map/ppermute | solution.py:642
  198.3 79.9 %collective-permute-start.18 = (bf16[2048,256]{1,0:T(8,128)(2,1)}, bf16[2048,256]{1,0:T(8,128)(2,1)}, u32[]{:S(2)}, u32[]{:S(2)}) collective-permute-start(bf16[2048,256]{1,0:T(8,128)(2,1)} %collective-permute-done.17.refs_4_), channel_id=1, source_target_pairs={{8,16},{16,8},{9,17},{17,9},{10,18},{18,10},{11,19},{19,11},{12,20... | collective-permute-start | bytes 3145736 | tf_op jit(solution)/shard_map/ppermute | solution.py:648
  220.7 58.9 %collective-permute-start.15 = (bf16[2048,256]{1,0:T(8,128)(2,1)S(1)}, bf16[2048,256]{1,0:T(8,128)(2,1)}, u32[]{:S(2)}, u32[]{:S(2)}) collective-permute-start(bf16[2048,256]{1,0:T(8,128)(2,1)S(1)} %collective-permute-done.13.refs_5_), channel_id=1, source_target_pairs={{8,16},{16,8},{9,17},{17,9},{10,18},{18,10},{11,19},{19,11},{12,20... | collective-permute-start | bytes 3145736 | tf_op jit(solution)/shard_map/ppermute | solution.py:648
  243.2 37.6 %collective-permute-start.11 = (bf16[2048,256]{1,0:T(8,128)(2,1)}, bf16[2048,256]{1,0:T(8,128)(2,1)}, u32[]{:S(2)}, u32[]{:S(2)}) collective-permute-start(bf16[2048,256]{1,0:T(8,128)(2,1)} %collective-permute-done.9.refs_6_), channel_id=1, source_target_pairs={{8,16},{16,8},{9,17},{17,9},{10,18},{18,10},{11,19},{19,11},{12,20... | collective-permute-start | bytes 3145736 | tf_op jit(solution)/shard_map/ppermute | solution.py:648
  244.9 43.3 %collective-permute-start.7 = (bf16[2048,256]{1,0:T(8,128)(2,1)}, bf16[2048,256]{1,0:T(8,128)(2,1)}, u32[]{:S(2)}, u32[]{:S(2)}) collective-permute-start(bf16[2048,256]{1,0:T(8,128)(2,1)} %collective-permute-done.6.refs_11_), channel_id=1, source_target_pairs={{8,0},{16,24},{9,1},{17,25},{10,2},{18,26},{11,3},{19,27},{12,4},{... | collective-permute-start | bytes 3145736 | tf_op jit(solution)/shard_map/ppermute | solution.py:642
  266.6 21.6 %collective-permute-start.5 = (bf16[2048,256]{1,0:T(8,128)(2,1)}, bf16[2048,256]{1,0:T(8,128)(2,1)}, u32[]{:S(2)}, u32[]{:S(2)}) collective-permute-start(bf16[2048,256]{1,0:T(8,128)(2,1)} %collective-permute-done.1.refs_7_), channel_id=1, source_target_pairs={{8,16},{16,8},{9,17},{17,9},{10,18},{18,10},{11,19},{19,11},{12,20... | collective-permute-start | bytes 3145736 | tf_op jit(solution)/shard_map/ppermute | solution.py:648
  278.3 48.7 %collective-permute-start.19 = (bf16[2048,256]{1,0:T(8,128)(2,1)}, bf16[2048,256]{1,0:T(8,128)(2,1)S(1)}, u32[]{:S(2)}, u32[]{:S(2)}) collective-permute-start(bf16[2048,256]{1,0:T(8,128)(2,1)} %collective-permute-done.18.refs_0_), channel_id=1, source_target_pairs={{8,0},{16,24},{9,1},{17,25},{10,2},{18,26},{11,3},{19,27},{12,4},{... | collective-permute-start | bytes 3145736 | tf_op jit(solution)/shard_map/ppermute | solution.py:654
  279.6 57.2 %collective-permute-start.16 = (bf16[2048,256]{1,0:T(8,128)(2,1)}, bf16[2048,256]{1,0:T(8,128)(2,1)S(1)}, u32[]{:S(2)}, u32[]{:S(2)}) collective-permute-start(bf16[2048,256]{1,0:T(8,128)(2,1)} %collective-permute-done.15.refs_0_), channel_id=1, source_target_pairs={{8,0},{16,24},{9,1},{17,25},{10,2},{18,26},{11,3},{19,27},{12,4},{... | collective-permute-start | bytes 3145736 | tf_op jit(solution)/shard_map/ppermute | solution.py:654
  280.9 74.6 %collective-permute-start.12 = (bf16[2048,256]{1,0:T(8,128)(2,1)}, bf16[2048,256]{1,0:T(8,128)(2,1)S(1)}, u32[]{:S(2)}, u32[]{:S(2)}) collective-permute-start(bf16[2048,256]{1,0:T(8,128)(2,1)} %collective-permute-done.11.refs_0_), channel_id=1, source_target_pairs={{8,0},{16,24},{9,1},{17,25},{10,2},{18,26},{11,3},{19,27},{12,4},{... | collective-permute-start | bytes 3145736 | tf_op jit(solution)/shard_map/ppermute | solution.py:654
  288.2 89.8 %collective-permute-start.8 = (bf16[2048,256]{1,0:T(8,128)(2,1)}, bf16[2048,256]{1,0:T(8,128)(2,1)}, u32[]{:S(2)}, u32[]{:S(2)}) collective-permute-start(bf16[2048,256]{1,0:T(8,128)(2,1)} %collective-permute-done.5.refs_0_), channel_id=1, source_target_pairs={{8,0},{16,24},{9,1},{17,25},{10,2},{18,26},{11,3},{19,27},{12,4},{... | collective-permute-start | bytes 3145736 | tf_op jit(solution)/shard_map/ppermute | solution.py:654
  (23 other events, 154.9 us)
Sparse Core Ops, SparseCore 0:
  49.8 171.0 all-gather.2

commit v8 on v7

--- a/solution.py
+++ b/solution.py
@@ -46,12 +46,12 @@
         grid_spec=pltpu.PrefetchScalarGridSpec(
             num_scalar_prefetch=2,
             grid=(1,),
-            in_specs=[pl.BlockSpec(memory_space=pl.ANY)],
+            in_specs=[pl.BlockSpec(memory_space=pltpu.HBM)],
             out_specs=pl.BlockSpec((n, BLK, BLK), lambda i, *_: (0, 0, 0)),
             scratch_shapes=[pltpu.SemaphoreType.DMA((n,))],
         ),
         out_shape=jax.ShapeDtypeStruct((n, BLK, BLK), F32),
-        compiler_params=pltpu.CompilerParams(vmem_limit_bytes=56 * MIB),
+        compiler_params=pltpu.CompilerParams(vmem_limit_bytes=60 * MIB),
         cost_estimate=pl.CostEstimate(
             flops=0, bytes_accessed=2 * n * BLK * BLK * 4, transcendentals=0
         ),
@@ -96,8 +96,8 @@
     return pl.pallas_call(
         kernel,
         grid=(1,),
-        in_specs=[pl.BlockSpec(memory_space=pl.ANY)],
-        out_specs=[pl.BlockSpec(memory_space=pl.ANY)] * parts,
+        in_specs=[pl.BlockSpec(memory_space=pltpu.HBM)],
+        out_specs=[pl.BlockSpec(memory_space=pltpu.HBM)] * parts,
         scratch_shapes=[
             pltpu.VMEM((steps, bm, cols), F32),
             pltpu.VMEM((steps, bm, cols), BF16),
@@ -105,7 +105,7 @@
             pltpu.SemaphoreType.DMA((steps, parts)),
         ],
         out_shape=[jax.ShapeDtypeStruct((rows, wide), BF16)] * parts,
-        compiler_params=pltpu.CompilerParams(vmem_limit_bytes=56 * MIB),
+        compiler_params=pltpu.CompilerParams(vmem_limit_bytes=60 * MIB),
         cost_estimate=pl.CostEstimate(
             flops=rows * cols, bytes_accessed=rows * cols * 6, transcendentals=0
         ),
@@ -177,8 +177,8 @@
         grid_spec=pltpu.PrefetchScalarGridSpec(
             num_scalar_prefetch=3,
             grid=(1,),
-            in_specs=[whole, whole] + [pl.BlockSpec(memory_space=pl.ANY)] * parts,
-            out_specs=[pl.BlockSpec(memory_space=pl.ANY)] * parts,
+            in_specs=[whole, whole] + [pl.BlockSpec(memory_space=pltpu.HBM)] * parts,
+            out_specs=[pl.BlockSpec(memory_space=pltpu.HBM)] * parts,
             scratch_shapes=[
                 pltpu.VMEM((n, BLK, BLK), F32),
                 pltpu.VMEM((n, BLK, BLK), BF16),
@@ -187,7 +187,7 @@
         ),
         out_shape=[jax.ShapeDtypeStruct(x.shape, x.dtype) for x in low],
         input_output_aliases={5 + p: p for p in range(parts)},
-        compiler_params=pltpu.CompilerParams(vmem_limit_bytes=40 * MIB),
+        compiler_params=pltpu.CompilerParams(vmem_limit_bytes=60 * MIB),
         cost_estimate=pl.CostEstimate(
             flops=n * BLK * BLK, bytes_accessed=n * BLK * BLK * 8, transcendentals=0
         ),
@@ -225,7 +225,7 @@
         ),
         out_shape=[jax.ShapeDtypeStruct((tdev, npts, local), BF16)] * 2
         + [jax.ShapeDtypeStruct((tdev, local, npts), BF16)] * 2,
-        compiler_params=pltpu.CompilerParams(vmem_limit_bytes=40 * MIB),
+        compiler_params=pltpu.CompilerParams(vmem_limit_bytes=60 * MIB),
         cost_estimate=pl.CostEstimate(
             flops=4 * phi.size, bytes_accessed=12 * phi.size, transcendentals=0
         ),
@@ -304,7 +304,7 @@
             ],
         ),
         out_shape=jax.ShapeDtypeStruct((n, BLK, BLK), BF16),
-        compiler_params=pltpu.CompilerParams(vmem_limit_bytes=44 * MIB),
+        compiler_params=pltpu.CompilerParams(vmem_limit_bytes=60 * MIB),
         cost_estimate=pl.CostEstimate(
             flops=flops, bytes_accessed=tdev * npts * local * 8, transcendentals=0
         ),
@@ -402,7 +402,7 @@
             scratch_shapes=scratch,
         ),
         out_shape=[jax.ShapeDtypeStruct((rows, wide), dtype)] * parts,
-        compiler_params=pltpu.CompilerParams(vmem_limit_bytes=56 * MIB),
+        compiler_params=pltpu.CompilerParams(vmem_limit_bytes=60 * MIB),
         cost_estimate=pl.CostEstimate(
             flops=rows * cols, bytes_accessed=rows * cols * 6, transcendentals=0
         ),
@@ -472,7 +472,7 @@
             + [pltpu.SemaphoreType.DMA((npiece,))],
         ),
         out_shape=jax.ShapeDtypeStruct((rows, cols), F32),
-        compiler_params=pltpu.CompilerParams(vmem_limit_bytes=56 * MIB),
+        compiler_params=pltpu.CompilerParams(vmem_limit_bytes=60 * MIB),
         cost_estimate=pl.CostEstimate(
             flops=2 * npiece * rows * depth * cols,
             bytes_accessed=npiece * (rows + cols) * depth * 2 + rows * cols * 4,
@@ -557,7 +557,7 @@
         ),
         out_shape=jax.ShapeDtypeStruct(total.shape, F32),
         input_output_aliases={2 + nh: 0},
-        compiler_params=pltpu.CompilerParams(vmem_limit_bytes=56 * MIB),
+        compiler_params=pltpu.CompilerParams(vmem_limit_bytes=60 * MIB),
         cost_estimate=pl.CostEstimate(
             flops=2 * rows * depth * wide,
             bytes_accessed=(rows + wide) * depth * 2 + rows * wide * 8,

time: 395 us -> 396 us (level)
  local copies, waits for them, and re-layouts: 19.5 us -> 8.8 us
  Pallas kernels: 120 us -> 130 us
    unnamed x65 -> x35, local copies, waits for them, and re-layouts: 18 us -> 5.12 us
    pallas_call x1, Pallas kernels: 11.8 us -> 16 us  [tile_ham(): pl.pallas_call(tile_kernel, grid_spec=pltpu.PrefetchScalarGridSpec(num_sc...]
  transfers between devices with their start and end apart: 23 -> 23, of which waited for: 12 -> 12; matrix products, arithmetic and copies ran while one was open for 1% -> 2% of each run, Pallas kernels for 27% -> 29%
where the time goes in v8:
time: 396 us; the launch traced here: 395 us
  waiting for transfers between devices  190 us (48%)
  Pallas kernels  130 us (33%)
  starting transfers between devices  44.6 us (11%)
  between operations  14.5 us (4%)
  local copies, waits for them, and re-layouts  8.8 us (2%)
  other arithmetic  7.37 us (2%)
    ppermute x4, waiting for transfers between devices, body(): pair.append(lax.ppermute(ready, 'row', swap))  75 us
    ppermute x4, waiting for transfers between devices, body(): near_end = [lax.ppermute(x, 'row', outward) for x in near_mid]  65.3 us
    pallas_call x1, Pallas kernels, product(): pl.pallas_call(kernel, grid_spec=pltpu.PrefetchScalarGridSpec(num_scalar_...  37.2 us
    pallas_call x4, Pallas kernels, product_add(): pl.pallas_call(kernel, grid_spec=pltpu.PrefetchScalarGridSpec(num_scalar_...  35.5 us
    ppermute x4, waiting for transfers between devices, body(): far_end.append(lax.ppermute(ready, 'row', outward))  21.4 us
    pallas_call x1, Pallas kernels, tile_ham(): pl.pallas_call(tile_kernel, grid_spec=pltpu.PrefetchScalarGridSpec(num_sc...  16 us
    all_to_all x1, waiting for transfers between devices, body(): lax.all_to_all(returning, ('row', 'col'), split_axis=0, concat_axis=0, ti...  14.7 us
    ppermute x4, starting transfers between devices, body(): pair.append(lax.ppermute(ready, 'row', swap))  13.7 us
  transfers between devices with their start and end apart: 23, of which 12 were waited for; matrix products, arithmetic and copies ran while one was open for 2% of the time, Pallas kernels for 29%

profile of v8, /device:TPU:0, one launch (start us, length us, event | category | flops | bytes accessed | tf_op | source)
XLA Modules:
  0.0 394.6 jit_solution(8971728984959628096)
XLA Ops:
  9.0 4.5 %gather_blocks.2 = f32[32,128,128]{2,1,0:T(8,128)} custom-call(s32[32]{0:T(128)} %get-tuple-element.71.row_ref, s32[32]{0:T(128)} %get-tuple-element.70.col_ref, f32[2048,1024]{1,0:T(8,128)} %x_ref.2), custom_call_target="tpu_custom_call" | custom-call | bytes 4194304 | tf_op jit(solution)/shard_map/gather_blocks/pallas_call | solution.py:44
  13.5 2.9 multiply_convert_fusion
  16.3 7.2 %all-to-all-start = ((f16[32,128,128]{2,1,0:T(8,128)(2,1)}), f16[32,128,128]{2,1,0:T(8,128)(2,1)S(1)}, u32[]{:S(2)}, u32[]{:S(2)}) async-start(f16[32,128,128]{2,1,0:T(8,128)(2,1)} %multiply_convert_fusion), calls=%async_computation | async-start | bytes 2097152 | tf_op jit(solution)/shard_map/all_to_all | solution.py:615
  23.7 6.2 %round_parts.2 = bf16[2048,1024]{1,0:T(8,128)(2,1)} custom-call(f32[2048,1024]{1,0:T(8,128)} %x_ref.2), custom_call_target="tpu_custom_call" | custom-call | flops 2097152 | bytes 12582912 | tf_op jit(solution)/shard_map/round_parts/pallas_call | solution.py:96
  30.4 6.1 %split_basis.1 = (bf16[2,1024,512]{2,1,0:T(8,128)(2,1)}, bf16[2,1024,512]{2,1,0:T(8,128)(2,1)}, bf16[2,512,1024]{2,1,0:T(8,128)(2,1)}, bf16[2,512,1024]{2,1,0:T(8,128)(2,1)}) custom-call(s32[2]{0:T(128)} %dynamic-slice_bitcast_fusion.count_ref, f32[2,1024,512]{2,1,0:T(8,128)} %phi_ref.1), custom_call_target="tpu_custom_call" | custom-call | flops 4194304 | bytes 12582912 | tf_op jit(solution)/shard_map/split_basis/pallas_call | solution.py:218
  36.5 13.3 %all-to-all-done = f16[32,128,128]{2,1,0:T(8,128)(2,1)S(1)} async-done(((f16[32,128,128]{2,1,0:T(8,128)(2,1)}), f16[32,128,128]{2,1,0:T(8,128)(2,1)S(1)}, u32[]{:S(2)}, u32[]{:S(2)}) %all-to-all-start) | async-done | bytes 1048608 | tf_op jit(solution)/shard_map/all_to_all | solution.py:615
  53.5 16.0 %tile_ham.1 = bf16[32,128,128]{2,1,0:T(8,128)(2,1)} custom-call(s32[2,16]{1,0:T(2,128)} %add.54.hold_ref, s32[2]{0:T(128)} %dynamic-slice_bitcast_fusion.count_ref, f32[32,128,128]{2,1,0:T(8,128)} %convert_element_type.12.in_ref, bf16[2,1024,512]{2,1,0:T(8,128)(2,1)} %get-tuple-element.41.hi_ref, bf16[2,1024,512]{2,1,0:T(8,128)(2,1)} %get-tuple-element.42.lo_ref, ...), custom_call_target="tpu_custom_call" | custom-call | flops 6442450944 | bytes 8388608 | tf_op jit(solution)/shard_map/tile_ham/pallas_call | solution.py:287
  69.6 2.6 all-to-all-start.1
  72.3 4.2 %gather_blocks.3.h_ref = f32[32,128,128]{2,1,0:T(8,128)} custom-call(s32[32]{0:T(128)} %get-tuple-element.71.row_ref, s32[32]{0:T(128)} %get-tuple-element.70.col_ref, f32[2048,1024]{1,0:T(8,128)} %h_ref.1), custom_call_target="tpu_custom_call" | custom-call | bytes 4194304 | tf_op jit(solution)/shard_map/gather_blocks/pallas_call | solution.py:44
  76.6 6.4 %round_parts.3 = (bf16[2048,256]{1,0:T(8,128)(2,1)}, bf16[2048,256]{1,0:T(8,128)(2,1)}, bf16[2048,256]{1,0:T(8,128)(2,1)}, bf16[2048,256]{1,0:T(8,128)(2,1)}) custom-call(f32[2048,1024]{1,0:T(8,128)} %h_ref.1), custom_call_target="tpu_custom_call" | custom-call | flops 2097152 | bytes 12582912 | tf_op jit(solution)/shard_map/round_parts/pallas_call | solution.py:96
  83.7 14.7 %all-to-all-done.1.in_ref = bf16[32,128,128]{2,1,0:T(8,128)(2,1)S(1)} async-done(((bf16[32,128,128]{2,1,0:T(8,128)(2,1)}), bf16[32,128,128]{2,1,0:T(8,128)(2,1)S(1)}, u32[]{:S(2)}, u32[]{:S(2)}) %all-to-all-start.1) | async-done | bytes 1048608 | tf_op jit(solution)/shard_map/all_to_all | solution.py:622
  99.4 4.7 %update_blocks.1 = (bf16[2048,256]{1,0:T(8,128)(2,1)}, bf16[2048,256]{1,0:T(8,128)(2,1)}, bf16[2048,256]{1,0:T(8,128)(2,1)}, bf16[2048,256]{1,0:T(8,128)(2,1)}) custom-call(s32[32]{0:T(128)} %get-tuple-element.71.row_ref, s32[32]{0:T(128)} %get-tuple-element.70.col_ref, ...), custom_call_target="tpu_custom_call", output_to_operand_aliasing={{0}: (5, {}), {1}: (6, {}), {2}: (7, {}), {3}: (8, {})} | custom-call | flops 524288 | bytes 4194304 | tf_op jit(solution)/shard_map/update_blocks/pallas_call | solution.py:175
  104.9 2.6 collective-permute-start.13
  108.2 3.0 collective-permute-start.17
  113.2 18.5 %collective-permute-done.13.refs_5_ = bf16[2048,256]{1,0:T(8,128)(2,1)S(1)} collective-permute-done((bf16[2048,256]{1,0:T(8,128)(2,1)}, bf16[2048,256]{1,0:T(8,128)(2,1)S(1)}, u32[]{:S(2)}, u32[]{:S(2)}) %collective-permute-start.13) | collective-permute-done | bytes 1048608 | tf_op jit(solution)/shard_map/ppermute | solution.py:640
  131.7 5.3 %collective-permute-start.9 = (bf16[2048,256]{1,0:T(8,128)(2,1)}, bf16[2048,256]{1,0:T(8,128)(2,1)}, u32[]{:S(2)}, u32[]{:S(2)}) collective-permute-start(bf16[2048,256]{1,0:T(8,128)(2,1)} %get-tuple-element.60.refs_2_), channel_id=1, source_target_pairs={{0,8},{8,0},{16,24},{24,16},{1,9},{9,1},{17,25},{25,17},{2,10},{10... | collective-permute-start | bytes 3145736 | tf_op jit(solution)/shard_map/ppermute | solution.py:640
  138.3 16.0 %collective-permute-done.17.refs_4_ = bf16[2048,256]{1,0:T(8,128)(2,1)} collective-permute-done((bf16[2048,256]{1,0:T(8,128)(2,1)}, bf16[2048,256]{1,0:T(8,128)(2,1)}, u32[]{:S(2)}, u32[]{:S(2)}) %collective-permute-start.17) | collective-permute-done | bytes 1048608 | tf_op jit(solution)/shard_map/ppermute | solution.py:640
  154.3 2.9 collective-permute-start.1
  157.2 19.5 %collective-permute-done.14.refs_12_ = bf16[2048,256]{1,0:T(8,128)(2,1)S(1)} collective-permute-done((bf16[2048,256]{1,0:T(8,128)(2,1)S(1)}, bf16[2048,256]{1,0:T(8,128)(2,1)S(1)}, u32[]{:S(2)}, u32[]{:S(2)}) %collective-permute-start.14) | collective-permute-done | bytes 1048608 | tf_op jit(solution)/shard_map/ppermute | solution.py:642
  179.6 19.6 %collective-permute-done.9.refs_6_ = bf16[2048,256]{1,0:T(8,128)(2,1)} collective-permute-done((bf16[2048,256]{1,0:T(8,128)(2,1)}, bf16[2048,256]{1,0:T(8,128)(2,1)}, u32[]{:S(2)}, u32[]{:S(2)}) %collective-permute-start.9) | collective-permute-done | bytes 1048608 | tf_op jit(solution)/shard_map/ppermute | solution.py:640
  200.9 20.7 %collective-permute-done.10.refs_13_ = bf16[2048,256]{1,0:T(8,128)(2,1)S(1)} collective-permute-done((bf16[2048,256]{1,0:T(8,128)(2,1)S(1)}, bf16[2048,256]{1,0:T(8,128)(2,1)S(1)}, u32[]{:S(2)}, u32[]{:S(2)}) %collective-permute-start.10) | collective-permute-done | bytes 1048608 | tf_op jit(solution)/shard_map/ppermute | solution.py:642
  223.3 20.9 %collective-permute-done.1.refs_7_ = bf16[2048,256]{1,0:T(8,128)(2,1)} collective-permute-done((bf16[2048,256]{1,0:T(8,128)(2,1)}, bf16[2048,256]{1,0:T(8,128)(2,1)}, u32[]{:S(2)}, u32[]{:S(2)}) %collective-permute-start.1) | collective-permute-done | bytes 1048608 | tf_op jit(solution)/shard_map/ppermute | solution.py:640
  247.1 19.4 %collective-permute-done.4.refs_14_ = bf16[2048,256]{1,0:T(8,128)(2,1)S(1)} collective-permute-done((bf16[2048,256]{1,0:T(8,128)(2,1)S(1)}, bf16[2048,256]{1,0:T(8,128)(2,1)S(1)}, u32[]{:S(2)}, u32[]{:S(2)}) %collective-permute-start.4) | collective-permute-done | bytes 1048608 | tf_op jit(solution)/shard_map/ppermute | solution.py:642
  270.5 8.9 %assemble.1 = f32[2048,1024]{1,0:T(8,128)} custom-call(s32[32]{0:T(128)} %get-tuple-element.71.row_ref, s32[32]{0:T(128)} %get-tuple-element.70.col_ref, s32[32]{0:T(128)} %copy-done.15, bf16[32,128,128]{2,1,0:T(8,128)(2,1)} %copy-done, f32[2048,1024]{1,0:T(8,128)} %h_ref.1), custom_call_target="tpu_custom_call" | custom-call | flops 2097152 | bytes 12582912 | tf_op jit(solution)/shard_map/assemble/pallas_call | solution.py:392
  283.4 5.7 %collective-permute-done.7.refs_15_ = bf16[2048,256]{1,0:T(8,128)(2,1)} collective-permute-done((bf16[2048,256]{1,0:T(8,128)(2,1)}, bf16[2048,256]{1,0:T(8,128)(2,1)}, u32[]{:S(2)}, u32[]{:S(2)}) %collective-permute-start.7) | collective-permute-done | bytes 1048608 | tf_op jit(solution)/shard_map/ppermute | solution.py:642
  290.6 37.2 %product.1.refs_3_ = f32[2048,1024]{1,0:T(8,128)} custom-call(s32[6]{0:T(128)} %stack.41.sc_ref, bf16[2048,256]{1,0:T(8,128)(2,1)} %get-tuple-element.59.refs_0_, bf16[2048,256]{1,0:T(8,128)(2,1)} %get-tuple-element.56.refs_1_, bf16[2048,256]{1,0:T(8,128)(2,1)} %get-tuple-element.60.refs_2_, bf16[2048,256]{1,0:T(8,128)(2,1)} %get-tuple-element.57.refs_3_, ...), custom_call_target="tpu_custom_call" | custom-call | flops 25769803776 | bytes 46137344 | tf_op jit(solution)/shard_map/product/pallas_call | solution.py:463
  328.9 8.9 %product_add.4.refs_3_ = f32[2048,1024]{1,0:T(8,128)} custom-call(s32[2]{0:T(128)} %pad_add_fusion.sc_ref, bf16[2048,256]{1,0:T(8,128)(2,1)} %collective-permute-done.18.refs_0_, bf16[2048,256]{1,0:T(8,128)(2,1)} %copy-done.8, bf16[8,2048,1024]{2,1,0:T(8,128)(2,1)} %bitcast.31, f32[2048,1024]{1,0:T(8,128)} %product.1.refs_3_), custom_call_target="tpu_custom_call", output_to_operand_aliasing={{}: (4, {})} | custom-call | flops 2147483648 | bytes 13631488 | tf_op jit(solution)/shard_map/product_add/pallas_call | solution.py:541
  338.8 8.9 %product_add.5.refs_3_ = f32[2048,1024]{1,0:T(8,128)} custom-call(s32[2]{0:T(128)} %pad_add_fusion.sc_ref, bf16[2048,256]{1,0:T(8,128)(2,1)} %collective-permute-done.15.refs_0_, bf16[2048,256]{1,0:T(8,128)(2,1)} %copy-done.9, bf16[8,2048,1024]{2,1,0:T(8,128)(2,1)} %bitcast.32, f32[2048,1024]{1,0:T(8,128)} %product_add.4.refs_3_), custom_call_target="tpu_custom_call", output_to_operand_aliasing={{}: (4, {})} | custom-call | flops 2147483648 | bytes 13631488 | tf_op jit(solution)/shard_map/product_add/pallas_call | solution.py:541
  347.7 8.8 %collective-permute-done.12.refs_1_ = bf16[2048,256]{1,0:T(8,128)(2,1)S(1)} collective-permute-done((bf16[2048,256]{1,0:T(8,128)(2,1)}, bf16[2048,256]{1,0:T(8,128)(2,1)S(1)}, u32[]{:S(2)}, u32[]{:S(2)}) %collective-permute-start.12) | collective-permute-done | bytes 1048608 | tf_op jit(solution)/shard_map/ppermute | solution.py:654
  357.4 8.9 %product_add.6.refs_3_ = f32[2048,1024]{1,0:T(8,128)} custom-call(s32[2]{0:T(128)} %pad_add_fusion.sc_ref, bf16[2048,256]{1,0:T(8,128)(2,1)} %collective-permute-done.11.refs_0_, bf16[2048,256]{1,0:T(8,128)(2,1)} %copy-done.10, bf16[8,2048,1024]{2,1,0:T(8,128)(2,1)} %bitcast.33, f32[2048,1024]{1,0:T(8,128)} %product_add.5.refs_3_), custom_call_target="tpu_custom_call", output_to_operand_aliasing={{}: (4, {})} | custom-call | flops 2147483648 | bytes 13631488 | tf_op jit(solution)/shard_map/product_add/pallas_call | solution.py:541
  366.3 12.5 %collective-permute-done.8.refs_1_ = bf16[2048,256]{1,0:T(8,128)(2,1)} collective-permute-done((bf16[2048,256]{1,0:T(8,128)(2,1)}, bf16[2048,256]{1,0:T(8,128)(2,1)}, u32[]{:S(2)}, u32[]{:S(2)}) %collective-permute-start.8) | collective-permute-done | bytes 1048608 | tf_op jit(solution)/shard_map/ppermute | solution.py:654
  378.9 8.9 %product_add.7 = f32[2048,1024]{1,0:T(8,128)} custom-call(s32[2]{0:T(128)} %pad_add_fusion.sc_ref, bf16[2048,256]{1,0:T(8,128)(2,1)} %collective-permute-done.5.refs_0_, bf16[2048,256]{1,0:T(8,128)(2,1)} %collective-permute-done.8.refs_1_, bf16[8,2048,1024]{2,1,0:T(8,128)(2,1)} %bitcast.34, ...), custom_call_target="tpu_custom_call", output_to_operand_aliasing={{}: (4, {})} | custom-call | flops 2147483648 | bytes 13631488 | tf_op jit(solution)/shard_map/product_add/pallas_call | solution.py:541
  (85 shorter events, 34.3 us)
Async XLA Ops:
  13.5 10.2 %copy-start.16 = (s32[64]{0:T(128)S(1)}, s32[64]{0:T(128)}, u32[]{:S(2)}) copy-start(s32[64]{0:T(128)} %param.11) | copy-start | bytes 772
  16.3 33.5 %all-to-all-start = ((f16[32,128,128]{2,1,0:T(8,128)(2,1)}), f16[32,128,128]{2,1,0:T(8,128)(2,1)S(1)}, u32[]{:S(2)}, u32[]{:S(2)}) async-start(f16[32,128,128]{2,1,0:T(8,128)(2,1)} %multiply_convert_fusion), calls=%async_computation | async-start | bytes 2097152 | tf_op jit(solution)/shard_map/all_to_all | solution.py:615
  23.6 267.1 %all-gather.3.cloned.1.call-start = ((), (), s32[]{:S(2)}) async-start(), calls=%async_computation.2 | async-start | bytes 37748736 | tf_op jit(solution)/shard_map/all_gather | solution.py:619
  30.4 19.4 %copy-start.14 = (s32[64,4]{0,1:T(4,128)S(1)}, s32[64,4]{0,1:T(4,128)}, u32[]{:S(2)}) copy-start(s32[64,4]{0,1:T(4,128)} %param.10) | copy-start | bytes 3076
  30.4 20.2 %copy-start.13 = (f32[2,1024]{1,0:T(2,128)S(1)}, f32[2,1024]{1,0:T(2,128)}, u32[]{:S(2)}) copy-start(f32[2,1024]{1,0:T(2,128)} %param.9) | copy-start | bytes 24580
  69.6 28.9 %all-to-all-start.1 = ((bf16[32,128,128]{2,1,0:T(8,128)(2,1)}), bf16[32,128,128]{2,1,0:T(8,128)(2,1)S(1)}, u32[]{:S(2)}, u32[]{:S(2)}) async-start(bf16[32,128,128]{2,1,0:T(8,128)(2,1)} %tile_ham.1), calls=%async_computation.1 | async-start | bytes 2097152 | tf_op jit(solution)/shard_map/all_to_all | solution.py:622
  104.2 7.0 %collective-permute-start.2 = (bf16[2048,256]{1,0:T(8,128)(2,1)}, bf16[2048,256]{1,0:T(8,128)(2,1)S(1)}, u32[]{:S(2)}, u32[]{:S(2)}) collective-permute-start(bf16[2048,256]{1,0:T(8,128)(2,1)} %get-tuple-element.59.refs_0_), channel_id=1, source_target_pairs={{8,16},{16,8},{9,17},{17,9},{10,18},{18,10},{11,19},{19,11},{12,20... | collective-permute-start | bytes 3145736 | tf_op jit(solution)/shard_map/ppermute | solution.py:641
  104.9 26.8 %collective-permute-start.13 = (bf16[2048,256]{1,0:T(8,128)(2,1)}, bf16[2048,256]{1,0:T(8,128)(2,1)S(1)}, u32[]{:S(2)}, u32[]{:S(2)}) collective-permute-start(bf16[2048,256]{1,0:T(8,128)(2,1)} %get-tuple-element.56.refs_1_), channel_id=1, source_target_pairs={{0,8},{8,0},{16,24},{24,16},{1,9},{9,1},{17,25},{25,17},{2,10},{10... | collective-permute-start | bytes 3145736 | tf_op jit(solution)/shard_map/ppermute | solution.py:640
  107.5 29.5 %collective-permute-start = (bf16[2048,256]{1,0:T(8,128)(2,1)}, bf16[2048,256]{1,0:T(8,128)(2,1)S(1)}, u32[]{:S(2)}, u32[]{:S(2)}) collective-permute-start(bf16[2048,256]{1,0:T(8,128)(2,1)} %get-tuple-element.56.refs_1_), channel_id=1, source_target_pairs={{8,16},{16,8},{9,17},{17,9},{10,18},{18,10},{11,19},{19,11},{12,20... | collective-permute-start | bytes 3145736 | tf_op jit(solution)/shard_map/ppermute | solution.py:641
  108.2 46.1 %collective-permute-start.17 = (bf16[2048,256]{1,0:T(8,128)(2,1)}, bf16[2048,256]{1,0:T(8,128)(2,1)}, u32[]{:S(2)}, u32[]{:S(2)}) collective-permute-start(bf16[2048,256]{1,0:T(8,128)(2,1)} %get-tuple-element.59.refs_0_), channel_id=1, source_target_pairs={{0,8},{8,0},{16,24},{24,16},{1,9},{9,1},{17,25},{25,17},{2,10},{10... | collective-permute-start | bytes 3145736 | tf_op jit(solution)/shard_map/ppermute | solution.py:640
  111.2 168.2 %copy-start.1 = (bf16[2048,256]{1,0:T(8,128)(2,1)}, bf16[2048,256]{1,0:T(8,128)(2,1)S(1)}, u32[]{:S(2)}) copy-start(bf16[2048,256]{1,0:T(8,128)(2,1)S(1)} %collective-permute-done.2.refs_8_) | copy-start | bytes 3145732
  111.2 65.5 %collective-permute-start.14 = (bf16[2048,256]{1,0:T(8,128)(2,1)S(1)}, bf16[2048,256]{1,0:T(8,128)(2,1)S(1)}, u32[]{:S(2)}, u32[]{:S(2)}) collective-permute-start(bf16[2048,256]{1,0:T(8,128)(2,1)S(1)} %collective-permute-done.2.refs_8_), channel_id=1, source_target_pairs={{8,0},{16,24},{9,1},{17,25},{10,2},{18,26},{11,3},{19,27},{12,4},{... | collective-permute-start | bytes 3145736 | tf_op jit(solution)/shard_map/ppermute | solution.py:642
  112.5 65.8 %collective-permute-start.3 = (bf16[2048,256]{1,0:T(8,128)(2,1)}, bf16[2048,256]{1,0:T(8,128)(2,1)S(1)}, u32[]{:S(2)}, u32[]{:S(2)}) collective-permute-start(bf16[2048,256]{1,0:T(8,128)(2,1)} %get-tuple-element.60.refs_2_), channel_id=1, source_target_pairs={{8,16},{16,8},{9,17},{17,9},{10,18},{18,10},{11,19},{19,11},{12,20... | collective-permute-start | bytes 3145736 | tf_op jit(solution)/shard_map/ppermute | solution.py:641
  131.7 147.7 %copy-start.2 = (bf16[2048,256]{1,0:T(8,128)(2,1)}, bf16[2048,256]{1,0:T(8,128)(2,1)S(1)}, u32[]{:S(2)}) copy-start(bf16[2048,256]{1,0:T(8,128)(2,1)S(1)} %collective-permute-done.13.refs_5_) | copy-start | bytes 3145732
  131.7 67.5 %collective-permute-start.9 = (bf16[2048,256]{1,0:T(8,128)(2,1)}, bf16[2048,256]{1,0:T(8,128)(2,1)}, u32[]{:S(2)}, u32[]{:S(2)}) collective-permute-start(bf16[2048,256]{1,0:T(8,128)(2,1)} %get-tuple-element.60.refs_2_), channel_id=1, source_target_pairs={{0,8},{8,0},{16,24},{24,16},{1,9},{9,1},{17,25},{25,17},{2,10},{10... | collective-permute-start | bytes 3145736 | tf_op jit(solution)/shard_map/ppermute | solution.py:640
  137.0 142.4 %copy-start.3 = (bf16[2048,256]{1,0:T(8,128)(2,1)}, bf16[2048,256]{1,0:T(8,128)(2,1)S(1)}, u32[]{:S(2)}) copy-start(bf16[2048,256]{1,0:T(8,128)(2,1)S(1)} %collective-permute-done.refs_9_) | copy-start | bytes 3145732
  137.0 84.6 %collective-permute-start.10 = (bf16[2048,256]{1,0:T(8,128)(2,1)S(1)}, bf16[2048,256]{1,0:T(8,128)(2,1)S(1)}, u32[]{:S(2)}, u32[]{:S(2)}) collective-permute-start(bf16[2048,256]{1,0:T(8,128)(2,1)S(1)} %collective-permute-done.refs_9_), channel_id=1, source_target_pairs={{8,0},{16,24},{9,1},{17,25},{10,2},{18,26},{11,3},{19,27},{12,4},{... | collective-permute-start | bytes 3145736 | tf_op jit(solution)/shard_map/ppermute | solution.py:642
  154.3 89.9 %collective-permute-start.1 = (bf16[2048,256]{1,0:T(8,128)(2,1)}, bf16[2048,256]{1,0:T(8,128)(2,1)}, u32[]{:S(2)}, u32[]{:S(2)}) collective-permute-start(bf16[2048,256]{1,0:T(8,128)(2,1)} %get-tuple-element.57.refs_3_), channel_id=1, source_target_pairs={{0,8},{8,0},{16,24},{24,16},{1,9},{9,1},{17,25},{25,17},{2,10},{10... | collective-permute-start | bytes 3145736 | tf_op jit(solution)/shard_map/ppermute | solution.py:640
  176.7 44.9 %copy-start.4 = (bf16[2048,256]{1,0:T(8,128)(2,1)}, bf16[2048,256]{1,0:T(8,128)(2,1)S(1)}, u32[]{:S(2)}) copy-start(bf16[2048,256]{1,0:T(8,128)(2,1)S(1)} %collective-permute-done.14.refs_12_) | copy-start | bytes 3145732
  176.7 69.2 %collective-permute-start.6 = (bf16[2048,256]{1,0:T(8,128)(2,1)}, bf16[2048,256]{1,0:T(8,128)(2,1)}, u32[]{:S(2)}, u32[]{:S(2)}) collective-permute-start(bf16[2048,256]{1,0:T(8,128)(2,1)} %get-tuple-element.57.refs_3_), channel_id=1, source_target_pairs={{8,16},{16,8},{9,17},{17,9},{10,18},{18,10},{11,19},{19,11},{12,20... | collective-permute-start | bytes 3145736 | tf_op jit(solution)/shard_map/ppermute | solution.py:641
  178.3 44.9 %copy-start.5 = (bf16[2048,256]{1,0:T(8,128)(2,1)}, bf16[2048,256]{1,0:T(8,128)(2,1)S(1)}, u32[]{:S(2)}) copy-start(bf16[2048,256]{1,0:T(8,128)(2,1)S(1)} %collective-permute-done.3.refs_10_) | copy-start | bytes 3145732
  178.3 88.2 %collective-permute-start.4 = (bf16[2048,256]{1,0:T(8,128)(2,1)S(1)}, bf16[2048,256]{1,0:T(8,128)(2,1)S(1)}, u32[]{:S(2)}, u32[]{:S(2)}) collective-permute-start(bf16[2048,256]{1,0:T(8,128)(2,1)S(1)} %collective-permute-done.3.refs_10_), channel_id=1, source_target_pairs={{8,0},{16,24},{9,1},{17,25},{10,2},{18,26},{11,3},{19,27},{12,4},{... | collective-permute-start | bytes 3145736 | tf_op jit(solution)/shard_map/ppermute | solution.py:642
  199.3 80.2 %collective-permute-start.18 = (bf16[2048,256]{1,0:T(8,128)(2,1)}, bf16[2048,256]{1,0:T(8,128)(2,1)}, u32[]{:S(2)}, u32[]{:S(2)}) collective-permute-start(bf16[2048,256]{1,0:T(8,128)(2,1)} %collective-permute-done.17.refs_4_), channel_id=1, source_target_pairs={{8,16},{16,8},{9,17},{17,9},{10,18},{18,10},{11,19},{19,11},{12,20... | collective-permute-start | bytes 3145736 | tf_op jit(solution)/shard_map/ppermute | solution.py:648
  221.6 44.9 %copy-start.6 = (bf16[2048,256]{1,0:T(8,128)(2,1)}, bf16[2048,256]{1,0:T(8,128)(2,1)S(1)}, u32[]{:S(2)}) copy-start(bf16[2048,256]{1,0:T(8,128)(2,1)S(1)} %collective-permute-done.10.refs_13_) | copy-start | bytes 3145732
  221.6 59.2 %collective-permute-start.15 = (bf16[2048,256]{1,0:T(8,128)(2,1)S(1)}, bf16[2048,256]{1,0:T(8,128)(2,1)}, u32[]{:S(2)}, u32[]{:S(2)}) collective-permute-start(bf16[2048,256]{1,0:T(8,128)(2,1)S(1)} %collective-permute-done.13.refs_5_), channel_id=1, source_target_pairs={{8,16},{16,8},{9,17},{17,9},{10,18},{18,10},{11,19},{19,11},{12,20... | collective-permute-start | bytes 3145736 | tf_op jit(solution)/shard_map/ppermute | solution.py:648
  244.2 37.9 %collective-permute-start.11 = (bf16[2048,256]{1,0:T(8,128)(2,1)}, bf16[2048,256]{1,0:T(8,128)(2,1)}, u32[]{:S(2)}, u32[]{:S(2)}) collective-permute-start(bf16[2048,256]{1,0:T(8,128)(2,1)} %collective-permute-done.9.refs_6_), channel_id=1, source_target_pairs={{8,16},{16,8},{9,17},{17,9},{10,18},{18,10},{11,19},{19,11},{12,20... | collective-permute-start | bytes 3145736 | tf_op jit(solution)/shard_map/ppermute | solution.py:648
  245.8 43.3 %collective-permute-start.7 = (bf16[2048,256]{1,0:T(8,128)(2,1)}, bf16[2048,256]{1,0:T(8,128)(2,1)}, u32[]{:S(2)}, u32[]{:S(2)}) collective-permute-start(bf16[2048,256]{1,0:T(8,128)(2,1)} %collective-permute-done.6.refs_11_), channel_id=1, source_target_pairs={{8,0},{16,24},{9,1},{17,25},{10,2},{18,26},{11,3},{19,27},{12,4},{... | collective-permute-start | bytes 3145736 | tf_op jit(solution)/shard_map/ppermute | solution.py:642
  267.6 21.6 %collective-permute-start.5 = (bf16[2048,256]{1,0:T(8,128)(2,1)}, bf16[2048,256]{1,0:T(8,128)(2,1)}, u32[]{:S(2)}, u32[]{:S(2)}) collective-permute-start(bf16[2048,256]{1,0:T(8,128)(2,1)} %collective-permute-done.1.refs_7_), channel_id=1, source_target_pairs={{8,16},{16,8},{9,17},{17,9},{10,18},{18,10},{11,19},{19,11},{12,20... | collective-permute-start | bytes 3145736 | tf_op jit(solution)/shard_map/ppermute | solution.py:648
  279.5 48.4 %collective-permute-start.19 = (bf16[2048,256]{1,0:T(8,128)(2,1)}, bf16[2048,256]{1,0:T(8,128)(2,1)S(1)}, u32[]{:S(2)}, u32[]{:S(2)}) collective-permute-start(bf16[2048,256]{1,0:T(8,128)(2,1)} %collective-permute-done.18.refs_0_), channel_id=1, source_target_pairs={{8,0},{16,24},{9,1},{17,25},{10,2},{18,26},{11,3},{19,27},{12,4},{... | collective-permute-start | bytes 3145736 | tf_op jit(solution)/shard_map/ppermute | solution.py:654
  280.8 56.9 %collective-permute-start.16 = (bf16[2048,256]{1,0:T(8,128)(2,1)}, bf16[2048,256]{1,0:T(8,128)(2,1)S(1)}, u32[]{:S(2)}, u32[]{:S(2)}) collective-permute-start(bf16[2048,256]{1,0:T(8,128)(2,1)} %collective-permute-done.15.refs_0_), channel_id=1, source_target_pairs={{8,0},{16,24},{9,1},{17,25},{10,2},{18,26},{11,3},{19,27},{12,4},{... | collective-permute-start | bytes 3145736 | tf_op jit(solution)/shard_map/ppermute | solution.py:654
  282.1 74.3 %collective-permute-start.12 = (bf16[2048,256]{1,0:T(8,128)(2,1)}, bf16[2048,256]{1,0:T(8,128)(2,1)S(1)}, u32[]{:S(2)}, u32[]{:S(2)}) collective-permute-start(bf16[2048,256]{1,0:T(8,128)(2,1)} %collective-permute-done.11.refs_0_), channel_id=1, source_target_pairs={{8,0},{16,24},{9,1},{17,25},{10,2},{18,26},{11,3},{19,27},{12,4},{... | collective-permute-start | bytes 3145736 | tf_op jit(solution)/shard_map/ppermute | solution.py:654
  289.1 89.7 %collective-permute-start.8 = (bf16[2048,256]{1,0:T(8,128)(2,1)}, bf16[2048,256]{1,0:T(8,128)(2,1)}, u32[]{:S(2)}, u32[]{:S(2)}) collective-permute-start(bf16[2048,256]{1,0:T(8,128)(2,1)} %collective-permute-done.5.refs_0_), channel_id=1, source_target_pairs={{8,0},{16,24},{9,1},{17,25},{10,2},{18,26},{11,3},{19,27},{12,4},{... | collective-permute-start | bytes 3145736 | tf_op jit(solution)/shard_map/ppermute | solution.py:654
  (8 other events, 24.2 us)
Sparse Core Ops, SparseCore 0:
  49.9 171.0 all-gather.2

commit v9 on v8

--- a/solution.py
+++ b/solution.py
@@ -51,7 +51,7 @@
             scratch_shapes=[pltpu.SemaphoreType.DMA((n,))],
         ),
         out_shape=jax.ShapeDtypeStruct((n, BLK, BLK), F32),
-        compiler_params=pltpu.CompilerParams(vmem_limit_bytes=60 * MIB),
+        compiler_params=pltpu.CompilerParams(vmem_limit_bytes=57 * MIB),
         cost_estimate=pl.CostEstimate(
             flops=0, bytes_accessed=2 * n * BLK * BLK * 4, transcendentals=0
         ),
@@ -225,7 +225,7 @@
         ),
         out_shape=[jax.ShapeDtypeStruct((tdev, npts, local), BF16)] * 2
         + [jax.ShapeDtypeStruct((tdev, local, npts), BF16)] * 2,
-        compiler_params=pltpu.CompilerParams(vmem_limit_bytes=60 * MIB),
+        compiler_params=pltpu.CompilerParams(vmem_limit_bytes=24 * MIB),
         cost_estimate=pl.CostEstimate(
             flops=4 * phi.size, bytes_accessed=12 * phi.size, transcendentals=0
         ),
@@ -278,7 +278,7 @@
                 ]
 
 
-def tile_ham(incoming, basis, v_ext, hold, counts):
+def tile_ham(incoming, basis, v_column, hold, counts):
     n = incoming.shape[0]
     tdev, npts, local = basis[0].shape
     flops = tdev * 3 * 2 * 2 * npts * local * local
@@ -304,12 +304,12 @@
             ],
         ),
         out_shape=jax.ShapeDtypeStruct((n, BLK, BLK), BF16),
-        compiler_params=pltpu.CompilerParams(vmem_limit_bytes=60 * MIB),
+        compiler_params=pltpu.CompilerParams(vmem_limit_bytes=34 * MIB),
         cost_estimate=pl.CostEstimate(
             flops=flops, bytes_accessed=tdev * npts * local * 8, transcendentals=0
         ),
         name="tile_ham",
-    )(hold, counts, incoming, *basis, v_ext[:, :, None])
+    )(hold, counts, incoming, *basis, v_column)
 
 
 def assemble(h_core, arriving, picks, dtype, first, parts, wide):
@@ -615,10 +615,11 @@
     incoming = lax.all_to_all(outgoing, ("row", "col"), split_axis=0, concat_axis=0, tiled=True)
     basis = split_basis(phi, my_counts)
     (dm_low,) = round_parts(density, 1)
-    incoming, (dm_low, basis) = tie(incoming, (dm_low, basis))
+    v_column = v_ext[:, :, None]
+    incoming, (dm_low, basis, v_column) = tie(incoming, (dm_low, basis, v_column))
     dm_panel = lax.all_gather(dm_low, "col", axis=0, tiled=False)
 
-    returning = tile_ham(incoming.astype(F32), basis, v_ext, hold, my_counts)
+    returning = tile_ham(incoming.astype(F32), basis, v_column, hold, my_counts)
     arriving = lax.all_to_all(returning, ("row", "col"), split_axis=0, concat_axis=0, tiled=True)
     parts = PARTS if line and cols_loc % (PARTS * BLK) == 0 else 1
     wide = cols_loc // parts

time: 396 us -> 394 us (level)
  local copies, waits for them, and re-layouts: 8.8 us -> 20.8 us
  Pallas kernels: 130 us -> 120 us
    unnamed x35 -> x53, local copies, waits for them, and re-layouts: 5.12 us -> 19.4 us
    pallas_call x1, Pallas kernels: 16 us -> 9.74 us  [tile_ham(): pl.pallas_call(tile_kernel, grid_spec=pltpu.PrefetchScalarGridSpec(num_sc...]
  transfers between devices with their start and end apart: 23 -> 23, of which waited for: 12 -> 12; matrix products, arithmetic and copies ran while one was open for 2% -> 1% of each run, Pallas kernels for 29% -> 27%
where the time goes in v9:
time: 394 us; the launch traced here: 393 us
  waiting for transfers between devices  187 us (47%)
  Pallas kernels  120 us (30%)
  starting transfers between devices  44.8 us (11%)
  local copies, waits for them, and re-layouts  20.8 us (5%)
  between operations  14.5 us (4%)
  other arithmetic  5.98 us (2%)
    ppermute x4, waiting for transfers between devices, body(): pair.append(lax.ppermute(ready, 'row', swap))  75.2 us
    ppermute x4, waiting for transfers between devices, body(): near_end = [lax.ppermute(x, 'row', outward) for x in near_mid]  65.4 us
    pallas_call x1, Pallas kernels, product(): pl.pallas_call(kernel, grid_spec=pltpu.PrefetchScalarGridSpec(num_scalar_...  37.2 us
    pallas_call x4, Pallas kernels, product_add(): pl.pallas_call(kernel, grid_spec=pltpu.PrefetchScalarGridSpec(num_scalar_...  35.5 us
    ppermute x4, waiting for transfers between devices, body(): far_end.append(lax.ppermute(ready, 'row', outward))  21.3 us
    unnamed x53, local copies, waits for them, and re-layouts  19.4 us
    all_to_all x1, waiting for transfers between devices, body(): lax.all_to_all(returning, ('row', 'col'), split_axis=0, concat_axis=0, ti...  14.4 us
    ppermute x4, starting transfers between devices, body(): pair.append(lax.ppermute(ready, 'row', swap))  13.7 us
  transfers between devices with their start and end apart: 23, of which 12 were waited for; matrix products, arithmetic and copies ran while one was open for 1% of the time, Pallas kernels for 27%

profile of v9, /device:TPU:0, one launch (start us, length us, event | category | flops | bytes accessed | tf_op | source)
XLA Modules:
  0.0 392.8 jit_solution(18004561704426336843)
XLA Ops:
  9.0 4.5 %gather_blocks.2 = f32[32,128,128]{2,1,0:T(8,128)} custom-call(s32[32]{0:T(128)} %get-tuple-element.73.row_ref, s32[32]{0:T(128)} %get-tuple-element.72.col_ref, f32[2048,1024]{1,0:T(8,128)} %x_ref.2), custom_call_target="tpu_custom_call" | custom-call | bytes 4194304 | tf_op jit(solution)/shard_map/gather_blocks/pallas_call | solution.py:44
  13.5 2.9 multiply_convert_fusion
  16.4 7.1 %all-to-all-start = ((f16[32,128,128]{2,1,0:T(8,128)(2,1)}), f16[32,128,128]{2,1,0:T(8,128)(2,1)S(1)}, u32[]{:S(2)}, u32[]{:S(2)}) async-start(f16[32,128,128]{2,1,0:T(8,128)(2,1)} %multiply_convert_fusion), calls=%async_computation | async-start | bytes 2097152 | tf_op jit(solution)/shard_map/all_to_all | solution.py:615
  23.7 6.2 %round_parts.2 = bf16[2048,1024]{1,0:T(8,128)(2,1)} custom-call(f32[2048,1024]{1,0:T(8,128)} %x_ref.2), custom_call_target="tpu_custom_call" | custom-call | flops 2097152 | bytes 12582912 | tf_op jit(solution)/shard_map/round_parts/pallas_call | solution.py:96
  32.1 2.2 split_basis.1
  39.5 10.2 %all-to-all-done = f16[32,128,128]{2,1,0:T(8,128)(2,1)S(1)} async-done(((f16[32,128,128]{2,1,0:T(8,128)(2,1)}), f16[32,128,128]{2,1,0:T(8,128)(2,1)S(1)}, u32[]{:S(2)}, u32[]{:S(2)}) %all-to-all-start) | async-done | bytes 1048608 | tf_op jit(solution)/shard_map/all_to_all | solution.py:615
  57.5 9.7 %tile_ham.1 = bf16[32,128,128]{2,1,0:T(8,128)(2,1)} custom-call(s32[2,16]{1,0:T(2,128)S(1)} %add.54.hold_ref, s32[2]{0:T(128)S(1)} %dynamic-slice_bitcast_fusion.count_ref, f32[32,128,128]{2,1,0:T(8,128)S(1)} %convert_element_type.12.in_ref, bf16[2,1024,512]{2,1,0:T(8,128)(2,1)S(1)} %copy-done.2, bf16[2,1024,512]{2,1,0:T(8,128)(2,1)S(1)} %copy-done.4, ...), custom_call_target="tpu_custom_call" | custom-call | flops 6442450944 | bytes 8388608 | tf_op jit(solution)/shard_map/tile_ham/pallas_call | solution.py:287
  67.3 3.1 all-to-all-start.1
  70.5 4.6 %gather_blocks.3.h_ref = f32[32,128,128]{2,1,0:T(8,128)} custom-call(s32[32]{0:T(128)} %get-tuple-element.73.row_ref, s32[32]{0:T(128)} %get-tuple-element.72.col_ref, f32[2048,1024]{1,0:T(8,128)} %h_ref.1), custom_call_target="tpu_custom_call" | custom-call | bytes 4194304 | tf_op jit(solution)/shard_map/gather_blocks/pallas_call | solution.py:44
  75.1 6.4 %round_parts.3 = (bf16[2048,256]{1,0:T(8,128)(2,1)}, bf16[2048,256]{1,0:T(8,128)(2,1)}, bf16[2048,256]{1,0:T(8,128)(2,1)}, bf16[2048,256]{1,0:T(8,128)(2,1)}) custom-call(f32[2048,1024]{1,0:T(8,128)} %h_ref.1), custom_call_target="tpu_custom_call" | custom-call | flops 2097152 | bytes 12582912 | tf_op jit(solution)/shard_map/round_parts/pallas_call | solution.py:96
  82.2 14.4 %all-to-all-done.1.in_ref = bf16[32,128,128]{2,1,0:T(8,128)(2,1)S(1)} async-done(((bf16[32,128,128]{2,1,0:T(8,128)(2,1)}), bf16[32,128,128]{2,1,0:T(8,128)(2,1)S(1)}, u32[]{:S(2)}, u32[]{:S(2)}) %all-to-all-start.1) | async-done | bytes 1048608 | tf_op jit(solution)/shard_map/all_to_all | solution.py:623
  97.6 4.5 %update_blocks.1 = (bf16[2048,256]{1,0:T(8,128)(2,1)}, bf16[2048,256]{1,0:T(8,128)(2,1)}, bf16[2048,256]{1,0:T(8,128)(2,1)}, bf16[2048,256]{1,0:T(8,128)(2,1)}) custom-call(s32[32]{0:T(128)} %get-tuple-element.73.row_ref, s32[32]{0:T(128)} %get-tuple-element.72.col_ref, ...), custom_call_target="tpu_custom_call", output_to_operand_aliasing={{0}: (5, {}), {1}: (6, {}), {2}: (7, {}), {3}: (8, {})} | custom-call | flops 524288 | bytes 4194304 | tf_op jit(solution)/shard_map/update_blocks/pallas_call | solution.py:175
  102.8 2.9 collective-permute-start.13
  106.5 2.8 collective-permute-start.17
  111.3 18.7 %collective-permute-done.13.refs_5_ = bf16[2048,256]{1,0:T(8,128)(2,1)S(1)} collective-permute-done((bf16[2048,256]{1,0:T(8,128)(2,1)}, bf16[2048,256]{1,0:T(8,128)(2,1)S(1)}, u32[]{:S(2)}, u32[]{:S(2)}) %collective-permute-start.13) | collective-permute-done | bytes 1048608 | tf_op jit(solution)/shard_map/ppermute | solution.py:641
  130.0 5.3 %collective-permute-start.9 = (bf16[2048,256]{1,0:T(8,128)(2,1)}, bf16[2048,256]{1,0:T(8,128)(2,1)}, u32[]{:S(2)}, u32[]{:S(2)}) collective-permute-start(bf16[2048,256]{1,0:T(8,128)(2,1)} %get-tuple-element.62.refs_2_), channel_id=1, source_target_pairs={{0,8},{8,0},{16,24},{24,16},{1,9},{9,1},{17,25},{25,17},{2,10},{10... | collective-permute-start | bytes 3145736 | tf_op jit(solution)/shard_map/ppermute | solution.py:641
  136.6 16.0 %collective-permute-done.17.refs_4_ = bf16[2048,256]{1,0:T(8,128)(2,1)} collective-permute-done((bf16[2048,256]{1,0:T(8,128)(2,1)}, bf16[2048,256]{1,0:T(8,128)(2,1)}, u32[]{:S(2)}, u32[]{:S(2)}) %collective-permute-start.17) | collective-permute-done | bytes 1048608 | tf_op jit(solution)/shard_map/ppermute | solution.py:641
  152.6 2.7 collective-permute-start.1
  155.3 19.6 %collective-permute-done.14.refs_12_ = bf16[2048,256]{1,0:T(8,128)(2,1)S(1)} collective-permute-done((bf16[2048,256]{1,0:T(8,128)(2,1)S(1)}, bf16[2048,256]{1,0:T(8,128)(2,1)S(1)}, u32[]{:S(2)}, u32[]{:S(2)}) %collective-permute-start.14) | collective-permute-done | bytes 1048608 | tf_op jit(solution)/shard_map/ppermute | solution.py:643
  177.9 19.6 %collective-permute-done.9.refs_6_ = bf16[2048,256]{1,0:T(8,128)(2,1)} collective-permute-done((bf16[2048,256]{1,0:T(8,128)(2,1)}, bf16[2048,256]{1,0:T(8,128)(2,1)}, u32[]{:S(2)}, u32[]{:S(2)}) %collective-permute-start.9) | collective-permute-done | bytes 1048608 | tf_op jit(solution)/shard_map/ppermute | solution.py:641
  199.1 20.7 %collective-permute-done.10.refs_13_ = bf16[2048,256]{1,0:T(8,128)(2,1)S(1)} collective-permute-done((bf16[2048,256]{1,0:T(8,128)(2,1)S(1)}, bf16[2048,256]{1,0:T(8,128)(2,1)S(1)}, u32[]{:S(2)}, u32[]{:S(2)}) %collective-permute-start.10) | collective-permute-done | bytes 1048608 | tf_op jit(solution)/shard_map/ppermute | solution.py:643
  221.5 21.0 %collective-permute-done.1.refs_7_ = bf16[2048,256]{1,0:T(8,128)(2,1)} collective-permute-done((bf16[2048,256]{1,0:T(8,128)(2,1)}, bf16[2048,256]{1,0:T(8,128)(2,1)}, u32[]{:S(2)}, u32[]{:S(2)}) %collective-permute-start.1) | collective-permute-done | bytes 1048608 | tf_op jit(solution)/shard_map/ppermute | solution.py:641
  245.4 19.4 %collective-permute-done.4.refs_14_ = bf16[2048,256]{1,0:T(8,128)(2,1)S(1)} collective-permute-done((bf16[2048,256]{1,0:T(8,128)(2,1)S(1)}, bf16[2048,256]{1,0:T(8,128)(2,1)S(1)}, u32[]{:S(2)}, u32[]{:S(2)}) %collective-permute-start.4) | collective-permute-done | bytes 1048608 | tf_op jit(solution)/shard_map/ppermute | solution.py:643
  268.6 9.2 %assemble.1 = f32[2048,1024]{1,0:T(8,128)} custom-call(s32[32]{0:T(128)} %get-tuple-element.73.row_ref, s32[32]{0:T(128)} %get-tuple-element.72.col_ref, s32[32]{0:T(128)} %copy-done.24, bf16[32,128,128]{2,1,0:T(8,128)(2,1)} %copy-done.9, f32[2048,1024]{1,0:T(8,128)} %h_ref.1), custom_call_target="tpu_custom_call" | custom-call | flops 2097152 | bytes 12582912 | tf_op jit(solution)/shard_map/assemble/pallas_call | solution.py:392
  281.8 5.6 %collective-permute-done.7.refs_15_ = bf16[2048,256]{1,0:T(8,128)(2,1)} collective-permute-done((bf16[2048,256]{1,0:T(8,128)(2,1)}, bf16[2048,256]{1,0:T(8,128)(2,1)}, u32[]{:S(2)}, u32[]{:S(2)}) %collective-permute-start.7) | collective-permute-done | bytes 1048608 | tf_op jit(solution)/shard_map/ppermute | solution.py:643
  288.9 37.2 %product.1.refs_3_ = f32[2048,1024]{1,0:T(8,128)} custom-call(s32[6]{0:T(128)} %stack.41.sc_ref, bf16[2048,256]{1,0:T(8,128)(2,1)} %get-tuple-element.61.refs_0_, bf16[2048,256]{1,0:T(8,128)(2,1)} %get-tuple-element.58.refs_1_, bf16[2048,256]{1,0:T(8,128)(2,1)} %get-tuple-element.62.refs_2_, bf16[2048,256]{1,0:T(8,128)(2,1)} %get-tuple-element.59.refs_3_, ...), custom_call_target="tpu_custom_call" | custom-call | flops 25769803776 | bytes 46137344 | tf_op jit(solution)/shard_map/product/pallas_call | solution.py:463
  327.1 8.9 %product_add.4.refs_3_ = f32[2048,1024]{1,0:T(8,128)} custom-call(s32[2]{0:T(128)} %pad_add_fusion.sc_ref, bf16[2048,256]{1,0:T(8,128)(2,1)} %collective-permute-done.18.refs_0_, bf16[2048,256]{1,0:T(8,128)(2,1)} %copy-done.17, bf16[8,2048,1024]{2,1,0:T(8,128)(2,1)} %bitcast.31, f32[2048,1024]{1,0:T(8,128)} %product.1.refs_3_), custom_call_target="tpu_custom_call", output_to_operand_aliasing={{}: (4, {})} | custom-call | flops 2147483648 | bytes 13631488 | tf_op jit(solution)/shard_map/product_add/pallas_call | solution.py:541
  337.0 8.9 %product_add.5.refs_3_ = f32[2048,1024]{1,0:T(8,128)} custom-call(s32[2]{0:T(128)} %pad_add_fusion.sc_ref, bf16[2048,256]{1,0:T(8,128)(2,1)} %collective-permute-done.15.refs_0_, bf16[2048,256]{1,0:T(8,128)(2,1)} %copy-done.18, bf16[8,2048,1024]{2,1,0:T(8,128)(2,1)} %bitcast.32, f32[2048,1024]{1,0:T(8,128)} %product_add.4.refs_3_), custom_call_target="tpu_custom_call", output_to_operand_aliasing={{}: (4, {})} | custom-call | flops 2147483648 | bytes 13631488 | tf_op jit(solution)/shard_map/product_add/pallas_call | solution.py:541
  345.9 8.8 %collective-permute-done.12.refs_1_ = bf16[2048,256]{1,0:T(8,128)(2,1)S(1)} collective-permute-done((bf16[2048,256]{1,0:T(8,128)(2,1)}, bf16[2048,256]{1,0:T(8,128)(2,1)S(1)}, u32[]{:S(2)}, u32[]{:S(2)}) %collective-permute-start.12) | collective-permute-done | bytes 1048608 | tf_op jit(solution)/shard_map/ppermute | solution.py:655
  355.6 8.9 %product_add.6.refs_3_ = f32[2048,1024]{1,0:T(8,128)} custom-call(s32[2]{0:T(128)} %pad_add_fusion.sc_ref, bf16[2048,256]{1,0:T(8,128)(2,1)} %collective-permute-done.11.refs_0_, bf16[2048,256]{1,0:T(8,128)(2,1)} %copy-done.19, bf16[8,2048,1024]{2,1,0:T(8,128)(2,1)} %bitcast.33, f32[2048,1024]{1,0:T(8,128)} %product_add.5.refs_3_), custom_call_target="tpu_custom_call", output_to_operand_aliasing={{}: (4, {})} | custom-call | flops 2147483648 | bytes 13631488 | tf_op jit(solution)/shard_map/product_add/pallas_call | solution.py:541
  364.5 12.5 %collective-permute-done.8.refs_1_ = bf16[2048,256]{1,0:T(8,128)(2,1)} collective-permute-done((bf16[2048,256]{1,0:T(8,128)(2,1)}, bf16[2048,256]{1,0:T(8,128)(2,1)}, u32[]{:S(2)}, u32[]{:S(2)}) %collective-permute-start.8) | collective-permute-done | bytes 1048608 | tf_op jit(solution)/shard_map/ppermute | solution.py:655
  377.0 8.9 %product_add.7 = f32[2048,1024]{1,0:T(8,128)} custom-call(s32[2]{0:T(128)} %pad_add_fusion.sc_ref, bf16[2048,256]{1,0:T(8,128)(2,1)} %collective-permute-done.5.refs_0_, bf16[2048,256]{1,0:T(8,128)(2,1)} %collective-permute-done.8.refs_1_, bf16[8,2048,1024]{2,1,0:T(8,128)(2,1)} %bitcast.34, ...), custom_call_target="tpu_custom_call", output_to_operand_aliasing={{}: (4, {})} | custom-call | flops 2147483648 | bytes 13631488 | tf_op jit(solution)/shard_map/product_add/pallas_call | solution.py:541
  (103 shorter events, 44.9 us)
Async XLA Ops:
  13.5 10.0 %copy-start.25 = (s32[64]{0:T(128)S(1)}, s32[64]{0:T(128)}, u32[]{:S(2)}) copy-start(s32[64]{0:T(128)} %param.11) | copy-start | bytes 772
  16.4 33.3 %all-to-all-start = ((f16[32,128,128]{2,1,0:T(8,128)(2,1)}), f16[32,128,128]{2,1,0:T(8,128)(2,1)S(1)}, u32[]{:S(2)}, u32[]{:S(2)}) async-start(f16[32,128,128]{2,1,0:T(8,128)(2,1)} %multiply_convert_fusion), calls=%async_computation | async-start | bytes 2097152 | tf_op jit(solution)/shard_map/all_to_all | solution.py:615
  23.5 265.4 %all-gather.3.cloned.1.call-start = ((), (), s32[]{:S(2)}) async-start(), calls=%async_computation.2 | async-start | bytes 37748736 | tf_op jit(solution)/shard_map/all_gather | solution.py:620
  32.1 17.7 %copy-start.23 = (s32[64,4]{0,1:T(4,128)S(1)}, s32[64,4]{0,1:T(4,128)}, u32[]{:S(2)}) copy-start(s32[64,4]{0,1:T(4,128)} %param.10) | copy-start | bytes 3076
  39.5 10.7 %copy-start.22 = (f32[2,1024]{1,0:T(2,128)S(1)}, f32[2,1024]{1,0:T(2,128)}, u32[]{:S(2)}) copy-start(f32[2,1024]{1,0:T(2,128)} %param.9) | copy-start | bytes 24580
  67.3 29.3 %all-to-all-start.1 = ((bf16[32,128,128]{2,1,0:T(8,128)(2,1)}), bf16[32,128,128]{2,1,0:T(8,128)(2,1)S(1)}, u32[]{:S(2)}, u32[]{:S(2)}) async-start(bf16[32,128,128]{2,1,0:T(8,128)(2,1)} %tile_ham.1), calls=%async_computation.1 | async-start | bytes 2097152 | tf_op jit(solution)/shard_map/all_to_all | solution.py:623
  102.1 7.2 %collective-permute-start.2 = (bf16[2048,256]{1,0:T(8,128)(2,1)}, bf16[2048,256]{1,0:T(8,128)(2,1)S(1)}, u32[]{:S(2)}, u32[]{:S(2)}) collective-permute-start(bf16[2048,256]{1,0:T(8,128)(2,1)} %get-tuple-element.61.refs_0_), channel_id=1, source_target_pairs={{8,16},{16,8},{9,17},{17,9},{10,18},{18,10},{11,19},{19,11},{12,20... | collective-permute-start | bytes 3145736 | tf_op jit(solution)/shard_map/ppermute | solution.py:642
  102.8 27.1 %collective-permute-start.13 = (bf16[2048,256]{1,0:T(8,128)(2,1)}, bf16[2048,256]{1,0:T(8,128)(2,1)S(1)}, u32[]{:S(2)}, u32[]{:S(2)}) collective-permute-start(bf16[2048,256]{1,0:T(8,128)(2,1)} %get-tuple-element.58.refs_1_), channel_id=1, source_target_pairs={{0,8},{8,0},{16,24},{24,16},{1,9},{9,1},{17,25},{25,17},{2,10},{10... | collective-permute-start | bytes 3145736 | tf_op jit(solution)/shard_map/ppermute | solution.py:641
  105.8 29.5 %collective-permute-start = (bf16[2048,256]{1,0:T(8,128)(2,1)}, bf16[2048,256]{1,0:T(8,128)(2,1)S(1)}, u32[]{:S(2)}, u32[]{:S(2)}) collective-permute-start(bf16[2048,256]{1,0:T(8,128)(2,1)} %get-tuple-element.58.refs_1_), channel_id=1, source_target_pairs={{8,16},{16,8},{9,17},{17,9},{10,18},{18,10},{11,19},{19,11},{12,20... | collective-permute-start | bytes 3145736 | tf_op jit(solution)/shard_map/ppermute | solution.py:642
  106.5 46.1 %collective-permute-start.17 = (bf16[2048,256]{1,0:T(8,128)(2,1)}, bf16[2048,256]{1,0:T(8,128)(2,1)}, u32[]{:S(2)}, u32[]{:S(2)}) collective-permute-start(bf16[2048,256]{1,0:T(8,128)(2,1)} %get-tuple-element.61.refs_0_), channel_id=1, source_target_pairs={{0,8},{8,0},{16,24},{24,16},{1,9},{9,1},{17,25},{25,17},{2,10},{10... | collective-permute-start | bytes 3145736 | tf_op jit(solution)/shard_map/ppermute | solution.py:641
  109.3 168.5 %copy-start.10 = (bf16[2048,256]{1,0:T(8,128)(2,1)}, bf16[2048,256]{1,0:T(8,128)(2,1)S(1)}, u32[]{:S(2)}) copy-start(bf16[2048,256]{1,0:T(8,128)(2,1)S(1)} %collective-permute-done.2.refs_8_) | copy-start | bytes 3145732
  109.3 65.6 %collective-permute-start.14 = (bf16[2048,256]{1,0:T(8,128)(2,1)S(1)}, bf16[2048,256]{1,0:T(8,128)(2,1)S(1)}, u32[]{:S(2)}, u32[]{:S(2)}) collective-permute-start(bf16[2048,256]{1,0:T(8,128)(2,1)S(1)} %collective-permute-done.2.refs_8_), channel_id=1, source_target_pairs={{8,0},{16,24},{9,1},{17,25},{10,2},{18,26},{11,3},{19,27},{12,4},{... | collective-permute-start | bytes 3145736 | tf_op jit(solution)/shard_map/ppermute | solution.py:643
  110.6 66.0 %collective-permute-start.3 = (bf16[2048,256]{1,0:T(8,128)(2,1)}, bf16[2048,256]{1,0:T(8,128)(2,1)S(1)}, u32[]{:S(2)}, u32[]{:S(2)}) collective-permute-start(bf16[2048,256]{1,0:T(8,128)(2,1)} %get-tuple-element.62.refs_2_), channel_id=1, source_target_pairs={{8,16},{16,8},{9,17},{17,9},{10,18},{18,10},{11,19},{19,11},{12,20... | collective-permute-start | bytes 3145736 | tf_op jit(solution)/shard_map/ppermute | solution.py:642
  130.0 147.8 %copy-start.11 = (bf16[2048,256]{1,0:T(8,128)(2,1)}, bf16[2048,256]{1,0:T(8,128)(2,1)S(1)}, u32[]{:S(2)}) copy-start(bf16[2048,256]{1,0:T(8,128)(2,1)S(1)} %collective-permute-done.13.refs_5_) | copy-start | bytes 3145732
  130.0 67.5 %collective-permute-start.9 = (bf16[2048,256]{1,0:T(8,128)(2,1)}, bf16[2048,256]{1,0:T(8,128)(2,1)}, u32[]{:S(2)}, u32[]{:S(2)}) collective-permute-start(bf16[2048,256]{1,0:T(8,128)(2,1)} %get-tuple-element.62.refs_2_), channel_id=1, source_target_pairs={{0,8},{8,0},{16,24},{24,16},{1,9},{9,1},{17,25},{25,17},{2,10},{10... | collective-permute-start | bytes 3145736 | tf_op jit(solution)/shard_map/ppermute | solution.py:641
  135.3 142.5 %copy-start.12 = (bf16[2048,256]{1,0:T(8,128)(2,1)}, bf16[2048,256]{1,0:T(8,128)(2,1)S(1)}, u32[]{:S(2)}) copy-start(bf16[2048,256]{1,0:T(8,128)(2,1)S(1)} %collective-permute-done.refs_9_) | copy-start | bytes 3145732
  135.3 84.6 %collective-permute-start.10 = (bf16[2048,256]{1,0:T(8,128)(2,1)S(1)}, bf16[2048,256]{1,0:T(8,128)(2,1)S(1)}, u32[]{:S(2)}, u32[]{:S(2)}) collective-permute-start(bf16[2048,256]{1,0:T(8,128)(2,1)S(1)} %collective-permute-done.refs_9_), channel_id=1, source_target_pairs={{8,0},{16,24},{9,1},{17,25},{10,2},{18,26},{11,3},{19,27},{12,4},{... | collective-permute-start | bytes 3145736 | tf_op jit(solution)/shard_map/ppermute | solution.py:643
  152.6 89.9 %collective-permute-start.1 = (bf16[2048,256]{1,0:T(8,128)(2,1)}, bf16[2048,256]{1,0:T(8,128)(2,1)}, u32[]{:S(2)}, u32[]{:S(2)}) collective-permute-start(bf16[2048,256]{1,0:T(8,128)(2,1)} %get-tuple-element.59.refs_3_), channel_id=1, source_target_pairs={{0,8},{8,0},{16,24},{24,16},{1,9},{9,1},{17,25},{25,17},{2,10},{10... | collective-permute-start | bytes 3145736 | tf_op jit(solution)/shard_map/ppermute | solution.py:641
  174.9 44.9 %copy-start.13 = (bf16[2048,256]{1,0:T(8,128)(2,1)}, bf16[2048,256]{1,0:T(8,128)(2,1)S(1)}, u32[]{:S(2)}) copy-start(bf16[2048,256]{1,0:T(8,128)(2,1)S(1)} %collective-permute-done.14.refs_12_) | copy-start | bytes 3145732
  174.9 69.2 %collective-permute-start.6 = (bf16[2048,256]{1,0:T(8,128)(2,1)}, bf16[2048,256]{1,0:T(8,128)(2,1)}, u32[]{:S(2)}, u32[]{:S(2)}) collective-permute-start(bf16[2048,256]{1,0:T(8,128)(2,1)} %get-tuple-element.59.refs_3_), channel_id=1, source_target_pairs={{8,16},{16,8},{9,17},{17,9},{10,18},{18,10},{11,19},{19,11},{12,20... | collective-permute-start | bytes 3145736 | tf_op jit(solution)/shard_map/ppermute | solution.py:642
  176.6 44.9 %copy-start.14 = (bf16[2048,256]{1,0:T(8,128)(2,1)}, bf16[2048,256]{1,0:T(8,128)(2,1)S(1)}, u32[]{:S(2)}) copy-start(bf16[2048,256]{1,0:T(8,128)(2,1)S(1)} %collective-permute-done.3.refs_10_) | copy-start | bytes 3145732
  176.6 88.2 %collective-permute-start.4 = (bf16[2048,256]{1,0:T(8,128)(2,1)S(1)}, bf16[2048,256]{1,0:T(8,128)(2,1)S(1)}, u32[]{:S(2)}, u32[]{:S(2)}) collective-permute-start(bf16[2048,256]{1,0:T(8,128)(2,1)S(1)} %collective-permute-done.3.refs_10_), channel_id=1, source_target_pairs={{8,0},{16,24},{9,1},{17,25},{10,2},{18,26},{11,3},{19,27},{12,4},{... | collective-permute-start | bytes 3145736 | tf_op jit(solution)/shard_map/ppermute | solution.py:643
  197.5 80.3 %collective-permute-start.18 = (bf16[2048,256]{1,0:T(8,128)(2,1)}, bf16[2048,256]{1,0:T(8,128)(2,1)}, u32[]{:S(2)}, u32[]{:S(2)}) collective-permute-start(bf16[2048,256]{1,0:T(8,128)(2,1)} %collective-permute-done.17.refs_4_), channel_id=1, source_target_pairs={{8,16},{16,8},{9,17},{17,9},{10,18},{18,10},{11,19},{19,11},{12,20... | collective-permute-start | bytes 3145736 | tf_op jit(solution)/shard_map/ppermute | solution.py:649
  219.9 44.9 %copy-start.15 = (bf16[2048,256]{1,0:T(8,128)(2,1)}, bf16[2048,256]{1,0:T(8,128)(2,1)S(1)}, u32[]{:S(2)}) copy-start(bf16[2048,256]{1,0:T(8,128)(2,1)S(1)} %collective-permute-done.10.refs_13_) | copy-start | bytes 3145732
  219.9 59.3 %collective-permute-start.15 = (bf16[2048,256]{1,0:T(8,128)(2,1)S(1)}, bf16[2048,256]{1,0:T(8,128)(2,1)}, u32[]{:S(2)}, u32[]{:S(2)}) collective-permute-start(bf16[2048,256]{1,0:T(8,128)(2,1)S(1)} %collective-permute-done.13.refs_5_), channel_id=1, source_target_pairs={{8,16},{16,8},{9,17},{17,9},{10,18},{18,10},{11,19},{19,11},{12,20... | collective-permute-start | bytes 3145736 | tf_op jit(solution)/shard_map/ppermute | solution.py:649
  242.4 38.0 %collective-permute-start.11 = (bf16[2048,256]{1,0:T(8,128)(2,1)}, bf16[2048,256]{1,0:T(8,128)(2,1)}, u32[]{:S(2)}, u32[]{:S(2)}) collective-permute-start(bf16[2048,256]{1,0:T(8,128)(2,1)} %collective-permute-done.9.refs_6_), channel_id=1, source_target_pairs={{8,16},{16,8},{9,17},{17,9},{10,18},{18,10},{11,19},{19,11},{12,20... | collective-permute-start | bytes 3145736 | tf_op jit(solution)/shard_map/ppermute | solution.py:649
  244.1 43.3 %collective-permute-start.7 = (bf16[2048,256]{1,0:T(8,128)(2,1)}, bf16[2048,256]{1,0:T(8,128)(2,1)}, u32[]{:S(2)}, u32[]{:S(2)}) collective-permute-start(bf16[2048,256]{1,0:T(8,128)(2,1)} %collective-permute-done.6.refs_11_), channel_id=1, source_target_pairs={{8,0},{16,24},{9,1},{17,25},{10,2},{18,26},{11,3},{19,27},{12,4},{... | collective-permute-start | bytes 3145736 | tf_op jit(solution)/shard_map/ppermute | solution.py:643
  265.8 21.6 %collective-permute-start.5 = (bf16[2048,256]{1,0:T(8,128)(2,1)}, bf16[2048,256]{1,0:T(8,128)(2,1)}, u32[]{:S(2)}, u32[]{:S(2)}) collective-permute-start(bf16[2048,256]{1,0:T(8,128)(2,1)} %collective-permute-done.1.refs_7_), channel_id=1, source_target_pairs={{8,16},{16,8},{9,17},{17,9},{10,18},{18,10},{11,19},{19,11},{12,20... | collective-permute-start | bytes 3145736 | tf_op jit(solution)/shard_map/ppermute | solution.py:649
  277.8 48.3 %collective-permute-start.19 = (bf16[2048,256]{1,0:T(8,128)(2,1)}, bf16[2048,256]{1,0:T(8,128)(2,1)S(1)}, u32[]{:S(2)}, u32[]{:S(2)}) collective-permute-start(bf16[2048,256]{1,0:T(8,128)(2,1)} %collective-permute-done.18.refs_0_), channel_id=1, source_target_pairs={{8,0},{16,24},{9,1},{17,25},{10,2},{18,26},{11,3},{19,27},{12,4},{... | collective-permute-start | bytes 3145736 | tf_op jit(solution)/shard_map/ppermute | solution.py:655
  279.2 56.8 %collective-permute-start.16 = (bf16[2048,256]{1,0:T(8,128)(2,1)}, bf16[2048,256]{1,0:T(8,128)(2,1)S(1)}, u32[]{:S(2)}, u32[]{:S(2)}) collective-permute-start(bf16[2048,256]{1,0:T(8,128)(2,1)} %collective-permute-done.15.refs_0_), channel_id=1, source_target_pairs={{8,0},{16,24},{9,1},{17,25},{10,2},{18,26},{11,3},{19,27},{12,4},{... | collective-permute-start | bytes 3145736 | tf_op jit(solution)/shard_map/ppermute | solution.py:655
  280.5 74.2 %collective-permute-start.12 = (bf16[2048,256]{1,0:T(8,128)(2,1)}, bf16[2048,256]{1,0:T(8,128)(2,1)S(1)}, u32[]{:S(2)}, u32[]{:S(2)}) collective-permute-start(bf16[2048,256]{1,0:T(8,128)(2,1)} %collective-permute-done.11.refs_0_), channel_id=1, source_target_pairs={{8,0},{16,24},{9,1},{17,25},{10,2},{18,26},{11,3},{19,27},{12,4},{... | collective-permute-start | bytes 3145736 | tf_op jit(solution)/shard_map/ppermute | solution.py:655
  287.4 89.6 %collective-permute-start.8 = (bf16[2048,256]{1,0:T(8,128)(2,1)}, bf16[2048,256]{1,0:T(8,128)(2,1)}, u32[]{:S(2)}, u32[]{:S(2)}) collective-permute-start(bf16[2048,256]{1,0:T(8,128)(2,1)} %collective-permute-done.5.refs_0_), channel_id=1, source_target_pairs={{8,0},{16,24},{9,1},{17,25},{10,2},{18,26},{11,3},{19,27},{12,4},{... | collective-permute-start | bytes 3145736 | tf_op jit(solution)/shard_map/ppermute | solution.py:655
  (17 other events, 38.5 us)
Sparse Core Ops, SparseCore 0:
  49.9 171.0 all-gather.2

commit v10 on v9

--- a/solution.py
+++ b/solution.py
@@ -225,7 +225,7 @@
         ),
         out_shape=[jax.ShapeDtypeStruct((tdev, npts, local), BF16)] * 2
         + [jax.ShapeDtypeStruct((tdev, local, npts), BF16)] * 2,
-        compiler_params=pltpu.CompilerParams(vmem_limit_bytes=24 * MIB),
+        compiler_params=pltpu.CompilerParams(vmem_limit_bytes=60 * MIB),
         cost_estimate=pl.CostEstimate(
             flops=4 * phi.size, bytes_accessed=12 * phi.size, transcendentals=0
         ),
@@ -243,14 +243,30 @@
     in_ref,
     hi_ref,
     lo_ref,
+    v_ref,
     hit_ref,
     lot_ref,
-    v_ref,
     out_ref,
     dh_ref,
     dl_ref,
+    mht_ref,
+    mlt_ref,
+    sems,
 ):
     t = pl.program_id(0)
+
+    def fetch(k):
+        return (
+            pltpu.make_async_copy(hit_ref.at[k], mht_ref.at[k], sems.at[0, k]),
+            pltpu.make_async_copy(lot_ref.at[k], mlt_ref.at[k], sems.at[1, k]),
+        )
+
+    @pl.when(t == 0)
+    def _():
+        for k in range(mht_ref.shape[0]):
+            for copy in fetch(k):
+                copy.start()
+
     maxb = hi_ref.shape[2] // BLK
     for i in range(maxb):
         for j in range(maxb):
@@ -266,7 +282,9 @@
     rho = jnp.sum(spread * masked, axis=1, keepdims=True)
     potential = v_ref[0] + rho + cube_coef * rho * rho * rho
     wh, wl = split(masked * (potential * cell_volume))
-    mht, mlt = hit_ref[0], lot_ref[0]
+    for copy in fetch(t):
+        copy.wait()
+    mht, mlt = mht_ref[t], mlt_ref[t]
     ham = (mm(mht, wh) + (mm(mlt, wh) + mm(mht, wl))).astype(BF16)
     for i in range(maxb):
         for j in range(maxb):
@@ -283,7 +301,6 @@
     tdev, npts, local = basis[0].shape
     flops = tdev * 3 * 2 * 2 * npts * local * local
     spec = pl.BlockSpec((1, npts, local), lambda t, *_: (t, 0, 0))
-    spec_t = pl.BlockSpec((1, local, npts), lambda t, *_: (t, 0, 0))
     return pl.pallas_call(
         tile_kernel,
         grid_spec=pltpu.PrefetchScalarGridSpec(
@@ -293,23 +310,26 @@
                 pl.BlockSpec((n, BLK, BLK), lambda t, *_: (0, 0, 0)),
                 spec,
                 spec,
-                spec_t,
-                spec_t,
                 pl.BlockSpec((1, npts, 1), lambda t, *_: (t, 0, 0)),
+                pl.BlockSpec(memory_space=pltpu.HBM),
+                pl.BlockSpec(memory_space=pltpu.HBM),
             ],
             out_specs=pl.BlockSpec((n, BLK, BLK), lambda t, *_: (0, 0, 0)),
             scratch_shapes=[
                 pltpu.VMEM((local, local), BF16),
                 pltpu.VMEM((local, local), BF16),
+                pltpu.VMEM((tdev, local, npts), BF16),
+                pltpu.VMEM((tdev, local, npts), BF16),
+                pltpu.SemaphoreType.DMA((2, tdev)),
             ],
         ),
         out_shape=jax.ShapeDtypeStruct((n, BLK, BLK), BF16),
-        compiler_params=pltpu.CompilerParams(vmem_limit_bytes=34 * MIB),
+        compiler_params=pltpu.CompilerParams(vmem_limit_bytes=60 * MIB),
         cost_estimate=pl.CostEstimate(
             flops=flops, bytes_accessed=tdev * npts * local * 8, transcendentals=0
         ),
         name="tile_ham",
-    )(hold, counts, incoming, *basis, v_column)
+    )(hold, counts, incoming, *basis[:2], v_column, *basis[2:])
 
 
 def assemble(h_core, arriving, picks, dtype, first, parts, wide):

time: 394 us -> 397 us (level)
  local copies, waits for them, and re-layouts: 20.8 us -> 8.8 us
  Pallas kernels: 120 us -> 130 us
    unnamed x53 -> x35, local copies, waits for them, and re-layouts: 19.4 us -> 5.12 us
    pallas_call x1, Pallas kernels: 9.74 us -> 16.7 us  [tile_ham(): pl.pallas_call(tile_kernel, grid_spec=pltpu.PrefetchScalarGridSpec(num_sc...]
  transfers between devices with their start and end apart: 23 -> 23, of which waited for: 12 -> 12; matrix products, arithmetic and copies ran while one was open for 1% -> 2% of each run, Pallas kernels for 27% -> 30%
where the time goes in v10:
time: 397 us; the launch traced here: 395 us
  waiting for transfers between devices  190 us (48%)
  Pallas kernels  130 us (33%)
  starting transfers between devices  44.7 us (11%)
  between operations  14.5 us (4%)
  local copies, waits for them, and re-layouts  8.8 us (2%)
  other arithmetic  7.37 us (2%)
    ppermute x4, waiting for transfers between devices, body(): pair.append(lax.ppermute(ready, 'row', swap))  75.1 us
    ppermute x4, waiting for transfers between devices, body(): near_end = [lax.ppermute(x, 'row', outward) for x in near_mid]  65.1 us
    pallas_call x1, Pallas kernels, product(): pl.pallas_call(kernel, grid_spec=pltpu.PrefetchScalarGridSpec(num_scalar_...  37.2 us
    pallas_call x4, Pallas kernels, product_add(): pl.pallas_call(kernel, grid_spec=pltpu.PrefetchScalarGridSpec(num_scalar_...  35.5 us
    ppermute x4, waiting for transfers between devices, body(): far_end.append(lax.ppermute(ready, 'row', outward))  21.3 us
    pallas_call x1, Pallas kernels, tile_ham(): pl.pallas_call(tile_kernel, grid_spec=pltpu.PrefetchScalarGridSpec(num_sc...  16.7 us
    all_to_all x1, waiting for transfers between devices, body(): lax.all_to_all(returning, ('row', 'col'), split_axis=0, concat_axis=0, ti...  14.8 us
    ppermute x4, starting transfers between devices, body(): pair.append(lax.ppermute(ready, 'row', swap))  13.8 us
  transfers between devices with their start and end apart: 23, of which 12 were waited for; matrix products, arithmetic and copies ran while one was open for 2% of the time, Pallas kernels for 30%

profile of v10, /device:TPU:0, one launch (start us, length us, event | category | flops | bytes accessed | tf_op | source)
XLA Modules:
  0.0 395.4 jit_solution(14684881500502543666)
XLA Ops:
  9.0 4.4 %gather_blocks.2 = f32[32,128,128]{2,1,0:T(8,128)} custom-call(s32[32]{0:T(128)} %get-tuple-element.73.row_ref, s32[32]{0:T(128)} %get-tuple-element.72.col_ref, f32[2048,1024]{1,0:T(8,128)} %x_ref.2), custom_call_target="tpu_custom_call" | custom-call | bytes 4194304 | tf_op jit(solution)/shard_map/gather_blocks/pallas_call | solution.py:44
  13.4 2.9 multiply_convert_fusion
  16.2 7.2 %all-to-all-start = ((f16[32,128,128]{2,1,0:T(8,128)(2,1)}), f16[32,128,128]{2,1,0:T(8,128)(2,1)S(1)}, u32[]{:S(2)}, u32[]{:S(2)}) async-start(f16[32,128,128]{2,1,0:T(8,128)(2,1)} %multiply_convert_fusion), calls=%async_computation | async-start | bytes 2097152 | tf_op jit(solution)/shard_map/all_to_all | solution.py:635
  23.6 6.2 %round_parts.2 = bf16[2048,1024]{1,0:T(8,128)(2,1)} custom-call(f32[2048,1024]{1,0:T(8,128)} %x_ref.2), custom_call_target="tpu_custom_call" | custom-call | flops 2097152 | bytes 12582912 | tf_op jit(solution)/shard_map/round_parts/pallas_call | solution.py:96
  30.4 6.1 %split_basis.1 = (bf16[2,1024,512]{2,1,0:T(8,128)(2,1)}, bf16[2,1024,512]{2,1,0:T(8,128)(2,1)}, bf16[2,512,1024]{2,1,0:T(8,128)(2,1)}, bf16[2,512,1024]{2,1,0:T(8,128)(2,1)}) custom-call(s32[2]{0:T(128)} %dynamic-slice_bitcast_fusion.count_ref, f32[2,1024,512]{2,1,0:T(8,128)} %phi_ref.1), custom_call_target="tpu_custom_call" | custom-call | flops 4194304 | bytes 12582912 | tf_op jit(solution)/shard_map/split_basis/pallas_call | solution.py:218
  36.5 13.3 %all-to-all-done = f16[32,128,128]{2,1,0:T(8,128)(2,1)S(1)} async-done(((f16[32,128,128]{2,1,0:T(8,128)(2,1)}), f16[32,128,128]{2,1,0:T(8,128)(2,1)S(1)}, u32[]{:S(2)}, u32[]{:S(2)}) %all-to-all-start) | async-done | bytes 1048608 | tf_op jit(solution)/shard_map/all_to_all | solution.py:635
  53.5 16.7 %tile_ham.1 = bf16[32,128,128]{2,1,0:T(8,128)(2,1)} custom-call(s32[2,16]{1,0:T(2,128)} %add.54.hold_ref, s32[2]{0:T(128)} %dynamic-slice_bitcast_fusion.count_ref, f32[32,128,128]{2,1,0:T(8,128)} %convert_element_type.12.in_ref, bf16[2,1024,512]{2,1,0:T(8,128)(2,1)} %get-tuple-element.42.hi_ref, bf16[2,1024,512]{2,1,0:T(8,128)(2,1)} %get-tuple-element.43.lo_ref, ...), custom_call_target="tpu_custom_call" | custom-call | flops 6442450944 | bytes 8388608 | tf_op jit(solution)/shard_map/tile_ham/pallas_call | solution.py:304
  70.2 2.7 all-to-all-start.1
  73.0 4.1 %gather_blocks.3.h_ref = f32[32,128,128]{2,1,0:T(8,128)} custom-call(s32[32]{0:T(128)} %get-tuple-element.73.row_ref, s32[32]{0:T(128)} %get-tuple-element.72.col_ref, f32[2048,1024]{1,0:T(8,128)} %h_ref.1), custom_call_target="tpu_custom_call" | custom-call | bytes 4194304 | tf_op jit(solution)/shard_map/gather_blocks/pallas_call | solution.py:44
  77.1 6.4 %round_parts.3 = (bf16[2048,256]{1,0:T(8,128)(2,1)}, bf16[2048,256]{1,0:T(8,128)(2,1)}, bf16[2048,256]{1,0:T(8,128)(2,1)}, bf16[2048,256]{1,0:T(8,128)(2,1)}) custom-call(f32[2048,1024]{1,0:T(8,128)} %h_ref.1), custom_call_target="tpu_custom_call" | custom-call | flops 2097152 | bytes 12582912 | tf_op jit(solution)/shard_map/round_parts/pallas_call | solution.py:96
  84.3 14.8 %all-to-all-done.1.in_ref = bf16[32,128,128]{2,1,0:T(8,128)(2,1)S(1)} async-done(((bf16[32,128,128]{2,1,0:T(8,128)(2,1)}), bf16[32,128,128]{2,1,0:T(8,128)(2,1)S(1)}, u32[]{:S(2)}, u32[]{:S(2)}) %all-to-all-start.1) | async-done | bytes 1048608 | tf_op jit(solution)/shard_map/all_to_all | solution.py:643
  100.1 4.7 %update_blocks.1 = (bf16[2048,256]{1,0:T(8,128)(2,1)}, bf16[2048,256]{1,0:T(8,128)(2,1)}, bf16[2048,256]{1,0:T(8,128)(2,1)}, bf16[2048,256]{1,0:T(8,128)(2,1)}) custom-call(s32[32]{0:T(128)} %get-tuple-element.73.row_ref, s32[32]{0:T(128)} %get-tuple-element.72.col_ref, ...), custom_call_target="tpu_custom_call", output_to_operand_aliasing={{0}: (5, {}), {1}: (6, {}), {2}: (7, {}), {3}: (8, {})} | custom-call | flops 524288 | bytes 4194304 | tf_op jit(solution)/shard_map/update_blocks/pallas_call | solution.py:175
  105.5 2.8 collective-permute-start.13
  109.0 2.9 collective-permute-start.17
  114.0 18.5 %collective-permute-done.13.refs_5_ = bf16[2048,256]{1,0:T(8,128)(2,1)S(1)} collective-permute-done((bf16[2048,256]{1,0:T(8,128)(2,1)}, bf16[2048,256]{1,0:T(8,128)(2,1)S(1)}, u32[]{:S(2)}, u32[]{:S(2)}) %collective-permute-start.13) | collective-permute-done | bytes 1048608 | tf_op jit(solution)/shard_map/ppermute | solution.py:661
  132.5 5.3 %collective-permute-start.9 = (bf16[2048,256]{1,0:T(8,128)(2,1)}, bf16[2048,256]{1,0:T(8,128)(2,1)}, u32[]{:S(2)}, u32[]{:S(2)}) collective-permute-start(bf16[2048,256]{1,0:T(8,128)(2,1)} %get-tuple-element.62.refs_2_), channel_id=1, source_target_pairs={{0,8},{8,0},{16,24},{24,16},{1,9},{9,1},{17,25},{25,17},{2,10},{10... | collective-permute-start | bytes 3145736 | tf_op jit(solution)/shard_map/ppermute | solution.py:661
  139.1 16.0 %collective-permute-done.17.refs_4_ = bf16[2048,256]{1,0:T(8,128)(2,1)} collective-permute-done((bf16[2048,256]{1,0:T(8,128)(2,1)}, bf16[2048,256]{1,0:T(8,128)(2,1)}, u32[]{:S(2)}, u32[]{:S(2)}) %collective-permute-start.17) | collective-permute-done | bytes 1048608 | tf_op jit(solution)/shard_map/ppermute | solution.py:661
  155.1 2.9 collective-permute-start.1
  158.0 19.5 %collective-permute-done.14.refs_12_ = bf16[2048,256]{1,0:T(8,128)(2,1)S(1)} collective-permute-done((bf16[2048,256]{1,0:T(8,128)(2,1)S(1)}, bf16[2048,256]{1,0:T(8,128)(2,1)S(1)}, u32[]{:S(2)}, u32[]{:S(2)}) %collective-permute-start.14) | collective-permute-done | bytes 1048608 | tf_op jit(solution)/shard_map/ppermute | solution.py:663
  180.4 19.6 %collective-permute-done.9.refs_6_ = bf16[2048,256]{1,0:T(8,128)(2,1)} collective-permute-done((bf16[2048,256]{1,0:T(8,128)(2,1)}, bf16[2048,256]{1,0:T(8,128)(2,1)}, u32[]{:S(2)}, u32[]{:S(2)}) %collective-permute-start.9) | collective-permute-done | bytes 1048608 | tf_op jit(solution)/shard_map/ppermute | solution.py:661
  201.7 20.7 %collective-permute-done.10.refs_13_ = bf16[2048,256]{1,0:T(8,128)(2,1)S(1)} collective-permute-done((bf16[2048,256]{1,0:T(8,128)(2,1)S(1)}, bf16[2048,256]{1,0:T(8,128)(2,1)S(1)}, u32[]{:S(2)}, u32[]{:S(2)}) %collective-permute-start.10) | collective-permute-done | bytes 1048608 | tf_op jit(solution)/shard_map/ppermute | solution.py:663
  224.1 20.9 %collective-permute-done.1.refs_7_ = bf16[2048,256]{1,0:T(8,128)(2,1)} collective-permute-done((bf16[2048,256]{1,0:T(8,128)(2,1)}, bf16[2048,256]{1,0:T(8,128)(2,1)}, u32[]{:S(2)}, u32[]{:S(2)}) %collective-permute-start.1) | collective-permute-done | bytes 1048608 | tf_op jit(solution)/shard_map/ppermute | solution.py:661
  247.9 19.4 %collective-permute-done.4.refs_14_ = bf16[2048,256]{1,0:T(8,128)(2,1)S(1)} collective-permute-done((bf16[2048,256]{1,0:T(8,128)(2,1)S(1)}, bf16[2048,256]{1,0:T(8,128)(2,1)S(1)}, u32[]{:S(2)}, u32[]{:S(2)}) %collective-permute-start.4) | collective-permute-done | bytes 1048608 | tf_op jit(solution)/shard_map/ppermute | solution.py:663
  271.3 9.2 %assemble.1 = f32[2048,1024]{1,0:T(8,128)} custom-call(s32[32]{0:T(128)} %get-tuple-element.73.row_ref, s32[32]{0:T(128)} %get-tuple-element.72.col_ref, s32[32]{0:T(128)} %copy-done.15, bf16[32,128,128]{2,1,0:T(8,128)(2,1)} %copy-done, f32[2048,1024]{1,0:T(8,128)} %h_ref.1), custom_call_target="tpu_custom_call" | custom-call | flops 2097152 | bytes 12582912 | tf_op jit(solution)/shard_map/assemble/pallas_call | solution.py:412
  284.4 5.5 %collective-permute-done.7.refs_15_ = bf16[2048,256]{1,0:T(8,128)(2,1)} collective-permute-done((bf16[2048,256]{1,0:T(8,128)(2,1)}, bf16[2048,256]{1,0:T(8,128)(2,1)}, u32[]{:S(2)}, u32[]{:S(2)}) %collective-permute-start.7) | collective-permute-done | bytes 1048608 | tf_op jit(solution)/shard_map/ppermute | solution.py:663
  291.4 37.2 %product.1.refs_3_ = f32[2048,1024]{1,0:T(8,128)} custom-call(s32[6]{0:T(128)} %stack.41.sc_ref, bf16[2048,256]{1,0:T(8,128)(2,1)} %get-tuple-element.61.refs_0_, bf16[2048,256]{1,0:T(8,128)(2,1)} %get-tuple-element.58.refs_1_, bf16[2048,256]{1,0:T(8,128)(2,1)} %get-tuple-element.62.refs_2_, bf16[2048,256]{1,0:T(8,128)(2,1)} %get-tuple-element.59.refs_3_, ...), custom_call_target="tpu_custom_call" | custom-call | flops 25769803776 | bytes 46137344 | tf_op jit(solution)/shard_map/product/pallas_call | solution.py:483
  329.6 8.9 %product_add.4.refs_3_ = f32[2048,1024]{1,0:T(8,128)} custom-call(s32[2]{0:T(128)} %pad_add_fusion.sc_ref, bf16[2048,256]{1,0:T(8,128)(2,1)} %collective-permute-done.18.refs_0_, bf16[2048,256]{1,0:T(8,128)(2,1)} %copy-done.8, bf16[8,2048,1024]{2,1,0:T(8,128)(2,1)} %bitcast.31, f32[2048,1024]{1,0:T(8,128)} %product.1.refs_3_), custom_call_target="tpu_custom_call", output_to_operand_aliasing={{}: (4, {})} | custom-call | flops 2147483648 | bytes 13631488 | tf_op jit(solution)/shard_map/product_add/pallas_call | solution.py:561
  339.6 8.9 %product_add.5.refs_3_ = f32[2048,1024]{1,0:T(8,128)} custom-call(s32[2]{0:T(128)} %pad_add_fusion.sc_ref, bf16[2048,256]{1,0:T(8,128)(2,1)} %collective-permute-done.15.refs_0_, bf16[2048,256]{1,0:T(8,128)(2,1)} %copy-done.9, bf16[8,2048,1024]{2,1,0:T(8,128)(2,1)} %bitcast.32, f32[2048,1024]{1,0:T(8,128)} %product_add.4.refs_3_), custom_call_target="tpu_custom_call", output_to_operand_aliasing={{}: (4, {})} | custom-call | flops 2147483648 | bytes 13631488 | tf_op jit(solution)/shard_map/product_add/pallas_call | solution.py:561
  348.4 8.8 %collective-permute-done.12.refs_1_ = bf16[2048,256]{1,0:T(8,128)(2,1)S(1)} collective-permute-done((bf16[2048,256]{1,0:T(8,128)(2,1)}, bf16[2048,256]{1,0:T(8,128)(2,1)S(1)}, u32[]{:S(2)}, u32[]{:S(2)}) %collective-permute-start.12) | collective-permute-done | bytes 1048608 | tf_op jit(solution)/shard_map/ppermute | solution.py:675
  358.2 8.9 %product_add.6.refs_3_ = f32[2048,1024]{1,0:T(8,128)} custom-call(s32[2]{0:T(128)} %pad_add_fusion.sc_ref, bf16[2048,256]{1,0:T(8,128)(2,1)} %collective-permute-done.11.refs_0_, bf16[2048,256]{1,0:T(8,128)(2,1)} %copy-done.10, bf16[8,2048,1024]{2,1,0:T(8,128)(2,1)} %bitcast.33, f32[2048,1024]{1,0:T(8,128)} %product_add.5.refs_3_), custom_call_target="tpu_custom_call", output_to_operand_aliasing={{}: (4, {})} | custom-call | flops 2147483648 | bytes 13631488 | tf_op jit(solution)/shard_map/product_add/pallas_call | solution.py:561
  367.1 12.5 %collective-permute-done.8.refs_1_ = bf16[2048,256]{1,0:T(8,128)(2,1)} collective-permute-done((bf16[2048,256]{1,0:T(8,128)(2,1)}, bf16[2048,256]{1,0:T(8,128)(2,1)}, u32[]{:S(2)}, u32[]{:S(2)}) %collective-permute-start.8) | collective-permute-done | bytes 1048608 | tf_op jit(solution)/shard_map/ppermute | solution.py:675
  379.6 8.9 %product_add.7 = f32[2048,1024]{1,0:T(8,128)} custom-call(s32[2]{0:T(128)} %pad_add_fusion.sc_ref, bf16[2048,256]{1,0:T(8,128)(2,1)} %collective-permute-done.5.refs_0_, bf16[2048,256]{1,0:T(8,128)(2,1)} %collective-permute-done.8.refs_1_, bf16[8,2048,1024]{2,1,0:T(8,128)(2,1)} %bitcast.34, ...), custom_call_target="tpu_custom_call", output_to_operand_aliasing={{}: (4, {})} | custom-call | flops 2147483648 | bytes 13631488 | tf_op jit(solution)/shard_map/product_add/pallas_call | solution.py:561
  (85 shorter events, 34.3 us)
Async XLA Ops:
  13.4 10.2 %copy-start.16 = (s32[64]{0:T(128)S(1)}, s32[64]{0:T(128)}, u32[]{:S(2)}) copy-start(s32[64]{0:T(128)} %param.11) | copy-start | bytes 772
  16.2 33.5 %all-to-all-start = ((f16[32,128,128]{2,1,0:T(8,128)(2,1)}), f16[32,128,128]{2,1,0:T(8,128)(2,1)S(1)}, u32[]{:S(2)}, u32[]{:S(2)}) async-start(f16[32,128,128]{2,1,0:T(8,128)(2,1)} %multiply_convert_fusion), calls=%async_computation | async-start | bytes 2097152 | tf_op jit(solution)/shard_map/all_to_all | solution.py:635
  23.5 267.9 %all-gather.3.cloned.1.call-start = ((), (), s32[]{:S(2)}) async-start(), calls=%async_computation.2 | async-start | bytes 37748736 | tf_op jit(solution)/shard_map/all_gather | solution.py:640
  30.4 19.4 %copy-start.14 = (s32[64,4]{0,1:T(4,128)S(1)}, s32[64,4]{0,1:T(4,128)}, u32[]{:S(2)}) copy-start(s32[64,4]{0,1:T(4,128)} %param.10) | copy-start | bytes 3076
  36.4 15.6 %copy-start.13 = (f32[2,1024]{1,0:T(2,128)S(1)}, f32[2,1024]{1,0:T(2,128)}, u32[]{:S(2)}) copy-start(f32[2,1024]{1,0:T(2,128)} %param.9) | copy-start | bytes 24580
  70.2 28.9 %all-to-all-start.1 = ((bf16[32,128,128]{2,1,0:T(8,128)(2,1)}), bf16[32,128,128]{2,1,0:T(8,128)(2,1)S(1)}, u32[]{:S(2)}, u32[]{:S(2)}) async-start(bf16[32,128,128]{2,1,0:T(8,128)(2,1)} %tile_ham.1), calls=%async_computation.1 | async-start | bytes 2097152 | tf_op jit(solution)/shard_map/all_to_all | solution.py:643
  104.8 7.1 %collective-permute-start.2 = (bf16[2048,256]{1,0:T(8,128)(2,1)}, bf16[2048,256]{1,0:T(8,128)(2,1)S(1)}, u32[]{:S(2)}, u32[]{:S(2)}) collective-permute-start(bf16[2048,256]{1,0:T(8,128)(2,1)} %get-tuple-element.61.refs_0_), channel_id=1, source_target_pairs={{8,16},{16,8},{9,17},{17,9},{10,18},{18,10},{11,19},{19,11},{12,20... | collective-permute-start | bytes 3145736 | tf_op jit(solution)/shard_map/ppermute | solution.py:662
  105.5 27.0 %collective-permute-start.13 = (bf16[2048,256]{1,0:T(8,128)(2,1)}, bf16[2048,256]{1,0:T(8,128)(2,1)S(1)}, u32[]{:S(2)}, u32[]{:S(2)}) collective-permute-start(bf16[2048,256]{1,0:T(8,128)(2,1)} %get-tuple-element.58.refs_1_), channel_id=1, source_target_pairs={{0,8},{8,0},{16,24},{24,16},{1,9},{9,1},{17,25},{25,17},{2,10},{10... | collective-permute-start | bytes 3145736 | tf_op jit(solution)/shard_map/ppermute | solution.py:661
  108.3 29.5 %collective-permute-start = (bf16[2048,256]{1,0:T(8,128)(2,1)}, bf16[2048,256]{1,0:T(8,128)(2,1)S(1)}, u32[]{:S(2)}, u32[]{:S(2)}) collective-permute-start(bf16[2048,256]{1,0:T(8,128)(2,1)} %get-tuple-element.58.refs_1_), channel_id=1, source_target_pairs={{8,16},{16,8},{9,17},{17,9},{10,18},{18,10},{11,19},{19,11},{12,20... | collective-permute-start | bytes 3145736 | tf_op jit(solution)/shard_map/ppermute | solution.py:662
  109.0 46.1 %collective-permute-start.17 = (bf16[2048,256]{1,0:T(8,128)(2,1)}, bf16[2048,256]{1,0:T(8,128)(2,1)}, u32[]{:S(2)}, u32[]{:S(2)}) collective-permute-start(bf16[2048,256]{1,0:T(8,128)(2,1)} %get-tuple-element.61.refs_0_), channel_id=1, source_target_pairs={{0,8},{8,0},{16,24},{24,16},{1,9},{9,1},{17,25},{25,17},{2,10},{10... | collective-permute-start | bytes 3145736 | tf_op jit(solution)/shard_map/ppermute | solution.py:661
  112.0 168.5 %copy-start.1 = (bf16[2048,256]{1,0:T(8,128)(2,1)}, bf16[2048,256]{1,0:T(8,128)(2,1)S(1)}, u32[]{:S(2)}) copy-start(bf16[2048,256]{1,0:T(8,128)(2,1)S(1)} %collective-permute-done.2.refs_8_) | copy-start | bytes 3145732
  112.0 65.5 %collective-permute-start.14 = (bf16[2048,256]{1,0:T(8,128)(2,1)S(1)}, bf16[2048,256]{1,0:T(8,128)(2,1)S(1)}, u32[]{:S(2)}, u32[]{:S(2)}) collective-permute-start(bf16[2048,256]{1,0:T(8,128)(2,1)S(1)} %collective-permute-done.2.refs_8_), channel_id=1, source_target_pairs={{8,0},{16,24},{9,1},{17,25},{10,2},{18,26},{11,3},{19,27},{12,4},{... | collective-permute-start | bytes 3145736 | tf_op jit(solution)/shard_map/ppermute | solution.py:663
  113.2 65.9 %collective-permute-start.3 = (bf16[2048,256]{1,0:T(8,128)(2,1)}, bf16[2048,256]{1,0:T(8,128)(2,1)S(1)}, u32[]{:S(2)}, u32[]{:S(2)}) collective-permute-start(bf16[2048,256]{1,0:T(8,128)(2,1)} %get-tuple-element.62.refs_2_), channel_id=1, source_target_pairs={{8,16},{16,8},{9,17},{17,9},{10,18},{18,10},{11,19},{19,11},{12,20... | collective-permute-start | bytes 3145736 | tf_op jit(solution)/shard_map/ppermute | solution.py:662
  132.5 147.9 %copy-start.2 = (bf16[2048,256]{1,0:T(8,128)(2,1)}, bf16[2048,256]{1,0:T(8,128)(2,1)S(1)}, u32[]{:S(2)}) copy-start(bf16[2048,256]{1,0:T(8,128)(2,1)S(1)} %collective-permute-done.13.refs_5_) | copy-start | bytes 3145732
  132.5 67.5 %collective-permute-start.9 = (bf16[2048,256]{1,0:T(8,128)(2,1)}, bf16[2048,256]{1,0:T(8,128)(2,1)}, u32[]{:S(2)}, u32[]{:S(2)}) collective-permute-start(bf16[2048,256]{1,0:T(8,128)(2,1)} %get-tuple-element.62.refs_2_), channel_id=1, source_target_pairs={{0,8},{8,0},{16,24},{24,16},{1,9},{9,1},{17,25},{25,17},{2,10},{10... | collective-permute-start | bytes 3145736 | tf_op jit(solution)/shard_map/ppermute | solution.py:661
  137.8 142.7 %copy-start.3 = (bf16[2048,256]{1,0:T(8,128)(2,1)}, bf16[2048,256]{1,0:T(8,128)(2,1)S(1)}, u32[]{:S(2)}) copy-start(bf16[2048,256]{1,0:T(8,128)(2,1)S(1)} %collective-permute-done.refs_9_) | copy-start | bytes 3145732
  137.8 84.6 %collective-permute-start.10 = (bf16[2048,256]{1,0:T(8,128)(2,1)S(1)}, bf16[2048,256]{1,0:T(8,128)(2,1)S(1)}, u32[]{:S(2)}, u32[]{:S(2)}) collective-permute-start(bf16[2048,256]{1,0:T(8,128)(2,1)S(1)} %collective-permute-done.refs_9_), channel_id=1, source_target_pairs={{8,0},{16,24},{9,1},{17,25},{10,2},{18,26},{11,3},{19,27},{12,4},{... | collective-permute-start | bytes 3145736 | tf_op jit(solution)/shard_map/ppermute | solution.py:663
  155.1 89.9 %collective-permute-start.1 = (bf16[2048,256]{1,0:T(8,128)(2,1)}, bf16[2048,256]{1,0:T(8,128)(2,1)}, u32[]{:S(2)}, u32[]{:S(2)}) collective-permute-start(bf16[2048,256]{1,0:T(8,128)(2,1)} %get-tuple-element.59.refs_3_), channel_id=1, source_target_pairs={{0,8},{8,0},{16,24},{24,16},{1,9},{9,1},{17,25},{25,17},{2,10},{10... | collective-permute-start | bytes 3145736 | tf_op jit(solution)/shard_map/ppermute | solution.py:661
  177.5 44.9 %copy-start.4 = (bf16[2048,256]{1,0:T(8,128)(2,1)}, bf16[2048,256]{1,0:T(8,128)(2,1)S(1)}, u32[]{:S(2)}) copy-start(bf16[2048,256]{1,0:T(8,128)(2,1)S(1)} %collective-permute-done.14.refs_12_) | copy-start | bytes 3145732
  177.5 69.2 %collective-permute-start.6 = (bf16[2048,256]{1,0:T(8,128)(2,1)}, bf16[2048,256]{1,0:T(8,128)(2,1)}, u32[]{:S(2)}, u32[]{:S(2)}) collective-permute-start(bf16[2048,256]{1,0:T(8,128)(2,1)} %get-tuple-element.59.refs_3_), channel_id=1, source_target_pairs={{8,16},{16,8},{9,17},{17,9},{10,18},{18,10},{11,19},{19,11},{12,20... | collective-permute-start | bytes 3145736 | tf_op jit(solution)/shard_map/ppermute | solution.py:662
  179.1 44.9 %copy-start.5 = (bf16[2048,256]{1,0:T(8,128)(2,1)}, bf16[2048,256]{1,0:T(8,128)(2,1)S(1)}, u32[]{:S(2)}) copy-start(bf16[2048,256]{1,0:T(8,128)(2,1)S(1)} %collective-permute-done.3.refs_10_) | copy-start | bytes 3145732
  179.1 88.2 %collective-permute-start.4 = (bf16[2048,256]{1,0:T(8,128)(2,1)S(1)}, bf16[2048,256]{1,0:T(8,128)(2,1)S(1)}, u32[]{:S(2)}, u32[]{:S(2)}) collective-permute-start(bf16[2048,256]{1,0:T(8,128)(2,1)S(1)} %collective-permute-done.3.refs_10_), channel_id=1, source_target_pairs={{8,0},{16,24},{9,1},{17,25},{10,2},{18,26},{11,3},{19,27},{12,4},{... | collective-permute-start | bytes 3145736 | tf_op jit(solution)/shard_map/ppermute | solution.py:663
  200.0 80.5 %collective-permute-start.18 = (bf16[2048,256]{1,0:T(8,128)(2,1)}, bf16[2048,256]{1,0:T(8,128)(2,1)}, u32[]{:S(2)}, u32[]{:S(2)}) collective-permute-start(bf16[2048,256]{1,0:T(8,128)(2,1)} %collective-permute-done.17.refs_4_), channel_id=1, source_target_pairs={{8,16},{16,8},{9,17},{17,9},{10,18},{18,10},{11,19},{19,11},{12,20... | collective-permute-start | bytes 3145736 | tf_op jit(solution)/shard_map/ppermute | solution.py:669
  222.4 44.9 %copy-start.6 = (bf16[2048,256]{1,0:T(8,128)(2,1)}, bf16[2048,256]{1,0:T(8,128)(2,1)S(1)}, u32[]{:S(2)}) copy-start(bf16[2048,256]{1,0:T(8,128)(2,1)S(1)} %collective-permute-done.10.refs_13_) | copy-start | bytes 3145732
  222.4 59.4 %collective-permute-start.15 = (bf16[2048,256]{1,0:T(8,128)(2,1)S(1)}, bf16[2048,256]{1,0:T(8,128)(2,1)}, u32[]{:S(2)}, u32[]{:S(2)}) collective-permute-start(bf16[2048,256]{1,0:T(8,128)(2,1)S(1)} %collective-permute-done.13.refs_5_), channel_id=1, source_target_pairs={{8,16},{16,8},{9,17},{17,9},{10,18},{18,10},{11,19},{19,11},{12,20... | collective-permute-start | bytes 3145736 | tf_op jit(solution)/shard_map/ppermute | solution.py:669
  245.0 38.1 %collective-permute-start.11 = (bf16[2048,256]{1,0:T(8,128)(2,1)}, bf16[2048,256]{1,0:T(8,128)(2,1)}, u32[]{:S(2)}, u32[]{:S(2)}) collective-permute-start(bf16[2048,256]{1,0:T(8,128)(2,1)} %collective-permute-done.9.refs_6_), channel_id=1, source_target_pairs={{8,16},{16,8},{9,17},{17,9},{10,18},{18,10},{11,19},{19,11},{12,20... | collective-permute-start | bytes 3145736 | tf_op jit(solution)/shard_map/ppermute | solution.py:669
  246.6 43.3 %collective-permute-start.7 = (bf16[2048,256]{1,0:T(8,128)(2,1)}, bf16[2048,256]{1,0:T(8,128)(2,1)}, u32[]{:S(2)}, u32[]{:S(2)}) collective-permute-start(bf16[2048,256]{1,0:T(8,128)(2,1)} %collective-permute-done.6.refs_11_), channel_id=1, source_target_pairs={{8,0},{16,24},{9,1},{17,25},{10,2},{18,26},{11,3},{19,27},{12,4},{... | collective-permute-start | bytes 3145736 | tf_op jit(solution)/shard_map/ppermute | solution.py:663
  268.4 21.6 %collective-permute-start.5 = (bf16[2048,256]{1,0:T(8,128)(2,1)}, bf16[2048,256]{1,0:T(8,128)(2,1)}, u32[]{:S(2)}, u32[]{:S(2)}) collective-permute-start(bf16[2048,256]{1,0:T(8,128)(2,1)} %collective-permute-done.1.refs_7_), channel_id=1, source_target_pairs={{8,16},{16,8},{9,17},{17,9},{10,18},{18,10},{11,19},{19,11},{12,20... | collective-permute-start | bytes 3145736 | tf_op jit(solution)/shard_map/ppermute | solution.py:669
  280.5 48.2 %collective-permute-start.19 = (bf16[2048,256]{1,0:T(8,128)(2,1)}, bf16[2048,256]{1,0:T(8,128)(2,1)S(1)}, u32[]{:S(2)}, u32[]{:S(2)}) collective-permute-start(bf16[2048,256]{1,0:T(8,128)(2,1)} %collective-permute-done.18.refs_0_), channel_id=1, source_target_pairs={{8,0},{16,24},{9,1},{17,25},{10,2},{18,26},{11,3},{19,27},{12,4},{... | collective-permute-start | bytes 3145736 | tf_op jit(solution)/shard_map/ppermute | solution.py:675
  281.8 56.7 %collective-permute-start.16 = (bf16[2048,256]{1,0:T(8,128)(2,1)}, bf16[2048,256]{1,0:T(8,128)(2,1)S(1)}, u32[]{:S(2)}, u32[]{:S(2)}) collective-permute-start(bf16[2048,256]{1,0:T(8,128)(2,1)} %collective-permute-done.15.refs_0_), channel_id=1, source_target_pairs={{8,0},{16,24},{9,1},{17,25},{10,2},{18,26},{11,3},{19,27},{12,4},{... | collective-permute-start | bytes 3145736 | tf_op jit(solution)/shard_map/ppermute | solution.py:675
  283.1 74.1 %collective-permute-start.12 = (bf16[2048,256]{1,0:T(8,128)(2,1)}, bf16[2048,256]{1,0:T(8,128)(2,1)S(1)}, u32[]{:S(2)}, u32[]{:S(2)}) collective-permute-start(bf16[2048,256]{1,0:T(8,128)(2,1)} %collective-permute-done.11.refs_0_), channel_id=1, source_target_pairs={{8,0},{16,24},{9,1},{17,25},{10,2},{18,26},{11,3},{19,27},{12,4},{... | collective-permute-start | bytes 3145736 | tf_op jit(solution)/shard_map/ppermute | solution.py:675
  289.9 89.7 %collective-permute-start.8 = (bf16[2048,256]{1,0:T(8,128)(2,1)}, bf16[2048,256]{1,0:T(8,128)(2,1)}, u32[]{:S(2)}, u32[]{:S(2)}) collective-permute-start(bf16[2048,256]{1,0:T(8,128)(2,1)} %collective-permute-done.5.refs_0_), channel_id=1, source_target_pairs={{8,0},{16,24},{9,1},{17,25},{10,2},{18,26},{11,3},{19,27},{12,4},{... | collective-permute-start | bytes 3145736 | tf_op jit(solution)/shard_map/ppermute | solution.py:675
  (8 other events, 24.2 us)
Sparse Core Ops, SparseCore 0:
  49.9 171.0 all-gather.2

commit v11 on v9

--- a/solution.py
+++ b/solution.py
@@ -225,7 +225,7 @@
         ),
         out_shape=[jax.ShapeDtypeStruct((tdev, npts, local), BF16)] * 2
         + [jax.ShapeDtypeStruct((tdev, local, npts), BF16)] * 2,
-        compiler_params=pltpu.CompilerParams(vmem_limit_bytes=24 * MIB),
+        compiler_params=pltpu.CompilerParams(vmem_limit_bytes=40 * MIB),
         cost_estimate=pl.CostEstimate(
             flops=4 * phi.size, bytes_accessed=12 * phi.size, transcendentals=0
         ),
@@ -304,7 +304,7 @@
             ],
         ),
         out_shape=jax.ShapeDtypeStruct((n, BLK, BLK), BF16),
-        compiler_params=pltpu.CompilerParams(vmem_limit_bytes=34 * MIB),
+        compiler_params=pltpu.CompilerParams(vmem_limit_bytes=44 * MIB),
         cost_estimate=pl.CostEstimate(
             flops=flops, bytes_accessed=tdev * npts * local * 8, transcendentals=0
         ),

time: 394 us -> 393 us (level)
    unnamed x53 -> x49, local copies, waits for them, and re-layouts: 19.4 us -> 15.6 us
  transfers between devices with their start and end apart: 23 -> 23, of which waited for: 12 -> 12; matrix products, arithmetic and copies ran while one was open for 1% -> 1% of each run, Pallas kernels for 27% -> 28%
where the time goes in v11:
time: 393 us; the launch traced here: 391 us
  waiting for transfers between devices  186 us (47%)
  Pallas kernels  122 us (31%)
  starting transfers between devices  45.3 us (12%)
  local copies, waits for them, and re-layouts  17.1 us (4%)
  between operations  14.5 us (4%)
  other arithmetic  6.11 us (2%)
    ppermute x4, waiting for transfers between devices, body(): pair.append(lax.ppermute(ready, 'row', swap))  75 us
    ppermute x4, waiting for transfers between devices, body(): near_end = [lax.ppermute(x, 'row', outward) for x in near_mid]  65.1 us
    pallas_call x1, Pallas kernels, product(): pl.pallas_call(kernel, grid_spec=pltpu.PrefetchScalarGridSpec(num_scalar_...  37.2 us
    pallas_call x4, Pallas kernels, product_add(): pl.pallas_call(kernel, grid_spec=pltpu.PrefetchScalarGridSpec(num_scalar_...  35.5 us
    ppermute x4, waiting for transfers between devices, body(): far_end.append(lax.ppermute(ready, 'row', outward))  21.5 us
    unnamed x49, local copies, waits for them, and re-layouts  15.6 us
    all_to_all x1, waiting for transfers between devices, body(): lax.all_to_all(returning, ('row', 'col'), split_axis=0, concat_axis=0, ti...  14.4 us
    ppermute x4, starting transfers between devices, body(): pair.append(lax.ppermute(ready, 'row', swap))  14 us
  transfers between devices with their start and end apart: 23, of which 12 were waited for; matrix products, arithmetic and copies ran while one was open for 1% of the time, Pallas kernels for 28%

profile of v11, /device:TPU:0, one launch (start us, length us, event | category | flops | bytes accessed | tf_op | source)
XLA Modules:
  0.0 391.1 jit_solution(4927552945654015624)
XLA Ops:
  9.0 4.4 %gather_blocks.2 = f32[32,128,128]{2,1,0:T(8,128)} custom-call(s32[32]{0:T(128)} %get-tuple-element.73.row_ref, s32[32]{0:T(128)} %get-tuple-element.72.col_ref, f32[2048,1024]{1,0:T(8,128)} %x_ref.2), custom_call_target="tpu_custom_call" | custom-call | bytes 4194304 | tf_op jit(solution)/shard_map/gather_blocks/pallas_call | solution.py:44
  13.4 2.9 multiply_convert_fusion
  16.2 7.3 %all-to-all-start = ((f16[32,128,128]{2,1,0:T(8,128)(2,1)}), f16[32,128,128]{2,1,0:T(8,128)(2,1)S(1)}, u32[]{:S(2)}, u32[]{:S(2)}) async-start(f16[32,128,128]{2,1,0:T(8,128)(2,1)} %multiply_convert_fusion), calls=%async_computation | async-start | bytes 2097152 | tf_op jit(solution)/shard_map/all_to_all | solution.py:615
  23.7 6.2 %round_parts.2 = bf16[2048,1024]{1,0:T(8,128)(2,1)} custom-call(f32[2048,1024]{1,0:T(8,128)} %x_ref.2), custom_call_target="tpu_custom_call" | custom-call | flops 2097152 | bytes 12582912 | tf_op jit(solution)/shard_map/round_parts/pallas_call | solution.py:96
  32.0 2.2 split_basis.1
  39.5 10.2 %all-to-all-done = f16[32,128,128]{2,1,0:T(8,128)(2,1)S(1)} async-done(((f16[32,128,128]{2,1,0:T(8,128)(2,1)}), f16[32,128,128]{2,1,0:T(8,128)(2,1)S(1)}, u32[]{:S(2)}, u32[]{:S(2)}) %all-to-all-start) | async-done | bytes 1048608 | tf_op jit(solution)/shard_map/all_to_all | solution.py:615
  53.8 11.8 %tile_ham.1 = bf16[32,128,128]{2,1,0:T(8,128)(2,1)} custom-call(s32[2,16]{1,0:T(2,128)S(1)} %add.54.hold_ref, s32[2]{0:T(128)S(1)} %dynamic-slice_bitcast_fusion.count_ref, f32[32,128,128]{2,1,0:T(8,128)S(1)} %convert_element_type.12.in_ref, bf16[2,1024,512]{2,1,0:T(8,128)(2,1)S(1)} %copy-done.2, bf16[2,1024,512]{2,1,0:T(8,128)(2,1)S(1)} %copy-done.4, ...), custom_call_target="tpu_custom_call" | custom-call | flops 6442450944 | bytes 8388608 | tf_op jit(solution)/shard_map/tile_ham/pallas_call | solution.py:287
  65.6 3.1 all-to-all-start.1
  68.8 4.5 %gather_blocks.3.h_ref = f32[32,128,128]{2,1,0:T(8,128)} custom-call(s32[32]{0:T(128)} %get-tuple-element.73.row_ref, s32[32]{0:T(128)} %get-tuple-element.72.col_ref, f32[2048,1024]{1,0:T(8,128)} %h_ref.1), custom_call_target="tpu_custom_call" | custom-call | bytes 4194304 | tf_op jit(solution)/shard_map/gather_blocks/pallas_call | solution.py:44
  73.4 6.4 %round_parts.3 = (bf16[2048,256]{1,0:T(8,128)(2,1)}, bf16[2048,256]{1,0:T(8,128)(2,1)}, bf16[2048,256]{1,0:T(8,128)(2,1)}, bf16[2048,256]{1,0:T(8,128)(2,1)}) custom-call(f32[2048,1024]{1,0:T(8,128)} %h_ref.1), custom_call_target="tpu_custom_call" | custom-call | flops 2097152 | bytes 12582912 | tf_op jit(solution)/shard_map/round_parts/pallas_call | solution.py:96
  80.5 14.4 %all-to-all-done.1.in_ref = bf16[32,128,128]{2,1,0:T(8,128)(2,1)S(1)} async-done(((bf16[32,128,128]{2,1,0:T(8,128)(2,1)}), bf16[32,128,128]{2,1,0:T(8,128)(2,1)S(1)}, u32[]{:S(2)}, u32[]{:S(2)}) %all-to-all-start.1) | async-done | bytes 1048608 | tf_op jit(solution)/shard_map/all_to_all | solution.py:623
  95.9 4.5 %update_blocks.1 = (bf16[2048,256]{1,0:T(8,128)(2,1)}, bf16[2048,256]{1,0:T(8,128)(2,1)}, bf16[2048,256]{1,0:T(8,128)(2,1)}, bf16[2048,256]{1,0:T(8,128)(2,1)}) custom-call(s32[32]{0:T(128)} %get-tuple-element.73.row_ref, s32[32]{0:T(128)} %get-tuple-element.72.col_ref, ...), custom_call_target="tpu_custom_call", output_to_operand_aliasing={{0}: (5, {}), {1}: (6, {}), {2}: (7, {}), {3}: (8, {})} | custom-call | flops 524288 | bytes 4194304 | tf_op jit(solution)/shard_map/update_blocks/pallas_call | solution.py:175
  101.2 2.8 collective-permute-start.13
  104.7 3.0 collective-permute-start.17
  109.7 18.4 %collective-permute-done.13.refs_5_ = bf16[2048,256]{1,0:T(8,128)(2,1)S(1)} collective-permute-done((bf16[2048,256]{1,0:T(8,128)(2,1)}, bf16[2048,256]{1,0:T(8,128)(2,1)S(1)}, u32[]{:S(2)}, u32[]{:S(2)}) %collective-permute-start.13) | collective-permute-done | bytes 1048608 | tf_op jit(solution)/shard_map/ppermute | solution.py:641
  128.2 5.3 %collective-permute-start.9 = (bf16[2048,256]{1,0:T(8,128)(2,1)}, bf16[2048,256]{1,0:T(8,128)(2,1)}, u32[]{:S(2)}, u32[]{:S(2)}) collective-permute-start(bf16[2048,256]{1,0:T(8,128)(2,1)} %get-tuple-element.62.refs_2_), channel_id=1, source_target_pairs={{0,8},{8,0},{16,24},{24,16},{1,9},{9,1},{17,25},{25,17},{2,10},{10... | collective-permute-start | bytes 3145736 | tf_op jit(solution)/shard_map/ppermute | solution.py:641
  134.7 16.0 %collective-permute-done.17.refs_4_ = bf16[2048,256]{1,0:T(8,128)(2,1)} collective-permute-done((bf16[2048,256]{1,0:T(8,128)(2,1)}, bf16[2048,256]{1,0:T(8,128)(2,1)}, u32[]{:S(2)}, u32[]{:S(2)}) %collective-permute-start.17) | collective-permute-done | bytes 1048608 | tf_op jit(solution)/shard_map/ppermute | solution.py:641
  150.7 3.0 collective-permute-start.1
  153.7 19.4 %collective-permute-done.14.refs_12_ = bf16[2048,256]{1,0:T(8,128)(2,1)S(1)} collective-permute-done((bf16[2048,256]{1,0:T(8,128)(2,1)S(1)}, bf16[2048,256]{1,0:T(8,128)(2,1)S(1)}, u32[]{:S(2)}, u32[]{:S(2)}) %collective-permute-start.14) | collective-permute-done | bytes 1048608 | tf_op jit(solution)/shard_map/ppermute | solution.py:643
  176.1 19.6 %collective-permute-done.9.refs_6_ = bf16[2048,256]{1,0:T(8,128)(2,1)} collective-permute-done((bf16[2048,256]{1,0:T(8,128)(2,1)}, bf16[2048,256]{1,0:T(8,128)(2,1)}, u32[]{:S(2)}, u32[]{:S(2)}) %collective-permute-start.9) | collective-permute-done | bytes 1048608 | tf_op jit(solution)/shard_map/ppermute | solution.py:641
  197.3 20.7 %collective-permute-done.10.refs_13_ = bf16[2048,256]{1,0:T(8,128)(2,1)S(1)} collective-permute-done((bf16[2048,256]{1,0:T(8,128)(2,1)S(1)}, bf16[2048,256]{1,0:T(8,128)(2,1)S(1)}, u32[]{:S(2)}, u32[]{:S(2)}) %collective-permute-start.10) | collective-permute-done | bytes 1048608 | tf_op jit(solution)/shard_map/ppermute | solution.py:643
  219.7 20.9 %collective-permute-done.1.refs_7_ = bf16[2048,256]{1,0:T(8,128)(2,1)} collective-permute-done((bf16[2048,256]{1,0:T(8,128)(2,1)}, bf16[2048,256]{1,0:T(8,128)(2,1)}, u32[]{:S(2)}, u32[]{:S(2)}) %collective-permute-start.1) | collective-permute-done | bytes 1048608 | tf_op jit(solution)/shard_map/ppermute | solution.py:641
  243.5 19.4 %collective-permute-done.4.refs_14_ = bf16[2048,256]{1,0:T(8,128)(2,1)S(1)} collective-permute-done((bf16[2048,256]{1,0:T(8,128)(2,1)S(1)}, bf16[2048,256]{1,0:T(8,128)(2,1)S(1)}, u32[]{:S(2)}, u32[]{:S(2)}) %collective-permute-start.4) | collective-permute-done | bytes 1048608 | tf_op jit(solution)/shard_map/ppermute | solution.py:643
  266.9 9.1 %assemble.1 = f32[2048,1024]{1,0:T(8,128)} custom-call(s32[32]{0:T(128)} %get-tuple-element.73.row_ref, s32[32]{0:T(128)} %get-tuple-element.72.col_ref, s32[32]{0:T(128)} %copy-done.22, bf16[32,128,128]{2,1,0:T(8,128)(2,1)} %copy-done.7, f32[2048,1024]{1,0:T(8,128)} %h_ref.1), custom_call_target="tpu_custom_call" | custom-call | flops 2097152 | bytes 12582912 | tf_op jit(solution)/shard_map/assemble/pallas_call | solution.py:392
  280.0 5.6 %collective-permute-done.7.refs_15_ = bf16[2048,256]{1,0:T(8,128)(2,1)} collective-permute-done((bf16[2048,256]{1,0:T(8,128)(2,1)}, bf16[2048,256]{1,0:T(8,128)(2,1)}, u32[]{:S(2)}, u32[]{:S(2)}) %collective-permute-start.7) | collective-permute-done | bytes 1048608 | tf_op jit(solution)/shard_map/ppermute | solution.py:643
  287.1 37.2 %product.1.refs_3_ = f32[2048,1024]{1,0:T(8,128)} custom-call(s32[6]{0:T(128)} %stack.41.sc_ref, bf16[2048,256]{1,0:T(8,128)(2,1)} %get-tuple-element.61.refs_0_, bf16[2048,256]{1,0:T(8,128)(2,1)} %get-tuple-element.58.refs_1_, bf16[2048,256]{1,0:T(8,128)(2,1)} %get-tuple-element.62.refs_2_, bf16[2048,256]{1,0:T(8,128)(2,1)} %get-tuple-element.59.refs_3_, ...), custom_call_target="tpu_custom_call" | custom-call | flops 25769803776 | bytes 46137344 | tf_op jit(solution)/shard_map/product/pallas_call | solution.py:463
  325.3 8.9 %product_add.4.refs_3_ = f32[2048,1024]{1,0:T(8,128)} custom-call(s32[2]{0:T(128)} %pad_add_fusion.sc_ref, bf16[2048,256]{1,0:T(8,128)(2,1)} %collective-permute-done.18.refs_0_, bf16[2048,256]{1,0:T(8,128)(2,1)} %copy-done.15, bf16[8,2048,1024]{2,1,0:T(8,128)(2,1)} %bitcast.31, f32[2048,1024]{1,0:T(8,128)} %product.1.refs_3_), custom_call_target="tpu_custom_call", output_to_operand_aliasing={{}: (4, {})} | custom-call | flops 2147483648 | bytes 13631488 | tf_op jit(solution)/shard_map/product_add/pallas_call | solution.py:541
  335.2 8.9 %product_add.5.refs_3_ = f32[2048,1024]{1,0:T(8,128)} custom-call(s32[2]{0:T(128)} %pad_add_fusion.sc_ref, bf16[2048,256]{1,0:T(8,128)(2,1)} %collective-permute-done.15.refs_0_, bf16[2048,256]{1,0:T(8,128)(2,1)} %copy-done.16, bf16[8,2048,1024]{2,1,0:T(8,128)(2,1)} %bitcast.32, f32[2048,1024]{1,0:T(8,128)} %product_add.4.refs_3_), custom_call_target="tpu_custom_call", output_to_operand_aliasing={{}: (4, {})} | custom-call | flops 2147483648 | bytes 13631488 | tf_op jit(solution)/shard_map/product_add/pallas_call | solution.py:541
  344.0 8.8 %collective-permute-done.12.refs_1_ = bf16[2048,256]{1,0:T(8,128)(2,1)S(1)} collective-permute-done((bf16[2048,256]{1,0:T(8,128)(2,1)}, bf16[2048,256]{1,0:T(8,128)(2,1)S(1)}, u32[]{:S(2)}, u32[]{:S(2)}) %collective-permute-start.12) | collective-permute-done | bytes 1048608 | tf_op jit(solution)/shard_map/ppermute | solution.py:655
  353.8 8.9 %product_add.6.refs_3_ = f32[2048,1024]{1,0:T(8,128)} custom-call(s32[2]{0:T(128)} %pad_add_fusion.sc_ref, bf16[2048,256]{1,0:T(8,128)(2,1)} %collective-permute-done.11.refs_0_, bf16[2048,256]{1,0:T(8,128)(2,1)} %copy-done.17, bf16[8,2048,1024]{2,1,0:T(8,128)(2,1)} %bitcast.33, f32[2048,1024]{1,0:T(8,128)} %product_add.5.refs_3_), custom_call_target="tpu_custom_call", output_to_operand_aliasing={{}: (4, {})} | custom-call | flops 2147483648 | bytes 13631488 | tf_op jit(solution)/shard_map/product_add/pallas_call | solution.py:541
  362.7 12.7 %collective-permute-done.8.refs_1_ = bf16[2048,256]{1,0:T(8,128)(2,1)} collective-permute-done((bf16[2048,256]{1,0:T(8,128)(2,1)}, bf16[2048,256]{1,0:T(8,128)(2,1)}, u32[]{:S(2)}, u32[]{:S(2)}) %collective-permute-start.8) | collective-permute-done | bytes 1048608 | tf_op jit(solution)/shard_map/ppermute | solution.py:655
  375.4 8.9 %product_add.7 = f32[2048,1024]{1,0:T(8,128)} custom-call(s32[2]{0:T(128)} %pad_add_fusion.sc_ref, bf16[2048,256]{1,0:T(8,128)(2,1)} %collective-permute-done.5.refs_0_, bf16[2048,256]{1,0:T(8,128)(2,1)} %collective-permute-done.8.refs_1_, bf16[8,2048,1024]{2,1,0:T(8,128)(2,1)} %bitcast.34, ...), custom_call_target="tpu_custom_call", output_to_operand_aliasing={{}: (4, {})} | custom-call | flops 2147483648 | bytes 13631488 | tf_op jit(solution)/shard_map/product_add/pallas_call | solution.py:541
  (99 shorter events, 41.3 us)
Async XLA Ops:
  13.3 10.2 %copy-start.23 = (s32[64]{0:T(128)S(1)}, s32[64]{0:T(128)}, u32[]{:S(2)}) copy-start(s32[64]{0:T(128)} %param.11) | copy-start | bytes 772
  16.2 33.5 %all-to-all-start = ((f16[32,128,128]{2,1,0:T(8,128)(2,1)}), f16[32,128,128]{2,1,0:T(8,128)(2,1)S(1)}, u32[]{:S(2)}, u32[]{:S(2)}) async-start(f16[32,128,128]{2,1,0:T(8,128)(2,1)} %multiply_convert_fusion), calls=%async_computation | async-start | bytes 2097152 | tf_op jit(solution)/shard_map/all_to_all | solution.py:615
  23.5 263.6 %all-gather.3.cloned.1.call-start = ((), (), s32[]{:S(2)}) async-start(), calls=%async_computation.2 | async-start | bytes 37748736 | tf_op jit(solution)/shard_map/all_gather | solution.py:620
  32.0 17.7 %copy-start.21 = (s32[64,4]{0,1:T(4,128)S(1)}, s32[64,4]{0,1:T(4,128)}, u32[]{:S(2)}) copy-start(s32[64,4]{0,1:T(4,128)} %param.10) | copy-start | bytes 3076
  39.5 10.7 %copy-start.20 = (f32[2,1024]{1,0:T(2,128)S(1)}, f32[2,1024]{1,0:T(2,128)}, u32[]{:S(2)}) copy-start(f32[2,1024]{1,0:T(2,128)} %param.9) | copy-start | bytes 24580
  65.6 29.4 %all-to-all-start.1 = ((bf16[32,128,128]{2,1,0:T(8,128)(2,1)}), bf16[32,128,128]{2,1,0:T(8,128)(2,1)S(1)}, u32[]{:S(2)}, u32[]{:S(2)}) async-start(bf16[32,128,128]{2,1,0:T(8,128)(2,1)} %tile_ham.1), calls=%async_computation.1 | async-start | bytes 2097152 | tf_op jit(solution)/shard_map/all_to_all | solution.py:623
  100.4 7.3 %collective-permute-start.2 = (bf16[2048,256]{1,0:T(8,128)(2,1)}, bf16[2048,256]{1,0:T(8,128)(2,1)S(1)}, u32[]{:S(2)}, u32[]{:S(2)}) collective-permute-start(bf16[2048,256]{1,0:T(8,128)(2,1)} %get-tuple-element.61.refs_0_), channel_id=1, source_target_pairs={{8,16},{16,8},{9,17},{17,9},{10,18},{18,10},{11,19},{19,11},{12,20... | collective-permute-start | bytes 3145736 | tf_op jit(solution)/shard_map/ppermute | solution.py:642
  101.2 27.0 %collective-permute-start.13 = (bf16[2048,256]{1,0:T(8,128)(2,1)}, bf16[2048,256]{1,0:T(8,128)(2,1)S(1)}, u32[]{:S(2)}, u32[]{:S(2)}) collective-permute-start(bf16[2048,256]{1,0:T(8,128)(2,1)} %get-tuple-element.58.refs_1_), channel_id=1, source_target_pairs={{0,8},{8,0},{16,24},{24,16},{1,9},{9,1},{17,25},{25,17},{2,10},{10... | collective-permute-start | bytes 3145736 | tf_op jit(solution)/shard_map/ppermute | solution.py:641
  103.9 29.5 %collective-permute-start = (bf16[2048,256]{1,0:T(8,128)(2,1)}, bf16[2048,256]{1,0:T(8,128)(2,1)S(1)}, u32[]{:S(2)}, u32[]{:S(2)}) collective-permute-start(bf16[2048,256]{1,0:T(8,128)(2,1)} %get-tuple-element.58.refs_1_), channel_id=1, source_target_pairs={{8,16},{16,8},{9,17},{17,9},{10,18},{18,10},{11,19},{19,11},{12,20... | collective-permute-start | bytes 3145736 | tf_op jit(solution)/shard_map/ppermute | solution.py:642
  104.7 46.1 %collective-permute-start.17 = (bf16[2048,256]{1,0:T(8,128)(2,1)}, bf16[2048,256]{1,0:T(8,128)(2,1)}, u32[]{:S(2)}, u32[]{:S(2)}) collective-permute-start(bf16[2048,256]{1,0:T(8,128)(2,1)} %get-tuple-element.61.refs_0_), channel_id=1, source_target_pairs={{0,8},{8,0},{16,24},{24,16},{1,9},{9,1},{17,25},{25,17},{2,10},{10... | collective-permute-start | bytes 3145736 | tf_op jit(solution)/shard_map/ppermute | solution.py:641
  107.7 168.3 %copy-start.8 = (bf16[2048,256]{1,0:T(8,128)(2,1)}, bf16[2048,256]{1,0:T(8,128)(2,1)S(1)}, u32[]{:S(2)}) copy-start(bf16[2048,256]{1,0:T(8,128)(2,1)S(1)} %collective-permute-done.2.refs_8_) | copy-start | bytes 3145732
  107.7 65.4 %collective-permute-start.14 = (bf16[2048,256]{1,0:T(8,128)(2,1)S(1)}, bf16[2048,256]{1,0:T(8,128)(2,1)S(1)}, u32[]{:S(2)}, u32[]{:S(2)}) collective-permute-start(bf16[2048,256]{1,0:T(8,128)(2,1)S(1)} %collective-permute-done.2.refs_8_), channel_id=1, source_target_pairs={{8,0},{16,24},{9,1},{17,25},{10,2},{18,26},{11,3},{19,27},{12,4},{... | collective-permute-start | bytes 3145736 | tf_op jit(solution)/shard_map/ppermute | solution.py:643
  109.0 65.8 %collective-permute-start.3 = (bf16[2048,256]{1,0:T(8,128)(2,1)}, bf16[2048,256]{1,0:T(8,128)(2,1)S(1)}, u32[]{:S(2)}, u32[]{:S(2)}) collective-permute-start(bf16[2048,256]{1,0:T(8,128)(2,1)} %get-tuple-element.62.refs_2_), channel_id=1, source_target_pairs={{8,16},{16,8},{9,17},{17,9},{10,18},{18,10},{11,19},{19,11},{12,20... | collective-permute-start | bytes 3145736 | tf_op jit(solution)/shard_map/ppermute | solution.py:642
  128.2 147.9 %copy-start.9 = (bf16[2048,256]{1,0:T(8,128)(2,1)}, bf16[2048,256]{1,0:T(8,128)(2,1)S(1)}, u32[]{:S(2)}) copy-start(bf16[2048,256]{1,0:T(8,128)(2,1)S(1)} %collective-permute-done.13.refs_5_) | copy-start | bytes 3145732
  128.2 67.5 %collective-permute-start.9 = (bf16[2048,256]{1,0:T(8,128)(2,1)}, bf16[2048,256]{1,0:T(8,128)(2,1)}, u32[]{:S(2)}, u32[]{:S(2)}) collective-permute-start(bf16[2048,256]{1,0:T(8,128)(2,1)} %get-tuple-element.62.refs_2_), channel_id=1, source_target_pairs={{0,8},{8,0},{16,24},{24,16},{1,9},{9,1},{17,25},{25,17},{2,10},{10... | collective-permute-start | bytes 3145736 | tf_op jit(solution)/shard_map/ppermute | solution.py:641
  133.5 142.6 %copy-start.10 = (bf16[2048,256]{1,0:T(8,128)(2,1)}, bf16[2048,256]{1,0:T(8,128)(2,1)S(1)}, u32[]{:S(2)}) copy-start(bf16[2048,256]{1,0:T(8,128)(2,1)S(1)} %collective-permute-done.refs_9_) | copy-start | bytes 3145732
  133.5 84.6 %collective-permute-start.10 = (bf16[2048,256]{1,0:T(8,128)(2,1)S(1)}, bf16[2048,256]{1,0:T(8,128)(2,1)S(1)}, u32[]{:S(2)}, u32[]{:S(2)}) collective-permute-start(bf16[2048,256]{1,0:T(8,128)(2,1)S(1)} %collective-permute-done.refs_9_), channel_id=1, source_target_pairs={{8,0},{16,24},{9,1},{17,25},{10,2},{18,26},{11,3},{19,27},{12,4},{... | collective-permute-start | bytes 3145736 | tf_op jit(solution)/shard_map/ppermute | solution.py:643
  150.7 89.9 %collective-permute-start.1 = (bf16[2048,256]{1,0:T(8,128)(2,1)}, bf16[2048,256]{1,0:T(8,128)(2,1)}, u32[]{:S(2)}, u32[]{:S(2)}) collective-permute-start(bf16[2048,256]{1,0:T(8,128)(2,1)} %get-tuple-element.59.refs_3_), channel_id=1, source_target_pairs={{0,8},{8,0},{16,24},{24,16},{1,9},{9,1},{17,25},{25,17},{2,10},{10... | collective-permute-start | bytes 3145736 | tf_op jit(solution)/shard_map/ppermute | solution.py:641
  173.1 44.9 %copy-start.11 = (bf16[2048,256]{1,0:T(8,128)(2,1)}, bf16[2048,256]{1,0:T(8,128)(2,1)S(1)}, u32[]{:S(2)}) copy-start(bf16[2048,256]{1,0:T(8,128)(2,1)S(1)} %collective-permute-done.14.refs_12_) | copy-start | bytes 3145732
  173.1 69.2 %collective-permute-start.6 = (bf16[2048,256]{1,0:T(8,128)(2,1)}, bf16[2048,256]{1,0:T(8,128)(2,1)}, u32[]{:S(2)}, u32[]{:S(2)}) collective-permute-start(bf16[2048,256]{1,0:T(8,128)(2,1)} %get-tuple-element.59.refs_3_), channel_id=1, source_target_pairs={{8,16},{16,8},{9,17},{17,9},{10,18},{18,10},{11,19},{19,11},{12,20... | collective-permute-start | bytes 3145736 | tf_op jit(solution)/shard_map/ppermute | solution.py:642
  174.8 44.9 %copy-start.12 = (bf16[2048,256]{1,0:T(8,128)(2,1)}, bf16[2048,256]{1,0:T(8,128)(2,1)S(1)}, u32[]{:S(2)}) copy-start(bf16[2048,256]{1,0:T(8,128)(2,1)S(1)} %collective-permute-done.3.refs_10_) | copy-start | bytes 3145732
  174.8 88.2 %collective-permute-start.4 = (bf16[2048,256]{1,0:T(8,128)(2,1)S(1)}, bf16[2048,256]{1,0:T(8,128)(2,1)S(1)}, u32[]{:S(2)}, u32[]{:S(2)}) collective-permute-start(bf16[2048,256]{1,0:T(8,128)(2,1)S(1)} %collective-permute-done.3.refs_10_), channel_id=1, source_target_pairs={{8,0},{16,24},{9,1},{17,25},{10,2},{18,26},{11,3},{19,27},{12,4},{... | collective-permute-start | bytes 3145736 | tf_op jit(solution)/shard_map/ppermute | solution.py:643
  195.7 80.4 %collective-permute-start.18 = (bf16[2048,256]{1,0:T(8,128)(2,1)}, bf16[2048,256]{1,0:T(8,128)(2,1)}, u32[]{:S(2)}, u32[]{:S(2)}) collective-permute-start(bf16[2048,256]{1,0:T(8,128)(2,1)} %collective-permute-done.17.refs_4_), channel_id=1, source_target_pairs={{8,16},{16,8},{9,17},{17,9},{10,18},{18,10},{11,19},{19,11},{12,20... | collective-permute-start | bytes 3145736 | tf_op jit(solution)/shard_map/ppermute | solution.py:649
  218.0 44.9 %copy-start.13 = (bf16[2048,256]{1,0:T(8,128)(2,1)}, bf16[2048,256]{1,0:T(8,128)(2,1)S(1)}, u32[]{:S(2)}) copy-start(bf16[2048,256]{1,0:T(8,128)(2,1)S(1)} %collective-permute-done.10.refs_13_) | copy-start | bytes 3145732
  218.0 59.3 %collective-permute-start.15 = (bf16[2048,256]{1,0:T(8,128)(2,1)S(1)}, bf16[2048,256]{1,0:T(8,128)(2,1)}, u32[]{:S(2)}, u32[]{:S(2)}) collective-permute-start(bf16[2048,256]{1,0:T(8,128)(2,1)S(1)} %collective-permute-done.13.refs_5_), channel_id=1, source_target_pairs={{8,16},{16,8},{9,17},{17,9},{10,18},{18,10},{11,19},{19,11},{12,20... | collective-permute-start | bytes 3145736 | tf_op jit(solution)/shard_map/ppermute | solution.py:649
  240.6 38.1 %collective-permute-start.11 = (bf16[2048,256]{1,0:T(8,128)(2,1)}, bf16[2048,256]{1,0:T(8,128)(2,1)}, u32[]{:S(2)}, u32[]{:S(2)}) collective-permute-start(bf16[2048,256]{1,0:T(8,128)(2,1)} %collective-permute-done.9.refs_6_), channel_id=1, source_target_pairs={{8,16},{16,8},{9,17},{17,9},{10,18},{18,10},{11,19},{19,11},{12,20... | collective-permute-start | bytes 3145736 | tf_op jit(solution)/shard_map/ppermute | solution.py:649
  242.3 43.3 %collective-permute-start.7 = (bf16[2048,256]{1,0:T(8,128)(2,1)}, bf16[2048,256]{1,0:T(8,128)(2,1)}, u32[]{:S(2)}, u32[]{:S(2)}) collective-permute-start(bf16[2048,256]{1,0:T(8,128)(2,1)} %collective-permute-done.6.refs_11_), channel_id=1, source_target_pairs={{8,0},{16,24},{9,1},{17,25},{10,2},{18,26},{11,3},{19,27},{12,4},{... | collective-permute-start | bytes 3145736 | tf_op jit(solution)/shard_map/ppermute | solution.py:643
  264.0 21.6 %collective-permute-start.5 = (bf16[2048,256]{1,0:T(8,128)(2,1)}, bf16[2048,256]{1,0:T(8,128)(2,1)}, u32[]{:S(2)}, u32[]{:S(2)}) collective-permute-start(bf16[2048,256]{1,0:T(8,128)(2,1)} %collective-permute-done.1.refs_7_), channel_id=1, source_target_pairs={{8,16},{16,8},{9,17},{17,9},{10,18},{18,10},{11,19},{19,11},{12,20... | collective-permute-start | bytes 3145736 | tf_op jit(solution)/shard_map/ppermute | solution.py:649
  276.1 48.2 %collective-permute-start.19 = (bf16[2048,256]{1,0:T(8,128)(2,1)}, bf16[2048,256]{1,0:T(8,128)(2,1)S(1)}, u32[]{:S(2)}, u32[]{:S(2)}) collective-permute-start(bf16[2048,256]{1,0:T(8,128)(2,1)} %collective-permute-done.18.refs_0_), channel_id=1, source_target_pairs={{8,0},{16,24},{9,1},{17,25},{10,2},{18,26},{11,3},{19,27},{12,4},{... | collective-permute-start | bytes 3145736 | tf_op jit(solution)/shard_map/ppermute | solution.py:655
  277.4 56.8 %collective-permute-start.16 = (bf16[2048,256]{1,0:T(8,128)(2,1)}, bf16[2048,256]{1,0:T(8,128)(2,1)S(1)}, u32[]{:S(2)}, u32[]{:S(2)}) collective-permute-start(bf16[2048,256]{1,0:T(8,128)(2,1)} %collective-permute-done.15.refs_0_), channel_id=1, source_target_pairs={{8,0},{16,24},{9,1},{17,25},{10,2},{18,26},{11,3},{19,27},{12,4},{... | collective-permute-start | bytes 3145736 | tf_op jit(solution)/shard_map/ppermute | solution.py:655
  278.7 74.2 %collective-permute-start.12 = (bf16[2048,256]{1,0:T(8,128)(2,1)}, bf16[2048,256]{1,0:T(8,128)(2,1)S(1)}, u32[]{:S(2)}, u32[]{:S(2)}) collective-permute-start(bf16[2048,256]{1,0:T(8,128)(2,1)} %collective-permute-done.11.refs_0_), channel_id=1, source_target_pairs={{8,0},{16,24},{9,1},{17,25},{10,2},{18,26},{11,3},{19,27},{12,4},{... | collective-permute-start | bytes 3145736 | tf_op jit(solution)/shard_map/ppermute | solution.py:655
  285.6 89.8 %collective-permute-start.8 = (bf16[2048,256]{1,0:T(8,128)(2,1)}, bf16[2048,256]{1,0:T(8,128)(2,1)}, u32[]{:S(2)}, u32[]{:S(2)}) collective-permute-start(bf16[2048,256]{1,0:T(8,128)(2,1)} %collective-permute-done.5.refs_0_), channel_id=1, source_target_pairs={{8,0},{16,24},{9,1},{17,25},{10,2},{18,26},{11,3},{19,27},{12,4},{... | collective-permute-start | bytes 3145736 | tf_op jit(solution)/shard_map/ppermute | solution.py:655
  (15 other events, 34.7 us)
Sparse Core Ops, SparseCore 0:
  49.9 171.0 all-gather.2
